TPU v7x, 32 devices: a whole 2x2x4 slice. The times are simulated.
32 devices in a mesh: frag: 8 (over z, x), aux: 4 (over y, core).
Axes of the slice: x: 2, y: 2, z: 4, core: 2. Of those that a mesh axis runs over, the one named last changes fastest.
Arguments:
- vir_grid: bfloat16 [32, 128, 4096], P('frag', None, 'aux'), may hold values from -6 to 6
- vir_energy: bfloat16 [32, 128], P('frag'), may hold values from 0.29882812 to 2.5
- occ_grid: bfloat16 [8, 3, 4096], P('frag', None, 'aux'), may hold values from -0.21875 to 0.21875
- occ_energy: float32 [8, 3], P('frag'), may hold values from -1.5 to -0.3
- vir_list: int32 [8, 8], replicated, may hold values from 0 to 31, as said below
- vir_rows: int32 [8, 8], replicated, may hold values from 32 to 128
- owner_map: int32 [32], replicated, may hold values from 0 to 31, as said below
Outputs:
- density_blocks: float32 [32, 128, 128], P('frag', 'aux')
Inputs may be any that keep to these rules, and one draw needn't show every extreme that they name: A permutation: block b is held in row owner_map[b] of vir_grid and vir_energy, and row s belongs to fragment index s // 4 of frag. `vir_list`: each row names 8 different blocks. For fragment f every named block b has |owner_map[b] // 4 - f| <= 3; at most 2 of them share one value of owner_map[b] // 4, and exactly 2 have the value f.
All inputs are finite; a program needn't handle non-finite values.
Results may differ from a plain program's by a relative error of at most 0.0018.
Values may be sent and summed in bfloat16 or wider, within the bound.
No kernel may reach another device: no remote copies, remote signals or barrier semaphores. Data moves between devices by JAX's collectives and lax.ppermute only.
A program may use at most 128 MiB of HBM per device.

v0:
```python
import jax
import jax.numpy as jnp
from jax import lax
from jax.sharding import PartitionSpec as P

EOS_OCC = 3
REACH = 3
CAP = 2


def from_behind(array, axis, by):
    peers = lax.axis_size(axis)
    pairs = [(i, i + by) for i in range(peers) if 0 <= i + by < peers]
    return lax.ppermute(array, axis, pairs)


def rank_order(owners, member):
    entries = owners.shape[1]
    same = (owners[:, :, None] == owners[:, None, :]) & member[:, None, :]
    earlier = jnp.arange(entries)[None, :] < jnp.arange(entries)[:, None]
    return jnp.sum(same & earlier[None, :, :], axis=2)


def chosen(fragment, owner, owners, keys, ranks, member, slot_count):
    frag_total = owners.shape[0]
    inside = (fragment >= 0) & (fragment < frag_total)
    list_row = jnp.clip(fragment, 0, frag_total - 1)
    wanted = (
        inside & jnp.take(member, list_row, axis=0) & (jnp.take(owners, list_row, axis=0) == owner)
    )
    select = wanted[None, :] & (
        jnp.take(ranks, list_row, axis=0)[None, :] == jnp.arange(slot_count)[:, None]
    )
    present = jnp.any(select, axis=1)
    picked = jnp.sum(jnp.where(select, jnp.take(keys, list_row, axis=0)[None, :], 0), axis=1)
    return (picked, present)


def owner_total(arrived, targets, present, own_count):
    flat_count = targets.size
    onehot = (
        targets.reshape(flat_count)[None, :] == jnp.arange(own_count)[:, None]
    ) & present.reshape(flat_count)[None, :]
    values = arrived.reshape(flat_count, -1)
    summed = jnp.dot(
        onehot.astype(jnp.float32),
        values,
        precision=lax.Precision.HIGHEST,
        preferred_element_type=jnp.float32,
    )
    return summed.reshape((own_count,) + arrived.shape[-2:])


def body(vir_grid, vir_energy, occ_grid, occ_energy, vir_list, vir_rows, owner_map):
    aux_count = lax.axis_size("aux")
    frag_index = lax.axis_index("frag")
    aux_index = lax.axis_index("aux")
    own_count = vir_grid.shape[0]
    block_rows = vir_grid.shape[1]
    aux_cols = vir_grid.shape[2]
    list_len = vir_list.shape[1]
    own_share = list_len // aux_count
    nvir = list_len * block_rows
    rows_here = nvir // aux_count
    slots = jnp.take(owner_map, vir_list, axis=0)
    owners = slots // own_count
    locals_in = slots % own_count
    everyone = jnp.ones(owners.shape, bool)
    positions = jnp.broadcast_to(jnp.arange(list_len, dtype=jnp.int32)[None, :], owners.shape)
    ranks_all = rank_order(owners, everyone)
    own_row = jnp.take(owners, frag_index, axis=0)
    rank_row = jnp.take(ranks_all, frag_index, axis=0)
    grid_stack = []
    energy_stack = []
    for offset in range(-REACH, REACH + 1):
        source, pack_present = chosen(
            frag_index + offset, frag_index, owners, locals_in, ranks_all, everyone, CAP
        )
        grid_part = jnp.where(pack_present[:, None, None], jnp.take(vir_grid, source, axis=0), 0)
        energy_part = jnp.where(pack_present[:, None], jnp.take(vir_energy, source, axis=0), 0)
        grid_part, energy_part = (grid_part, energy_part)
        if offset != 0:
            grid_part, energy_part = from_behind((grid_part, energy_part), "frag", offset)
        grid_stack.append(grid_part)
        energy_stack.append(energy_part)
    grid_came = jnp.stack(grid_stack)
    energy_came = jnp.stack(energy_stack)
    where_from = (frag_index - own_row + REACH) * CAP + rank_row
    grid_frag = jnp.take(grid_came.reshape((-1, block_rows, aux_cols)), where_from, axis=0)
    energy_frag = jnp.take(energy_came.reshape((-1, block_rows)), where_from, axis=0)
    rows_live = jnp.take(vir_rows, frag_index, axis=0)
    live = jnp.arange(block_rows)[None, :] < rows_live[:, None]
    grid_frag = jnp.where(live[:, :, None], grid_frag, 0).reshape(nvir, aux_cols)
    energy_all = energy_frag.astype(jnp.float32).reshape(nvir)
    energy_rows = lax.dynamic_slice_in_dim(energy_all, aux_index * rows_here, rows_here, 0)
    occ_levels = occ_energy[0]
    occ_rows = occ_grid[0].astype(jnp.float32)
    density = jnp.zeros((own_share, block_rows, block_rows), jnp.float32)
    for left_occ in range(EOS_OCC):
        for right_occ in range(left_occ, EOS_OCC):
            weight = occ_rows[left_occ] * occ_rows[right_occ]
            scaled = (grid_frag * weight[None, :]).astype(jnp.bfloat16)

            def pair_term(row_start, row_count, scaled=scaled):
                return lax.dot_general(
                    scaled, grid_frag, (((1,), (1,)), ((), ())), preferred_element_type=jnp.float32
                )

            integrals = lax.psum_scatter(
                pair_term(jnp.int32(0), rows_here * lax.axis_size("aux")),
                "aux",
                scatter_dimension=0,
                tiled=True,
            )
            energy_gap = (
                occ_levels[left_occ]
                + occ_levels[right_occ]
                - energy_rows[:, None]
                - energy_all[None, :]
            )
            amplitude = (
                (integrals / energy_gap).astype(jnp.bfloat16).reshape(own_share, block_rows, nvir)
            )
            density = density + jnp.einsum(
                "kac,kbc->kab", amplitude, amplitude, preferred_element_type=jnp.float32
            )
    pieces = jnp.zeros((list_len, block_rows, block_rows), jnp.float32)
    pieces = lax.dynamic_update_slice_in_dim(pieces, density, aux_index * own_share, 0)
    in_slice = jnp.arange(list_len) // own_share == aux_index
    member = jnp.broadcast_to(in_slice[None, :], owners.shape)
    slot_count = min(CAP, own_share)
    ranks_member = rank_order(owners, member)

    def pack_back(owner):
        entry, present = chosen(
            frag_index, owner, owners, positions, ranks_member, member, slot_count
        )
        return jnp.where(present[:, None, None], jnp.take(pieces, entry, axis=0), 0.0)

    arrived_stack = []
    target_stack = []
    present_stack = []
    for offset in range(-REACH, REACH + 1):
        outgoing = pack_back(frag_index + offset)
        if offset != 0:
            outgoing = from_behind(outgoing, "frag", offset)
        target_row, present_row = chosen(
            frag_index - offset, frag_index, owners, locals_in, ranks_member, member, slot_count
        )
        arrived_stack.append(outgoing)
        target_stack.append(target_row)
        present_stack.append(present_row)
    arrived = jnp.stack(arrived_stack)
    targets = jnp.stack(target_stack)
    present = jnp.stack(present_stack)
    owned = owner_total(arrived, targets, present, own_count)
    return lax.psum_scatter(owned, "aux", scatter_dimension=1, tiled=True)


def solution(mesh):
    return jax.shard_map(
        body,
        mesh=mesh,
        in_specs=(
            P("frag", None, "aux"),
            P("frag", None),
            P("frag", None, "aux"),
            P("frag", None),
            P(),
            P(),
            P(),
        ),
        out_specs=P("frag", "aux", None),
        check_vma=False,
    )
```

profile of v0, /device:TPU:0, one launch (start us, length us, event | category | flops | bytes accessed | tf_op | source)
XLA Modules:
  0.0 440.3 jit_solution(5871164420755740328)
XLA Ops:
  17.8 6.3 %collective-permute-start.3 = (bf16[2,128,1024]{2,1,0:T(8,128)(2,1)}, bf16[2,128,1024]{2,1,0:T(8,128)(2,1)}, u32[]{:S(2)}, u32[]{:S(2)}) collective-permute-start(bf16[2,128,1024]{2,1,0:T(8,128)(2,1)} %select_select_fusion.3), channel_id=1, source_target_pairs={{0,4},{4,8},{8,12},{12,16},{16,20},{20,24},{24,28},{1,5},{5,9},{9,... | collective-permute-start | bytes 1572872 | tf_op jit(solution)/shard_map/ppermute | solution.py:14
  25.9 4.7 %collective-permute-start.4 = (bf16[2,128,1024]{2,1,0:T(8,128)(2,1)}, bf16[2,128,1024]{2,1,0:T(8,128)(2,1)}, u32[]{:S(2)}, u32[]{:S(2)}) collective-permute-start(bf16[2,128,1024]{2,1,0:T(8,128)(2,1)} %select_select_fusion.2), channel_id=1, source_target_pairs={{0,8},{4,12},{8,16},{12,20},{16,24},{20,28},{1,9},{5,13},{9,17},{1... | collective-permute-start | bytes 1572872 | tf_op jit(solution)/shard_map/ppermute | solution.py:14
  34.3 6.2 %collective-permute-start.5 = (bf16[2,128,1024]{2,1,0:T(8,128)(2,1)}, bf16[2,128,1024]{2,1,0:T(8,128)(2,1)S(1)}, u32[]{:S(2)}, u32[]{:S(2)}) collective-permute-start(bf16[2,128,1024]{2,1,0:T(8,128)(2,1)} %select_select_fusion.1), channel_id=1, source_target_pairs={{0,12},{4,16},{8,20},{12,24},{16,28},{1,13},{5,17},{9,21},{13,25},... | collective-permute-start | bytes 1572872 | tf_op jit(solution)/shard_map/ppermute | solution.py:14
  44.0 12.1 %collective-permute-done.3 = bf16[2,128,1024]{2,1,0:T(8,128)(2,1)} collective-permute-done((bf16[2,128,1024]{2,1,0:T(8,128)(2,1)}, bf16[2,128,1024]{2,1,0:T(8,128)(2,1)}, u32[]{:S(2)}, u32[]{:S(2)}) %collective-permute-start.3) | collective-permute-done | bytes 524320 | tf_op jit(solution)/shard_map/ppermute | solution.py:14
  64.9 4.3 fusion.103
  70.8 6.3 %fusion.4 = (bf16[8,128,1024]{2,1,0:T(8,128)(2,1)}, bf16[8,128,1024]{2,1,0:T(8,128)(2,1)}, bf16[8,128,1024]{2,1,0:T(8,128)(2,1)}, bf16[8,128,1024]{2,1,0:T(8,128)(2,1)S(1)}, bf16[8,128,1024]{2,1,0:T(8,128)(2,1)}) fusion(bf16[8,128,1024]{2,1,0:T(8,128)(2,1)S(1)} %copy-done.4, f32[1024]{0:T(1024)S(1)} %bitcast.337, f32[1024]{0:T(1024)S(1)} %bitcast.339, ...), kind=kLoop, calls=%fused_computation.34 | loop fusion | flops 11534336 | bytes 12603392 | tf_op jit(solution)/shard_map/convert_element_type | solution.py:102
  77.1 4.3 fusion.99
  81.7 5.9 %fusion.100 = f32[1024,1024]{1,0:T(8,128)} fusion(bf16[1024,1024]{1,0:T(8,128)(2,1)} %bitcast.333, bf16[1024,1024]{1,0:T(8,128)(2,1)S(1)} %bitcast.319), kind=kOutput, calls=%fused_computation.394 | convolution fusion | flops 2147483648 | bytes 8388608 | tf_op jit(solution)/shard_map/dot_general | solution.py:105
  87.7 6.4 %fusion.101 = f32[1024,1024]{1,0:T(8,128)} fusion(bf16[1024,1024]{1,0:T(8,128)(2,1)} %bitcast.332, bf16[1024,1024]{1,0:T(8,128)(2,1)S(1)} %bitcast.320), kind=kOutput, calls=%fused_computation.395 | convolution fusion | flops 2147483648 | bytes 8388608 | tf_op jit(solution)/shard_map/dot_general | solution.py:105
  94.2 6.0 %fusion.102 = f32[1024,1024]{1,0:T(8,128)} fusion(bf16[1024,1024]{1,0:T(8,128)(2,1)} %bitcast.331, bf16[1024,1024]{1,0:T(8,128)(2,1)S(1)} %bitcast.321), kind=kOutput, calls=%fused_computation.396 | convolution fusion | flops 2147483648 | bytes 8388608 | tf_op jit(solution)/shard_map/dot_general | solution.py:105
  100.3 5.9 %fusion.97 = f32[1024,1024]{1,0:T(8,128)} fusion(bf16[1024,1024]{1,0:T(8,128)(2,1)} %bitcast.330, bf16[1024,1024]{1,0:T(8,128)(2,1)S(1)} %bitcast.322), kind=kOutput, calls=%fused_computation.391 | convolution fusion | flops 2147483648 | bytes 8388608 | tf_op jit(solution)/shard_map/dot_general | solution.py:105
  113.3 5.7 %collective-permute-start.9 = (bf16[2,128]{1,0:T(2,128)(2,1)S(1)}, bf16[2,128]{1,0:T(2,128)(2,1)S(1)}, u32[]{:S(2)}, u32[]{:S(2)}) collective-permute-start(bf16[2,128]{1,0:T(2,128)(2,1)S(1)} %broadcast_select_fusion.41), channel_id=1, source_target_pairs={{0,4},{4,8},{8,12},{12,16},{16,20},{20,24},{24,28},{1,5},{5,9},{9,... | collective-permute-start | bytes 1544 | tf_op jit(solution)/shard_map/ppermute | solution.py:14
  119.6 16.0 %collective-permute-start.10 = (bf16[2,128]{1,0:T(2,128)(2,1)S(1)}, bf16[2,128]{1,0:T(2,128)(2,1)S(1)}, u32[]{:S(2)}, u32[]{:S(2)}) collective-permute-start(bf16[2,128]{1,0:T(2,128)(2,1)S(1)} %broadcast_select_fusion.40), channel_id=1, source_target_pairs={{0,8},{4,12},{8,16},{12,20},{16,24},{20,28},{1,9},{5,13},{9,17},{1... | collective-permute-start | bytes 1544 | tf_op jit(solution)/shard_map/ppermute | solution.py:14
  146.8 6.3 %collective-permute-start.11 = (bf16[2,128]{1,0:T(2,128)(2,1)S(1)}, bf16[2,128]{1,0:T(2,128)(2,1)S(1)}, u32[]{:S(2)}, u32[]{:S(2)}) collective-permute-start(bf16[2,128]{1,0:T(2,128)(2,1)S(1)} %broadcast_select_fusion.39), channel_id=1, source_target_pairs={{0,12},{4,16},{8,20},{12,24},{16,28},{1,13},{5,17},{9,21},{13,25},... | collective-permute-start | bytes 1544 | tf_op jit(solution)/shard_map/ppermute | solution.py:14
  155.1 21.3 %reduce-scatter.9.cloned.1.call-done = f32[256,1024]{1,0:T(8,128)} async-done(((f32[1024,1024]{1,0:T(8,128)}), f32[256,1024]{1,0:T(8,128)}) %reduce-scatter.9.cloned.1.call-update) | async-done | bytes 1048592 | tf_op jit(solution)/shard_map/reduce_scatter | solution.py:109
  176.4 47.1 %reduce-scatter.11.cloned.1.call-done = f32[256,1024]{1,0:T(8,128)} async-done(((f32[1024,1024]{1,0:T(8,128)}), f32[256,1024]{1,0:T(8,128)}) %reduce-scatter.11.cloned.1.call-update) | async-done | bytes 1048592 | tf_op jit(solution)/shard_map/reduce_scatter | solution.py:109
  223.5 47.1 %reduce-scatter.13.cloned.1.call-done = f32[256,1024]{1,0:T(8,128)} async-done(((f32[1024,1024]{1,0:T(8,128)}), f32[256,1024]{1,0:T(8,128)}) %reduce-scatter.13.cloned.1.call-update) | async-done | bytes 1048592 | tf_op jit(solution)/shard_map/reduce_scatter | solution.py:109
  270.5 46.9 %reduce-scatter.15.cloned.1.call-done = f32[256,1024]{1,0:T(8,128)} async-done(((f32[1024,1024]{1,0:T(8,128)}), f32[256,1024]{1,0:T(8,128)}) %reduce-scatter.15.cloned.1.call-update) | async-done | bytes 1048592 | tf_op jit(solution)/shard_map/reduce_scatter | solution.py:109
  317.5 47.1 %reduce-scatter.7.cloned.1.call-done = f32[256,1024]{1,0:T(8,128)} async-done(((f32[1024,1024]{1,0:T(8,128)}), f32[256,1024]{1,0:T(8,128)}) %reduce-scatter.7.cloned.1.call-update) | async-done | bytes 1048592 | tf_op jit(solution)/shard_map/reduce_scatter | solution.py:109
  364.5 3.7 divide_convert_fusion
  377.2 4.6 %collective-permute-start.15 = (f32[2,128,128]{2,1,0:T(8,128)S(1)}, f32[2,128,128]{2,1,0:T(8,128)S(1)}, u32[]{:S(2)}, u32[]{:S(2)}) collective-permute-start(f32[2,128,128]{2,1,0:T(8,128)S(1)} %select_select_fusion.10), channel_id=1, source_target_pairs={{0,4},{4,8},{8,12},{12,16},{16,20},{20,24},{24,28},{1,5},{5,9},{9,... | collective-permute-start | bytes 393224 | tf_op jit(solution)/shard_map/ppermute | solution.py:14
  382.4 4.6 %collective-permute-start.16 = (f32[2,128,128]{2,1,0:T(8,128)S(1)}, f32[2,128,128]{2,1,0:T(8,128)S(1)}, u32[]{:S(2)}, u32[]{:S(2)}) collective-permute-start(f32[2,128,128]{2,1,0:T(8,128)S(1)} %select_select_fusion.9), channel_id=1, source_target_pairs={{0,8},{4,12},{8,16},{12,20},{16,24},{20,28},{1,9},{5,13},{9,17},{1... | collective-permute-start | bytes 393224 | tf_op jit(solution)/shard_map/ppermute | solution.py:14
  387.7 6.3 %collective-permute-start.17 = (f32[2,128,128]{2,1,0:T(8,128)S(1)}, f32[2,128,128]{2,1,0:T(8,128)S(1)}, u32[]{:S(2)}, u32[]{:S(2)}) collective-permute-start(f32[2,128,128]{2,1,0:T(8,128)S(1)} %select_select_fusion.8), channel_id=1, source_target_pairs={{0,12},{4,16},{8,20},{12,24},{16,28},{1,13},{5,17},{9,21},{13,25},... | collective-permute-start | bytes 393224 | tf_op jit(solution)/shard_map/ppermute | solution.py:14
  399.6 32.5 %all-reduce.3.cloned.1.call-done = f32[4,128,128]{2,0,1:T(4,128)} async-done(((f32[4,128,128]{2,0,1:T(4,128)}), f32[4,128,128]{2,0,1:T(4,128)}) %all-reduce.3.cloned.1.call-update) | async-done | bytes 262160
  (231 shorter events, 59.8 us)
Async XLA Ops:
  6.5 148.5 %reduce-scatter.17.cloned.1.call-start = ((), (), s32[]{:S(2)}) async-start(), calls=%async_computation.11 | async-start | bytes 5242880 | tf_op jit(solution)/shard_map/reduce_scatter | solution.py:109
  9.9 24.4 %collective-permute-start = (bf16[2,128,1024]{2,1,0:T(8,128)(2,1)S(1)}, bf16[2,128,1024]{2,1,0:T(8,128)(2,1)}, u32[]{:S(2)}, u32[]{:S(2)}) collective-permute-start(bf16[2,128,1024]{2,1,0:T(8,128)(2,1)S(1)} %select_select_fusion.7), channel_id=1, source_target_pairs={{12,0},{16,4},{20,8},{24,12},{28,16},{13,1},{17,5},{21,9},{25,13},... | collective-permute-start | bytes 1572872 | tf_op jit(solution)/shard_map/ppermute | solution.py:14
  12.3 29.3 %collective-permute-start.1 = (bf16[2,128,1024]{2,1,0:T(8,128)(2,1)S(1)}, bf16[2,128,1024]{2,1,0:T(8,128)(2,1)}, u32[]{:S(2)}, u32[]{:S(2)}) collective-permute-start(bf16[2,128,1024]{2,1,0:T(8,128)(2,1)S(1)} %select_select_fusion.6), channel_id=1, source_target_pairs={{8,0},{12,4},{16,8},{20,12},{24,16},{28,20},{9,1},{13,5},{17,9},{2... | collective-permute-start | bytes 1572872 | tf_op jit(solution)/shard_map/ppermute | solution.py:14
  14.6 28.1 %collective-permute-start.2 = (bf16[2,128,1024]{2,1,0:T(8,128)(2,1)S(1)}, bf16[2,128,1024]{2,1,0:T(8,128)(2,1)}, u32[]{:S(2)}, u32[]{:S(2)}) collective-permute-start(bf16[2,128,1024]{2,1,0:T(8,128)(2,1)S(1)} %select_select_fusion.5), channel_id=1, source_target_pairs={{4,0},{8,4},{12,8},{16,12},{20,16},{24,20},{28,24},{5,1},{9,5},{13... | collective-permute-start | bytes 1572872 | tf_op jit(solution)/shard_map/ppermute | solution.py:14
  17.8 38.3 %collective-permute-start.3 = (bf16[2,128,1024]{2,1,0:T(8,128)(2,1)}, bf16[2,128,1024]{2,1,0:T(8,128)(2,1)}, u32[]{:S(2)}, u32[]{:S(2)}) collective-permute-start(bf16[2,128,1024]{2,1,0:T(8,128)(2,1)} %select_select_fusion.3), channel_id=1, source_target_pairs={{0,4},{4,8},{8,12},{12,16},{16,20},{20,24},{24,28},{1,5},{5,9},{9,... | collective-permute-start | bytes 1572872 | tf_op jit(solution)/shard_map/ppermute | solution.py:14
  25.9 31.3 %collective-permute-start.4 = (bf16[2,128,1024]{2,1,0:T(8,128)(2,1)}, bf16[2,128,1024]{2,1,0:T(8,128)(2,1)}, u32[]{:S(2)}, u32[]{:S(2)}) collective-permute-start(bf16[2,128,1024]{2,1,0:T(8,128)(2,1)} %select_select_fusion.2), channel_id=1, source_target_pairs={{0,8},{4,12},{8,16},{12,20},{16,24},{20,28},{1,9},{5,13},{9,17},{1... | collective-permute-start | bytes 1572872 | tf_op jit(solution)/shard_map/ppermute | solution.py:14
  34.3 24.0 %collective-permute-start.5 = (bf16[2,128,1024]{2,1,0:T(8,128)(2,1)}, bf16[2,128,1024]{2,1,0:T(8,128)(2,1)S(1)}, u32[]{:S(2)}, u32[]{:S(2)}) collective-permute-start(bf16[2,128,1024]{2,1,0:T(8,128)(2,1)} %select_select_fusion.1), channel_id=1, source_target_pairs={{0,12},{4,16},{8,20},{12,24},{16,28},{1,13},{5,17},{9,21},{13,25},... | collective-permute-start | bytes 1572872 | tf_op jit(solution)/shard_map/ppermute | solution.py:14
  69.3 107.1 %reduce-scatter.9.cloned.1.call-start = ((), (), s32[]{:S(2)}) async-start(), calls=%async_computation.7 | async-start | bytes 5242880 | tf_op jit(solution)/shard_map/reduce_scatter | solution.py:109
  81.5 142.0 %reduce-scatter.11.cloned.1.call-start = ((), (), s32[]{:S(2)}) async-start(), calls=%async_computation.8 | async-start | bytes 5242880 | tf_op jit(solution)/shard_map/reduce_scatter | solution.py:109
  87.7 182.9 %reduce-scatter.13.cloned.1.call-start = ((), (), s32[]{:S(2)}) async-start(), calls=%async_computation.9 | async-start | bytes 5242880 | tf_op jit(solution)/shard_map/reduce_scatter | solution.py:109
  94.1 223.3 %reduce-scatter.15.cloned.1.call-start = ((), (), s32[]{:S(2)}) async-start(), calls=%async_computation.10 | async-start | bytes 5242880 | tf_op jit(solution)/shard_map/reduce_scatter | solution.py:109
  100.2 264.3 %reduce-scatter.7.cloned.1.call-start = ((), (), s32[]{:S(2)}) async-start(), calls=%async_computation.6 | async-start | bytes 5242880 | tf_op jit(solution)/shard_map/reduce_scatter | solution.py:109
  106.2 325.8 %all-reduce.3.cloned.1.call-start = ((), (), s32[]{:S(2)}) async-start(), calls=%async_computation.12 | async-start | bytes 524288
  107.5 39.2 %collective-permute-start.6 = (bf16[2,128]{1,0:T(2,128)(2,1)S(1)}, bf16[2,128]{1,0:T(2,128)(2,1)S(1)}, u32[]{:S(2)}, u32[]{:S(2)}) collective-permute-start(bf16[2,128]{1,0:T(2,128)(2,1)S(1)} %broadcast_select_fusion.45), channel_id=1, source_target_pairs={{12,0},{16,4},{20,8},{24,12},{28,16},{13,1},{17,5},{21,9},{25,13},... | collective-permute-start | bytes 1544 | tf_op jit(solution)/shard_map/ppermute | solution.py:14
  109.5 43.6 %collective-permute-start.7 = (bf16[2,128]{1,0:T(2,128)(2,1)S(1)}, bf16[2,128]{1,0:T(2,128)(2,1)S(1)}, u32[]{:S(2)}, u32[]{:S(2)}) collective-permute-start(bf16[2,128]{1,0:T(2,128)(2,1)S(1)} %broadcast_select_fusion.44), channel_id=1, source_target_pairs={{8,0},{12,4},{16,8},{20,12},{24,16},{28,20},{9,1},{13,5},{17,9},{2... | collective-permute-start | bytes 1544 | tf_op jit(solution)/shard_map/ppermute | solution.py:14
  111.4 41.7 %collective-permute-start.8 = (bf16[2,128]{1,0:T(2,128)(2,1)S(1)}, bf16[2,128]{1,0:T(2,128)(2,1)S(1)}, u32[]{:S(2)}, u32[]{:S(2)}) collective-permute-start(bf16[2,128]{1,0:T(2,128)(2,1)S(1)} %broadcast_select_fusion.43), channel_id=1, source_target_pairs={{4,0},{8,4},{12,8},{16,12},{20,16},{24,20},{28,24},{5,1},{9,5},{13... | collective-permute-start | bytes 1544 | tf_op jit(solution)/shard_map/ppermute | solution.py:14
  113.3 39.9 %collective-permute-start.9 = (bf16[2,128]{1,0:T(2,128)(2,1)S(1)}, bf16[2,128]{1,0:T(2,128)(2,1)S(1)}, u32[]{:S(2)}, u32[]{:S(2)}) collective-permute-start(bf16[2,128]{1,0:T(2,128)(2,1)S(1)} %broadcast_select_fusion.41), channel_id=1, source_target_pairs={{0,4},{4,8},{8,12},{12,16},{16,20},{20,24},{24,28},{1,5},{5,9},{9,... | collective-permute-start | bytes 1544 | tf_op jit(solution)/shard_map/ppermute | solution.py:14
  119.6 33.6 %collective-permute-start.10 = (bf16[2,128]{1,0:T(2,128)(2,1)S(1)}, bf16[2,128]{1,0:T(2,128)(2,1)S(1)}, u32[]{:S(2)}, u32[]{:S(2)}) collective-permute-start(bf16[2,128]{1,0:T(2,128)(2,1)S(1)} %broadcast_select_fusion.40), channel_id=1, source_target_pairs={{0,8},{4,12},{8,16},{12,20},{16,24},{20,28},{1,9},{5,13},{9,17},{1... | collective-permute-start | bytes 1544 | tf_op jit(solution)/shard_map/ppermute | solution.py:14
  370.8 16.9 %collective-permute-start.12 = (f32[2,128,128]{2,1,0:T(8,128)S(1)}, f32[2,128,128]{2,1,0:T(8,128)S(1)}, u32[]{:S(2)}, u32[]{:S(2)}) collective-permute-start(f32[2,128,128]{2,1,0:T(8,128)S(1)} %select_select_fusion.14), channel_id=1, source_target_pairs={{12,0},{16,4},{20,8},{24,12},{28,16},{13,1},{17,5},{21,9},{25,13},... | collective-permute-start | bytes 393224 | tf_op jit(solution)/shard_map/ppermute | solution.py:14
  372.7 21.3 %collective-permute-start.13 = (f32[2,128,128]{2,1,0:T(8,128)S(1)}, f32[2,128,128]{2,1,0:T(8,128)S(1)}, u32[]{:S(2)}, u32[]{:S(2)}) collective-permute-start(f32[2,128,128]{2,1,0:T(8,128)S(1)} %select_select_fusion.13), channel_id=1, source_target_pairs={{8,0},{12,4},{16,8},{20,12},{24,16},{28,20},{9,1},{13,5},{17,9},{2... | collective-permute-start | bytes 393224 | tf_op jit(solution)/shard_map/ppermute | solution.py:14
  374.7 19.4 %collective-permute-start.14 = (f32[2,128,128]{2,1,0:T(8,128)S(1)}, f32[2,128,128]{2,1,0:T(8,128)S(1)}, u32[]{:S(2)}, u32[]{:S(2)}) collective-permute-start(f32[2,128,128]{2,1,0:T(8,128)S(1)} %select_select_fusion.12), channel_id=1, source_target_pairs={{4,0},{8,4},{12,8},{16,12},{20,16},{24,20},{28,24},{5,1},{9,5},{13... | collective-permute-start | bytes 393224 | tf_op jit(solution)/shard_map/ppermute | solution.py:14
  377.2 17.0 %collective-permute-start.15 = (f32[2,128,128]{2,1,0:T(8,128)S(1)}, f32[2,128,128]{2,1,0:T(8,128)S(1)}, u32[]{:S(2)}, u32[]{:S(2)}) collective-permute-start(f32[2,128,128]{2,1,0:T(8,128)S(1)} %select_select_fusion.10), channel_id=1, source_target_pairs={{0,4},{4,8},{8,12},{12,16},{16,20},{20,24},{24,28},{1,5},{5,9},{9,... | collective-permute-start | bytes 393224 | tf_op jit(solution)/shard_map/ppermute | solution.py:14
  382.4 11.8 %collective-permute-start.16 = (f32[2,128,128]{2,1,0:T(8,128)S(1)}, f32[2,128,128]{2,1,0:T(8,128)S(1)}, u32[]{:S(2)}, u32[]{:S(2)}) collective-permute-start(f32[2,128,128]{2,1,0:T(8,128)S(1)} %select_select_fusion.9), channel_id=1, source_target_pairs={{0,8},{4,12},{8,16},{12,20},{16,24},{20,28},{1,9},{5,13},{9,17},{1... | collective-permute-start | bytes 393224 | tf_op jit(solution)/shard_map/ppermute | solution.py:14
  387.7 8.8 %collective-permute-start.17 = (f32[2,128,128]{2,1,0:T(8,128)S(1)}, f32[2,128,128]{2,1,0:T(8,128)S(1)}, u32[]{:S(2)}, u32[]{:S(2)}) collective-permute-start(f32[2,128,128]{2,1,0:T(8,128)S(1)} %select_select_fusion.8), channel_id=1, source_target_pairs={{0,12},{4,16},{8,20},{12,24},{16,28},{1,13},{5,17},{9,21},{13,25},... | collective-permute-start | bytes 393224 | tf_op jit(solution)/shard_map/ppermute | solution.py:14
  (12 other events, 106.0 us)
Sparse Core Ops, SparseCore 0:
  69.4 59.7 reduce-scatter.16
  131.8 44.4 reduce-scatter.8
  178.9 44.5 reduce-scatter.10
  226.0 44.4 reduce-scatter.12
  272.9 44.5 reduce-scatter.14
  320.0 44.4 reduce-scatter.6
  398.4 33.5 all-reduce.2
where the time goes:
time: 442 us; the launch traced here: 440 us
  waiting for transfers between devices  258 us (58%)
  starting transfers between devices  72.6 us (16%)
  matrix products  36.4 us (8%)
  local copies, waits for them, and re-layouts  29.9 us (7%)
  between operations  23.1 us (5%)
  other arithmetic  20.8 us (5%)
    reduce_scatter x6, waiting for transfers between devices, body(): lax.psum_scatter(pair_term(jnp.int32(0), rows_here * lax.axis_size('aux')...  209 us
    ppermute x18, starting transfers between devices, from_behind(): return lax.ppermute(array, axis, pairs)  72.2 us
    dot_general x6, matrix products, pair_term(): lax.dot_general(scaled, grid_frag, (((1,), (1,)), ((), ())), preferred_el...  32.9 us
    unnamed x8, waiting for transfers between devices  32.6 us
    ppermute x18, waiting for transfers between devices, from_behind(): return lax.ppermute(array, axis, pairs)  15.5 us
    unnamed x39, local copies, waits for them, and re-layouts  12.2 us
  transfers between devices with their start and end apart: 25, of which 9 were waited for; matrix products, arithmetic and copies ran while one was open for 14% of the time, Pallas kernels for 0%

commit v1 on v0

v1 whole, which is shorter than its diff:
```python
import functools

import jax
import jax.numpy as jnp
from jax import lax
from jax.experimental import pallas as pl
from jax.experimental.pallas import tpu as pltpu
from jax.sharding import PartitionSpec as P

ROUNDS = ((1, 0), (1, 1), (2, 0), (2, 1), (3, 0), (3, 1))
CAP = 2
PAIRS = tuple((i, j) for i in range(3) for j in range(i, 3))
VMEM_LIMIT = 56 * 2**20
ANY = pl.BlockSpec(memory_space=pl.ANY)
SMEM = pl.BlockSpec(memory_space=pltpu.SMEM)
VMEM = pl.BlockSpec(memory_space=pltpu.VMEM)


def round_pairs(distance, parity, frags):
    up = [(i, i + distance) for i in range(frags - distance) if (i // distance) % 2 == parity]
    return up + [(b, a) for a, b in up]


def plan_kernel(frags, own_count, list_len, me_ref, map_ref, list_ref, table, *refs):
    outs, own, plan, sems = refs[:6], refs[6], refs[7], refs[8]
    me = me_ref[0]
    copies = []

    def pick(fragment, owner):
        count = jnp.int32(0)
        picked = [jnp.int32(0)] * CAP
        for k in range(list_len):
            row = map_ref[list_ref[fragment, k]]
            hit = row // own_count == owner
            for r in range(CAP):
                picked[r] = jnp.where(hit & (count == r), row % own_count, picked[r])
            count = count + hit.astype(jnp.int32)
        return picked, count

    for index, (distance, parity) in enumerate(ROUNDS):
        up = (me // distance) % 2 == parity
        partner = jnp.where(up, me + distance, me - distance)
        inside = (partner >= 0) & (partner < frags)
        picked, count = pick(jnp.clip(partner, 0, frags - 1), me)
        for r in range(CAP):
            copies.append((
                inside & (count > r),
                pltpu.make_async_copy(table.at[picked[r]], outs[index].at[r], sems.at[index, r]),
            ))
        if index == 0:
            picked, count = pick(me, me)
            for r in range(CAP):
                copies.append((
                    count > r,
                    pltpu.make_async_copy(table.at[picked[r]], own.at[r], sems.at[6, r]),
                ))
    for needed, copy in copies:
        pl.when(needed)(copy.start)

    rows, owners, codes, classes = [], [], [], []
    for k in range(list_len):
        row = map_ref[list_ref[me, k]]
        owner = row // own_count
        low = jnp.minimum(me, owner)
        far = jnp.abs(owner - me)
        code = jnp.int32(0)
        for index, (distance, parity) in enumerate(ROUNDS):
            code = jnp.where(
                (far == distance) & ((low // distance) % 2 == parity), index + 1, code
            )
        rows.append(row)
        owners.append(owner)
        codes.append(code)
        classes.append(jnp.where(code == 0, 0, jnp.maximum(code - 3, 1)))
    for k in range(list_len):
        place = jnp.int32(0)
        rank = jnp.int32(0)
        for j in range(list_len):
            if j < k:
                place += (classes[j] <= classes[k]).astype(jnp.int32)
                rank += (owners[j] == owners[k]).astype(jnp.int32)
            elif j > k:
                place += (classes[j] < classes[k]).astype(jnp.int32)
        plan[0, place] = codes[k]
        plan[1, place] = rank
        plan[2, place] = rows[k]
        plan[3, place] = jnp.int32(k)
    for needed, copy in copies:
        pl.when(needed)(copy.wait)


def plan_and_pack(me, owner_map, vir_list, table, frags):
    own_count, block_rows, cols = table.shape
    list_len = vir_list.shape[1]
    part = jax.ShapeDtypeStruct((CAP, block_rows, cols), table.dtype)
    return pl.pallas_call(
        functools.partial(plan_kernel, frags, own_count, list_len),
        out_shape=(part,) * 7 + (jax.ShapeDtypeStruct((4, list_len), jnp.int32),),
        in_specs=[SMEM, SMEM, SMEM, ANY],
        out_specs=(ANY,) * 7 + (SMEM,),
        scratch_shapes=[pltpu.SemaphoreType.DMA((7, CAP))],
        name="plan_and_pack",
    )(me, owner_map, vir_list, table)


def pack_kernel(first, codes, plan, *refs):
    arrived, out, sems = refs[: len(codes)], refs[len(codes)], refs[len(codes) + 1]
    for i in range(2):
        code = plan[0, first + i]
        rank = plan[1, first + i]
        for source, ref in zip(codes, arrived):

            @pl.when(code == source)
            def _(ref=ref):
                pltpu.make_async_copy(ref.at[rank], out.at[i], sems.at[i]).start()

    for i in range(2):
        pltpu.make_async_copy(arrived[0].at[0], out.at[i], sems.at[i]).wait()


def pack_group(first, plan, arrived):
    codes = tuple(arrived)
    refs = [arrived[c] for c in codes]
    return pl.pallas_call(
        functools.partial(pack_kernel, first, codes),
        out_shape=jax.ShapeDtypeStruct(refs[0].shape, refs[0].dtype),
        in_specs=[SMEM] + [ANY] * len(refs),
        out_specs=ANY,
        scratch_shapes=[pltpu.SemaphoreType.DMA((2,))],
        name="pack_group",
    )(plan, *refs)


def contract_kernel(
    list_len, block, width, where, plan, levels, rows_ref, weights, energy, *refs
):
    groups = list_len // 2
    parts, (out, grid, scaled, total, amps, sems) = refs[: groups * 4], refs[groups * 4 :]
    me, aux = where[0], where[1]
    quarter_of = (aux, aux ^ 2, aux ^ 1, aux ^ 3)
    copies = {}
    for quarter in range(4):
        for group in range(groups):
            for i in range(2):
                copy = pltpu.make_async_copy(
                    parts[group * 4 + quarter].at[i],
                    grid.at[pl.ds((group * 2 + i) * block, block), pl.ds(quarter * width, width)],
                    sems.at[quarter, group, i],
                )
                copy.start()
                copies[quarter, group, i] = copy
    nvir = list_len * block
    mine = (aux, list_len - 1 - aux)
    for quarter in range(4):
        for group in range(groups):
            for i in range(2):
                copies[quarter, group, i].wait()
        cols = pl.ds(quarter * width, width)
        begin = pl.multiple_of(quarter_of[quarter] * width, width)
        occ = [weights[i : i + 1, pl.ds(begin, width)] for i in range(3)]
        for b in range(2):
            left = grid[pl.ds(pl.multiple_of(mine[b] * block, block), block), cols].astype(
                jnp.float32
            )
            for p, (i, j) in enumerate(PAIRS):
                scaled[pl.ds((p * 2 + b) * block, block), :] = (
                    left * (occ[i] * occ[j])
                ).astype(jnp.bfloat16)

        def rows_step(step, carry, quarter=quarter, cols=cols):
            rows = pl.ds(pl.multiple_of(step * 512, 512), 512)
            for half in range(2):
                right = pl.ds(half * 512, 512)
                term = lax.dot_general(
                    scaled[rows, :],
                    grid[right, cols],
                    (((1,), (1,)), ((), ())),
                    preferred_element_type=jnp.float32,
                )
                if quarter == 0:
                    total[rows, right] = term
                else:
                    total[rows, right] += term
            return carry

        lax.fori_loop(0, 3, rows_step, 0)

    lane = lax.broadcasted_iota(jnp.int32, (block, block), 1)
    sub = lax.broadcasted_iota(jnp.int32, (block, block), 0)
    for b in range(2):
        own_row = energy[pl.ds(plan[2, mine[b]], 1), :]
        own_energy = jnp.transpose(jnp.broadcast_to(own_row, (block, block)))
        own_live = sub < rows_ref[me, plan[3, mine[b]]]
        for q in range(list_len):
            their_energy = energy[pl.ds(plan[2, q], 1), :]
            live = own_live & (lane < rows_ref[me, plan[3, q]])
            for p, (i, j) in enumerate(PAIRS):
                gap = (levels[0, i] + levels[0, j]) - own_energy - their_energy
                value = total[pl.ds((p * 2 + b) * block, block), pl.ds(q * block, block)]
                amps[:, pl.ds(p * nvir + q * block, block)] = jnp.where(
                    live, value / gap, 0.0
                ).astype(jnp.bfloat16)
        out[b] = lax.dot_general(
            amps[...], amps[...], (((1,), (1,)), ((), ())), preferred_element_type=jnp.float32
        )


def contract(where, plan, levels, vir_rows, weights, energy, parts):
    list_len = vir_rows.shape[1]
    block, width = parts[0].shape[1:]
    nvir = list_len * block
    pair_count = len(PAIRS)
    flops = 2 * pair_count * 2 * block * nvir * 4 * width
    return pl.pallas_call(
        functools.partial(contract_kernel, list_len, block, width),
        out_shape=jax.ShapeDtypeStruct((2, block, block), jnp.float32),
        in_specs=[SMEM, SMEM, SMEM, SMEM, VMEM, VMEM] + [ANY] * len(parts),
        out_specs=VMEM,
        scratch_shapes=[
            pltpu.VMEM((nvir, 4 * width), jnp.bfloat16),
            pltpu.VMEM((pair_count * 2 * block, width), jnp.bfloat16),
            pltpu.VMEM((pair_count * 2 * block, nvir), jnp.float32),
            pltpu.VMEM((block, pair_count * nvir), jnp.bfloat16),
            pltpu.SemaphoreType.DMA((4, list_len // 2, 2)),
        ],
        compiler_params=pltpu.CompilerParams(vmem_limit_bytes=VMEM_LIMIT),
        cost_estimate=pl.CostEstimate(
            flops=flops, bytes_accessed=nvir * 4 * width * 2, transcendentals=0
        ),
        name="contract",
    )(where, plan, levels, vir_rows, weights, energy, *parts)


def spread_kernel(own_count, list_len, where, plan, kept, came, out):
    aux = where[1]
    out[...] = jnp.zeros_like(out)
    holders = (aux, aux ^ 2, aux ^ 1, aux ^ 3)
    for index, holder in enumerate(holders):
        source = kept if index < 2 else came
        for b in range(2):
            place = holder if b == 0 else list_len - 1 - holder
            out[plan[2, place] // own_count, plan[1, place]] = source[2 * (index % 2) + b]


def spread(where, plan, kept, came, frags, own_count, list_len):
    return pl.pallas_call(
        functools.partial(spread_kernel, own_count, list_len),
        out_shape=jax.ShapeDtypeStruct((frags, CAP) + kept.shape[1:], kept.dtype),
        in_specs=[SMEM, SMEM, VMEM, VMEM],
        out_specs=VMEM,
        name="spread",
    )(where, plan, kept, came)


def collect_kernel(own_count, list_len, where, map_ref, list_ref, came, out):
    me = where[0]
    out[...] = jnp.zeros_like(out)

    def one(fragment, carry):
        count = jnp.int32(0)
        for k in range(list_len):
            row = map_ref[list_ref[fragment, k]]
            hit = row // own_count == me

            @pl.when(hit)
            def _(row=row, count=count):
                out[row % own_count] += came[fragment, count]

            count = count + hit.astype(jnp.int32)
        return carry

    lax.fori_loop(0, list_ref.shape[0], one, 0)


def collect(where, owner_map, vir_list, came, own_count):
    return pl.pallas_call(
        functools.partial(collect_kernel, own_count, vir_list.shape[1]),
        out_shape=jax.ShapeDtypeStruct((own_count,) + came.shape[2:], came.dtype),
        in_specs=[SMEM, SMEM, SMEM, VMEM],
        out_specs=VMEM,
        name="collect",
    )(where, owner_map, vir_list, came)


def body(vir_grid, vir_energy, occ_grid, occ_energy, vir_list, vir_rows, owner_map):
    frags = lax.axis_size("frag")
    aux_count = lax.axis_size("aux")
    me = lax.axis_index("frag").astype(jnp.int32)
    aux = lax.axis_index("aux").astype(jnp.int32)
    own_count, block, width = vir_grid.shape
    list_len = vir_list.shape[1]
    where = jnp.stack([me, aux])
    far_pairs = [(i, i ^ 2) for i in range(aux_count)]
    near_pairs = [(i, i ^ 1) for i in range(aux_count)]

    energy = lax.psum(
        lax.dynamic_update_slice(
            jnp.zeros((frags * own_count, block), jnp.float32),
            vir_energy.astype(jnp.float32),
            (me * own_count, 0),
        ),
        "frag",
    )
    weights = lax.psum(
        lax.dynamic_update_slice(
            jnp.zeros((occ_grid.shape[1], aux_count * width), jnp.float32),
            occ_grid[0].astype(jnp.float32),
            (0, aux * width),
        ),
        "aux",
    )
    *outgoing, own, plan = plan_and_pack(where, owner_map, vir_list, vir_grid, frags)
    arrived = {}
    for index, (distance, parity) in enumerate(ROUNDS):
        payload = outgoing[index]
        if index >= 4:
            payload = lax.optimization_barrier((payload, arrived[index - 3]))[0]
        arrived[index + 1] = lax.ppermute(
            payload, "frag", round_pairs(distance, parity, frags)
        )
    parts = []
    for group in range(list_len // 2):
        if group == 0:
            here = own
        else:
            known = {c: arrived[c] for c in range(1, 4 + group)}
            here = pack_group(2 * group, plan, known)
        far = lax.ppermute(here, "aux", far_pairs)
        near = lax.ppermute(here, "aux", near_pairs)
        far_near = lax.ppermute(far, "aux", near_pairs)
        parts += [here, far, near, far_near]
    density = contract(where, plan, occ_energy, vir_rows, weights, energy, parts)

    half = block // 2
    quarter = block // aux_count
    side = aux // 2
    sent = lax.dynamic_slice_in_dim(density, (1 - side) * half, half, 1)
    stay = lax.dynamic_slice_in_dim(density, side * half, half, 1)
    both = jnp.concatenate([stay, lax.ppermute(sent, "aux", far_pairs)], axis=0)
    core = aux % 2
    sent = lax.dynamic_slice_in_dim(both, (1 - core) * quarter, quarter, 1)
    kept = lax.dynamic_slice_in_dim(both, core * quarter, quarter, 1)
    came = lax.ppermute(sent, "aux", near_pairs)
    outgoing = spread(where, plan, kept, came, frags, own_count, list_len)
    incoming = lax.all_to_all(outgoing, "frag", 0, 0, tiled=True)
    return collect(where, owner_map, vir_list, incoming, own_count)


def solution(mesh):
    return jax.shard_map(
        body,
        mesh=mesh,
        in_specs=(
            P("frag", None, "aux"),
            P("frag", None),
            P("frag", None, "aux"),
            P("frag", None),
            P(),
            P(),
            P(),
        ),
        out_specs=P("frag", "aux", None),
        check_vma=False,
    )
```

time: 442 us -> 293 us (0.66)
  waiting for transfers between devices: 258 us -> 15.4 us
  Pallas kernels: 0 us -> 123 us
  blocking collectives: 0 us -> 61.6 us
  matrix products: 36.4 us -> 0 us
  local copies, waits for them, and re-layouts: 29.9 us -> 4.98 us
  between operations: 23.1 us -> 0.27 us
  other arithmetic: 20.8 us -> 1.21 us
  starting transfers between devices: 72.6 us -> 86.5 us
    reduce_scatter x6 -> x0, waiting for transfers between devices: 209 us -> none  [body(): lax.psum_scatter(pair_term(jnp.int32(0), rows_here * lax.axis_size('aux')...]
    pallas_call x0 -> x7, Pallas kernels: none -> 123 us  [the longest x3 53.1 us: pack_group(): pl.pallas_call(functools.partial(pack_kernel, first, codes), out_shape=ja...]
    psum x0 -> x2, blocking collectives: none -> 48 us  [the longest x1 36.8 us: body(): lax.psum(lax.dynamic_update_slice(jnp.zeros((frags * own_count, block), j...]
    dot_general x13 -> x0, matrix products: 36.4 us -> none  [the longest x6 32.9 us: pair_term(): lax.dot_general(scaled, grid_frag, (((1,), (1,)), ((), ())), preferred_el...]
    unnamed x8 -> x0, waiting for transfers between devices: 32.6 us -> none
    gather x25 -> x0, local copies, waits for them, and re-layouts: 16 us -> none  [the longest x7 4.06 us: body(): jnp.take(vir_grid, source, axis=0)]
    ppermute x18 -> x20, starting transfers between devices: 72.2 us -> 86.5 us  [the longest x6 77.8 us: body(): lax.ppermute(payload, 'frag', round_pairs(distance, parity, frags))]
    all_to_all x0 -> x1, blocking collectives: none -> 13.5 us  [body(): incoming = lax.all_to_all(outgoing, 'frag', 0, 0, tiled=True)]
  transfers between devices with their start and end apart: 25 -> 20, of which waited for: 9 -> 3; matrix products, arithmetic and copies ran while one was open for 14% -> 0% of each run, Pallas kernels for 0% -> 18%
where the time goes in v1:
time: 293 us
  Pallas kernels  123 us (42%)
  starting transfers between devices  86.5 us (30%)
  blocking collectives  61.6 us (21%)
  waiting for transfers between devices  15.4 us (5%)
  local copies, waits for them, and re-layouts  4.98 us (2%)
    ppermute x6, starting transfers between devices, body(): lax.ppermute(payload, 'frag', round_pairs(distance, parity, frags))  77.8 us
    pallas_call x3, Pallas kernels, pack_group(): pl.pallas_call(functools.partial(pack_kernel, first, codes), out_shape=ja...  53.1 us
    pallas_call x1, Pallas kernels, plan_and_pack(): pl.pallas_call(functools.partial(plan_kernel, frags, own_count, list_len)...  42.4 us
    psum x1, blocking collectives, body(): lax.psum(lax.dynamic_update_slice(jnp.zeros((frags * own_count, block), j...  36.8 us
    pallas_call x1, Pallas kernels, contract(): pl.pallas_call(functools.partial(contract_kernel, list_len, block, width)...  22.7 us
    all_to_all x1, blocking collectives, body(): incoming = lax.all_to_all(outgoing, 'frag', 0, 0, tiled=True)  13.5 us
    ppermute x4, waiting for transfers between devices, body(): far = lax.ppermute(here, 'aux', far_pairs)  11.6 us
    psum x1, blocking collectives, body(): lax.psum(lax.dynamic_update_slice(jnp.zeros((occ_grid.shape[1], aux_count...  11.2 us
  transfers between devices with their start and end apart: 20, of which 3 were waited for; matrix products, arithmetic and copies ran while one was open for 0% of the time, Pallas kernels for 18%

profile of v1, /device:TPU:0, one launch (start us, length us, event | category | flops | bytes accessed | tf_op | source)
XLA Modules:
  0.0 292.7 jit_solution(1571397842841556939)
XLA Ops:
  0.6 42.4 %plan_and_pack.1 = (bf16[2,128,1024]{2,1,0:T(8,128)(2,1)}, bf16[2,128,1024]{2,1,0:T(8,128)(2,1)}, bf16[2,128,1024]{2,1,0:T(8,128)(2,1)}, bf16[2,128,1024]{2,1,0:...) custom-call(s32[2]{0:T(128)} %pad_add_fusion.me_ref.where, ...), custom_call_target="tpu_custom_call" | custom-call | tf_op jit(solution)/shard_map/plan_and_pack/pallas_call | solution.py:96
  43.0 10.9 %collective-permute-start.3 = (bf16[2,128,1024]{2,1,0:T(8,128)(2,1)}, bf16[2,128,1024]{2,1,0:T(8,128)(2,1)S(1)}, u32[]{:S(2)}, u32[]{:S(2)}) collective-permute-start(bf16[2,128,1024]{2,1,0:T(8,128)(2,1)} %get-tuple-element.17), channel_id=1, source_target_pairs={{0,4},{8,12},{16,20},{24,28},{4,0},{12,8},{20,16},{28,24},{1,5},{9... | collective-permute-start | bytes 1572872 | tf_op jit(solution)/shard_map/ppermute | solution.py:318
  53.9 0.7 collective-permute-start.4
  54.6 42.6 %collective-permute-start.5 = (bf16[2,128,1024]{2,1,0:T(8,128)(2,1)}, bf16[2,128,1024]{2,1,0:T(8,128)(2,1)S(1)}, u32[]{:S(2)}, u32[]{:S(2)}) collective-permute-start(bf16[2,128,1024]{2,1,0:T(8,128)(2,1)} %get-tuple-element.19), channel_id=1, source_target_pairs={{0,8},{4,12},{16,24},{20,28},{8,0},{12,4},{24,16},{28,20},{1,9},{5... | collective-permute-start | bytes 1572872 | tf_op jit(solution)/shard_map/ppermute | solution.py:318
  97.9 1.6 collective-permute-start
  99.5 22.2 %collective-permute-start.10 = (bf16[2,128,1024]{2,1,0:T(8,128)(2,1)}, bf16[2,128,1024]{2,1,0:T(8,128)(2,1)S(1)}, u32[]{:S(2)}, u32[]{:S(2)}) collective-permute-start(bf16[2,128,1024]{2,1,0:T(8,128)(2,1)} %get-tuple-element.22), channel_id=1, source_target_pairs={{0,12},{4,16},{8,20},{12,0},{16,4},{20,8},{1,13},{5,17},{9,21},{13... | collective-permute-start | bytes 1572872 | tf_op jit(solution)/shard_map/ppermute | solution.py:318
  121.7 0.7 collective-permute-start.14
  123.4 17.7 %pack_group.3.refs_4_ = bf16[2,128,1024]{2,1,0:T(8,128)(2,1)} custom-call(s32[4,8]{1,0:T(4,128)} %get-tuple-element.15.plan, bf16[2,128,1024]{2,1,0:T(8,128)(2,1)} %copy-done, bf16[2,128,1024]{2,1,0:T(8,128)(2,1)} %copy-done.1, bf16[2,128,1024]{2,1,0:T(8,128)(2,1)} %copy-done.2, bf16[2,128,1024]{2,1,0:T(8,128)(2,1)} %copy-done.3), custom_call_target="tpu_custom_call" | custom-call | tf_op jit(solution)/shard_map/pack_group/pallas_call | solution.py:124
  141.1 1.6 collective-permute-start.7
  143.6 0.8 copy-done.6
  144.4 17.7 %pack_group.5.refs_12_ = bf16[2,128,1024]{2,1,0:T(8,128)(2,1)} custom-call(s32[4,8]{1,0:T(4,128)} %get-tuple-element.15.plan, bf16[2,128,1024]{2,1,0:T(8,128)(2,1)} %copy-done, bf16[2,128,1024]{2,1,0:T(8,128)(2,1)} %copy-done.1, bf16[2,128,1024]{2,1,0:T(8,128)(2,1)} %copy-done.2, bf16[2,128,1024]{2,1,0:T(8,128)(2,1)} %copy-done.3, ...), custom_call_target="tpu_custom_call" | custom-call | tf_op jit(solution)/shard_map/pack_group/pallas_call | solution.py:124
  162.7 17.7 %pack_group.4.refs_8_ = bf16[2,128,1024]{2,1,0:T(8,128)(2,1)} custom-call(s32[4,8]{1,0:T(4,128)} %get-tuple-element.15.plan, bf16[2,128,1024]{2,1,0:T(8,128)(2,1)} %copy-done, bf16[2,128,1024]{2,1,0:T(8,128)(2,1)} %copy-done.1, bf16[2,128,1024]{2,1,0:T(8,128)(2,1)} %copy-done.2, bf16[2,128,1024]{2,1,0:T(8,128)(2,1)} %copy-done.3, bf16[2,128,1024]{2,1,0:T(8,128)(2,1)} %copy-done.4), custom_call_target="tpu_custom_call" | custom-call | tf_op jit(solution)/shard_map/pack_group/pallas_call | solution.py:124
  180.4 1.6 collective-permute-start.11
  183.1 11.6 %collective-permute-done.11.refs_9_ = bf16[2,128,1024]{2,1,0:T(8,128)(2,1)S(1)} collective-permute-done((bf16[2,128,1024]{2,1,0:T(8,128)(2,1)}, bf16[2,128,1024]{2,1,0:T(8,128)(2,1)S(1)}, u32[]{:S(2)}, u32[]{:S(2)}) %collective-permute-start.11) | collective-permute-done | bytes 524320 | tf_op jit(solution)/shard_map/ppermute | solution.py:328
  195.4 36.8 %psum.15.energy = f32[32,128]{1,0:T(8,128)} all-reduce(f32[32,128]{1,0:T(8,128)S(1)} %convert_dynamic-update-slice_fusion.1), channel_id=1, replica_groups=mesh['frag'=8,'aux'=4] {'frag'}, use_global_device_ids=true, to_apply=%region_1.0 | all-reduce | flops 4096 | bytes 32768 | tf_op jit(solution)/shard_map/psum | solution.py:296
  232.9 11.2 %psum.14.weights = f32[3,4096]{1,0:T(4,128)} all-reduce(f32[3,4096]{1,0:T(4,128)S(1)} %convert_dynamic-update-slice_fusion), channel_id=1, replica_groups=mesh['frag'=8,'aux'=4] {'aux'}, use_global_device_ids=true, to_apply=%region_0.0 | all-reduce | flops 12288 | bytes 98304 | tf_op jit(solution)/shard_map/psum | solution.py:304
  244.2 22.7 %contract.1 = f32[2,128,128]{2,1,0:T(8,128)} custom-call(s32[2]{0:T(128)} %pad_add_fusion.me_ref.where, s32[4,8]{1,0:T(4,128)} %get-tuple-element.15.plan, f32[1,3]{1,0:T(1,128)} %levels.1, s32[8,8]{1,0:T(8,128)} %rows_ref.1, f32[3,4096]{1,0:T(4,128)} %psum.14.weights, f32[32,128]{1,0:T(8,128)} %psum.15.energy, ...), custom_call_target="tpu_custom_call" | custom-call | flops 12884901888 | bytes 8388608 | tf_op jit(solution)/shard_map/contract/pallas_call | solution.py:214
  266.9 0.9 constant_dynamic-slice_fusion
  267.8 1.8 collective-permute-start.18
  269.6 2.6 collective-permute-done.18
  272.8 1.3 collective-permute-done.19.came
  274.7 1.7 spread.1
  276.3 13.5 %all_to_all.5.came = f32[8,2,32,128]{3,2,1,0:T(8,128)} all-to-all(f32[8,2,32,128]{3,2,1,0:T(8,128)} %spread.1), channel_id=1, replica_groups=mesh['frag'=8,'aux'=4] {'frag'}, dimensions={0} | all-to-all | bytes 524288 | tf_op jit(solution)/shard_map/all_to_all | solution.py:345
  289.9 2.8 collect.1
  (61 shorter events, 7.4 us)
Async XLA Ops:
  43.0 56.5 %collective-permute-start.3 = (bf16[2,128,1024]{2,1,0:T(8,128)(2,1)}, bf16[2,128,1024]{2,1,0:T(8,128)(2,1)S(1)}, u32[]{:S(2)}, u32[]{:S(2)}) collective-permute-start(bf16[2,128,1024]{2,1,0:T(8,128)(2,1)} %get-tuple-element.17), channel_id=1, source_target_pairs={{0,4},{8,12},{16,20},{24,28},{4,0},{12,8},{20,16},{28,24},{1,5},{9... | collective-permute-start | bytes 1572872 | tf_op jit(solution)/shard_map/ppermute | solution.py:318
  53.9 67.7 %collective-permute-start.4 = (bf16[2,128,1024]{2,1,0:T(8,128)(2,1)}, bf16[2,128,1024]{2,1,0:T(8,128)(2,1)S(1)}, u32[]{:S(2)}, u32[]{:S(2)}) collective-permute-start(bf16[2,128,1024]{2,1,0:T(8,128)(2,1)} %get-tuple-element.18), channel_id=1, source_target_pairs={{4,8},{12,16},{20,24},{8,4},{16,12},{24,20},{5,9},{13,17},{21,25},... | collective-permute-start | bytes 1572872 | tf_op jit(solution)/shard_map/ppermute | solution.py:318
  54.6 67.8 %collective-permute-start.5 = (bf16[2,128,1024]{2,1,0:T(8,128)(2,1)}, bf16[2,128,1024]{2,1,0:T(8,128)(2,1)S(1)}, u32[]{:S(2)}, u32[]{:S(2)}) collective-permute-start(bf16[2,128,1024]{2,1,0:T(8,128)(2,1)} %get-tuple-element.19), channel_id=1, source_target_pairs={{0,8},{4,12},{16,24},{20,28},{8,0},{12,4},{24,16},{28,20},{1,9},{5... | collective-permute-start | bytes 1572872 | tf_op jit(solution)/shard_map/ppermute | solution.py:318
  97.2 25.3 %collective-permute-start.6 = (bf16[2,128,1024]{2,1,0:T(8,128)(2,1)}, bf16[2,128,1024]{2,1,0:T(8,128)(2,1)S(1)}, u32[]{:S(2)}, u32[]{:S(2)}) collective-permute-start(bf16[2,128,1024]{2,1,0:T(8,128)(2,1)} %get-tuple-element.20), channel_id=1, source_target_pairs={{8,16},{12,20},{16,8},{20,12},{9,17},{13,21},{17,9},{21,13},{10,18... | collective-permute-start | bytes 1572872 | tf_op jit(solution)/shard_map/ppermute | solution.py:318
  97.9 44.8 %collective-permute-start = (bf16[2,128,1024]{2,1,0:T(8,128)(2,1)}, bf16[2,128,1024]{2,1,0:T(8,128)(2,1)}, u32[]{:S(2)}, u32[]{:S(2)}) collective-permute-start(bf16[2,128,1024]{2,1,0:T(8,128)(2,1)} %get-tuple-element.16.refs_0_), channel_id=1, source_target_pairs={{0,2},{1,3},{2,0},{3,1},{4,6},{5,7},{6,4},{7,5},{8,10},{9,11},{10,... | collective-permute-start | bytes 1572872 | tf_op jit(solution)/shard_map/ppermute | solution.py:328
  99.5 43.3 %collective-permute-start.10 = (bf16[2,128,1024]{2,1,0:T(8,128)(2,1)}, bf16[2,128,1024]{2,1,0:T(8,128)(2,1)S(1)}, u32[]{:S(2)}, u32[]{:S(2)}) collective-permute-start(bf16[2,128,1024]{2,1,0:T(8,128)(2,1)} %get-tuple-element.22), channel_id=1, source_target_pairs={{0,12},{4,16},{8,20},{12,0},{16,4},{20,8},{1,13},{5,17},{9,21},{13... | collective-permute-start | bytes 1572872 | tf_op jit(solution)/shard_map/ppermute | solution.py:318
  121.7 21.6 %collective-permute-start.14 = (bf16[2,128,1024]{2,1,0:T(8,128)(2,1)}, bf16[2,128,1024]{2,1,0:T(8,128)(2,1)S(1)}, u32[]{:S(2)}, u32[]{:S(2)}) collective-permute-start(bf16[2,128,1024]{2,1,0:T(8,128)(2,1)} %get-tuple-element.24), channel_id=1, source_target_pairs={{12,24},{16,28},{24,12},{28,16},{13,25},{17,29},{25,13},{29,17},{1... | collective-permute-start | bytes 1572872 | tf_op jit(solution)/shard_map/ppermute | solution.py:318
  122.4 58.0 %collective-permute-start.1 = (bf16[2,128,1024]{2,1,0:T(8,128)(2,1)}, bf16[2,128,1024]{2,1,0:T(8,128)(2,1)}, u32[]{:S(2)}, u32[]{:S(2)}) collective-permute-start(bf16[2,128,1024]{2,1,0:T(8,128)(2,1)} %get-tuple-element.16.refs_0_), channel_id=1, source_target_pairs={{0,1},{1,0},{2,3},{3,2},{4,5},{5,4},{6,7},{7,6},{8,9},{9,8},{10,11... | collective-permute-start | bytes 1572872 | tf_op jit(solution)/shard_map/ppermute | solution.py:329
  141.1 40.9 %collective-permute-start.7 = (bf16[2,128,1024]{2,1,0:T(8,128)(2,1)}, bf16[2,128,1024]{2,1,0:T(8,128)(2,1)S(1)}, u32[]{:S(2)}, u32[]{:S(2)}) collective-permute-start(bf16[2,128,1024]{2,1,0:T(8,128)(2,1)} %pack_group.3.refs_4_), channel_id=1, source_target_pairs={{0,2},{1,3},{2,0},{3,1},{4,6},{5,7},{6,4},{7,5},{8,10},{9,11},{10,... | collective-permute-start | bytes 1572872 | tf_op jit(solution)/shard_map/ppermute | solution.py:328
  142.7 39.4 %collective-permute-start.8 = (bf16[2,128,1024]{2,1,0:T(8,128)(2,1)}, bf16[2,128,1024]{2,1,0:T(8,128)(2,1)S(1)}, u32[]{:S(2)}, u32[]{:S(2)}) collective-permute-start(bf16[2,128,1024]{2,1,0:T(8,128)(2,1)} %pack_group.3.refs_4_), channel_id=1, source_target_pairs={{0,1},{1,0},{2,3},{3,2},{4,5},{5,4},{6,7},{7,6},{8,9},{9,8},{10,11... | collective-permute-start | bytes 1572872 | tf_op jit(solution)/shard_map/ppermute | solution.py:329
  142.8 39.8 %collective-permute-start.2 = (bf16[2,128,1024]{2,1,0:T(8,128)(2,1)}, bf16[2,128,1024]{2,1,0:T(8,128)(2,1)}, u32[]{:S(2)}, u32[]{:S(2)}) collective-permute-start(bf16[2,128,1024]{2,1,0:T(8,128)(2,1)} %collective-permute-done.refs_1_), channel_id=1, source_target_pairs={{0,1},{1,0},{2,3},{3,2},{4,5},{5,4},{6,7},{7,6},{8,9},{9,8},{10,11... | collective-permute-start | bytes 1572872 | tf_op jit(solution)/shard_map/ppermute | solution.py:330
  162.1 20.6 %collective-permute-start.15 = (bf16[2,128,1024]{2,1,0:T(8,128)(2,1)}, bf16[2,128,1024]{2,1,0:T(8,128)(2,1)S(1)}, u32[]{:S(2)}, u32[]{:S(2)}) collective-permute-start(bf16[2,128,1024]{2,1,0:T(8,128)(2,1)} %pack_group.5.refs_12_), channel_id=1, source_target_pairs={{0,2},{1,3},{2,0},{3,1},{4,6},{5,7},{6,4},{7,5},{8,10},{9,11},{10,... | collective-permute-start | bytes 1572872 | tf_op jit(solution)/shard_map/ppermute | solution.py:328
  180.4 14.3 %collective-permute-start.11 = (bf16[2,128,1024]{2,1,0:T(8,128)(2,1)}, bf16[2,128,1024]{2,1,0:T(8,128)(2,1)S(1)}, u32[]{:S(2)}, u32[]{:S(2)}) collective-permute-start(bf16[2,128,1024]{2,1,0:T(8,128)(2,1)} %pack_group.4.refs_8_), channel_id=1, source_target_pairs={{0,2},{1,3},{2,0},{3,1},{4,6},{5,7},{6,4},{7,5},{8,10},{9,11},{10,... | collective-permute-start | bytes 1572872 | tf_op jit(solution)/shard_map/ppermute | solution.py:328
  182.0 62.2 %copy-start.10 = (bf16[2,128,1024]{2,1,0:T(8,128)(2,1)}, bf16[2,128,1024]{2,1,0:T(8,128)(2,1)S(1)}, u32[]{:S(2)}) copy-start(bf16[2,128,1024]{2,1,0:T(8,128)(2,1)S(1)} %collective-permute-done.7.refs_5_) | copy-start | bytes 1572868
  182.0 62.1 %collective-permute-start.16 = (bf16[2,128,1024]{2,1,0:T(8,128)(2,1)S(1)}, bf16[2,128,1024]{2,1,0:T(8,128)(2,1)}, u32[]{:S(2)}, u32[]{:S(2)}) collective-permute-start(bf16[2,128,1024]{2,1,0:T(8,128)(2,1)S(1)} %copy-done.5), channel_id=1, source_target_pairs={{0,1},{1,0},{2,3},{3,2},{4,5},{5,4},{6,7},{7,6},{8,9},{9,8},{10,11... | collective-permute-start | bytes 1572872 | tf_op jit(solution)/shard_map/ppermute | solution.py:329
  182.1 62.1 %copy-start.11 = (bf16[2,128,1024]{2,1,0:T(8,128)(2,1)}, bf16[2,128,1024]{2,1,0:T(8,128)(2,1)S(1)}, u32[]{:S(2)}) copy-start(bf16[2,128,1024]{2,1,0:T(8,128)(2,1)S(1)} %collective-permute-done.8.refs_6_) | copy-start | bytes 1572868
  182.1 62.0 %collective-permute-start.12 = (bf16[2,128,1024]{2,1,0:T(8,128)(2,1)}, bf16[2,128,1024]{2,1,0:T(8,128)(2,1)}, u32[]{:S(2)}, u32[]{:S(2)}) collective-permute-start(bf16[2,128,1024]{2,1,0:T(8,128)(2,1)} %pack_group.4.refs_8_), channel_id=1, source_target_pairs={{0,1},{1,0},{2,3},{3,2},{4,5},{5,4},{6,7},{7,6},{8,9},{9,8},{10,11... | collective-permute-start | bytes 1572872 | tf_op jit(solution)/shard_map/ppermute | solution.py:329
  182.6 61.5 %collective-permute-start.9 = (bf16[2,128,1024]{2,1,0:T(8,128)(2,1)S(1)}, bf16[2,128,1024]{2,1,0:T(8,128)(2,1)}, u32[]{:S(2)}, u32[]{:S(2)}) collective-permute-start(bf16[2,128,1024]{2,1,0:T(8,128)(2,1)S(1)} %collective-permute-done.7.refs_5_), channel_id=1, source_target_pairs={{0,1},{1,0},{2,3},{3,2},{4,5},{5,4},{6,7},{7,6},{8,9},{9,8},{10,11... | collective-permute-start | bytes 1572872 | tf_op jit(solution)/shard_map/ppermute | solution.py:330
  182.7 61.5 %copy-start.12 = (bf16[2,128,1024]{2,1,0:T(8,128)(2,1)}, bf16[2,128,1024]{2,1,0:T(8,128)(2,1)S(1)}, u32[]{:S(2)}) copy-start(bf16[2,128,1024]{2,1,0:T(8,128)(2,1)S(1)} %collective-permute-done.15.refs_13_) | copy-start | bytes 1572868
  182.7 61.4 %collective-permute-start.17 = (bf16[2,128,1024]{2,1,0:T(8,128)(2,1)S(1)}, bf16[2,128,1024]{2,1,0:T(8,128)(2,1)}, u32[]{:S(2)}, u32[]{:S(2)}) collective-permute-start(bf16[2,128,1024]{2,1,0:T(8,128)(2,1)S(1)} %collective-permute-done.15.refs_13_), channel_id=1, source_target_pairs={{0,1},{1,0},{2,3},{3,2},{4,5},{5,4},{6,7},{7,6},{8,9},{9,8},{10,11... | collective-permute-start | bytes 1572872 | tf_op jit(solution)/shard_map/ppermute | solution.py:330
  194.7 49.5 %copy-start.13 = (bf16[2,128,1024]{2,1,0:T(8,128)(2,1)}, bf16[2,128,1024]{2,1,0:T(8,128)(2,1)S(1)}, u32[]{:S(2)}) copy-start(bf16[2,128,1024]{2,1,0:T(8,128)(2,1)S(1)} %collective-permute-done.11.refs_9_) | copy-start | bytes 1572868
  194.7 49.5 %collective-permute-start.13 = (bf16[2,128,1024]{2,1,0:T(8,128)(2,1)S(1)}, bf16[2,128,1024]{2,1,0:T(8,128)(2,1)}, u32[]{:S(2)}, u32[]{:S(2)}) collective-permute-start(bf16[2,128,1024]{2,1,0:T(8,128)(2,1)S(1)} %collective-permute-done.11.refs_9_), channel_id=1, source_target_pairs={{0,1},{1,0},{2,3},{3,2},{4,5},{5,4},{6,7},{7,6},{8,9},{9,8},{10,11... | collective-permute-start | bytes 1572872 | tf_op jit(solution)/shard_map/ppermute | solution.py:330
  267.8 4.3 %collective-permute-start.18 = (f32[2,64,128]{2,1,0:T(8,128)S(1)}, f32[2,64,128]{2,1,0:T(8,128)S(1)}, u32[]{:S(2)}, u32[]{:S(2)}) collective-permute-start(f32[2,64,128]{2,1,0:T(8,128)S(1)} %get-tuple-element.27), channel_id=1, source_target_pairs={{0,2},{1,3},{2,0},{3,1},{4,6},{5,7},{6,4},{7,5},{8,10},{9,11},{10,... | collective-permute-start | bytes 196616 | tf_op jit(solution)/shard_map/ppermute | solution.py:339
  272.8 1.3 collective-permute-start.19
  (10 other events, 49.1 us)

commit v2 on v1

--- a/solution.py
+++ b/solution.py
@@ -9,6 +9,7 @@
 
 ROUNDS = ((1, 0), (1, 1), (2, 0), (2, 1), (3, 0), (3, 1))
 CAP = 2
+TAIL = 8
 PAIRS = tuple((i, j) for i in range(3) for j in range(i, 3))
 VMEM_LIMIT = 56 * 2**20
 ANY = pl.BlockSpec(memory_space=pl.ANY)
@@ -21,9 +22,12 @@
     return up + [(b, a) for a, b in up]
 
 
-def plan_kernel(frags, own_count, list_len, me_ref, map_ref, list_ref, table, *refs):
+def plan_kernel(
+    frags, own_count, list_len, where, map_ref, list_ref, frag_tail, aux_tail, table, *refs
+):
     outs, own, plan, sems = refs[:6], refs[6], refs[7], refs[8]
-    me = me_ref[0]
+    me = where[0]
+    block = table.shape[1]
     copies = []
 
     def pick(fragment, owner):
@@ -45,17 +49,24 @@
         for r in range(CAP):
             copies.append((
                 inside & (count > r),
-                pltpu.make_async_copy(table.at[picked[r]], outs[index].at[r], sems.at[index, r]),
+                pltpu.make_async_copy(
+                    table.at[picked[r]], outs[index].at[pl.ds(r * block, block)], sems.at[index, r]
+                ),
             ))
         if index == 0:
             picked, count = pick(me, me)
             for r in range(CAP):
                 copies.append((
                     count > r,
-                    pltpu.make_async_copy(table.at[picked[r]], own.at[r], sems.at[6, r]),
+                    pltpu.make_async_copy(
+                        table.at[picked[r]], own.at[pl.ds(r * block, block)], sems.at[6, r]
+                    ),
                 ))
     for needed, copy in copies:
         pl.when(needed)(copy.start)
+    for out in outs:
+        out[pl.ds(CAP * block, TAIL), :] = frag_tail[...]
+    own[pl.ds(CAP * block, TAIL), :] = aux_tail[...]
 
     rows, owners, codes, classes = [], [], [], []
     for k in range(list_len):
@@ -89,61 +100,64 @@
         pl.when(needed)(copy.wait)
 
 
-def plan_and_pack(me, owner_map, vir_list, table, frags):
+def plan_and_pack(where, owner_map, vir_list, frag_tail, aux_tail, table, frags):
     own_count, block_rows, cols = table.shape
     list_len = vir_list.shape[1]
-    part = jax.ShapeDtypeStruct((CAP, block_rows, cols), table.dtype)
+    part = jax.ShapeDtypeStruct((CAP * block_rows + TAIL, cols), table.dtype)
     return pl.pallas_call(
         functools.partial(plan_kernel, frags, own_count, list_len),
         out_shape=(part,) * 7 + (jax.ShapeDtypeStruct((4, list_len), jnp.int32),),
-        in_specs=[SMEM, SMEM, SMEM, ANY],
-        out_specs=(ANY,) * 7 + (SMEM,),
+        in_specs=[SMEM, SMEM, SMEM, VMEM, VMEM, ANY],
+        out_specs=(VMEM,) * 7 + (SMEM,),
         scratch_shapes=[pltpu.SemaphoreType.DMA((7, CAP))],
         name="plan_and_pack",
-    )(me, owner_map, vir_list, table)
-
-
-def pack_kernel(first, codes, plan, *refs):
+    )(where, owner_map, vir_list, frag_tail, aux_tail, table)
+
+
+def pack_kernel(first, codes, block, plan, *refs):
     arrived, out, sems = refs[: len(codes)], refs[len(codes)], refs[len(codes) + 1]
     for i in range(2):
         code = plan[0, first + i]
-        rank = plan[1, first + i]
+        begin = pl.multiple_of(plan[1, first + i] * block, block)
+        rows = pl.ds(i * block, block)
         for source, ref in zip(codes, arrived):
 
             @pl.when(code == source)
-            def _(ref=ref):
-                pltpu.make_async_copy(ref.at[rank], out.at[i], sems.at[i]).start()
+            def _(ref=ref, begin=begin, rows=rows):
+                pltpu.make_async_copy(
+                    ref.at[pl.ds(begin, block)], out.at[rows], sems.at[i]
+                ).start()
 
     for i in range(2):
-        pltpu.make_async_copy(arrived[0].at[0], out.at[i], sems.at[i]).wait()
-
-
-def pack_group(first, plan, arrived):
+        rows = pl.ds(i * block, block)
+        pltpu.make_async_copy(arrived[0].at[rows], out.at[rows], sems.at[i]).wait()
+
+
+def pack_group(first, block, plan, arrived):
     codes = tuple(arrived)
     refs = [arrived[c] for c in codes]
     return pl.pallas_call(
-        functools.partial(pack_kernel, first, codes),
-        out_shape=jax.ShapeDtypeStruct(refs[0].shape, refs[0].dtype),
+        functools.partial(pack_kernel, first, codes, block),
+        out_shape=jax.ShapeDtypeStruct((2 * block, refs[0].shape[1]), refs[0].dtype),
         in_specs=[SMEM] + [ANY] * len(refs),
-        out_specs=ANY,
+        out_specs=VMEM,
         scratch_shapes=[pltpu.SemaphoreType.DMA((2,))],
         name="pack_group",
     )(plan, *refs)
 
 
 def contract_kernel(
-    list_len, block, width, where, plan, levels, rows_ref, weights, energy, *refs
+    list_len, block, width, own_count, where, plan, levels, rows_ref, weights, energy, *refs
 ):
     groups = list_len // 2
     parts, (out, grid, scaled, total, amps, sems) = refs[: groups * 4], refs[groups * 4 :]
     me, aux = where[0], where[1]
-    quarter_of = (aux, aux ^ 2, aux ^ 1, aux ^ 3)
     copies = {}
     for quarter in range(4):
         for group in range(groups):
             for i in range(2):
                 copy = pltpu.make_async_copy(
-                    parts[group * 4 + quarter].at[i],
+                    parts[group * 4 + quarter].at[pl.ds(i * block, block)],
                     grid.at[pl.ds((group * 2 + i) * block, block), pl.ds(quarter * width, width)],
                     sems.at[quarter, group, i],
                 )
@@ -156,8 +170,7 @@
             for i in range(2):
                 copies[quarter, group, i].wait()
         cols = pl.ds(quarter * width, width)
-        begin = pl.multiple_of(quarter_of[quarter] * width, width)
-        occ = [weights[i : i + 1, pl.ds(begin, width)] for i in range(3)]
+        occ = [weights[quarter, i : i + 1, :].astype(jnp.float32) for i in range(3)]
         for b in range(2):
             left = grid[pl.ds(pl.multiple_of(mine[b] * block, block), block), cols].astype(
                 jnp.float32
@@ -187,12 +200,17 @@
 
     lane = lax.broadcasted_iota(jnp.int32, (block, block), 1)
     sub = lax.broadcasted_iota(jnp.int32, (block, block), 0)
+
+    def energy_of(place):
+        row = plan[0, place] * own_count + plan[2, place] % own_count
+        return energy[pl.ds(row, 1), :]
+
     for b in range(2):
-        own_row = energy[pl.ds(plan[2, mine[b]], 1), :]
+        own_row = energy_of(mine[b])
         own_energy = jnp.transpose(jnp.broadcast_to(own_row, (block, block)))
         own_live = sub < rows_ref[me, plan[3, mine[b]]]
         for q in range(list_len):
-            their_energy = energy[pl.ds(plan[2, q], 1), :]
+            their_energy = energy_of(q)
             live = own_live & (lane < rows_ref[me, plan[3, q]])
             for p, (i, j) in enumerate(PAIRS):
                 gap = (levels[0, i] + levels[0, j]) - own_energy - their_energy
@@ -205,14 +223,15 @@
         )
 
 
-def contract(where, plan, levels, vir_rows, weights, energy, parts):
+def contract(where, plan, levels, vir_rows, weights, energy, parts, own_count):
     list_len = vir_rows.shape[1]
-    block, width = parts[0].shape[1:]
+    width = parts[0].shape[1]
+    block = parts[-1].shape[0] // 2
     nvir = list_len * block
     pair_count = len(PAIRS)
     flops = 2 * pair_count * 2 * block * nvir * 4 * width
     return pl.pallas_call(
-        functools.partial(contract_kernel, list_len, block, width),
+        functools.partial(contract_kernel, list_len, block, width, own_count),
         out_shape=jax.ShapeDtypeStruct((2, block, block), jnp.float32),
         in_specs=[SMEM, SMEM, SMEM, SMEM, VMEM, VMEM] + [ANY] * len(parts),
         out_specs=VMEM,
@@ -293,23 +312,11 @@
     far_pairs = [(i, i ^ 2) for i in range(aux_count)]
     near_pairs = [(i, i ^ 1) for i in range(aux_count)]
 
-    energy = lax.psum(
-        lax.dynamic_update_slice(
-            jnp.zeros((frags * own_count, block), jnp.float32),
-            vir_energy.astype(jnp.float32),
-            (me * own_count, 0),
-        ),
-        "frag",
+    frag_tail = jnp.pad(vir_energy, ((0, TAIL - own_count), (0, width - block)))
+    aux_tail = jnp.pad(occ_grid[0], ((0, TAIL - occ_grid.shape[1]), (0, 0)))
+    *outgoing, own, plan = plan_and_pack(
+        where, owner_map, vir_list, frag_tail, aux_tail, vir_grid, frags
     )
-    weights = lax.psum(
-        lax.dynamic_update_slice(
-            jnp.zeros((occ_grid.shape[1], aux_count * width), jnp.float32),
-            occ_grid[0].astype(jnp.float32),
-            (0, aux * width),
-        ),
-        "aux",
-    )
-    *outgoing, own, plan = plan_and_pack(where, owner_map, vir_list, vir_grid, frags)
     arrived = {}
     for index, (distance, parity) in enumerate(ROUNDS):
         payload = outgoing[index]
@@ -324,12 +331,19 @@
             here = own
         else:
             known = {c: arrived[c] for c in range(1, 4 + group)}
-            here = pack_group(2 * group, plan, known)
+            here = pack_group(2 * group, block, plan, known)
         far = lax.ppermute(here, "aux", far_pairs)
         near = lax.ppermute(here, "aux", near_pairs)
         far_near = lax.ppermute(far, "aux", near_pairs)
         parts += [here, far, near, far_near]
-    density = contract(where, plan, occ_energy, vir_rows, weights, energy, parts)
+    tail = CAP * block
+    energy = jnp.concatenate(
+        [vir_energy] + [arrived[c][tail : tail + own_count, :block] for c in sorted(arrived)]
+    ).astype(jnp.float32)
+    weights = jnp.stack([part[tail:] for part in parts[:4]])
+    density = contract(
+        where, plan, occ_energy, vir_rows, weights, energy, parts, own_count
+    )
 
     half = block // 2
     quarter = block // aux_count

time: 293 us -> 147 us (0.50)
  Pallas kernels: 123 us -> 39.4 us
  starting transfers between devices: 86.5 us -> 21.9 us
  blocking collectives: 61.6 us -> 17.6 us
  waiting for transfers between devices: 15.4 us -> 51.3 us
  local copies, waits for them, and re-layouts: 4.98 us -> 12.9 us
    ppermute x6, starting transfers between devices: 77.8 us -> 13.8 us  [body(): lax.ppermute(payload, 'frag', round_pairs(distance, parity, frags))]
    psum x2 -> x0, blocking collectives: 48 us -> none  [the longest x1 36.8 us: body(): lax.psum(lax.dynamic_update_slice(jnp.zeros((frags * own_count, block), j...]
    pallas_call x4, Pallas kernels: 75.8 us -> 30.4 us  [the longest x1 22.8 us: contract(): pl.pallas_call(functools.partial(contract_kernel, list_len, block, width,...]
    pallas_call x1, Pallas kernels: 42.4 us -> 4.46 us  [plan_and_pack(): pl.pallas_call(functools.partial(plan_kernel, frags, own_count, list_len)...]
    ppermute x6, waiting for transfers between devices: 0.02 us -> 31.5 us  [body(): lax.ppermute(payload, 'frag', round_pairs(distance, parity, frags))]
    all_to_all x1, blocking collectives: 13.5 us -> 17.6 us  [body(): incoming = lax.all_to_all(outgoing, 'frag', 0, 0, tiled=True)]
    slice x0 -> x6, local copies, waits for them, and re-layouts: none -> 3.98 us  [body(): arrived[c][tail:tail + own_count, :block]]
    ppermute x4, waiting for transfers between devices: 11.6 us -> 15.6 us  [body(): far = lax.ppermute(here, 'aux', far_pairs)]
  transfers between devices with their start and end apart: 20 -> 20, of which waited for: 3 -> 6; matrix products, arithmetic and copies ran while one was open for 0% -> 6% of each run, Pallas kernels for 18% -> 5%
where the time goes in v2:
time: 147 us; the launch traced here: 146 us
  waiting for transfers between devices  51.3 us (35%)
  Pallas kernels  39.4 us (27%)
  starting transfers between devices  21.9 us (15%)
  blocking collectives  17.6 us (12%)
  local copies, waits for them, and re-layouts  12.9 us (9%)
  other arithmetic  2.53 us (2%)
    ppermute x6, waiting for transfers between devices, body(): lax.ppermute(payload, 'frag', round_pairs(distance, parity, frags))  31.5 us
    pallas_call x1, Pallas kernels, contract(): pl.pallas_call(functools.partial(contract_kernel, list_len, block, width,...  22.8 us
    all_to_all x1, blocking collectives, body(): incoming = lax.all_to_all(outgoing, 'frag', 0, 0, tiled=True)  17.6 us
    ppermute x4, waiting for transfers between devices, body(): far = lax.ppermute(here, 'aux', far_pairs)  15.6 us
    ppermute x6, starting transfers between devices, body(): lax.ppermute(payload, 'frag', round_pairs(distance, parity, frags))  13.8 us
    pallas_call x3, Pallas kernels, pack_group(): pl.pallas_call(functools.partial(pack_kernel, first, codes, block), out_s...  7.64 us
    ppermute x4, starting transfers between devices, body(): far = lax.ppermute(here, 'aux', far_pairs)  5.28 us
    pallas_call x1, Pallas kernels, plan_and_pack(): pl.pallas_call(functools.partial(plan_kernel, frags, own_count, list_len)...  4.46 us
  transfers between devices with their start and end apart: 20, of which 6 were waited for; matrix products, arithmetic and copies ran while one was open for 6% of the time, Pallas kernels for 5%

profile of v2, /device:TPU:0, one launch (start us, length us, event | category | flops | bytes accessed | tf_op | source)
XLA Modules:
  0.0 145.8 jit_solution(15294624092989758243)
XLA Ops:
  2.6 4.5 %plan_and_pack.1 = (bf16[264,1024]{1,0:T(8,128)(2,1)}, bf16[264,1024]{1,0:T(8,128)(2,1)}, bf16[264,1024]{1,0:T(8,128)(2,1)}, bf16[264,1024]{1,0:T(8,128)(2,1)}, ...) custom-call(s32[2]{0:T(128)} %pad_add_fusion.where, ...), custom_call_target="tpu_custom_call" | custom-call | tf_op jit(solution)/shard_map/plan_and_pack/pallas_call | solution.py:107
  7.1 3.2 %collective-permute-start.3 = (bf16[264,1024]{1,0:T(8,128)(2,1)}, bf16[264,1024]{1,0:T(8,128)(2,1)S(1)}, u32[]{:S(2)}, u32[]{:S(2)}) collective-permute-start(bf16[264,1024]{1,0:T(8,128)(2,1)} %get-tuple-element.17), channel_id=1, source_target_pairs={{0,4},{8,12},{16,20},{24,28},{4,0},{12,8},{20,16},{28,24},{1,5},{9... | collective-permute-start | bytes 1622024 | tf_op jit(solution)/shard_map/ppermute | solution.py:325
  11.0 3.1 %collective-permute-start.5 = (bf16[264,1024]{1,0:T(8,128)(2,1)}, bf16[264,1024]{1,0:T(8,128)(2,1)S(1)}, u32[]{:S(2)}, u32[]{:S(2)}) collective-permute-start(bf16[264,1024]{1,0:T(8,128)(2,1)} %get-tuple-element.19), channel_id=1, source_target_pairs={{0,8},{4,12},{16,24},{20,28},{8,0},{12,4},{24,16},{28,20},{1,9},{5... | collective-permute-start | bytes 1622024 | tf_op jit(solution)/shard_map/ppermute | solution.py:325
  14.1 1.5 %collective-permute-start = (bf16[264,1024]{1,0:T(8,128)(2,1)}, bf16[264,1024]{1,0:T(8,128)(2,1)}, u32[]{:S(2)}, u32[]{:S(2)}) collective-permute-start(bf16[264,1024]{1,0:T(8,128)(2,1)} %get-tuple-element.16.refs_0_), channel_id=1, source_target_pairs={{0,2},{1,3},{2,0},{3,1},{4,6},{5,7},{6,4},{7,5},{8,10},{9,11},{10,... | collective-permute-start | bytes 1622024 | tf_op jit(solution)/shard_map/ppermute | solution.py:335
  16.3 17.5 %collective-permute-done.3.refs_0_ = bf16[264,1024]{1,0:T(8,128)(2,1)S(1)} collective-permute-done((bf16[264,1024]{1,0:T(8,128)(2,1)}, bf16[264,1024]{1,0:T(8,128)(2,1)S(1)}, u32[]{:S(2)}, u32[]{:S(2)}) %collective-permute-start.3) | collective-permute-done | bytes 540704 | tf_op jit(solution)/shard_map/ppermute | solution.py:325
  33.8 5.5 %collective-permute-start.7 = (bf16[264,1024]{1,0:T(8,128)(2,1)}, bf16[264,1024]{1,0:T(8,128)(2,1)S(1)}, u32[]{:S(2)}, u32[]{:S(2)}) collective-permute-start(bf16[264,1024]{1,0:T(8,128)(2,1)} %get-tuple-element.22), channel_id=1, source_target_pairs={{0,12},{4,16},{8,20},{12,0},{16,4},{20,8},{1,13},{5,17},{9,21},{13... | collective-permute-start | bytes 1622024 | tf_op jit(solution)/shard_map/ppermute | solution.py:325
  41.4 2.5 %pack_group.3.refs_4_ = bf16[256,1024]{1,0:T(8,128)(2,1)} custom-call(s32[4,8]{1,0:T(4,128)} %get-tuple-element.15.plan, bf16[264,1024]{1,0:T(8,128)(2,1)} %copy-done, bf16[264,1024]{1,0:T(8,128)(2,1)} %copy-done.1, bf16[264,1024]{1,0:T(8,128)(2,1)} %copy-done.2, bf16[264,1024]{1,0:T(8,128)(2,1)} %copy-done.3), custom_call_target="tpu_custom_call" | custom-call | tf_op jit(solution)/shard_map/pack_group/pallas_call | solution.py:139
  43.9 1.6 %collective-permute-start.9 = (bf16[256,1024]{1,0:T(8,128)(2,1)}, bf16[256,1024]{1,0:T(8,128)(2,1)S(1)}, u32[]{:S(2)}, u32[]{:S(2)}) collective-permute-start(bf16[256,1024]{1,0:T(8,128)(2,1)} %pack_group.3.refs_4_), channel_id=1, source_target_pairs={{0,2},{1,3},{2,0},{3,1},{4,6},{5,7},{6,4},{7,5},{8,10},{9,11},{10,... | collective-permute-start | bytes 1572872 | tf_op jit(solution)/shard_map/ppermute | solution.py:335
  45.5 14.0 %collective-permute-done.7.refs_4_ = bf16[264,1024]{1,0:T(8,128)(2,1)S(1)} collective-permute-done((bf16[264,1024]{1,0:T(8,128)(2,1)}, bf16[264,1024]{1,0:T(8,128)(2,1)S(1)}, u32[]{:S(2)}, u32[]{:S(2)}) %collective-permute-start.7) | collective-permute-done | bytes 540704 | tf_op jit(solution)/shard_map/ppermute | solution.py:325
  59.5 0.8 copy-done.4
  60.3 0.8 copy-done.5
  61.2 2.5 %pack_group.5.refs_12_ = bf16[256,1024]{1,0:T(8,128)(2,1)} custom-call(s32[4,8]{1,0:T(4,128)} %get-tuple-element.15.plan, bf16[264,1024]{1,0:T(8,128)(2,1)} %copy-done, bf16[264,1024]{1,0:T(8,128)(2,1)} %copy-done.1, bf16[264,1024]{1,0:T(8,128)(2,1)} %copy-done.2, bf16[264,1024]{1,0:T(8,128)(2,1)} %copy-done.3, bf16[264,1024]{1,0:T(8,128)(2,1)} %copy-done.4, ...), custom_call_target="tpu_custom_call" | custom-call | tf_op jit(solution)/shard_map/pack_group/pallas_call | solution.py:139
  63.7 1.6 %collective-permute-start.15 = (bf16[256,1024]{1,0:T(8,128)(2,1)}, bf16[256,1024]{1,0:T(8,128)(2,1)S(1)}, u32[]{:S(2)}, u32[]{:S(2)}) collective-permute-start(bf16[256,1024]{1,0:T(8,128)(2,1)} %pack_group.5.refs_12_), channel_id=1, source_target_pairs={{0,2},{1,3},{2,0},{3,1},{4,6},{5,7},{6,4},{7,5},{8,10},{9,11},{10,... | collective-permute-start | bytes 1572872 | tf_op jit(solution)/shard_map/ppermute | solution.py:335
  65.3 2.6 %pack_group.4.refs_8_ = bf16[256,1024]{1,0:T(8,128)(2,1)} custom-call(s32[4,8]{1,0:T(4,128)} %get-tuple-element.15.plan, bf16[264,1024]{1,0:T(8,128)(2,1)} %copy-done, bf16[264,1024]{1,0:T(8,128)(2,1)} %copy-done.1, bf16[264,1024]{1,0:T(8,128)(2,1)} %copy-done.2, bf16[264,1024]{1,0:T(8,128)(2,1)} %copy-done.3, bf16[264,1024]{1,0:T(8,128)(2,1)} %copy-done.4), custom_call_target="tpu_custom_call" | custom-call | tf_op jit(solution)/shard_map/pack_group/pallas_call | solution.py:139
  73.2 5.6 %collective-permute-done.15.refs_13_ = bf16[256,1024]{1,0:T(8,128)(2,1)S(1)} collective-permute-done((bf16[256,1024]{1,0:T(8,128)(2,1)}, bf16[256,1024]{1,0:T(8,128)(2,1)S(1)}, u32[]{:S(2)}, u32[]{:S(2)}) %collective-permute-start.15) | collective-permute-done | bytes 524320 | tf_op jit(solution)/shard_map/ppermute | solution.py:335
  78.8 9.9 %collective-permute-done.12.refs_9_ = bf16[256,1024]{1,0:T(8,128)(2,1)S(1)} collective-permute-done((bf16[256,1024]{1,0:T(8,128)(2,1)}, bf16[256,1024]{1,0:T(8,128)(2,1)S(1)}, u32[]{:S(2)}, u32[]{:S(2)}) %collective-permute-start.12) | collective-permute-done | bytes 524320 | tf_op jit(solution)/shard_map/ppermute | solution.py:335
  93.0 22.8 %contract.1 = f32[2,128,128]{2,1,0:T(8,128)} custom-call(s32[2]{0:T(128)} %pad_add_fusion.where, s32[4,8]{1,0:T(4,128)} %get-tuple-element.15.plan, f32[1,3]{1,0:T(1,128)} %levels.1, s32[8,8]{1,0:T(8,128)} %rows_ref.1, bf16[4,8,1024]{2,1,0:T(8,128)(2,1)} %pad_maximum_fusion.weights, f32[28,128]{1,0:T(8,128)} %convert_element_type.7.energy, ...), custom_call_target="tpu_custom_call" | custom-call | flops 12884901888 | bytes 8388608 | tf_op jit(solution)/shard_map/contract/pallas_call | solution.py:233
  115.7 0.9 constant_dynamic-slice_fusion
  116.6 1.6 %collective-permute-start.18 = (f32[2,64,128]{2,1,0:T(8,128)S(1)}, f32[2,64,128]{2,1,0:T(8,128)S(1)}, u32[]{:S(2)}, u32[]{:S(2)}) collective-permute-start(f32[2,64,128]{2,1,0:T(8,128)S(1)} %get-tuple-element.27), channel_id=1, source_target_pairs={{0,2},{1,3},{2,0},{3,1},{4,6},{5,7},{6,4},{7,5},{8,10},{9,11},{10,... | collective-permute-start | bytes 196616 | tf_op jit(solution)/shard_map/ppermute | solution.py:353
  118.2 3.0 %collective-permute-done.18 = f32[2,64,128]{2,1,0:T(8,128)S(1)} collective-permute-done((f32[2,64,128]{2,1,0:T(8,128)S(1)}, f32[2,64,128]{2,1,0:T(8,128)S(1)}, u32[]{:S(2)}, u32[]{:S(2)}) %collective-permute-start.18) | collective-permute-done | bytes 65568 | tf_op jit(solution)/shard_map/ppermute | solution.py:353
  121.9 1.3 collective-permute-done.19.came
  123.7 1.7 %spread.1 = f32[8,2,32,128]{3,2,1,0:T(8,128)} custom-call(s32[2]{0:T(128)} %pad_add_fusion.where, s32[4,8]{1,0:T(4,128)} %get-tuple-element.15.plan, f32[4,32,128]{2,1,0:T(8,128)} %get-tuple-element.26.kept, f32[4,32,128]{2,1,0:T(8,128)} %copy-done.7), custom_call_target="tpu_custom_call" | custom-call | tf_op jit(solution)/shard_map/spread/pallas_call | solution.py:265
  125.4 17.6 %all_to_all.5.came = f32[8,2,32,128]{3,2,1,0:T(8,128)} all-to-all(f32[8,2,32,128]{3,2,1,0:T(8,128)} %spread.1), channel_id=1, replica_groups=mesh['frag'=8,'aux'=4] {'frag'}, dimensions={0} | all-to-all | bytes 524288 | tf_op jit(solution)/shard_map/all_to_all | solution.py:359
  143.0 2.8 %collect.1 = f32[4,32,128]{2,1,0:T(8,128)} custom-call(s32[2]{0:T(128)} %pad_add_fusion.where, s32[32]{0:T(128)} %map_ref.3, s32[8,8]{1,0:T(8,128)} %list_ref.3, f32[8,2,32,128]{3,2,1,0:T(8,128)} %all_to_all.5.came), custom_call_target="tpu_custom_call" | custom-call | tf_op jit(solution)/shard_map/collect/pallas_call | solution.py:295
  (70 shorter events, 16.8 us)
Async XLA Ops:
  7.1 26.6 %collective-permute-start.3 = (bf16[264,1024]{1,0:T(8,128)(2,1)}, bf16[264,1024]{1,0:T(8,128)(2,1)S(1)}, u32[]{:S(2)}, u32[]{:S(2)}) collective-permute-start(bf16[264,1024]{1,0:T(8,128)(2,1)} %get-tuple-element.17), channel_id=1, source_target_pairs={{0,4},{8,12},{16,20},{24,28},{4,0},{12,8},{20,16},{28,24},{1,5},{9... | collective-permute-start | bytes 1622024 | tf_op jit(solution)/shard_map/ppermute | solution.py:325
  10.3 28.9 %collective-permute-start.4 = (bf16[264,1024]{1,0:T(8,128)(2,1)}, bf16[264,1024]{1,0:T(8,128)(2,1)S(1)}, u32[]{:S(2)}, u32[]{:S(2)}) collective-permute-start(bf16[264,1024]{1,0:T(8,128)(2,1)} %get-tuple-element.18), channel_id=1, source_target_pairs={{4,8},{12,16},{20,24},{8,4},{16,12},{24,20},{5,9},{13,17},{21,25},... | collective-permute-start | bytes 1622024 | tf_op jit(solution)/shard_map/ppermute | solution.py:325
  11.0 29.0 %collective-permute-start.5 = (bf16[264,1024]{1,0:T(8,128)(2,1)}, bf16[264,1024]{1,0:T(8,128)(2,1)S(1)}, u32[]{:S(2)}, u32[]{:S(2)}) collective-permute-start(bf16[264,1024]{1,0:T(8,128)(2,1)} %get-tuple-element.19), channel_id=1, source_target_pairs={{0,8},{4,12},{16,24},{20,28},{8,0},{12,4},{24,16},{28,20},{1,9},{5... | collective-permute-start | bytes 1622024 | tf_op jit(solution)/shard_map/ppermute | solution.py:325
  14.1 26.0 %collective-permute-start = (bf16[264,1024]{1,0:T(8,128)(2,1)}, bf16[264,1024]{1,0:T(8,128)(2,1)}, u32[]{:S(2)}, u32[]{:S(2)}) collective-permute-start(bf16[264,1024]{1,0:T(8,128)(2,1)} %get-tuple-element.16.refs_0_), channel_id=1, source_target_pairs={{0,2},{1,3},{2,0},{3,1},{4,6},{5,7},{6,4},{7,5},{8,10},{9,11},{10,... | collective-permute-start | bytes 1622024 | tf_op jit(solution)/shard_map/ppermute | solution.py:335
  15.6 25.0 %collective-permute-start.6 = (bf16[264,1024]{1,0:T(8,128)(2,1)}, bf16[264,1024]{1,0:T(8,128)(2,1)S(1)}, u32[]{:S(2)}, u32[]{:S(2)}) collective-permute-start(bf16[264,1024]{1,0:T(8,128)(2,1)} %get-tuple-element.20), channel_id=1, source_target_pairs={{8,16},{12,20},{16,8},{20,12},{9,17},{13,21},{17,9},{21,13},{10,18... | collective-permute-start | bytes 1622024 | tf_op jit(solution)/shard_map/ppermute | solution.py:325
  33.8 25.8 %collective-permute-start.7 = (bf16[264,1024]{1,0:T(8,128)(2,1)}, bf16[264,1024]{1,0:T(8,128)(2,1)S(1)}, u32[]{:S(2)}, u32[]{:S(2)}) collective-permute-start(bf16[264,1024]{1,0:T(8,128)(2,1)} %get-tuple-element.22), channel_id=1, source_target_pairs={{0,12},{4,16},{8,20},{12,0},{16,4},{20,8},{1,13},{5,17},{9,21},{13... | collective-permute-start | bytes 1622024 | tf_op jit(solution)/shard_map/ppermute | solution.py:325
  39.3 20.3 %collective-permute-start.8 = (bf16[264,1024]{1,0:T(8,128)(2,1)}, bf16[264,1024]{1,0:T(8,128)(2,1)S(1)}, u32[]{:S(2)}, u32[]{:S(2)}) collective-permute-start(bf16[264,1024]{1,0:T(8,128)(2,1)} %get-tuple-element.24), channel_id=1, source_target_pairs={{12,24},{16,28},{24,12},{28,16},{13,25},{17,29},{25,13},{29,17},{1... | collective-permute-start | bytes 1622024 | tf_op jit(solution)/shard_map/ppermute | solution.py:325
  40.0 27.9 %collective-permute-start.1 = (bf16[264,1024]{1,0:T(8,128)(2,1)}, bf16[264,1024]{1,0:T(8,128)(2,1)}, u32[]{:S(2)}, u32[]{:S(2)}) collective-permute-start(bf16[264,1024]{1,0:T(8,128)(2,1)} %get-tuple-element.16.refs_0_), channel_id=1, source_target_pairs={{0,1},{1,0},{2,3},{3,2},{4,5},{5,4},{6,7},{7,6},{8,9},{9,8},{10,11... | collective-permute-start | bytes 1622024 | tf_op jit(solution)/shard_map/ppermute | solution.py:336
  40.1 33.0 %collective-permute-start.2 = (bf16[264,1024]{1,0:T(8,128)(2,1)}, bf16[264,1024]{1,0:T(8,128)(2,1)}, u32[]{:S(2)}, u32[]{:S(2)}) collective-permute-start(bf16[264,1024]{1,0:T(8,128)(2,1)} %collective-permute-done.refs_1_), channel_id=1, source_target_pairs={{0,1},{1,0},{2,3},{3,2},{4,5},{5,4},{6,7},{7,6},{8,9},{9,8},{10,11... | collective-permute-start | bytes 1622024 | tf_op jit(solution)/shard_map/ppermute | solution.py:337
  43.9 28.6 %collective-permute-start.9 = (bf16[256,1024]{1,0:T(8,128)(2,1)}, bf16[256,1024]{1,0:T(8,128)(2,1)S(1)}, u32[]{:S(2)}, u32[]{:S(2)}) collective-permute-start(bf16[256,1024]{1,0:T(8,128)(2,1)} %pack_group.3.refs_4_), channel_id=1, source_target_pairs={{0,2},{1,3},{2,0},{3,1},{4,6},{5,7},{6,4},{7,5},{8,10},{9,11},{10,... | collective-permute-start | bytes 1572872 | tf_op jit(solution)/shard_map/ppermute | solution.py:335
  59.5 13.0 %collective-permute-start.10 = (bf16[256,1024]{1,0:T(8,128)(2,1)}, bf16[256,1024]{1,0:T(8,128)(2,1)S(1)}, u32[]{:S(2)}, u32[]{:S(2)}) collective-permute-start(bf16[256,1024]{1,0:T(8,128)(2,1)} %pack_group.3.refs_4_), channel_id=1, source_target_pairs={{0,1},{1,0},{2,3},{3,2},{4,5},{5,4},{6,7},{7,6},{8,9},{9,8},{10,11... | collective-permute-start | bytes 1572872 | tf_op jit(solution)/shard_map/ppermute | solution.py:336
  63.7 8.8 %copy-start.6 = (bf16[256,1024]{1,0:T(8,128)(2,1)S(1)}, bf16[256,1024]{1,0:T(8,128)(2,1)}, u32[]{:S(2)}) copy-start(bf16[256,1024]{1,0:T(8,128)(2,1)} %pack_group.5.refs_12_) | copy-start | bytes 1572868
  63.7 15.1 %collective-permute-start.15 = (bf16[256,1024]{1,0:T(8,128)(2,1)}, bf16[256,1024]{1,0:T(8,128)(2,1)S(1)}, u32[]{:S(2)}, u32[]{:S(2)}) collective-permute-start(bf16[256,1024]{1,0:T(8,128)(2,1)} %pack_group.5.refs_12_), channel_id=1, source_target_pairs={{0,2},{1,3},{2,0},{3,1},{4,6},{5,7},{6,4},{7,5},{8,10},{9,11},{10,... | collective-permute-start | bytes 1572872 | tf_op jit(solution)/shard_map/ppermute | solution.py:335
  67.9 20.9 %collective-permute-start.12 = (bf16[256,1024]{1,0:T(8,128)(2,1)}, bf16[256,1024]{1,0:T(8,128)(2,1)S(1)}, u32[]{:S(2)}, u32[]{:S(2)}) collective-permute-start(bf16[256,1024]{1,0:T(8,128)(2,1)} %pack_group.4.refs_8_), channel_id=1, source_target_pairs={{0,2},{1,3},{2,0},{3,1},{4,6},{5,7},{6,4},{7,5},{8,10},{9,11},{10,... | collective-permute-start | bytes 1572872 | tf_op jit(solution)/shard_map/ppermute | solution.py:335
  72.5 20.4 %copy-start.10 = (bf16[256,1024]{1,0:T(8,128)(2,1)}, bf16[256,1024]{1,0:T(8,128)(2,1)S(1)}, u32[]{:S(2)}) copy-start(bf16[256,1024]{1,0:T(8,128)(2,1)S(1)} %collective-permute-done.9.refs_5_) | copy-start | bytes 1572868
  72.5 20.4 %collective-permute-start.11 = (bf16[256,1024]{1,0:T(8,128)(2,1)S(1)}, bf16[256,1024]{1,0:T(8,128)(2,1)}, u32[]{:S(2)}, u32[]{:S(2)}) collective-permute-start(bf16[256,1024]{1,0:T(8,128)(2,1)S(1)} %collective-permute-done.9.refs_5_), channel_id=1, source_target_pairs={{0,1},{1,0},{2,3},{3,2},{4,5},{5,4},{6,7},{7,6},{8,9},{9,8},{10,11... | collective-permute-start | bytes 1572872 | tf_op jit(solution)/shard_map/ppermute | solution.py:337
  72.5 20.4 %copy-start.11 = (bf16[256,1024]{1,0:T(8,128)(2,1)}, bf16[256,1024]{1,0:T(8,128)(2,1)S(1)}, u32[]{:S(2)}) copy-start(bf16[256,1024]{1,0:T(8,128)(2,1)S(1)} %collective-permute-done.10.refs_6_) | copy-start | bytes 1572868
  72.6 20.3 %collective-permute-start.16 = (bf16[256,1024]{1,0:T(8,128)(2,1)S(1)}, bf16[256,1024]{1,0:T(8,128)(2,1)}, u32[]{:S(2)}, u32[]{:S(2)}) collective-permute-start(bf16[256,1024]{1,0:T(8,128)(2,1)S(1)} %copy-done.6), channel_id=1, source_target_pairs={{0,1},{1,0},{2,3},{3,2},{4,5},{5,4},{6,7},{7,6},{8,9},{9,8},{10,11... | collective-permute-start | bytes 1572872 | tf_op jit(solution)/shard_map/ppermute | solution.py:336
  73.1 19.8 %collective-permute-start.13 = (bf16[256,1024]{1,0:T(8,128)(2,1)}, bf16[256,1024]{1,0:T(8,128)(2,1)}, u32[]{:S(2)}, u32[]{:S(2)}) collective-permute-start(bf16[256,1024]{1,0:T(8,128)(2,1)} %pack_group.4.refs_8_), channel_id=1, source_target_pairs={{0,1},{1,0},{2,3},{3,2},{4,5},{5,4},{6,7},{7,6},{8,9},{9,8},{10,11... | collective-permute-start | bytes 1572872 | tf_op jit(solution)/shard_map/ppermute | solution.py:336
  78.8 14.1 %copy-start.12 = (bf16[256,1024]{1,0:T(8,128)(2,1)}, bf16[256,1024]{1,0:T(8,128)(2,1)S(1)}, u32[]{:S(2)}) copy-start(bf16[256,1024]{1,0:T(8,128)(2,1)S(1)} %collective-permute-done.15.refs_13_) | copy-start | bytes 1572868
  78.8 14.1 %collective-permute-start.17 = (bf16[256,1024]{1,0:T(8,128)(2,1)S(1)}, bf16[256,1024]{1,0:T(8,128)(2,1)}, u32[]{:S(2)}, u32[]{:S(2)}) collective-permute-start(bf16[256,1024]{1,0:T(8,128)(2,1)S(1)} %collective-permute-done.15.refs_13_), channel_id=1, source_target_pairs={{0,1},{1,0},{2,3},{3,2},{4,5},{5,4},{6,7},{7,6},{8,9},{9,8},{10,11... | collective-permute-start | bytes 1572872 | tf_op jit(solution)/shard_map/ppermute | solution.py:337
  88.7 4.2 %collective-permute-start.14 = (bf16[256,1024]{1,0:T(8,128)(2,1)S(1)}, bf16[256,1024]{1,0:T(8,128)(2,1)}, u32[]{:S(2)}, u32[]{:S(2)}) collective-permute-start(bf16[256,1024]{1,0:T(8,128)(2,1)S(1)} %collective-permute-done.12.refs_9_), channel_id=1, source_target_pairs={{0,1},{1,0},{2,3},{3,2},{4,5},{5,4},{6,7},{7,6},{8,9},{9,8},{10,11... | collective-permute-start | bytes 1572872 | tf_op jit(solution)/shard_map/ppermute | solution.py:337
  116.6 4.6 %collective-permute-start.18 = (f32[2,64,128]{2,1,0:T(8,128)S(1)}, f32[2,64,128]{2,1,0:T(8,128)S(1)}, u32[]{:S(2)}, u32[]{:S(2)}) collective-permute-start(f32[2,64,128]{2,1,0:T(8,128)S(1)} %get-tuple-element.27), channel_id=1, source_target_pairs={{0,2},{1,3},{2,0},{3,1},{4,6},{5,7},{6,4},{7,5},{8,10},{9,11},{10,... | collective-permute-start | bytes 196616 | tf_op jit(solution)/shard_map/ppermute | solution.py:353
  121.9 1.3 collective-permute-start.19
  (10 other events, 17.6 us)

commit v3 on v2

v3 whole, which is shorter than its diff:
```python
import functools

import jax
import jax.numpy as jnp
from jax import lax
from jax.experimental import pallas as pl
from jax.experimental.pallas import tpu as pltpu
from jax.sharding import PartitionSpec as P

ROUNDS = ((1, 0), (1, 1), (2, 0), (2, 1), (3, 0), (3, 1))
CAP = 2
TAIL = 16
PAIRS = tuple((i, j) for i in range(3) for j in range(i, 3))
MIB = 2**20
ANY = pl.BlockSpec(memory_space=pl.ANY)
SMEM = pl.BlockSpec(memory_space=pltpu.SMEM)
VMEM = pl.BlockSpec(memory_space=pltpu.VMEM)


def round_pairs(distance, parity, frags):
    up = [(i, i + distance) for i in range(frags - distance) if (i // distance) % 2 == parity]
    return up + [(b, a) for a, b in up]


def plan_kernel(
    frags, own_count, list_len, where, map_ref, list_ref, energy, occ, table, *refs
):
    outs, own, plan, sems = refs[:6], refs[6], refs[7], refs[8]
    me = where[0]
    block = table.shape[1]
    copies = []

    def pick(fragment, owner):
        count = jnp.int32(0)
        picked = [jnp.int32(0)] * CAP
        for k in range(list_len):
            row = map_ref[list_ref[fragment, k]]
            hit = row // own_count == owner
            for r in range(CAP):
                picked[r] = jnp.where(hit & (count == r), row % own_count, picked[r])
            count = count + hit.astype(jnp.int32)
        return picked, count

    for index, (distance, parity) in enumerate(ROUNDS):
        up = (me // distance) % 2 == parity
        partner = jnp.where(up, me + distance, me - distance)
        inside = (partner >= 0) & (partner < frags)
        picked, count = pick(jnp.clip(partner, 0, frags - 1), me)
        for r in range(CAP):
            copies.append((
                inside & (count > r),
                pltpu.make_async_copy(
                    table.at[picked[r]], outs[index].at[pl.ds(r * block, block)], sems.at[index, r]
                ),
            ))
        if index == 0:
            picked, count = pick(me, me)
            for r in range(CAP):
                copies.append((
                    count > r,
                    pltpu.make_async_copy(
                        table.at[picked[r]], own.at[pl.ds(r * block, block)], sems.at[6, r]
                    ),
                ))
    for needed, copy in copies:
        pl.when(needed)(copy.start)
    for out in outs + (own,):
        out[pl.ds(CAP * block, TAIL), :] = jnp.zeros((TAIL, out.shape[1]), out.dtype)
    for out in outs:
        out[pl.ds(CAP * block, own_count), pl.ds(0, block)] = energy[...]
    own[pl.ds(CAP * block, occ.shape[0]), :] = occ[...]

    rows, owners, codes, classes = [], [], [], []
    for k in range(list_len):
        row = map_ref[list_ref[me, k]]
        owner = row // own_count
        low = jnp.minimum(me, owner)
        far = jnp.abs(owner - me)
        code = jnp.int32(0)
        for index, (distance, parity) in enumerate(ROUNDS):
            code = jnp.where(
                (far == distance) & ((low // distance) % 2 == parity), index + 1, code
            )
        rows.append(row)
        owners.append(owner)
        codes.append(code)
        classes.append(jnp.where(code == 0, 0, jnp.maximum(code - 3, 1)))
    for k in range(list_len):
        place = jnp.int32(0)
        rank = jnp.int32(0)
        for j in range(list_len):
            if j < k:
                place += (classes[j] <= classes[k]).astype(jnp.int32)
                rank += (owners[j] == owners[k]).astype(jnp.int32)
            elif j > k:
                place += (classes[j] < classes[k]).astype(jnp.int32)
        plan[0, place] = codes[k]
        plan[1, place] = rank
        plan[2, place] = rows[k]
        plan[3, place] = jnp.int32(k)
    for needed, copy in copies:
        pl.when(needed)(copy.wait)


def plan_and_pack(where, owner_map, vir_list, energy, occ, table, frags):
    own_count, block_rows, cols = table.shape
    list_len = vir_list.shape[1]
    part = jax.ShapeDtypeStruct((CAP * block_rows + TAIL, cols), table.dtype)
    return pl.pallas_call(
        functools.partial(plan_kernel, frags, own_count, list_len),
        out_shape=(part,) * 7 + (jax.ShapeDtypeStruct((4, list_len), jnp.int32),),
        in_specs=[SMEM, SMEM, SMEM, VMEM, VMEM, ANY],
        out_specs=(VMEM,) * 7 + (SMEM,),
        scratch_shapes=[pltpu.SemaphoreType.DMA((7, CAP))],
        compiler_params=pltpu.CompilerParams(vmem_limit_bytes=8 * MIB),
        cost_estimate=pl.CostEstimate(
            flops=0, bytes_accessed=4 * 7 * CAP * block_rows * cols, transcendentals=0
        ),
        name="plan_and_pack",
    )(where, owner_map, vir_list, energy, occ, table)


def pack_kernel(first, codes, block, with_energy, plan, *refs):
    count = len(codes)
    if with_energy:
        own_energy, arrived, (out, levels, raw, wide, sems, tail_sems) = (
            refs[0],
            refs[1 : count + 1],
            refs[count + 1 :],
        )
    else:
        arrived, (out, sems) = refs[:count], refs[count:]
    for i in range(2):
        code = plan[0, first + i]
        begin = pl.multiple_of(plan[1, first + i] * block, block)
        rows = pl.ds(i * block, block)
        for source, ref in zip(codes, arrived):

            @pl.when(code == source)
            def _(ref=ref, begin=begin, rows=rows):
                pltpu.make_async_copy(
                    ref.at[pl.ds(begin, block)], out.at[rows], sems.at[i]
                ).start()

    if with_energy:
        own_count = own_energy.shape[0]
        copies = [
            pltpu.make_async_copy(
                ref.at[pl.ds(2 * block, TAIL), pl.ds(0, block)],
                raw.at[pl.ds(n * TAIL, TAIL)],
                tail_sems.at[n],
            )
            for n, ref in enumerate(arrived)
        ]
        for copy in copies:
            copy.start()
        wide[0:own_count, :] = own_energy[...].astype(jnp.float32)
        for copy in copies:
            copy.wait()
        wide[TAIL:, :] = raw[...].astype(jnp.float32)
        for place in range(levels.shape[0]):
            row = plan[0, place] * TAIL + plan[2, place] % own_count
            levels[place : place + 1, :] = wide[pl.ds(row, 1), :]
    for i in range(2):
        rows = pl.ds(i * block, block)
        pltpu.make_async_copy(arrived[0].at[rows], out.at[rows], sems.at[i]).wait()


def pack_group(first, block, plan, arrived, own_energy=None):
    codes = tuple(arrived)
    refs = [arrived[c] for c in codes]
    cols, dtype = refs[0].shape[1], refs[0].dtype
    shapes = [jax.ShapeDtypeStruct((2 * block, cols), dtype)]
    scratch = [pltpu.SemaphoreType.DMA((2,))]
    extra = []
    if own_energy is not None:
        shapes.append(jax.ShapeDtypeStruct((plan.shape[1], block), jnp.float32))
        scratch = [
            pltpu.VMEM((len(codes) * TAIL, block), dtype),
            pltpu.VMEM(((len(codes) + 1) * TAIL, block), jnp.float32),
            *scratch,
            pltpu.SemaphoreType.DMA((len(codes),)),
        ]
        extra = [own_energy]
    return pl.pallas_call(
        functools.partial(pack_kernel, first, codes, block, own_energy is not None),
        out_shape=tuple(shapes),
        in_specs=[SMEM] + [VMEM] * len(extra) + [ANY] * len(refs),
        out_specs=(VMEM,) * len(shapes),
        scratch_shapes=scratch,
        compiler_params=pltpu.CompilerParams(vmem_limit_bytes=4 * MIB),
        cost_estimate=pl.CostEstimate(
            flops=0, bytes_accessed=8 * block * cols, transcendentals=0
        ),
        name="pack_group",
    )(plan, *extra, *refs)


def place_of(aux, b):
    return jnp.where(aux < 2, 2 * aux + b, aux + 2 + 2 * b)


def contract_kernel(stage, block, width, where, plan, levels, rows_ref, energy, *refs):
    groups = stage + 2
    parts, rest = refs[: groups * 4], refs[groups * 4 :]
    if stage == 2:
        before, rest = rest[:2], rest[2:]
        sent, stay, left, grid, occ, scaled, total, amps, tall, dens = rest[:10]
        left_sems, grid_sems, occ_sems = rest[10:]
    else:
        out, left, grid, occ, scaled, total, amps, left_sems, grid_sems, occ_sems = rest
    me, aux = where[0], where[1]
    places = (place_of(aux, 0), place_of(aux, 1))

    def occ_copy(quarter):
        return pltpu.make_async_copy(
            parts[quarter].at[pl.ds(2 * block, TAIL)],
            occ.at[pl.ds(quarter * TAIL, TAIL)],
            occ_sems.at[quarter],
        )

    def left_copy(b, group, begin, quarter):
        return pltpu.make_async_copy(
            parts[group * 4 + quarter].at[pl.ds(begin, block)],
            left.at[pl.ds(b * block, block), pl.ds(quarter * width, width)],
            left_sems.at[b, quarter],
        )

    def grid_copy(slot, group, quarter):
        return pltpu.make_async_copy(
            parts[group * 4 + quarter].at[pl.ds(0, 2 * block)],
            grid.at[pl.ds(slot * 2 * block, 2 * block), pl.ds(quarter * width, width)],
            grid_sems.at[slot, quarter],
        )

    def run(row_count, group_list):
        for quarter in range(4):
            occ_copy(quarter).start()
            for b in range(row_count):
                begin = pl.multiple_of((places[b] % 2) * block, block)
                for group in range(groups):

                    @pl.when(places[b] // 2 == group)
                    def _(b=b, group=group, begin=begin, quarter=quarter):
                        left_copy(b, group, begin, quarter).start()

            for slot, group in enumerate(group_list):
                grid_copy(slot, group, quarter).start()
        height = len(PAIRS) * row_count * block
        span = len(group_list) * 2 * block
        for quarter in range(4):
            cols = pl.ds(quarter * width, width)
            occ_copy(quarter).wait()
            for b in range(row_count):
                left_copy(b, 0, 0, quarter).wait()
            orbit = [
                occ[quarter * TAIL + i : quarter * TAIL + i + 1, :].astype(jnp.float32)
                for i in range(3)
            ]
            for b in range(row_count):
                rows = left[pl.ds(b * block, block), cols].astype(jnp.float32)
                for p, (i, j) in enumerate(PAIRS):
                    scaled[pl.ds((p * row_count + b) * block, block), :] = (
                        rows * (orbit[i] * orbit[j])
                    ).astype(jnp.bfloat16)
            for slot, group in enumerate(group_list):
                grid_copy(slot, group, quarter).wait()

            def rows_step(step, carry, quarter=quarter, cols=cols):
                rows = pl.ds(pl.multiple_of(step * 768, 768), 768)
                term = lax.dot_general(
                    scaled[rows, :],
                    grid[pl.ds(0, span), cols],
                    (((1,), (1,)), ((), ())),
                    preferred_element_type=jnp.float32,
                )
                if quarter == 0:
                    total[rows, pl.ds(0, span)] = term
                else:
                    total[rows, pl.ds(0, span)] += term
                return carry

            lax.fori_loop(0, height // 768, rows_step, 0)
        lane = lax.broadcasted_iota(jnp.int32, (block, block), 1)
        sub = lax.broadcasted_iota(jnp.int32, (block, block), 0)
        sums = []
        for b in range(row_count):
            own_row = energy[pl.ds(places[b], 1), :]
            own_energy = jnp.transpose(jnp.broadcast_to(own_row, (block, block)))
            own_live = sub < rows_ref[me, plan[3, places[b]]]
            for q in range(2 * len(group_list)):
                place = 2 * group_list[q // 2] + q % 2
                their_energy = energy[place : place + 1, :]
                live = own_live & (lane < rows_ref[me, plan[3, place]])
                for p, (i, j) in enumerate(PAIRS):
                    gap = (levels[0, i] + levels[0, j]) - own_energy - their_energy
                    rows = pl.ds((p * row_count + b) * block, block)
                    value = total[rows, pl.ds(q * block, block)]
                    amp = jnp.where(live, value / gap, 0.0).astype(jnp.bfloat16)
                    amps[:, pl.ds(p * span + q * block, block)] = amp
                    if stage == 2:
                        early = amp if b == 0 else jnp.where(aux < 2, amp, jnp.zeros_like(amp))
                        tall[rows, pl.ds(q * block, block)] = early
            wide = amps[:, pl.ds(0, len(PAIRS) * span)]
            sums.append(
                lax.dot_general(
                    wide, wide, (((1,), (1,)), ((), ())), preferred_element_type=jnp.float32
                )
            )
        return sums

    if stage == 0:

        @pl.when(aux < 2)
        def _():
            out[0], out[1] = run(2, (0, 1))

        @pl.when(aux >= 2)
        def _():
            out[...] = jnp.zeros_like(out)
    elif stage == 1:

        @pl.when(aux < 2)
        def _():
            out[0], out[1] = run(2, (2,))

        @pl.when(aux >= 2)
        def _():
            out[0] = run(1, (0, 1, 2))[0]
            out[1] = jnp.zeros(out.shape[1:], out.dtype)
    else:
        sums = run(2, (3,))
        for b in range(2):
            dens[b] = sums[b] + (before[0][b] + before[1][b])
        for q in range(2):
            late = tall[:, pl.ds(q * block, block)]
            dens[2 + q] = lax.dot_general(
                late, late, (((0,), (0,)), ((), ())), preferred_element_type=jnp.float32
            )
        half = block // 2
        side = aux // 2
        stay[...] = dens[:, pl.ds(pl.multiple_of(side * half, half), half), :]
        sent[...] = dens[:, pl.ds(pl.multiple_of((1 - side) * half, half), half), :]


def contract(stage, where, plan, levels, vir_rows, energy, parts, before=()):
    block, width = energy.shape[1], parts[0].shape[1]
    height = len(PAIRS) * 2 * block
    spans = {0: (4, 1), 1: (6, 1), 2: (2, 1)}
    span = spans[stage][0] * block
    scratch = [
        pltpu.VMEM((2 * block, 4 * width), jnp.bfloat16),
        pltpu.VMEM((span, 4 * width), jnp.bfloat16),
        pltpu.VMEM((4 * TAIL, width), jnp.bfloat16),
        pltpu.VMEM((height, width), jnp.bfloat16),
        pltpu.VMEM((height, span), jnp.float32),
        pltpu.VMEM((block, len(PAIRS) * span), jnp.bfloat16),
    ]
    if stage == 2:
        scratch += [
            pltpu.VMEM((height, span), jnp.bfloat16),
            pltpu.VMEM((4, block, block), jnp.float32),
        ]
        out_shape = (jax.ShapeDtypeStruct((4, block // 2, block), jnp.float32),) * 2
        out_specs = (VMEM, VMEM)
    else:
        out_shape = jax.ShapeDtypeStruct((2, block, block), jnp.float32)
        out_specs = VMEM
    scratch += [
        pltpu.SemaphoreType.DMA((2, 4)),
        pltpu.SemaphoreType.DMA((3, 4)),
        pltpu.SemaphoreType.DMA((4,)),
    ]
    return pl.pallas_call(
        functools.partial(contract_kernel, stage, block, width),
        out_shape=out_shape,
        in_specs=[SMEM] * 4 + [VMEM] + [ANY] * len(parts) + [VMEM] * len(before),
        out_specs=out_specs,
        scratch_shapes=scratch,
        compiler_params=pltpu.CompilerParams(vmem_limit_bytes=22 * MIB),
        cost_estimate=pl.CostEstimate(
            flops=2 * height * min(span, 4 * block) * 4 * width,
            bytes_accessed=span * 4 * width * 2,
            transcendentals=0,
        ),
        name="contract",
    )(where, plan, levels, vir_rows, energy, *parts, *before)


def spread_kernel(own_count, where, plan, kept, came, out):
    aux = where[1]
    out[...] = jnp.zeros_like(out)
    holders = (aux, aux ^ 2, aux ^ 1, aux ^ 3)
    late = [kept[4 + q] + came[4 + q] for q in range(2)]
    for index, holder in enumerate(holders):
        source = kept if index < 2 else came
        for b in range(2):
            place = place_of(holder, b)
            value = source[2 * (index % 2) + b]
            if b == 1:
                value += jnp.where(place == 6, late[0], jnp.where(place == 7, late[1], 0.0))
            out[plan[2, place] // own_count, plan[1, place]] = value


def spread(where, plan, kept, came, frags, own_count):
    return pl.pallas_call(
        functools.partial(spread_kernel, own_count),
        out_shape=jax.ShapeDtypeStruct((frags, CAP) + kept.shape[1:], kept.dtype),
        in_specs=[SMEM, SMEM, VMEM, VMEM],
        out_specs=VMEM,
        name="spread",
    )(where, plan, kept, came)


def collect_kernel(own_count, list_len, where, map_ref, list_ref, came, out):
    me = where[0]
    out[...] = jnp.zeros_like(out)

    def one(fragment, carry):
        count = jnp.int32(0)
        for k in range(list_len):
            row = map_ref[list_ref[fragment, k]]
            hit = row // own_count == me

            @pl.when(hit)
            def _(row=row, count=count):
                out[row % own_count] += came[fragment, count]

            count = count + hit.astype(jnp.int32)
        return carry

    lax.fori_loop(0, list_ref.shape[0], one, 0)


def collect(where, owner_map, vir_list, came, own_count):
    return pl.pallas_call(
        functools.partial(collect_kernel, own_count, vir_list.shape[1]),
        out_shape=jax.ShapeDtypeStruct((own_count,) + came.shape[2:], came.dtype),
        in_specs=[SMEM, SMEM, SMEM, VMEM],
        out_specs=VMEM,
        name="collect",
    )(where, owner_map, vir_list, came)


def body(vir_grid, vir_energy, occ_grid, occ_energy, vir_list, vir_rows, owner_map):
    frags = lax.axis_size("frag")
    aux_count = lax.axis_size("aux")
    me = lax.axis_index("frag").astype(jnp.int32)
    aux = lax.axis_index("aux").astype(jnp.int32)
    own_count, block, width = vir_grid.shape
    list_len = vir_list.shape[1]
    where = jnp.stack([me, aux])
    far_pairs = [(i, i ^ 2) for i in range(aux_count)]
    near_pairs = [(i, i ^ 1) for i in range(aux_count)]

    *outgoing, own, plan = plan_and_pack(
        where, owner_map, vir_list, vir_energy, occ_grid[0], vir_grid, frags
    )

    def over_aux(here):
        far = lax.ppermute(here, "aux", far_pairs)
        near = lax.ppermute(here, "aux", near_pairs)
        return [here, far, near, lax.ppermute(far, "aux", near_pairs)]

    def after(value, *others):
        return lax.optimization_barrier((value, *others))[0]

    def send(index, *others):
        distance, parity = ROUNDS[index]
        payload = after(outgoing[index], *others) if others else outgoing[index]
        return lax.ppermute(payload, "frag", round_pairs(distance, parity, frags))

    arrived = {code: send(code - 1) for code in (1, 2, 3, 4)}
    parts = over_aux(own)
    arrived[5] = send(4, *(arrived[c] for c in (1, 2, 3, 4)), parts[1])
    here = pack_group(2, block, plan, {c: arrived[c] for c in range(1, 5)})[0]
    arrived[6] = send(5, arrived[5], here)
    parts += over_aux(here)
    here = pack_group(4, block, plan, {c: arrived[c] for c in range(1, 6)})[0]
    parts += over_aux(here)
    here, energy = pack_group(6, block, plan, arrived, vir_energy)
    parts += over_aux(here)
    shared = (where, plan, occ_energy, vir_rows, energy)
    first = contract(0, *shared, parts[:8])
    second = contract(1, *shared, parts[:12])
    sent, stay = contract(2, *shared, parts, (first, second))

    quarter = block // aux_count
    core = aux % 2
    met = lax.ppermute(sent, "aux", far_pairs)
    both = jnp.concatenate([stay[:2], met[:2], stay[2:] + met[2:]], axis=0)
    sent = lax.dynamic_slice_in_dim(both, (1 - core) * quarter, quarter, 1)
    kept = lax.dynamic_slice_in_dim(both, core * quarter, quarter, 1)
    came = lax.ppermute(sent, "aux", near_pairs)
    outgoing = spread(where, plan, kept, came, frags, own_count)
    incoming = lax.all_to_all(outgoing, "frag", 0, 0, tiled=True)
    return collect(where, owner_map, vir_list, incoming, own_count)


def solution(mesh):
    return jax.shard_map(
        body,
        mesh=mesh,
        in_specs=(
            P("frag", None, "aux"),
            P("frag", None),
            P("frag", None, "aux"),
            P("frag", None),
            P(),
            P(),
            P(),
        ),
        out_specs=P("frag", "aux", None),
        check_vma=False,
    )
```

time: 147 us -> 140 us (0.952)
  local copies, waits for them, and re-layouts: 12.9 us -> 3.24 us
  waiting for transfers between devices: 51.3 us -> 57.3 us
  other arithmetic: 2.53 us -> 0.11 us
    ppermute x19, waiting for transfers between devices: 50 us -> 56 us  [the longest x6 27 us: send(): return lax.ppermute(payload, 'frag', round_pairs(distance, parity, frags))]
    slice x6 -> x0, local copies, waits for them, and re-layouts: 3.98 us -> none  [body(): arrived[c][tail:tail + own_count, :block]]
    another operation x4 -> x0, local copies, waits for them, and re-layouts: 2.87 us -> none  [body(): weights = jnp.stack([part[tail:] for part in parts[:4]])]
    pallas_call x5 -> x7, Pallas kernels: 32.1 us -> 34.4 us  [the longest x3 30.5 us: contract(): pl.pallas_call(functools.partial(contract_kernel, stage, block, width), o...]
    pallas_call x1, Pallas kernels: 4.46 us -> 2.49 us  [plan_and_pack(): pl.pallas_call(functools.partial(plan_kernel, frags, own_count, list_len)...]
    unnamed x28 -> x20, local copies, waits for them, and re-layouts: 3.88 us -> 2.58 us
  transfers between devices with their start and end apart: 20 -> 20, of which waited for: 6 -> 9; matrix products, arithmetic and copies ran while one was open for 6% -> 0% of each run, Pallas kernels for 5% -> 17%
where the time goes in v3:
time: 140 us
  waiting for transfers between devices  57.3 us (41%)
  Pallas kernels  39.7 us (28%)
  starting transfers between devices  22.2 us (16%)
  blocking collectives  17 us (12%)
  local copies, waits for them, and re-layouts  3.24 us (2%)
    pallas_call x3, Pallas kernels, contract(): pl.pallas_call(functools.partial(contract_kernel, stage, block, width), o...  30.5 us
    ppermute x6, waiting for transfers between devices, send(): return lax.ppermute(payload, 'frag', round_pairs(distance, parity, frags))  27 us
    ppermute x4, waiting for transfers between devices, over_aux(): far = lax.ppermute(here, 'aux', far_pairs)  24.8 us
    all_to_all x1, blocking collectives, body(): incoming = lax.all_to_all(outgoing, 'frag', 0, 0, tiled=True)  17 us
    ppermute x6, starting transfers between devices, send(): return lax.ppermute(payload, 'frag', round_pairs(distance, parity, frags))  11.3 us
    ppermute x4, starting transfers between devices, over_aux(): far = lax.ppermute(here, 'aux', far_pairs)  6.33 us
    ppermute x1, waiting for transfers between devices, body(): met = lax.ppermute(sent, 'aux', far_pairs)  4.15 us
    ppermute x1, starting transfers between devices, body(): met = lax.ppermute(sent, 'aux', far_pairs)  3.27 us
  transfers between devices with their start and end apart: 20, of which 9 were waited for; matrix products, arithmetic and copies ran while one was open for 0% of the time, Pallas kernels for 17%

profile of v3, /device:TPU:0, one launch (start us, length us, event | category | flops | bytes accessed | tf_op | source)
XLA Modules:
  0.0 139.7 jit_solution(846126395062409964)
XLA Ops:
  0.8 1.2 copy-done
  2.0 2.5 %plan_and_pack.1 = (bf16[272,1024]{1,0:T(8,128)(2,1)S(1)}, bf16[272,1024]{1,0:T(8,128)(2,1)S(1)}, bf16[272,1024]{1,0:T(8,128)(2,1)S(1)}, bf16[272,1024]{1,0:T(8,...) custom-call(s32[2]{0:T(128)S(1)} %pad_add_fusion.where, ...), custom_call_target="tpu_custom_call" | custom-call | bytes 7340032 | tf_op jit(solution)/shard_map/plan_and_pack/pallas_call | solution.py:109
  4.5 3.0 %collective-permute-start.4 = (bf16[272,1024]{1,0:T(8,128)(2,1)S(1)}, bf16[272,1024]{1,0:T(8,128)(2,1)S(1)}, u32[]{:S(2)}, u32[]{:S(2)}) collective-permute-start(bf16[272,1024]{1,0:T(8,128)(2,1)S(1)} %get-tuple-element.25.refs_0_), channel_id=1, source_target_pairs={{0,2},{1,3},{2,0},{3,1},{4,6},{5,7},{6,4},{7,5},{8,10},{9,11},{10,... | collective-permute-start | bytes 1671176 | tf_op jit(solution)/shard_map/ppermute | solution.py:461
  7.5 1.5 %collective-permute-start = (bf16[272,1024]{1,0:T(8,128)(2,1)S(1)}, bf16[272,1024]{1,0:T(8,128)(2,1)S(1)}, u32[]{:S(2)}, u32[]{:S(2)}) collective-permute-start(bf16[272,1024]{1,0:T(8,128)(2,1)S(1)} %get-tuple-element.20), channel_id=1, source_target_pairs={{0,4},{8,12},{16,20},{24,28},{4,0},{12,8},{20,16},{28,24},{1,5},{9... | collective-permute-start | bytes 1671176 | tf_op jit(solution)/shard_map/ppermute | solution.py:471
  9.8 3.2 %collective-permute-start.2 = (bf16[272,1024]{1,0:T(8,128)(2,1)S(1)}, bf16[272,1024]{1,0:T(8,128)(2,1)S(1)}, u32[]{:S(2)}, u32[]{:S(2)}) collective-permute-start(bf16[272,1024]{1,0:T(8,128)(2,1)S(1)} %get-tuple-element.22), channel_id=1, source_target_pairs={{0,8},{4,12},{16,24},{20,28},{8,0},{12,4},{24,16},{28,20},{1,9},{5... | collective-permute-start | bytes 1671176 | tf_op jit(solution)/shard_map/ppermute | solution.py:471
  13.7 6.5 %collective-permute-done.4.refs_1_ = bf16[272,1024]{1,0:T(8,128)(2,1)S(1)} collective-permute-done((bf16[272,1024]{1,0:T(8,128)(2,1)S(1)}, bf16[272,1024]{1,0:T(8,128)(2,1)S(1)}, u32[]{:S(2)}, u32[]{:S(2)}) %collective-permute-start.4) | collective-permute-done | bytes 557088 | tf_op jit(solution)/shard_map/ppermute | solution.py:461
  20.2 12.4 %collective-permute-done.refs_0_.refs_1_ = bf16[272,1024]{1,0:T(8,128)(2,1)S(1)} collective-permute-done((bf16[272,1024]{1,0:T(8,128)(2,1)S(1)}, bf16[272,1024]{1,0:T(8,128)(2,1)S(1)}, u32[]{:S(2)}, u32[]{:S(2)}) %collective-permute-start) | collective-permute-done | bytes 557088 | tf_op jit(solution)/shard_map/ppermute | solution.py:471
  32.6 4.1 %collective-permute-done.2.refs_2_.refs_3_ = bf16[272,1024]{1,0:T(8,128)(2,1)S(1)} collective-permute-done((bf16[272,1024]{1,0:T(8,128)(2,1)S(1)}, bf16[272,1024]{1,0:T(8,128)(2,1)S(1)}, u32[]{:S(2)}, u32[]{:S(2)}) %collective-permute-start.2) | collective-permute-done | bytes 557088 | tf_op jit(solution)/shard_map/ppermute | solution.py:471
  36.7 4.5 %collective-permute-start.5 = (bf16[272,1024]{1,0:T(8,128)(2,1)S(1)}, bf16[272,1024]{1,0:T(8,128)(2,1)S(1)}, u32[]{:S(2)}, u32[]{:S(2)}) collective-permute-start(bf16[272,1024]{1,0:T(8,128)(2,1)S(1)} %get-tuple-element.26), channel_id=1, source_target_pairs={{0,12},{4,16},{8,20},{12,0},{16,4},{20,8},{1,13},{5,17},{9,21},{13... | collective-permute-start | bytes 1671176 | tf_op jit(solution)/shard_map/ppermute | solution.py:471
  41.9 10.5 %collective-permute-done.5.refs_5_.refs_4_ = bf16[272,1024]{1,0:T(8,128)(2,1)S(1)} collective-permute-done((bf16[272,1024]{1,0:T(8,128)(2,1)S(1)}, bf16[272,1024]{1,0:T(8,128)(2,1)S(1)}, u32[]{:S(2)}, u32[]{:S(2)}) %collective-permute-start.5) | collective-permute-done | bytes 557088 | tf_op jit(solution)/shard_map/ppermute | solution.py:471
  53.1 0.9 collective-permute-start.9
  55.2 1.3 collective-permute-start.12
  56.5 11.6 %collective-permute-done.9.refs_5_ = bf16[256,1024]{1,0:T(8,128)(2,1)S(1)} collective-permute-done((bf16[256,1024]{1,0:T(8,128)(2,1)S(1)}, bf16[256,1024]{1,0:T(8,128)(2,1)S(1)}, u32[]{:S(2)}, u32[]{:S(2)}) %collective-permute-start.9) | collective-permute-done | bytes 524320 | tf_op jit(solution)/shard_map/ppermute | solution.py:461
  69.4 6.3 %collective-permute-done.12.refs_9_ = bf16[256,1024]{1,0:T(8,128)(2,1)S(1)} collective-permute-done((bf16[256,1024]{1,0:T(8,128)(2,1)S(1)}, bf16[256,1024]{1,0:T(8,128)(2,1)S(1)}, u32[]{:S(2)}, u32[]{:S(2)}) %collective-permute-start.12) | collective-permute-done | bytes 524320 | tf_op jit(solution)/shard_map/ppermute | solution.py:461
  75.7 1.1 collective-permute-start.15
  77.0 12.6 %contract.3.refs_16_ = f32[2,128,128]{2,1,0:T(8,128)S(1)} custom-call(s32[2]{0:T(128)S(1)} %pad_add_fusion.where, s32[4,8]{1,0:T(4,128)S(1)} %get-tuple-element.19.plan, f32[1,3]{1,0:T(1,128)S(1)} %copy-done.8, s32[8,8]{1,0:T(8,128)S(1)} %copy-done.7, f32[8,128]{1,0:T(8,128)S(1)} %get-tuple-element.29.energy, ...), custom_call_target="tpu_custom_call" | custom-call | flops 6442450944 | bytes 4194304 | tf_op jit(solution)/shard_map/contract/pallas_call | solution.py:374
  90.1 9.0 %contract.4.refs_17_ = f32[2,128,128]{2,1,0:T(8,128)S(1)} custom-call(s32[2]{0:T(128)S(1)} %pad_add_fusion.where, s32[4,8]{1,0:T(4,128)S(1)} %get-tuple-element.19.plan, f32[1,3]{1,0:T(1,128)S(1)} %copy-done.8, s32[8,8]{1,0:T(8,128)S(1)} %copy-done.7, f32[8,128]{1,0:T(8,128)S(1)} %get-tuple-element.29.energy, ...), custom_call_target="tpu_custom_call" | custom-call | flops 6442450944 | bytes 6291456 | tf_op jit(solution)/shard_map/contract/pallas_call | solution.py:374
  99.1 9.0 %contract.5 = (f32[4,64,128]{2,1,0:T(8,128)S(1)}, f32[4,64,128]{2,1,0:T(8,128)S(1)}) custom-call(s32[2]{0:T(128)S(1)} %pad_add_fusion.where, s32[4,8]{1,0:T(4,128)S(1)} %get-tuple-element.19.plan, f32[1,3]{1,0:T(1,128)S(1)} %copy-done.8, s32[8,8]{1,0:T(8,128)S(1)} %copy-done.7, f32[8,128]{1,0:T(8,128)S(1)} %get-tuple-element.29.energy, ...), custom_call_target="tpu_custom_call" | custom-call | flops 3221225472 | bytes 2097152 | tf_op jit(solution)/shard_map/contract/pallas_call | solution.py:374
  108.1 3.3 %collective-permute-start.18 = (f32[4,64,128]{2,1,0:T(8,128)S(1)}, f32[4,64,128]{2,1,0:T(8,128)S(1)}, u32[]{:S(2)}, u32[]{:S(2)}) collective-permute-start(f32[4,64,128]{2,1,0:T(8,128)S(1)} %get-tuple-element.32), channel_id=1, source_target_pairs={{0,2},{1,3},{2,0},{3,1},{4,6},{5,7},{6,4},{7,5},{8,10},{9,11},{10,... | collective-permute-start | bytes 393224 | tf_op jit(solution)/shard_map/ppermute | solution.py:490
  111.4 4.2 %collective-permute-done.18 = f32[4,64,128]{2,1,0:T(8,128)S(1)} collective-permute-done((f32[4,64,128]{2,1,0:T(8,128)S(1)}, f32[4,64,128]{2,1,0:T(8,128)S(1)}, u32[]{:S(2)}, u32[]{:S(2)}) %collective-permute-start.18) | collective-permute-done | bytes 131104 | tf_op jit(solution)/shard_map/ppermute | solution.py:490
  116.2 1.3 collective-permute-done.19.came
  118.2 1.7 %spread.1 = f32[8,2,32,128]{3,2,1,0:T(8,128)} custom-call(s32[2]{0:T(128)} %copy-done.4, s32[4,8]{1,0:T(4,128)} %copy-done.1, f32[6,32,128]{2,1,0:T(8,128)} %get-tuple-element.34.kept, f32[6,32,128]{2,1,0:T(8,128)} %copy-done.9), custom_call_target="tpu_custom_call" | custom-call | tf_op jit(solution)/shard_map/spread/pallas_call | solution.py:406
  119.9 17.0 %all_to_all.5.came = f32[8,2,32,128]{3,2,1,0:T(8,128)} all-to-all(f32[8,2,32,128]{3,2,1,0:T(8,128)} %spread.1), channel_id=1, replica_groups=mesh['frag'=8,'aux'=4] {'frag'}, dimensions={0} | all-to-all | bytes 524288 | tf_op jit(solution)/shard_map/all_to_all | solution.py:496
  136.9 2.8 %collect.1 = f32[4,32,128]{2,1,0:T(8,128)} custom-call(s32[2]{0:T(128)} %copy-done.4, s32[32]{0:T(128)} %map_ref.3, s32[8,8]{1,0:T(8,128)} %list_ref.3, f32[8,2,32,128]{3,2,1,0:T(8,128)} %all_to_all.5.came), custom_call_target="tpu_custom_call" | custom-call | tf_op jit(solution)/shard_map/collect/pallas_call | solution.py:436
  (50 shorter events, 8.1 us)
Async XLA Ops:
  0.1 99.0 %copy-start.4 = (s32[2]{0:T(128)}, s32[2]{0:T(128)S(1)}, u32[]{:S(2)}) copy-start(s32[2]{0:T(128)S(1)} %pad_add_fusion.where) | copy-start | bytes 28
  4.5 94.6 %copy-start.1 = (s32[4,8]{1,0:T(4,128)}, s32[4,8]{1,0:T(4,128)S(1)}, u32[]{:S(2)}) copy-start(s32[4,8]{1,0:T(4,128)S(1)} %get-tuple-element.19.plan) | copy-start | bytes 388
  4.5 15.7 %collective-permute-start.4 = (bf16[272,1024]{1,0:T(8,128)(2,1)S(1)}, bf16[272,1024]{1,0:T(8,128)(2,1)S(1)}, u32[]{:S(2)}, u32[]{:S(2)}) collective-permute-start(bf16[272,1024]{1,0:T(8,128)(2,1)S(1)} %get-tuple-element.25.refs_0_), channel_id=1, source_target_pairs={{0,2},{1,3},{2,0},{3,1},{4,6},{5,7},{6,4},{7,5},{8,10},{9,11},{10,... | collective-permute-start | bytes 1671176 | tf_op jit(solution)/shard_map/ppermute | solution.py:461
  7.5 25.1 %collective-permute-start = (bf16[272,1024]{1,0:T(8,128)(2,1)S(1)}, bf16[272,1024]{1,0:T(8,128)(2,1)S(1)}, u32[]{:S(2)}, u32[]{:S(2)}) collective-permute-start(bf16[272,1024]{1,0:T(8,128)(2,1)S(1)} %get-tuple-element.20), channel_id=1, source_target_pairs={{0,4},{8,12},{16,20},{24,28},{4,0},{12,8},{20,16},{28,24},{1,5},{9... | collective-permute-start | bytes 1671176 | tf_op jit(solution)/shard_map/ppermute | solution.py:471
  9.1 23.5 %collective-permute-start.1 = (bf16[272,1024]{1,0:T(8,128)(2,1)S(1)}, bf16[272,1024]{1,0:T(8,128)(2,1)S(1)}, u32[]{:S(2)}, u32[]{:S(2)}) collective-permute-start(bf16[272,1024]{1,0:T(8,128)(2,1)S(1)} %get-tuple-element.21), channel_id=1, source_target_pairs={{4,8},{12,16},{20,24},{8,4},{16,12},{24,20},{5,9},{13,17},{21,25},... | collective-permute-start | bytes 1671176 | tf_op jit(solution)/shard_map/ppermute | solution.py:471
  9.8 26.9 %collective-permute-start.2 = (bf16[272,1024]{1,0:T(8,128)(2,1)S(1)}, bf16[272,1024]{1,0:T(8,128)(2,1)S(1)}, u32[]{:S(2)}, u32[]{:S(2)}) collective-permute-start(bf16[272,1024]{1,0:T(8,128)(2,1)S(1)} %get-tuple-element.22), channel_id=1, source_target_pairs={{0,8},{4,12},{16,24},{20,28},{8,0},{12,4},{24,16},{28,20},{1,9},{5... | collective-permute-start | bytes 1671176 | tf_op jit(solution)/shard_map/ppermute | solution.py:471
  13.0 23.7 %collective-permute-start.3 = (bf16[272,1024]{1,0:T(8,128)(2,1)S(1)}, bf16[272,1024]{1,0:T(8,128)(2,1)S(1)}, u32[]{:S(2)}, u32[]{:S(2)}) collective-permute-start(bf16[272,1024]{1,0:T(8,128)(2,1)S(1)} %get-tuple-element.23), channel_id=1, source_target_pairs={{8,16},{12,20},{16,8},{20,12},{9,17},{13,21},{17,9},{21,13},{10,18... | collective-permute-start | bytes 1671176 | tf_op jit(solution)/shard_map/ppermute | solution.py:471
  36.7 15.7 %collective-permute-start.5 = (bf16[272,1024]{1,0:T(8,128)(2,1)S(1)}, bf16[272,1024]{1,0:T(8,128)(2,1)S(1)}, u32[]{:S(2)}, u32[]{:S(2)}) collective-permute-start(bf16[272,1024]{1,0:T(8,128)(2,1)S(1)} %get-tuple-element.26), channel_id=1, source_target_pairs={{0,12},{4,16},{8,20},{12,0},{16,4},{20,8},{1,13},{5,17},{9,21},{13... | collective-permute-start | bytes 1671176 | tf_op jit(solution)/shard_map/ppermute | solution.py:471
  52.4 15.6 %collective-permute-start.6 = (bf16[272,1024]{1,0:T(8,128)(2,1)S(1)}, bf16[272,1024]{1,0:T(8,128)(2,1)S(1)}, u32[]{:S(2)}, u32[]{:S(2)}) collective-permute-start(bf16[272,1024]{1,0:T(8,128)(2,1)S(1)} %get-tuple-element.28), channel_id=1, source_target_pairs={{12,24},{16,28},{24,12},{28,16},{13,25},{17,29},{25,13},{29,17},{1... | collective-permute-start | bytes 1671176 | tf_op jit(solution)/shard_map/ppermute | solution.py:471
  53.1 14.9 %collective-permute-start.9 = (bf16[256,1024]{1,0:T(8,128)(2,1)S(1)}, bf16[256,1024]{1,0:T(8,128)(2,1)S(1)}, u32[]{:S(2)}, u32[]{:S(2)}) collective-permute-start(bf16[256,1024]{1,0:T(8,128)(2,1)S(1)} %pack_group.3.refs_4_), channel_id=1, source_target_pairs={{0,2},{1,3},{2,0},{3,1},{4,6},{5,7},{6,4},{7,5},{8,10},{9,11},{10,... | collective-permute-start | bytes 1572872 | tf_op jit(solution)/shard_map/ppermute | solution.py:461
  53.9 15.4 %collective-permute-start.7 = (bf16[272,1024]{1,0:T(8,128)(2,1)S(1)}, bf16[272,1024]{1,0:T(8,128)(2,1)S(1)}, u32[]{:S(2)}, u32[]{:S(2)}) collective-permute-start(bf16[272,1024]{1,0:T(8,128)(2,1)S(1)} %get-tuple-element.25.refs_0_), channel_id=1, source_target_pairs={{0,1},{1,0},{2,3},{3,2},{4,5},{5,4},{6,7},{7,6},{8,9},{9,8},{10,11... | collective-permute-start | bytes 1671176 | tf_op jit(solution)/shard_map/ppermute | solution.py:462
  53.9 22.9 %collective-permute-start.8 = (bf16[272,1024]{1,0:T(8,128)(2,1)S(1)}, bf16[272,1024]{1,0:T(8,128)(2,1)S(1)}, u32[]{:S(2)}, u32[]{:S(2)}) collective-permute-start(bf16[272,1024]{1,0:T(8,128)(2,1)S(1)} %collective-permute-done.4.refs_1_), channel_id=1, source_target_pairs={{0,1},{1,0},{2,3},{3,2},{4,5},{5,4},{6,7},{7,6},{8,9},{9,8},{10,11... | collective-permute-start | bytes 1671176 | tf_op jit(solution)/shard_map/ppermute | solution.py:463
  55.1 21.9 %copy-start.7 = (s32[8,8]{1,0:T(8,128)S(1)}, s32[8,8]{1,0:T(8,128)}, u32[]{:S(2)}) copy-start(s32[8,8]{1,0:T(8,128)} %rows_ref.5) | copy-start | bytes 772
  55.2 20.5 %collective-permute-start.12 = (bf16[256,1024]{1,0:T(8,128)(2,1)S(1)}, bf16[256,1024]{1,0:T(8,128)(2,1)S(1)}, u32[]{:S(2)}, u32[]{:S(2)}) collective-permute-start(bf16[256,1024]{1,0:T(8,128)(2,1)S(1)} %pack_group.5.refs_8_), channel_id=1, source_target_pairs={{0,2},{1,3},{2,0},{3,1},{4,6},{5,7},{6,4},{7,5},{8,10},{9,11},{10,... | collective-permute-start | bytes 1572872 | tf_op jit(solution)/shard_map/ppermute | solution.py:461
  68.0 7.7 %collective-permute-start.10 = (bf16[256,1024]{1,0:T(8,128)(2,1)S(1)}, bf16[256,1024]{1,0:T(8,128)(2,1)S(1)}, u32[]{:S(2)}, u32[]{:S(2)}) collective-permute-start(bf16[256,1024]{1,0:T(8,128)(2,1)S(1)} %pack_group.3.refs_4_), channel_id=1, source_target_pairs={{0,1},{1,0},{2,3},{3,2},{4,5},{5,4},{6,7},{7,6},{8,9},{9,8},{10,11... | collective-permute-start | bytes 1572872 | tf_op jit(solution)/shard_map/ppermute | solution.py:462
  68.0 9.0 %collective-permute-start.11 = (bf16[256,1024]{1,0:T(8,128)(2,1)S(1)}, bf16[256,1024]{1,0:T(8,128)(2,1)S(1)}, u32[]{:S(2)}, u32[]{:S(2)}) collective-permute-start(bf16[256,1024]{1,0:T(8,128)(2,1)S(1)} %collective-permute-done.9.refs_5_), channel_id=1, source_target_pairs={{0,1},{1,0},{2,3},{3,2},{4,5},{5,4},{6,7},{7,6},{8,9},{9,8},{10,11... | collective-permute-start | bytes 1572872 | tf_op jit(solution)/shard_map/ppermute | solution.py:463
  69.3 20.7 %collective-permute-start.13 = (bf16[256,1024]{1,0:T(8,128)(2,1)S(1)}, bf16[256,1024]{1,0:T(8,128)(2,1)S(1)}, u32[]{:S(2)}, u32[]{:S(2)}) collective-permute-start(bf16[256,1024]{1,0:T(8,128)(2,1)S(1)} %pack_group.5.refs_8_), channel_id=1, source_target_pairs={{0,1},{1,0},{2,3},{3,2},{4,5},{5,4},{6,7},{7,6},{8,9},{9,8},{10,11... | collective-permute-start | bytes 1572872 | tf_op jit(solution)/shard_map/ppermute | solution.py:462
  75.7 14.4 %collective-permute-start.14 = (bf16[256,1024]{1,0:T(8,128)(2,1)S(1)}, bf16[256,1024]{1,0:T(8,128)(2,1)S(1)}, u32[]{:S(2)}, u32[]{:S(2)}) collective-permute-start(bf16[256,1024]{1,0:T(8,128)(2,1)S(1)} %collective-permute-done.12.refs_9_), channel_id=1, source_target_pairs={{0,1},{1,0},{2,3},{3,2},{4,5},{5,4},{6,7},{7,6},{8,9},{9,8},{10,11... | collective-permute-start | bytes 1572872 | tf_op jit(solution)/shard_map/ppermute | solution.py:463
  75.7 1.3 copy-start.8
  75.7 14.3 %collective-permute-start.15 = (bf16[256,1024]{1,0:T(8,128)(2,1)S(1)}, bf16[256,1024]{1,0:T(8,128)(2,1)S(1)}, u32[]{:S(2)}, u32[]{:S(2)}) collective-permute-start(bf16[256,1024]{1,0:T(8,128)(2,1)S(1)} %get-tuple-element.30.refs_12_), channel_id=1, source_target_pairs={{0,2},{1,3},{2,0},{3,1},{4,6},{5,7},{6,4},{7,5},{8,10},{9,11},{10,... | collective-permute-start | bytes 1572872 | tf_op jit(solution)/shard_map/ppermute | solution.py:461
  76.9 22.2 %collective-permute-start.16 = (bf16[256,1024]{1,0:T(8,128)(2,1)S(1)}, bf16[256,1024]{1,0:T(8,128)(2,1)S(1)}, u32[]{:S(2)}, u32[]{:S(2)}) collective-permute-start(bf16[256,1024]{1,0:T(8,128)(2,1)S(1)} %get-tuple-element.30.refs_12_), channel_id=1, source_target_pairs={{0,1},{1,0},{2,3},{3,2},{4,5},{5,4},{6,7},{7,6},{8,9},{9,8},{10,11... | collective-permute-start | bytes 1572872 | tf_op jit(solution)/shard_map/ppermute | solution.py:462
  90.0 9.0 %collective-permute-start.17 = (bf16[256,1024]{1,0:T(8,128)(2,1)S(1)}, bf16[256,1024]{1,0:T(8,128)(2,1)S(1)}, u32[]{:S(2)}, u32[]{:S(2)}) collective-permute-start(bf16[256,1024]{1,0:T(8,128)(2,1)S(1)} %collective-permute-done.15.refs_13_), channel_id=1, source_target_pairs={{0,1},{1,0},{2,3},{3,2},{4,5},{5,4},{6,7},{7,6},{8,9},{9,8},{10,11... | collective-permute-start | bytes 1572872 | tf_op jit(solution)/shard_map/ppermute | solution.py:463
  108.1 7.4 %collective-permute-start.18 = (f32[4,64,128]{2,1,0:T(8,128)S(1)}, f32[4,64,128]{2,1,0:T(8,128)S(1)}, u32[]{:S(2)}, u32[]{:S(2)}) collective-permute-start(f32[4,64,128]{2,1,0:T(8,128)S(1)} %get-tuple-element.32), channel_id=1, source_target_pairs={{0,2},{1,3},{2,0},{3,1},{4,6},{5,7},{6,4},{7,5},{8,10},{9,11},{10,... | collective-permute-start | bytes 393224 | tf_op jit(solution)/shard_map/ppermute | solution.py:490
  116.2 1.3 collective-permute-start.19
  (6 other events, 4.6 us)

commit v4 on v3

--- a/solution.py
+++ b/solution.py
@@ -12,6 +12,7 @@
 TAIL = 16
 PAIRS = tuple((i, j) for i in range(3) for j in range(i, 3))
 MIB = 2**20
+NO_COST = pl.CostEstimate(flops=0, bytes_accessed=0, transcendentals=0)
 ANY = pl.BlockSpec(memory_space=pl.ANY)
 SMEM = pl.BlockSpec(memory_space=pltpu.SMEM)
 VMEM = pl.BlockSpec(memory_space=pltpu.VMEM)
@@ -25,7 +26,7 @@
 def plan_kernel(
     frags, own_count, list_len, where, map_ref, list_ref, energy, occ, table, *refs
 ):
-    outs, own, plan, sems = refs[:6], refs[6], refs[7], refs[8]
+    outs, own, plan, target, sems = refs[:6], refs[6], refs[7], refs[8], refs[9]
     me = where[0]
     block = table.shape[1]
     copies = []
@@ -98,6 +99,14 @@
         plan[1, place] = rank
         plan[2, place] = rows[k]
         plan[3, place] = jnp.int32(k)
+
+    def one(fragment, carry):
+        picked, _ = pick(fragment, me)
+        for r in range(CAP):
+            target[fragment, r] = picked[r]
+        return carry
+
+    lax.fori_loop(0, frags, one, 0)
     for needed, copy in copies:
         pl.when(needed)(copy.wait)
 
@@ -108,14 +117,16 @@
     part = jax.ShapeDtypeStruct((CAP * block_rows + TAIL, cols), table.dtype)
     return pl.pallas_call(
         functools.partial(plan_kernel, frags, own_count, list_len),
-        out_shape=(part,) * 7 + (jax.ShapeDtypeStruct((4, list_len), jnp.int32),),
+        out_shape=(part,) * 7
+        + (
+            jax.ShapeDtypeStruct((4, list_len), jnp.int32),
+            jax.ShapeDtypeStruct((frags, CAP), jnp.int32),
+        ),
         in_specs=[SMEM, SMEM, SMEM, VMEM, VMEM, ANY],
-        out_specs=(VMEM,) * 7 + (SMEM,),
+        out_specs=(VMEM,) * 7 + (SMEM, SMEM),
         scratch_shapes=[pltpu.SemaphoreType.DMA((7, CAP))],
         compiler_params=pltpu.CompilerParams(vmem_limit_bytes=8 * MIB),
-        cost_estimate=pl.CostEstimate(
-            flops=0, bytes_accessed=4 * 7 * CAP * block_rows * cols, transcendentals=0
-        ),
+        cost_estimate=NO_COST,
         name="plan_and_pack",
     )(where, owner_map, vir_list, energy, occ, table)
 
@@ -158,7 +169,8 @@
         for copy in copies:
             copy.wait()
         wide[TAIL:, :] = raw[...].astype(jnp.float32)
-        for place in range(levels.shape[0]):
+        levels[...] = jnp.zeros_like(levels)
+        for place in range(first + 2):
             row = plan[0, place] * TAIL + plan[2, place] % own_count
             levels[place : place + 1, :] = wide[pl.ds(row, 1), :]
     for i in range(2):
@@ -189,9 +201,7 @@
         out_specs=(VMEM,) * len(shapes),
         scratch_shapes=scratch,
         compiler_params=pltpu.CompilerParams(vmem_limit_bytes=4 * MIB),
-        cost_estimate=pl.CostEstimate(
-            flops=0, bytes_accessed=8 * block * cols, transcendentals=0
-        ),
+        cost_estimate=NO_COST,
         name="pack_group",
     )(plan, *extra, *refs)
 
@@ -248,11 +258,9 @@
                 grid_copy(slot, group, quarter).start()
         height = len(PAIRS) * row_count * block
         span = len(group_list) * 2 * block
-        for quarter in range(4):
+
+        def scale(quarter):
             cols = pl.ds(quarter * width, width)
-            occ_copy(quarter).wait()
-            for b in range(row_count):
-                left_copy(b, 0, 0, quarter).wait()
             orbit = [
                 occ[quarter * TAIL + i : quarter * TAIL + i + 1, :].astype(jnp.float32)
                 for i in range(3)
@@ -260,16 +268,28 @@
             for b in range(row_count):
                 rows = left[pl.ds(b * block, block), cols].astype(jnp.float32)
                 for p, (i, j) in enumerate(PAIRS):
-                    scaled[pl.ds((p * row_count + b) * block, block), :] = (
+                    scaled[quarter % 2, pl.ds((p * row_count + b) * block, block), :] = (
                         rows * (orbit[i] * orbit[j])
                     ).astype(jnp.bfloat16)
+
+        def wait_left(quarter):
+            occ_copy(quarter).wait()
+            for b in range(row_count):
+                left_copy(b, 0, 0, quarter).wait()
+
+        wait_left(0)
+        scale(0)
+        for quarter in range(4):
+            cols = pl.ds(quarter * width, width)
             for slot, group in enumerate(group_list):
                 grid_copy(slot, group, quarter).wait()
-
-            def rows_step(step, carry, quarter=quarter, cols=cols):
-                rows = pl.ds(pl.multiple_of(step * 768, 768), 768)
+            if quarter < 3:
+                wait_left(quarter + 1)
+                scale(quarter + 1)
+            for step in range(height // 768):
+                rows = pl.ds(step * 768, 768)
                 term = lax.dot_general(
-                    scaled[rows, :],
+                    scaled[quarter % 2, rows, :],
                     grid[pl.ds(0, span), cols],
                     (((1,), (1,)), ((), ())),
                     preferred_element_type=jnp.float32,
@@ -278,9 +298,6 @@
                     total[rows, pl.ds(0, span)] = term
                 else:
                     total[rows, pl.ds(0, span)] += term
-                return carry
-
-            lax.fori_loop(0, height // 768, rows_step, 0)
         lane = lax.broadcasted_iota(jnp.int32, (block, block), 1)
         sub = lax.broadcasted_iota(jnp.int32, (block, block), 0)
         sums = []
@@ -352,7 +369,7 @@
         pltpu.VMEM((2 * block, 4 * width), jnp.bfloat16),
         pltpu.VMEM((span, 4 * width), jnp.bfloat16),
         pltpu.VMEM((4 * TAIL, width), jnp.bfloat16),
-        pltpu.VMEM((height, width), jnp.bfloat16),
+        pltpu.VMEM((2, height, width), jnp.bfloat16),
         pltpu.VMEM((height, span), jnp.float32),
         pltpu.VMEM((block, len(PAIRS) * span), jnp.bfloat16),
     ]
@@ -371,18 +388,20 @@
         pltpu.SemaphoreType.DMA((3, 4)),
         pltpu.SemaphoreType.DMA((4,)),
     ]
+    cost = NO_COST
+    if stage < 2:
+        units = (8, 6)[stage] * len(PAIRS) * block * block
+        cost = pl.CostEstimate(
+            flops=2 * units * 4 * width, bytes_accessed=units * 4, transcendentals=0
+        )
     return pl.pallas_call(
         functools.partial(contract_kernel, stage, block, width),
         out_shape=out_shape,
         in_specs=[SMEM] * 4 + [VMEM] + [ANY] * len(parts) + [VMEM] * len(before),
         out_specs=out_specs,
         scratch_shapes=scratch,
-        compiler_params=pltpu.CompilerParams(vmem_limit_bytes=22 * MIB),
-        cost_estimate=pl.CostEstimate(
-            flops=2 * height * min(span, 4 * block) * 4 * width,
-            bytes_accessed=span * 4 * width * 2,
-            transcendentals=0,
-        ),
+        compiler_params=pltpu.CompilerParams(vmem_limit_bytes=26 * MIB),
+        cost_estimate=cost,
         name="contract",
     )(where, plan, levels, vir_rows, energy, *parts, *before)
 
@@ -412,34 +431,25 @@
     )(where, plan, kept, came)
 
 
-def collect_kernel(own_count, list_len, where, map_ref, list_ref, came, out):
-    me = where[0]
+def collect_kernel(target, came, out):
     out[...] = jnp.zeros_like(out)
 
     def one(fragment, carry):
-        count = jnp.int32(0)
-        for k in range(list_len):
-            row = map_ref[list_ref[fragment, k]]
-            hit = row // own_count == me
-
-            @pl.when(hit)
-            def _(row=row, count=count):
-                out[row % own_count] += came[fragment, count]
-
-            count = count + hit.astype(jnp.int32)
+        for r in range(CAP):
+            out[target[fragment, r]] += came[fragment, r]
         return carry
 
-    lax.fori_loop(0, list_ref.shape[0], one, 0)
-
-
-def collect(where, owner_map, vir_list, came, own_count):
+    lax.fori_loop(0, came.shape[0], one, 0)
+
+
+def collect(target, came, own_count):
     return pl.pallas_call(
-        functools.partial(collect_kernel, own_count, vir_list.shape[1]),
+        collect_kernel,
         out_shape=jax.ShapeDtypeStruct((own_count,) + came.shape[2:], came.dtype),
-        in_specs=[SMEM, SMEM, SMEM, VMEM],
+        in_specs=[SMEM, VMEM],
         out_specs=VMEM,
         name="collect",
-    )(where, owner_map, vir_list, came)
+    )(target, came)
 
 
 def body(vir_grid, vir_energy, occ_grid, occ_energy, vir_list, vir_rows, owner_map):
@@ -453,14 +463,15 @@
     far_pairs = [(i, i ^ 2) for i in range(aux_count)]
     near_pairs = [(i, i ^ 1) for i in range(aux_count)]
 
-    *outgoing, own, plan = plan_and_pack(
+    *outgoing, own, plan, target = plan_and_pack(
         where, owner_map, vir_list, vir_energy, occ_grid[0], vir_grid, frags
     )
 
-    def over_aux(here):
+    def over_aux(here, *others):
         far = lax.ppermute(here, "aux", far_pairs)
         near = lax.ppermute(here, "aux", near_pairs)
-        return [here, far, near, lax.ppermute(far, "aux", near_pairs)]
+        onward = after(far, *others) if others else far
+        return [here, far, near, lax.ppermute(onward, "aux", near_pairs)]
 
     def after(value, *others):
         return lax.optimization_barrier((value, *others))[0]
@@ -474,16 +485,19 @@
     parts = over_aux(own)
     arrived[5] = send(4, *(arrived[c] for c in (1, 2, 3, 4)), parts[1])
     here = pack_group(2, block, plan, {c: arrived[c] for c in range(1, 5)})[0]
-    arrived[6] = send(5, arrived[5], here)
     parts += over_aux(here)
-    here = pack_group(4, block, plan, {c: arrived[c] for c in range(1, 6)})[0]
-    parts += over_aux(here)
+    arrived[6] = send(5, arrived[5], parts[5])
+    here, early_energy = pack_group(
+        4, block, plan, {c: arrived[c] for c in range(1, 6)}, vir_energy
+    )
+    shared = (where, plan, occ_energy, vir_rows)
+    first = contract(0, *shared, early_energy, parts[:8])
+    parts += over_aux(here, first)
+    arrived[6] = after(arrived[6], first)
     here, energy = pack_group(6, block, plan, arrived, vir_energy)
-    parts += over_aux(here)
-    shared = (where, plan, occ_energy, vir_rows, energy)
-    first = contract(0, *shared, parts[:8])
-    second = contract(1, *shared, parts[:12])
-    sent, stay = contract(2, *shared, parts, (first, second))
+    second = contract(1, *shared, early_energy, parts[:12])
+    parts += over_aux(here, second)
+    sent, stay = contract(2, *shared, energy, parts, (first, second))
 
     quarter = block // aux_count
     core = aux % 2
@@ -494,7 +508,7 @@
     came = lax.ppermute(sent, "aux", near_pairs)
     outgoing = spread(where, plan, kept, came, frags, own_count)
     incoming = lax.all_to_all(outgoing, "frag", 0, 0, tiled=True)
-    return collect(where, owner_map, vir_list, incoming, own_count)
+    return collect(target, incoming, own_count)
 
 
 def solution(mesh):

time: 140 us -> 124 us (0.89)
  waiting for transfers between devices: 57.3 us -> 46.2 us
  starting transfers between devices: 22.2 us -> 18.6 us
  Pallas kernels: 39.7 us -> 37.5 us
    ppermute x4, waiting for transfers between devices: 24.8 us -> 11 us  [over_aux(): far = lax.ppermute(here, 'aux', far_pairs)]
    ppermute x1, starting transfers between devices: 3.27 us -> 0.32 us  [body(): met = lax.ppermute(sent, 'aux', far_pairs)]
    ppermute x4, waiting for transfers between devices: 0.01 us -> 2.47 us  [over_aux(): return [here, far, near, lax.ppermute(onward, 'aux', near_pairs)]]
    pallas_call x3, Pallas kernels: 30.5 us -> 28.6 us  [contract(): pl.pallas_call(functools.partial(contract_kernel, stage, block, width), o...]
    ppermute x4, starting transfers between devices: 6.33 us -> 4.46 us  [over_aux(): far = lax.ppermute(here, 'aux', far_pairs)]
  transfers between devices with their start and end apart: 20 -> 20, of which waited for: 9 -> 9; matrix products, arithmetic and copies ran while one was open for 0% -> 0% of each run, Pallas kernels for 17% -> 18%
where the time goes in v4:
time: 124 us
  waiting for transfers between devices  46.2 us (37%)
  Pallas kernels  37.5 us (30%)
  starting transfers between devices  18.6 us (15%)
  blocking collectives  18.1 us (15%)
  local copies, waits for them, and re-layouts  3.24 us (3%)
    pallas_call x3, Pallas kernels, contract(): pl.pallas_call(functools.partial(contract_kernel, stage, block, width), o...  28.6 us
    ppermute x6, waiting for transfers between devices, send(): return lax.ppermute(payload, 'frag', round_pairs(distance, parity, frags))  26.1 us
    all_to_all x1, blocking collectives, body(): incoming = lax.all_to_all(outgoing, 'frag', 0, 0, tiled=True)  18.1 us
    ppermute x6, starting transfers between devices, send(): return lax.ppermute(payload, 'frag', round_pairs(distance, parity, frags))  12.5 us
    ppermute x4, waiting for transfers between devices, over_aux(): far = lax.ppermute(here, 'aux', far_pairs)  11 us
    ppermute x1, waiting for transfers between devices, body(): met = lax.ppermute(sent, 'aux', far_pairs)  5.25 us
    ppermute x4, starting transfers between devices, over_aux(): far = lax.ppermute(here, 'aux', far_pairs)  4.46 us
    pallas_call x1, Pallas kernels, plan_and_pack(): pl.pallas_call(functools.partial(plan_kernel, frags, own_count, list_len)...  3.18 us
  transfers between devices with their start and end apart: 20, of which 9 were waited for; matrix products, arithmetic and copies ran while one was open for 0% of the time, Pallas kernels for 18%

profile of v4, /device:TPU:0, one launch (start us, length us, event | category | flops | bytes accessed | tf_op | source)
XLA Modules:
  0.0 123.8 jit_solution(9667381257665467274)
XLA Ops:
  0.8 1.2 copy-done
  2.0 3.2 %plan_and_pack.1 = (bf16[272,1024]{1,0:T(8,128)(2,1)S(1)}, bf16[272,1024]{1,0:T(8,128)(2,1)S(1)}, bf16[272,1024]{1,0:T(8,128)(2,1)S(1)}, bf16[272,1024]{1,0:T(8,...) custom-call(s32[2]{0:T(128)S(1)} %pad_add_fusion.where, ...), custom_call_target="tpu_custom_call" | custom-call | tf_op jit(solution)/shard_map/plan_and_pack/pallas_call | solution.py:118
  5.2 3.0 %collective-permute-start = (bf16[272,1024]{1,0:T(8,128)(2,1)S(1)}, bf16[272,1024]{1,0:T(8,128)(2,1)S(1)}, u32[]{:S(2)}, u32[]{:S(2)}) collective-permute-start(bf16[272,1024]{1,0:T(8,128)(2,1)S(1)} %get-tuple-element.27), channel_id=1, source_target_pairs={{0,4},{8,12},{16,20},{24,28},{4,0},{12,8},{20,16},{28,24},{1,5},{9... | collective-permute-start | bytes 1671176 | tf_op jit(solution)/shard_map/ppermute | solution.py:482
  8.9 2.9 %collective-permute-start.2 = (bf16[272,1024]{1,0:T(8,128)(2,1)S(1)}, bf16[272,1024]{1,0:T(8,128)(2,1)S(1)}, u32[]{:S(2)}, u32[]{:S(2)}) collective-permute-start(bf16[272,1024]{1,0:T(8,128)(2,1)S(1)} %get-tuple-element.29), channel_id=1, source_target_pairs={{0,8},{4,12},{16,24},{20,28},{8,0},{12,4},{24,16},{28,20},{1,9},{5... | collective-permute-start | bytes 1671176 | tf_op jit(solution)/shard_map/ppermute | solution.py:482
  12.5 1.9 %collective-permute-start.4 = (bf16[272,1024]{1,0:T(8,128)(2,1)S(1)}, bf16[272,1024]{1,0:T(8,128)(2,1)S(1)}, u32[]{:S(2)}, u32[]{:S(2)}) collective-permute-start(bf16[272,1024]{1,0:T(8,128)(2,1)S(1)} %get-tuple-element.32.refs_0_), channel_id=1, source_target_pairs={{0,2},{1,3},{2,0},{3,1},{4,6},{5,7},{6,4},{7,5},{8,10},{9,11},{10,... | collective-permute-start | bytes 1671176 | tf_op jit(solution)/shard_map/ppermute | solution.py:471
  14.5 17.6 %collective-permute-done.refs_0_.refs_1_ = bf16[272,1024]{1,0:T(8,128)(2,1)S(1)} collective-permute-done((bf16[272,1024]{1,0:T(8,128)(2,1)S(1)}, bf16[272,1024]{1,0:T(8,128)(2,1)S(1)}, u32[]{:S(2)}, u32[]{:S(2)}) %collective-permute-start) | collective-permute-done | bytes 557088 | tf_op jit(solution)/shard_map/ppermute | solution.py:482
  32.0 4.0 %collective-permute-done.2.refs_2_.refs_3_ = bf16[272,1024]{1,0:T(8,128)(2,1)S(1)} collective-permute-done((bf16[272,1024]{1,0:T(8,128)(2,1)S(1)}, bf16[272,1024]{1,0:T(8,128)(2,1)S(1)}, u32[]{:S(2)}, u32[]{:S(2)}) %collective-permute-start.2) | collective-permute-done | bytes 557088 | tf_op jit(solution)/shard_map/ppermute | solution.py:482
  36.8 1.6 %collective-permute-start.6 = (bf16[256,1024]{1,0:T(8,128)(2,1)S(1)}, bf16[256,1024]{1,0:T(8,128)(2,1)S(1)}, u32[]{:S(2)}, u32[]{:S(2)}) collective-permute-start(bf16[256,1024]{1,0:T(8,128)(2,1)S(1)} %pack_group.3.refs_4_), channel_id=1, source_target_pairs={{0,2},{1,3},{2,0},{3,1},{4,6},{5,7},{6,4},{7,5},{8,10},{9,11},{10,... | collective-permute-start | bytes 1572872 | tf_op jit(solution)/shard_map/ppermute | solution.py:471
  38.4 4.5 %collective-permute-start.5 = (bf16[272,1024]{1,0:T(8,128)(2,1)S(1)}, bf16[272,1024]{1,0:T(8,128)(2,1)S(1)}, u32[]{:S(2)}, u32[]{:S(2)}) collective-permute-start(bf16[272,1024]{1,0:T(8,128)(2,1)S(1)} %get-tuple-element.33), channel_id=1, source_target_pairs={{0,12},{4,16},{8,20},{12,0},{16,4},{20,8},{1,13},{5,17},{9,21},{13... | collective-permute-start | bytes 1671176 | tf_op jit(solution)/shard_map/ppermute | solution.py:482
  43.5 6.1 %collective-permute-done.6.refs_5_ = bf16[256,1024]{1,0:T(8,128)(2,1)S(1)} collective-permute-done((bf16[256,1024]{1,0:T(8,128)(2,1)S(1)}, bf16[256,1024]{1,0:T(8,128)(2,1)S(1)}, u32[]{:S(2)}, u32[]{:S(2)}) %collective-permute-start.6) | collective-permute-done | bytes 524320 | tf_op jit(solution)/shard_map/ppermute | solution.py:471
  49.7 4.5 %collective-permute-done.5.refs_5_ = bf16[272,1024]{1,0:T(8,128)(2,1)S(1)} collective-permute-done((bf16[272,1024]{1,0:T(8,128)(2,1)S(1)}, bf16[272,1024]{1,0:T(8,128)(2,1)S(1)}, u32[]{:S(2)}, u32[]{:S(2)}) %collective-permute-start.5) | collective-permute-done | bytes 557088 | tf_op jit(solution)/shard_map/ppermute | solution.py:482
  54.1 0.8 pack_group.4
  54.9 0.8 collective-permute-start.12
  56.5 12.3 %contract.3.refs_16_ = f32[2,128,128]{2,1,0:T(8,128)S(1)} custom-call(s32[2]{0:T(128)S(1)} %pad_add_fusion.where, s32[4,8]{1,0:T(4,128)S(1)} %get-tuple-element.26.plan, f32[1,3]{1,0:T(1,128)S(1)} %copy-done.9, s32[8,8]{1,0:T(8,128)S(1)} %copy-done.6, f32[8,128]{1,0:T(8,128)S(1)} %get-tuple-element.36.energy, ...), custom_call_target="tpu_custom_call" | custom-call | flops 6442450944 | bytes 3145728 | tf_op jit(solution)/shard_map/contract/pallas_call | solution.py:397
  69.4 0.8 pack_group.5
  70.9 8.3 %contract.4.refs_17_ = f32[2,128,128]{2,1,0:T(8,128)S(1)} custom-call(s32[2]{0:T(128)S(1)} %pad_add_fusion.where, s32[4,8]{1,0:T(4,128)S(1)} %get-tuple-element.26.plan, f32[1,3]{1,0:T(1,128)S(1)} %copy-done.9, s32[8,8]{1,0:T(8,128)S(1)} %copy-done.6, f32[8,128]{1,0:T(8,128)S(1)} %get-tuple-element.36.energy, ...), custom_call_target="tpu_custom_call" | custom-call | flops 4831838208 | bytes 2359296 | tf_op jit(solution)/shard_map/contract/pallas_call | solution.py:397
  79.2 4.9 %collective-permute-done.15.refs_13_ = bf16[256,1024]{1,0:T(8,128)(2,1)S(1)} collective-permute-done((bf16[256,1024]{1,0:T(8,128)(2,1)S(1)}, bf16[256,1024]{1,0:T(8,128)(2,1)S(1)}, u32[]{:S(2)}, u32[]{:S(2)}) %collective-permute-start.15) | collective-permute-done | bytes 524320 | tf_op jit(solution)/shard_map/ppermute | solution.py:471
  84.1 1.9 %collective-permute-done.17.refs_15_ = bf16[256,1024]{1,0:T(8,128)(2,1)S(1)} collective-permute-done((bf16[256,1024]{1,0:T(8,128)(2,1)S(1)}, bf16[256,1024]{1,0:T(8,128)(2,1)S(1)}, u32[]{:S(2)}, u32[]{:S(2)}) %collective-permute-start.17) | collective-permute-done | bytes 524320 | tf_op jit(solution)/shard_map/ppermute | solution.py:474
  86.0 8.1 %contract.5 = (f32[4,64,128]{2,1,0:T(8,128)S(1)}, f32[4,64,128]{2,1,0:T(8,128)S(1)}) custom-call(s32[2]{0:T(128)S(1)} %pad_add_fusion.where, s32[4,8]{1,0:T(4,128)S(1)} %get-tuple-element.26.plan, f32[1,3]{1,0:T(1,128)S(1)} %copy-done.9, s32[8,8]{1,0:T(8,128)S(1)} %copy-done.6, f32[8,128]{1,0:T(8,128)S(1)} %get-tuple-element.38.energy, ...), custom_call_target="tpu_custom_call" | custom-call | tf_op jit(solution)/shard_map/contract/pallas_call | solution.py:397
  94.4 5.3 %collective-permute-done.18 = f32[4,64,128]{2,1,0:T(8,128)S(1)} collective-permute-done((f32[4,64,128]{2,1,0:T(8,128)S(1)}, f32[4,64,128]{2,1,0:T(8,128)S(1)}, u32[]{:S(2)}, u32[]{:S(2)}) %collective-permute-start.18) | collective-permute-done | bytes 131104 | tf_op jit(solution)/shard_map/ppermute | solution.py:504
  100.4 1.3 %collective-permute-done.19.came = f32[6,32,128]{2,1,0:T(8,128)S(1)} collective-permute-done((f32[6,32,128]{2,1,0:T(8,128)S(1)}, f32[6,32,128]{2,1,0:T(8,128)S(1)}, u32[]{:S(2)}, u32[]{:S(2)}) %collective-permute-start.19) | collective-permute-done | bytes 98336 | tf_op jit(solution)/shard_map/ppermute | solution.py:508
  102.3 1.7 %spread.1 = f32[8,2,32,128]{3,2,1,0:T(8,128)} custom-call(s32[2]{0:T(128)} %copy-done.4, s32[4,8]{1,0:T(4,128)} %copy-done.1, f32[6,32,128]{2,1,0:T(8,128)} %get-tuple-element.46.kept, f32[6,32,128]{2,1,0:T(8,128)} %copy-done.10), custom_call_target="tpu_custom_call" | custom-call | tf_op jit(solution)/shard_map/spread/pallas_call | solution.py:425
  104.1 18.1 %all_to_all.5.came = f32[8,2,32,128]{3,2,1,0:T(8,128)} all-to-all(f32[8,2,32,128]{3,2,1,0:T(8,128)} %spread.1), channel_id=1, replica_groups=mesh['frag'=8,'aux'=4] {'frag'}, dimensions={0} | all-to-all | bytes 524288 | tf_op jit(solution)/shard_map/all_to_all | solution.py:510
  122.1 1.7 %collect.1 = f32[4,32,128]{2,1,0:T(8,128)} custom-call(s32[8,2]{1,0:T(8,128)} %copy-done.7, f32[8,2,32,128]{3,2,1,0:T(8,128)} %all_to_all.5.came), custom_call_target="tpu_custom_call" | custom-call | tf_op jit(solution)/shard_map/collect/pallas_call | solution.py:446
  (52 shorter events, 7.1 us)
Async XLA Ops:
  0.1 85.9 %copy-start.4 = (s32[2]{0:T(128)}, s32[2]{0:T(128)S(1)}, u32[]{:S(2)}) copy-start(s32[2]{0:T(128)S(1)} %pad_add_fusion.where) | copy-start | bytes 28
  5.2 7.4 %copy-start.7 = (s32[8,2]{1,0:T(8,128)}, s32[8,2]{1,0:T(8,128)S(1)}, u32[]{:S(2)}) copy-start(s32[8,2]{1,0:T(8,128)S(1)} %get-tuple-element.25.target) | copy-start | bytes 196
  5.2 80.8 %copy-start.1 = (s32[4,8]{1,0:T(4,128)}, s32[4,8]{1,0:T(4,128)S(1)}, u32[]{:S(2)}) copy-start(s32[4,8]{1,0:T(4,128)S(1)} %get-tuple-element.26.plan) | copy-start | bytes 388
  5.2 26.8 %collective-permute-start = (bf16[272,1024]{1,0:T(8,128)(2,1)S(1)}, bf16[272,1024]{1,0:T(8,128)(2,1)S(1)}, u32[]{:S(2)}, u32[]{:S(2)}) collective-permute-start(bf16[272,1024]{1,0:T(8,128)(2,1)S(1)} %get-tuple-element.27), channel_id=1, source_target_pairs={{0,4},{8,12},{16,20},{24,28},{4,0},{12,8},{20,16},{28,24},{1,5},{9... | collective-permute-start | bytes 1671176 | tf_op jit(solution)/shard_map/ppermute | solution.py:482
  8.2 23.8 %collective-permute-start.1 = (bf16[272,1024]{1,0:T(8,128)(2,1)S(1)}, bf16[272,1024]{1,0:T(8,128)(2,1)S(1)}, u32[]{:S(2)}, u32[]{:S(2)}) collective-permute-start(bf16[272,1024]{1,0:T(8,128)(2,1)S(1)} %get-tuple-element.28), channel_id=1, source_target_pairs={{4,8},{12,16},{20,24},{8,4},{16,12},{24,20},{5,9},{13,17},{21,25},... | collective-permute-start | bytes 1671176 | tf_op jit(solution)/shard_map/ppermute | solution.py:482
  8.9 27.2 %collective-permute-start.2 = (bf16[272,1024]{1,0:T(8,128)(2,1)S(1)}, bf16[272,1024]{1,0:T(8,128)(2,1)S(1)}, u32[]{:S(2)}, u32[]{:S(2)}) collective-permute-start(bf16[272,1024]{1,0:T(8,128)(2,1)S(1)} %get-tuple-element.29), channel_id=1, source_target_pairs={{0,8},{4,12},{16,24},{20,28},{8,0},{12,4},{24,16},{28,20},{1,9},{5... | collective-permute-start | bytes 1671176 | tf_op jit(solution)/shard_map/ppermute | solution.py:482
  11.8 24.2 %collective-permute-start.3 = (bf16[272,1024]{1,0:T(8,128)(2,1)S(1)}, bf16[272,1024]{1,0:T(8,128)(2,1)S(1)}, u32[]{:S(2)}, u32[]{:S(2)}) collective-permute-start(bf16[272,1024]{1,0:T(8,128)(2,1)S(1)} %get-tuple-element.30), channel_id=1, source_target_pairs={{8,16},{12,20},{16,8},{20,12},{9,17},{13,21},{17,9},{21,13},{10,18... | collective-permute-start | bytes 1671176 | tf_op jit(solution)/shard_map/ppermute | solution.py:482
  12.5 25.9 %collective-permute-start.4 = (bf16[272,1024]{1,0:T(8,128)(2,1)S(1)}, bf16[272,1024]{1,0:T(8,128)(2,1)S(1)}, u32[]{:S(2)}, u32[]{:S(2)}) collective-permute-start(bf16[272,1024]{1,0:T(8,128)(2,1)S(1)} %get-tuple-element.32.refs_0_), channel_id=1, source_target_pairs={{0,2},{1,3},{2,0},{3,1},{4,6},{5,7},{6,4},{7,5},{8,10},{9,11},{10,... | collective-permute-start | bytes 1671176 | tf_op jit(solution)/shard_map/ppermute | solution.py:471
  36.8 12.9 %collective-permute-start.6 = (bf16[256,1024]{1,0:T(8,128)(2,1)S(1)}, bf16[256,1024]{1,0:T(8,128)(2,1)S(1)}, u32[]{:S(2)}, u32[]{:S(2)}) collective-permute-start(bf16[256,1024]{1,0:T(8,128)(2,1)S(1)} %pack_group.3.refs_4_), channel_id=1, source_target_pairs={{0,2},{1,3},{2,0},{3,1},{4,6},{5,7},{6,4},{7,5},{8,10},{9,11},{10,... | collective-permute-start | bytes 1572872 | tf_op jit(solution)/shard_map/ppermute | solution.py:471
  38.4 15.7 %collective-permute-start.5 = (bf16[272,1024]{1,0:T(8,128)(2,1)S(1)}, bf16[272,1024]{1,0:T(8,128)(2,1)S(1)}, u32[]{:S(2)}, u32[]{:S(2)}) collective-permute-start(bf16[272,1024]{1,0:T(8,128)(2,1)S(1)} %get-tuple-element.33), channel_id=1, source_target_pairs={{0,12},{4,16},{8,20},{12,0},{16,4},{20,8},{1,13},{5,17},{9,21},{13... | collective-permute-start | bytes 1671176 | tf_op jit(solution)/shard_map/ppermute | solution.py:482
  42.9 12.9 %collective-permute-start.8 = (bf16[272,1024]{1,0:T(8,128)(2,1)S(1)}, bf16[272,1024]{1,0:T(8,128)(2,1)S(1)}, u32[]{:S(2)}, u32[]{:S(2)}) collective-permute-start(bf16[272,1024]{1,0:T(8,128)(2,1)S(1)} %get-tuple-element.32.refs_0_), channel_id=1, source_target_pairs={{0,1},{1,0},{2,3},{3,2},{4,5},{5,4},{6,7},{7,6},{8,9},{9,8},{10,11... | collective-permute-start | bytes 1671176 | tf_op jit(solution)/shard_map/ppermute | solution.py:472
  43.0 13.5 %collective-permute-start.9 = (bf16[272,1024]{1,0:T(8,128)(2,1)S(1)}, bf16[272,1024]{1,0:T(8,128)(2,1)S(1)}, u32[]{:S(2)}, u32[]{:S(2)}) collective-permute-start(bf16[272,1024]{1,0:T(8,128)(2,1)S(1)} %collective-permute-done.4.refs_1_), channel_id=1, source_target_pairs={{0,1},{1,0},{2,3},{3,2},{4,5},{5,4},{6,7},{7,6},{8,9},{9,8},{10,11... | collective-permute-start | bytes 1671176 | tf_op jit(solution)/shard_map/ppermute | solution.py:474
  43.5 12.3 %collective-permute-start.10 = (bf16[256,1024]{1,0:T(8,128)(2,1)S(1)}, bf16[256,1024]{1,0:T(8,128)(2,1)S(1)}, u32[]{:S(2)}, u32[]{:S(2)}) collective-permute-start(bf16[256,1024]{1,0:T(8,128)(2,1)S(1)} %pack_group.3.refs_4_), channel_id=1, source_target_pairs={{0,1},{1,0},{2,3},{3,2},{4,5},{5,4},{6,7},{7,6},{8,9},{9,8},{10,11... | collective-permute-start | bytes 1572872 | tf_op jit(solution)/shard_map/ppermute | solution.py:472
  49.6 6.8 %collective-permute-start.11 = (bf16[256,1024]{1,0:T(8,128)(2,1)S(1)}, bf16[256,1024]{1,0:T(8,128)(2,1)S(1)}, u32[]{:S(2)}, u32[]{:S(2)}) collective-permute-start(bf16[256,1024]{1,0:T(8,128)(2,1)S(1)} %collective-permute-done.6.refs_5_), channel_id=1, source_target_pairs={{0,1},{1,0},{2,3},{3,2},{4,5},{5,4},{6,7},{7,6},{8,9},{9,8},{10,11... | collective-permute-start | bytes 1572872 | tf_op jit(solution)/shard_map/ppermute | solution.py:474
  54.1 2.4 %copy-start.6 = (s32[8,8]{1,0:T(8,128)S(1)}, s32[8,8]{1,0:T(8,128)}, u32[]{:S(2)}) copy-start(s32[8,8]{1,0:T(8,128)} %rows_ref.5) | copy-start | bytes 772
  54.9 13.9 %collective-permute-start.12 = (bf16[256,1024]{1,0:T(8,128)(2,1)S(1)}, bf16[256,1024]{1,0:T(8,128)(2,1)S(1)}, u32[]{:S(2)}, u32[]{:S(2)}) collective-permute-start(bf16[256,1024]{1,0:T(8,128)(2,1)S(1)} %get-tuple-element.39.refs_8_), channel_id=1, source_target_pairs={{0,2},{1,3},{2,0},{3,1},{4,6},{5,7},{6,4},{7,5},{8,10},{9,11},{10,... | collective-permute-start | bytes 1572872 | tf_op jit(solution)/shard_map/ppermute | solution.py:471
  55.7 14.6 %collective-permute-start.13 = (bf16[256,1024]{1,0:T(8,128)(2,1)S(1)}, bf16[256,1024]{1,0:T(8,128)(2,1)S(1)}, u32[]{:S(2)}, u32[]{:S(2)}) collective-permute-start(bf16[256,1024]{1,0:T(8,128)(2,1)S(1)} %get-tuple-element.39.refs_8_), channel_id=1, source_target_pairs={{0,1},{1,0},{2,3},{3,2},{4,5},{5,4},{6,7},{7,6},{8,9},{9,8},{10,11... | collective-permute-start | bytes 1572872 | tf_op jit(solution)/shard_map/ppermute | solution.py:472
  55.7 13.6 %collective-permute-start.7 = (bf16[272,1024]{1,0:T(8,128)(2,1)S(1)}, bf16[272,1024]{1,0:T(8,128)(2,1)S(1)}, u32[]{:S(2)}, u32[]{:S(2)}) collective-permute-start(bf16[272,1024]{1,0:T(8,128)(2,1)S(1)} %get-tuple-element.35), channel_id=1, source_target_pairs={{12,24},{16,28},{24,12},{28,16},{13,25},{17,29},{25,13},{29,17},{1... | collective-permute-start | bytes 1671176 | tf_op jit(solution)/shard_map/ppermute | solution.py:482
  68.8 2.1 %collective-permute-start.14 = (bf16[256,1024]{1,0:T(8,128)(2,1)S(1)}, bf16[256,1024]{1,0:T(8,128)(2,1)S(1)}, u32[]{:S(2)}, u32[]{:S(2)}) collective-permute-start(bf16[256,1024]{1,0:T(8,128)(2,1)S(1)} %collective-permute-done.12.refs_9_), channel_id=1, source_target_pairs={{0,1},{1,0},{2,3},{3,2},{4,5},{5,4},{6,7},{7,6},{8,9},{9,8},{10,11... | collective-permute-start | bytes 1572872 | tf_op jit(solution)/shard_map/ppermute | solution.py:474
  70.2 13.9 %collective-permute-start.15 = (bf16[256,1024]{1,0:T(8,128)(2,1)S(1)}, bf16[256,1024]{1,0:T(8,128)(2,1)S(1)}, u32[]{:S(2)}, u32[]{:S(2)}) collective-permute-start(bf16[256,1024]{1,0:T(8,128)(2,1)S(1)} %get-tuple-element.41.refs_12_), channel_id=1, source_target_pairs={{0,2},{1,3},{2,0},{3,1},{4,6},{5,7},{6,4},{7,5},{8,10},{9,11},{10,... | collective-permute-start | bytes 1572872 | tf_op jit(solution)/shard_map/ppermute | solution.py:471
  70.2 13.8 %collective-permute-start.16 = (bf16[256,1024]{1,0:T(8,128)(2,1)S(1)}, bf16[256,1024]{1,0:T(8,128)(2,1)S(1)}, u32[]{:S(2)}, u32[]{:S(2)}) collective-permute-start(bf16[256,1024]{1,0:T(8,128)(2,1)S(1)} %get-tuple-element.41.refs_12_), channel_id=1, source_target_pairs={{0,1},{1,0},{2,3},{3,2},{4,5},{5,4},{6,7},{7,6},{8,9},{9,8},{10,11... | collective-permute-start | bytes 1572872 | tf_op jit(solution)/shard_map/ppermute | solution.py:472
  84.1 1.9 %collective-permute-start.17 = (bf16[256,1024]{1,0:T(8,128)(2,1)S(1)}, bf16[256,1024]{1,0:T(8,128)(2,1)S(1)}, u32[]{:S(2)}, u32[]{:S(2)}) collective-permute-start(bf16[256,1024]{1,0:T(8,128)(2,1)S(1)} %collective-permute-done.15.refs_13_), channel_id=1, source_target_pairs={{0,1},{1,0},{2,3},{3,2},{4,5},{5,4},{6,7},{7,6},{8,9},{9,8},{10,11... | collective-permute-start | bytes 1572872 | tf_op jit(solution)/shard_map/ppermute | solution.py:474
  94.1 5.6 %collective-permute-start.18 = (f32[4,64,128]{2,1,0:T(8,128)S(1)}, f32[4,64,128]{2,1,0:T(8,128)S(1)}, u32[]{:S(2)}, u32[]{:S(2)}) collective-permute-start(f32[4,64,128]{2,1,0:T(8,128)S(1)} %get-tuple-element.44), channel_id=1, source_target_pairs={{0,2},{1,3},{2,0},{3,1},{4,6},{5,7},{6,4},{7,5},{8,10},{9,11},{10,... | collective-permute-start | bytes 393224 | tf_op jit(solution)/shard_map/ppermute | solution.py:504
  100.4 1.3 %collective-permute-start.19 = (f32[6,32,128]{2,1,0:T(8,128)S(1)}, f32[6,32,128]{2,1,0:T(8,128)S(1)}, u32[]{:S(2)}, u32[]{:S(2)}) collective-permute-start(f32[6,32,128]{2,1,0:T(8,128)S(1)} %get-tuple-element.45), channel_id=1, source_target_pairs={{0,1},{1,0},{2,3},{3,2},{4,5},{5,4},{6,7},{7,6},{8,9},{9,8},{10,11... | collective-permute-start | bytes 294920 | tf_op jit(solution)/shard_map/ppermute | solution.py:508
  (7 other events, 6.2 us)

commit v5 on v4

--- a/solution.py
+++ b/solution.py
@@ -23,54 +23,67 @@
     return up + [(b, a) for a, b in up]
 
 
-def plan_kernel(
-    frags, own_count, list_len, where, map_ref, list_ref, energy, occ, table, *refs
-):
-    outs, own, plan, target, sems = refs[:6], refs[6], refs[7], refs[8], refs[9]
+def pick(map_ref, list_ref, list_len, own_count, fragment, owner):
+    count = jnp.int32(0)
+    picked = [jnp.int32(0)] * CAP
+    for k in range(list_len):
+        row = map_ref[list_ref[fragment, k]]
+        hit = row // own_count == owner
+        for r in range(CAP):
+            picked[r] = jnp.where(hit & (count == r), row % own_count, picked[r])
+        count = count + hit.astype(jnp.int32)
+    return picked, count
+
+
+def send_kernel(frags, own_count, list_len, where, map_ref, list_ref, energy, occ, table, *refs):
+    outs, own, sems = refs[:6], refs[6], refs[7]
     me = where[0]
     block = table.shape[1]
     copies = []
 
-    def pick(fragment, owner):
-        count = jnp.int32(0)
-        picked = [jnp.int32(0)] * CAP
-        for k in range(list_len):
-            row = map_ref[list_ref[fragment, k]]
-            hit = row // own_count == owner
-            for r in range(CAP):
-                picked[r] = jnp.where(hit & (count == r), row % own_count, picked[r])
-            count = count + hit.astype(jnp.int32)
-        return picked, count
+    def start(out, index, fragment, inside):
+        picked, count = pick(map_ref, list_ref, list_len, own_count, fragment, me)
+        for r in range(CAP):
+            copy = pltpu.make_async_copy(
+                table.at[picked[r]], out.at[pl.ds(r * block, block)], sems.at[index, r]
+            )
+            needed = inside & (count > r)
+            pl.when(needed)(copy.start)
+            copies.append((needed, copy))
 
     for index, (distance, parity) in enumerate(ROUNDS):
         up = (me // distance) % 2 == parity
         partner = jnp.where(up, me + distance, me - distance)
         inside = (partner >= 0) & (partner < frags)
-        picked, count = pick(jnp.clip(partner, 0, frags - 1), me)
-        for r in range(CAP):
-            copies.append((
-                inside & (count > r),
-                pltpu.make_async_copy(
-                    table.at[picked[r]], outs[index].at[pl.ds(r * block, block)], sems.at[index, r]
-                ),
-            ))
-        if index == 0:
-            picked, count = pick(me, me)
-            for r in range(CAP):
-                copies.append((
-                    count > r,
-                    pltpu.make_async_copy(
-                        table.at[picked[r]], own.at[pl.ds(r * block, block)], sems.at[6, r]
-                    ),
-                ))
-    for needed, copy in copies:
-        pl.when(needed)(copy.start)
+        start(outs[index], index, jnp.clip(partner, 0, frags - 1), inside)
+    start(own, 6, me, me >= 0)
     for out in outs + (own,):
         out[pl.ds(CAP * block, TAIL), :] = jnp.zeros((TAIL, out.shape[1]), out.dtype)
     for out in outs:
         out[pl.ds(CAP * block, own_count), pl.ds(0, block)] = energy[...]
     own[pl.ds(CAP * block, occ.shape[0]), :] = occ[...]
-
+    for needed, copy in copies:
+        pl.when(needed)(copy.wait)
+
+
+def pack_to_send(where, owner_map, vir_list, energy, occ, table, frags):
+    own_count, block_rows, cols = table.shape
+    list_len = vir_list.shape[1]
+    part = jax.ShapeDtypeStruct((CAP * block_rows + TAIL, cols), table.dtype)
+    return pl.pallas_call(
+        functools.partial(send_kernel, frags, own_count, list_len),
+        out_shape=(part,) * 7,
+        in_specs=[SMEM, SMEM, SMEM, VMEM, VMEM, ANY],
+        out_specs=(VMEM,) * 7,
+        scratch_shapes=[pltpu.SemaphoreType.DMA((7, CAP))],
+        compiler_params=pltpu.CompilerParams(vmem_limit_bytes=8 * MIB),
+        cost_estimate=NO_COST,
+        name="pack_to_send",
+    )(where, owner_map, vir_list, energy, occ, table)
+
+
+def plan_kernel(frags, own_count, list_len, where, map_ref, list_ref, plan, target):
+    me = where[0]
     rows, owners, codes, classes = [], [], [], []
     for k in range(list_len):
         row = map_ref[list_ref[me, k]]
@@ -101,34 +114,28 @@
         plan[3, place] = jnp.int32(k)
 
     def one(fragment, carry):
-        picked, _ = pick(fragment, me)
+        picked, _ = pick(map_ref, list_ref, list_len, own_count, fragment, me)
         for r in range(CAP):
             target[fragment, r] = picked[r]
         return carry
 
     lax.fori_loop(0, frags, one, 0)
-    for needed, copy in copies:
-        pl.when(needed)(copy.wait)
-
-
-def plan_and_pack(where, owner_map, vir_list, energy, occ, table, frags):
-    own_count, block_rows, cols = table.shape
+
+
+def plan_lists(where, owner_map, vir_list, own_count, frags):
     list_len = vir_list.shape[1]
-    part = jax.ShapeDtypeStruct((CAP * block_rows + TAIL, cols), table.dtype)
     return pl.pallas_call(
         functools.partial(plan_kernel, frags, own_count, list_len),
-        out_shape=(part,) * 7
-        + (
+        out_shape=(
             jax.ShapeDtypeStruct((4, list_len), jnp.int32),
             jax.ShapeDtypeStruct((frags, CAP), jnp.int32),
         ),
-        in_specs=[SMEM, SMEM, SMEM, VMEM, VMEM, ANY],
-        out_specs=(VMEM,) * 7 + (SMEM, SMEM),
-        scratch_shapes=[pltpu.SemaphoreType.DMA((7, CAP))],
-        compiler_params=pltpu.CompilerParams(vmem_limit_bytes=8 * MIB),
+        in_specs=[SMEM, SMEM, SMEM],
+        out_specs=(SMEM, SMEM),
+        compiler_params=pltpu.CompilerParams(vmem_limit_bytes=4 * MIB),
         cost_estimate=NO_COST,
-        name="plan_and_pack",
-    )(where, owner_map, vir_list, energy, occ, table)
+        name="plan_lists",
+    )(where, owner_map, vir_list)
 
 
 def pack_kernel(first, codes, block, with_energy, plan, *refs):
@@ -211,10 +218,14 @@
 
 
 def contract_kernel(stage, block, width, where, plan, levels, rows_ref, energy, *refs):
-    groups = stage + 2
+    groups = min(stage + 2, 4)
     parts, rest = refs[: groups * 4], refs[groups * 4 :]
+    quarters = {2: (0, 2), 3: (1, 3)}.get(stage, (0, 1, 2, 3))
+    partial = None
     if stage == 2:
-        before, rest = rest[:2], rest[2:]
+        total, left, grid, occ, scaled, left_sems, grid_sems, occ_sems = rest
+    elif stage == 3:
+        before, partial, rest = rest[:2], rest[2], rest[3:]
         sent, stay, left, grid, occ, scaled, total, amps, tall, dens = rest[:10]
         left_sems, grid_sems, occ_sems = rest[10:]
     else:
@@ -244,7 +255,7 @@
         )
 
     def run(row_count, group_list):
-        for quarter in range(4):
+        for quarter in quarters:
             occ_copy(quarter).start()
             for b in range(row_count):
                 begin = pl.multiple_of((places[b] % 2) * block, block)
@@ -259,7 +270,8 @@
         height = len(PAIRS) * row_count * block
         span = len(group_list) * 2 * block
 
-        def scale(quarter):
+        def scale(turn):
+            quarter = quarters[turn]
             cols = pl.ds(quarter * width, width)
             orbit = [
                 occ[quarter * TAIL + i : quarter * TAIL + i + 1, :].astype(jnp.float32)
@@ -268,36 +280,41 @@
             for b in range(row_count):
                 rows = left[pl.ds(b * block, block), cols].astype(jnp.float32)
                 for p, (i, j) in enumerate(PAIRS):
-                    scaled[quarter % 2, pl.ds((p * row_count + b) * block, block), :] = (
+                    scaled[turn % 2, pl.ds((p * row_count + b) * block, block), :] = (
                         rows * (orbit[i] * orbit[j])
                     ).astype(jnp.bfloat16)
 
-        def wait_left(quarter):
+        def wait_left(turn):
+            quarter = quarters[turn]
             occ_copy(quarter).wait()
             for b in range(row_count):
                 left_copy(b, 0, 0, quarter).wait()
 
         wait_left(0)
         scale(0)
-        for quarter in range(4):
+        for turn, quarter in enumerate(quarters):
             cols = pl.ds(quarter * width, width)
             for slot, group in enumerate(group_list):
                 grid_copy(slot, group, quarter).wait()
-            if quarter < 3:
-                wait_left(quarter + 1)
-                scale(quarter + 1)
+            if turn + 1 < len(quarters):
+                wait_left(turn + 1)
+                scale(turn + 1)
             for step in range(height // 768):
                 rows = pl.ds(step * 768, 768)
                 term = lax.dot_general(
-                    scaled[quarter % 2, rows, :],
+                    scaled[turn % 2, rows, :],
                     grid[pl.ds(0, span), cols],
                     (((1,), (1,)), ((), ())),
                     preferred_element_type=jnp.float32,
                 )
-                if quarter == 0:
+                if turn:
+                    total[rows, pl.ds(0, span)] += term
+                elif partial is not None:
+                    total[rows, pl.ds(0, span)] = term + partial[rows, :]
+                else:
                     total[rows, pl.ds(0, span)] = term
-                else:
-                    total[rows, pl.ds(0, span)] += term
+        if stage == 2:
+            return None
         lane = lax.broadcasted_iota(jnp.int32, (block, block), 1)
         sub = lax.broadcasted_iota(jnp.int32, (block, block), 0)
         sums = []
@@ -315,7 +332,7 @@
                     value = total[rows, pl.ds(q * block, block)]
                     amp = jnp.where(live, value / gap, 0.0).astype(jnp.bfloat16)
                     amps[:, pl.ds(p * span + q * block, block)] = amp
-                    if stage == 2:
+                    if stage == 3:
                         early = amp if b == 0 else jnp.where(aux < 2, amp, jnp.zeros_like(amp))
                         tall[rows, pl.ds(q * block, block)] = early
             wide = amps[:, pl.ds(0, len(PAIRS) * span)]
@@ -345,6 +362,8 @@
         def _():
             out[0] = run(1, (0, 1, 2))[0]
             out[1] = jnp.zeros(out.shape[1:], out.dtype)
+    elif stage == 2:
+        run(2, (3,))
     else:
         sums = run(2, (3,))
         for b in range(2):
@@ -363,34 +382,38 @@
 def contract(stage, where, plan, levels, vir_rows, energy, parts, before=()):
     block, width = energy.shape[1], parts[0].shape[1]
     height = len(PAIRS) * 2 * block
-    spans = {0: (4, 1), 1: (6, 1), 2: (2, 1)}
-    span = spans[stage][0] * block
+    span = (4, 6, 2, 2)[stage] * block
     scratch = [
         pltpu.VMEM((2 * block, 4 * width), jnp.bfloat16),
         pltpu.VMEM((span, 4 * width), jnp.bfloat16),
         pltpu.VMEM((4 * TAIL, width), jnp.bfloat16),
         pltpu.VMEM((2, height, width), jnp.bfloat16),
-        pltpu.VMEM((height, span), jnp.float32),
-        pltpu.VMEM((block, len(PAIRS) * span), jnp.bfloat16),
     ]
-    if stage == 2:
+    if stage != 2:
+        scratch += [
+            pltpu.VMEM((height, span), jnp.float32),
+            pltpu.VMEM((block, len(PAIRS) * span), jnp.bfloat16),
+        ]
+    out_specs = VMEM
+    if stage == 3:
         scratch += [
             pltpu.VMEM((height, span), jnp.bfloat16),
             pltpu.VMEM((4, block, block), jnp.float32),
         ]
         out_shape = (jax.ShapeDtypeStruct((4, block // 2, block), jnp.float32),) * 2
         out_specs = (VMEM, VMEM)
+    elif stage == 2:
+        out_shape = jax.ShapeDtypeStruct((height, span), jnp.float32)
     else:
         out_shape = jax.ShapeDtypeStruct((2, block, block), jnp.float32)
-        out_specs = VMEM
     scratch += [
         pltpu.SemaphoreType.DMA((2, 4)),
         pltpu.SemaphoreType.DMA((3, 4)),
         pltpu.SemaphoreType.DMA((4,)),
     ]
     cost = NO_COST
-    if stage < 2:
-        units = (8, 6)[stage] * len(PAIRS) * block * block
+    if stage in (1, 2):
+        units = (8, 6, 2)[stage] * len(PAIRS) * block * block
         cost = pl.CostEstimate(
             flops=2 * units * 4 * width, bytes_accessed=units * 4, transcendentals=0
         )
@@ -427,6 +450,7 @@
         out_shape=jax.ShapeDtypeStruct((frags, CAP) + kept.shape[1:], kept.dtype),
         in_specs=[SMEM, SMEM, VMEM, VMEM],
         out_specs=VMEM,
+        compiler_params=pltpu.CompilerParams(vmem_limit_bytes=4 * MIB),
         name="spread",
     )(where, plan, kept, came)
 
@@ -448,6 +472,7 @@
         out_shape=jax.ShapeDtypeStruct((own_count,) + came.shape[2:], came.dtype),
         in_specs=[SMEM, VMEM],
         out_specs=VMEM,
+        compiler_params=pltpu.CompilerParams(vmem_limit_bytes=4 * MIB),
         name="collect",
     )(target, came)
 
@@ -463,7 +488,7 @@
     far_pairs = [(i, i ^ 2) for i in range(aux_count)]
     near_pairs = [(i, i ^ 1) for i in range(aux_count)]
 
-    *outgoing, own, plan, target = plan_and_pack(
+    *outgoing, own = pack_to_send(
         where, owner_map, vir_list, vir_energy, occ_grid[0], vir_grid, frags
     )
 
@@ -483,21 +508,29 @@
 
     arrived = {code: send(code - 1) for code in (1, 2, 3, 4)}
     parts = over_aux(own)
-    arrived[5] = send(4, *(arrived[c] for c in (1, 2, 3, 4)), parts[1])
-    here = pack_group(2, block, plan, {c: arrived[c] for c in range(1, 5)})[0]
+    arrived[5] = send(4, arrived[3], arrived[4])
+    plan, target = plan_lists(
+        after(where, arrived[3]), owner_map, vir_list, own_count, frags
+    )
+    arrived[6] = send(5, arrived[5])
+    known = {c: arrived[c] for c in range(1, 6)}
+    here = pack_group(2, block, plan, known)[0]
     parts += over_aux(here)
-    arrived[6] = send(5, arrived[5], parts[5])
-    here, early_energy = pack_group(
-        4, block, plan, {c: arrived[c] for c in range(1, 6)}, vir_energy
-    )
+    here, early_energy = pack_group(4, block, plan, known, vir_energy)
+    here = after(here, parts[5])
     shared = (where, plan, occ_energy, vir_rows)
     first = contract(0, *shared, early_energy, parts[:8])
     parts += over_aux(here, first)
     arrived[6] = after(arrived[6], first)
     here, energy = pack_group(6, block, plan, arrived, vir_energy)
+    here = after(here, parts[9])
     second = contract(1, *shared, early_energy, parts[:12])
-    parts += over_aux(here, second)
-    sent, stay = contract(2, *shared, energy, parts, (first, second))
+    near = lax.ppermute(here, "aux", near_pairs)
+    partial = contract(2, *shared, energy, parts + [here, here, near, near])
+    far = lax.ppermute(here, "aux", far_pairs)
+    far_near = lax.ppermute(after(far, second, partial), "aux", near_pairs)
+    parts += [here, far, near, far_near]
+    sent, stay = contract(3, *shared, energy, parts, (first, second, partial))
 
     quarter = block // aux_count
     core = aux % 2

time: 124 us -> 131 us (1.056)
  starting transfers between devices: 18.6 us -> 27.4 us
  waiting for transfers between devices: 46.2 us -> 41 us
  blocking collectives: 18.1 us -> 20 us
    ppermute x1, starting transfers between devices: 0.32 us -> 5.13 us  [body(): met = lax.ppermute(sent, 'aux', far_pairs)]
    ppermute x4 -> x3, waiting for transfers between devices: 2.47 us -> 0.01 us  [over_aux(): return [here, far, near, lax.ppermute(onward, 'aux', near_pairs)]]
    ppermute x0 -> x3, starting transfers between devices: none -> 2.36 us  [the longest x1 1.52 us: body(): far = lax.ppermute(here, 'aux', far_pairs)]
    all_to_all x1, blocking collectives: 18.1 us -> 20 us  [body(): incoming = lax.all_to_all(outgoing, 'frag', 0, 0, tiled=True)]
    ppermute x6, starting transfers between devices: 12.5 us -> 14.2 us  [send(): return lax.ppermute(payload, 'frag', round_pairs(distance, parity, frags))]
    ppermute x0 -> x3, waiting for transfers between devices: none -> 1.61 us  [the longest x1 1.57 us: body(): far_near = lax.ppermute(after(far, second, partial), 'aux', near_pairs)]
    ppermute x4 -> x3, waiting for transfers between devices: 11 us -> 9.49 us  [over_aux(): far = lax.ppermute(here, 'aux', far_pairs)]
    ppermute x6, waiting for transfers between devices: 26.1 us -> 24.6 us  [send(): return lax.ppermute(payload, 'frag', round_pairs(distance, parity, frags))]
  transfers between devices with their start and end apart: 20 -> 20, of which waited for: 9 -> 8; matrix products, arithmetic and copies ran while one was open for 0% -> 0% of each run, Pallas kernels for 18% -> 22%
where the time goes in v5:
time: 131 us; the launch traced here: 130 us
  waiting for transfers between devices  41 us (31%)
  Pallas kernels  37.7 us (29%)
  starting transfers between devices  27.4 us (21%)
  blocking collectives  20 us (15%)
  local copies, waits for them, and re-layouts  3.98 us (3%)
    pallas_call x4, Pallas kernels, contract(): pl.pallas_call(functools.partial(contract_kernel, stage, block, width), o...  29.7 us
    ppermute x6, waiting for transfers between devices, send(): return lax.ppermute(payload, 'frag', round_pairs(distance, parity, frags))  24.6 us
    all_to_all x1, blocking collectives, body(): incoming = lax.all_to_all(outgoing, 'frag', 0, 0, tiled=True)  20 us
    ppermute x6, starting transfers between devices, send(): return lax.ppermute(payload, 'frag', round_pairs(distance, parity, frags))  14.2 us
    ppermute x3, waiting for transfers between devices, over_aux(): far = lax.ppermute(here, 'aux', far_pairs)  9.49 us
    ppermute x1, starting transfers between devices, body(): met = lax.ppermute(sent, 'aux', far_pairs)  5.13 us
    ppermute x3, starting transfers between devices, over_aux(): far = lax.ppermute(here, 'aux', far_pairs)  4.75 us
    ppermute x1, waiting for transfers between devices, body(): met = lax.ppermute(sent, 'aux', far_pairs)  4.01 us
  transfers between devices with their start and end apart: 20, of which 8 were waited for; matrix products, arithmetic and copies ran while one was open for 0% of the time, Pallas kernels for 22%

profile of v5, /device:TPU:0, one launch (start us, length us, event | category | flops | bytes accessed | tf_op | source)
XLA Modules:
  0.0 130.4 jit_solution(15356169073738880637)
XLA Ops:
  0.1 1.2 copy-done
  4.0 1.5 %pack_to_send.1 = (bf16[272,1024]{1,0:T(8,128)(2,1)S(1)}, bf16[272,1024]{1,0:T(8,128)(2,1)S(1)}, bf16[272,1024]{1,0:T(8,128)(2,1)S(1)}, bf16[272,1024]{1,0:T(8,1...) custom-call(s32[2]{0:T(128)S(1)} %pad_add_fusion.where, ...), custom_call_target="tpu_custom_call" | custom-call | tf_op jit(solution)/shard_map/pack_to_send/pallas_call | solution.py:73
  5.6 3.2 %collective-permute-start = (bf16[272,1024]{1,0:T(8,128)(2,1)S(1)}, bf16[272,1024]{1,0:T(8,128)(2,1)S(1)}, u32[]{:S(2)}, u32[]{:S(2)}) collective-permute-start(bf16[272,1024]{1,0:T(8,128)(2,1)S(1)} %get-tuple-element.28), channel_id=1, source_target_pairs={{0,8},{4,12},{16,24},{20,28},{8,0},{12,4},{24,16},{28,20},{1,9},{5... | collective-permute-start | bytes 1671176 | tf_op jit(solution)/shard_map/ppermute | solution.py:507
  9.4 1.6 %collective-permute-start.1 = (bf16[272,1024]{1,0:T(8,128)(2,1)S(1)}, bf16[272,1024]{1,0:T(8,128)(2,1)S(1)}, u32[]{:S(2)}, u32[]{:S(2)}) collective-permute-start(bf16[272,1024]{1,0:T(8,128)(2,1)S(1)} %get-tuple-element.32), channel_id=1, source_target_pairs={{0,4},{8,12},{16,20},{24,28},{4,0},{12,8},{20,16},{28,24},{1,5},{9... | collective-permute-start | bytes 1671176 | tf_op jit(solution)/shard_map/ppermute | solution.py:507
  11.7 10.5 %collective-permute-done.refs_3_.refs_2_ = bf16[272,1024]{1,0:T(8,128)(2,1)S(1)} collective-permute-done((bf16[272,1024]{1,0:T(8,128)(2,1)S(1)}, bf16[272,1024]{1,0:T(8,128)(2,1)S(1)}, u32[]{:S(2)}, u32[]{:S(2)}) %collective-permute-start) | collective-permute-done | bytes 557088 | tf_op jit(solution)/shard_map/ppermute | solution.py:507
  22.2 7.4 %collective-permute-start.4 = (bf16[272,1024]{1,0:T(8,128)(2,1)S(1)}, bf16[272,1024]{1,0:T(8,128)(2,1)S(1)}, u32[]{:S(2)}, u32[]{:S(2)}) collective-permute-start(bf16[272,1024]{1,0:T(8,128)(2,1)S(1)} %get-tuple-element.36), channel_id=1, source_target_pairs={{0,12},{4,16},{8,20},{12,0},{16,4},{20,8},{1,13},{5,17},{9,21},{13... | collective-permute-start | bytes 1671176 | tf_op jit(solution)/shard_map/ppermute | solution.py:507
  29.6 1.6 %collective-permute-start.6 = (bf16[272,1024]{1,0:T(8,128)(2,1)S(1)}, bf16[272,1024]{1,0:T(8,128)(2,1)S(1)}, u32[]{:S(2)}, u32[]{:S(2)}) collective-permute-start(bf16[272,1024]{1,0:T(8,128)(2,1)S(1)} %get-tuple-element.40.refs_0_), channel_id=1, source_target_pairs={{0,2},{1,3},{2,0},{3,1},{4,6},{5,7},{6,4},{7,5},{8,10},{9,11},{10,... | collective-permute-start | bytes 1671176 | tf_op jit(solution)/shard_map/ppermute | solution.py:496
  31.2 2.2 %plan_lists.1 = (s32[4,8]{1,0:T(4,128)S(1)}, s32[8,2]{1,0:T(8,128)S(1)}) custom-call(s32[2]{0:T(128)S(1)} %pad_add_fusion.where, s32[32]{0:T(128)S(1)} %copy-done.7, s32[8,8]{1,0:T(8,128)S(1)} %copy-done.2), custom_call_target="tpu_custom_call" | custom-call | tf_op jit(solution)/shard_map/plan_lists/pallas_call | solution.py:127
  33.4 1.2 collective-permute-done.1.refs_1_.refs_0_
  34.5 13.0 %collective-permute-done.4.refs_5_.refs_4_ = bf16[272,1024]{1,0:T(8,128)(2,1)S(1)} collective-permute-done((bf16[272,1024]{1,0:T(8,128)(2,1)S(1)}, bf16[272,1024]{1,0:T(8,128)(2,1)S(1)}, u32[]{:S(2)}, u32[]{:S(2)}) %collective-permute-start.4) | collective-permute-done | bytes 557088 | tf_op jit(solution)/shard_map/ppermute | solution.py:507
  48.2 1.6 %collective-permute-start.9 = (bf16[256,1024]{1,0:T(8,128)(2,1)S(1)}, bf16[256,1024]{1,0:T(8,128)(2,1)S(1)}, u32[]{:S(2)}, u32[]{:S(2)}) collective-permute-start(bf16[256,1024]{1,0:T(8,128)(2,1)S(1)} %pack_group.4.refs_4_), channel_id=1, source_target_pairs={{0,2},{1,3},{2,0},{3,1},{4,6},{5,7},{6,4},{7,5},{8,10},{9,11},{10,... | collective-permute-start | bytes 1572872 | tf_op jit(solution)/shard_map/ppermute | solution.py:496
  51.1 9.2 %collective-permute-done.9.refs_5_ = bf16[256,1024]{1,0:T(8,128)(2,1)S(1)} collective-permute-done((bf16[256,1024]{1,0:T(8,128)(2,1)S(1)}, bf16[256,1024]{1,0:T(8,128)(2,1)S(1)}, u32[]{:S(2)}, u32[]{:S(2)}) %collective-permute-start.9) | collective-permute-done | bytes 524320 | tf_op jit(solution)/shard_map/ppermute | solution.py:496
  61.1 1.6 %collective-permute-start.12 = (bf16[256,1024]{1,0:T(8,128)(2,1)S(1)}, bf16[256,1024]{1,0:T(8,128)(2,1)S(1)}, u32[]{:S(2)}, u32[]{:S(2)}) collective-permute-start(bf16[256,1024]{1,0:T(8,128)(2,1)S(1)} %get-tuple-element.44.refs_8_), channel_id=1, source_target_pairs={{0,2},{1,3},{2,0},{3,1},{4,6},{5,7},{6,4},{7,5},{8,10},{9,11},{10,... | collective-permute-start | bytes 1572872 | tf_op jit(solution)/shard_map/ppermute | solution.py:496
  62.9 12.3 %contract.4.refs_16_ = f32[2,128,128]{2,1,0:T(8,128)S(1)} custom-call(s32[2]{0:T(128)S(1)} %pad_add_fusion.where, s32[4,8]{1,0:T(4,128)S(1)} %get-tuple-element.31.plan, f32[1,3]{1,0:T(1,128)S(1)} %copy-done.6, s32[8,8]{1,0:T(8,128)S(1)} %copy-done.1, f32[8,128]{1,0:T(8,128)S(1)} %get-tuple-element.39.energy, ...), custom_call_target="tpu_custom_call" | custom-call | tf_op jit(solution)/shard_map/contract/pallas_call | solution.py:420
  76.9 1.5 %collective-permute-start.15 = (bf16[256,1024]{1,0:T(8,128)(2,1)S(1)}, bf16[256,1024]{1,0:T(8,128)(2,1)S(1)}, u32[]{:S(2)}, u32[]{:S(2)}) collective-permute-start(bf16[256,1024]{1,0:T(8,128)(2,1)S(1)} %get-tuple-element.47.refs_12_.refs_13_), channel_id=1, source_target_pairs={{0,2},{1,3},{2,0},{3,1},{4,6},{5,7},{6,4},{7,5},{8,10},{9,11},{10,... | collective-permute-start | bytes 1572872 | tf_op jit(solution)/shard_map/ppermute | solution.py:530
  78.4 4.1 %contract.6.refs_18_ = f32[1536,256]{1,0:T(8,128)S(1)} custom-call(s32[2]{0:T(128)S(1)} %pad_add_fusion.where, s32[4,8]{1,0:T(4,128)S(1)} %get-tuple-element.31.plan, f32[1,3]{1,0:T(1,128)S(1)} %copy-done.6, s32[8,8]{1,0:T(8,128)S(1)} %copy-done.1, f32[8,128]{1,0:T(8,128)S(1)} %get-tuple-element.42.energy, bf16[272,1024]{1,0:T(8,128)(2,1)S(1)} %get-tuple-element.40.refs_0_, ...), custom_call_target="tpu_custom_call" | custom-call | flops 1610612736 | bytes 786432 | tf_op jit(solution)/shard_map/contract/pallas_call | solution.py:420
  82.5 8.3 %contract.5.refs_17_ = f32[2,128,128]{2,1,0:T(8,128)S(1)} custom-call(s32[2]{0:T(128)S(1)} %pad_add_fusion.where, s32[4,8]{1,0:T(4,128)S(1)} %get-tuple-element.31.plan, f32[1,3]{1,0:T(1,128)S(1)} %copy-done.6, s32[8,8]{1,0:T(8,128)S(1)} %copy-done.1, f32[8,128]{1,0:T(8,128)S(1)} %get-tuple-element.39.energy, ...), custom_call_target="tpu_custom_call" | custom-call | flops 4831838208 | bytes 2359296 | tf_op jit(solution)/shard_map/contract/pallas_call | solution.py:420
  91.2 1.6 %collective-permute-done.17.refs_15_ = bf16[256,1024]{1,0:T(8,128)(2,1)S(1)} collective-permute-done((bf16[256,1024]{1,0:T(8,128)(2,1)S(1)}, bf16[256,1024]{1,0:T(8,128)(2,1)S(1)}, u32[]{:S(2)}, u32[]{:S(2)}) %collective-permute-start.17) | collective-permute-done | bytes 524320 | tf_op jit(solution)/shard_map/ppermute | solution.py:531
  92.8 5.0 %contract.7 = (f32[4,64,128]{2,1,0:T(8,128)S(1)}, f32[4,64,128]{2,1,0:T(8,128)S(1)}) custom-call(s32[2]{0:T(128)S(1)} %pad_add_fusion.where, s32[4,8]{1,0:T(4,128)S(1)} %get-tuple-element.31.plan, f32[1,3]{1,0:T(1,128)S(1)} %copy-done.6, s32[8,8]{1,0:T(8,128)S(1)} %copy-done.1, f32[8,128]{1,0:T(8,128)S(1)} %get-tuple-element.42.energy, ...), custom_call_target="tpu_custom_call" | custom-call | tf_op jit(solution)/shard_map/contract/pallas_call | solution.py:420
  97.8 5.1 %collective-permute-start.18 = (f32[4,64,128]{2,1,0:T(8,128)S(1)}, f32[4,64,128]{2,1,0:T(8,128)S(1)}, u32[]{:S(2)}, u32[]{:S(2)}) collective-permute-start(f32[4,64,128]{2,1,0:T(8,128)S(1)} %get-tuple-element.50), channel_id=1, source_target_pairs={{0,2},{1,3},{2,0},{3,1},{4,6},{5,7},{6,4},{7,5},{8,10},{9,11},{10,... | collective-permute-start | bytes 393224 | tf_op jit(solution)/shard_map/ppermute | solution.py:537
  102.9 4.0 %collective-permute-done.18 = f32[4,64,128]{2,1,0:T(8,128)S(1)} collective-permute-done((f32[4,64,128]{2,1,0:T(8,128)S(1)}, f32[4,64,128]{2,1,0:T(8,128)S(1)}, u32[]{:S(2)}, u32[]{:S(2)}) %collective-permute-start.18) | collective-permute-done | bytes 131104 | tf_op jit(solution)/shard_map/ppermute | solution.py:537
  107.1 1.3 collective-permute-done.19.came
  109.1 20.0 %all_to_all.5.came = f32[8,2,32,128]{3,2,1,0:T(8,128)S(1)} all-to-all(f32[8,2,32,128]{3,2,1,0:T(8,128)S(1)} %spread.1), channel_id=1, replica_groups=mesh['frag'=8,'aux'=4] {'frag'}, dimensions={0} | all-to-all | bytes 524288 | tf_op jit(solution)/shard_map/all_to_all | solution.py:543
  129.1 1.3 %collect.1 = f32[4,32,128]{2,1,0:T(8,128)} custom-call(s32[8,2]{1,0:T(8,128)S(1)} %get-tuple-element.30.target, f32[8,2,32,128]{3,2,1,0:T(8,128)S(1)} %all_to_all.5.came), custom_call_target="tpu_custom_call" | custom-call | tf_op jit(solution)/shard_map/collect/pallas_call | solution.py:470
  (48 shorter events, 10.0 us)
Async XLA Ops:
  0.1 1.2 copy-start
  5.6 16.6 %collective-permute-start = (bf16[272,1024]{1,0:T(8,128)(2,1)S(1)}, bf16[272,1024]{1,0:T(8,128)(2,1)S(1)}, u32[]{:S(2)}, u32[]{:S(2)}) collective-permute-start(bf16[272,1024]{1,0:T(8,128)(2,1)S(1)} %get-tuple-element.28), channel_id=1, source_target_pairs={{0,8},{4,12},{16,24},{20,28},{8,0},{12,4},{24,16},{28,20},{1,9},{5... | collective-permute-start | bytes 1671176 | tf_op jit(solution)/shard_map/ppermute | solution.py:507
  8.7 13.5 %collective-permute-start.3 = (bf16[272,1024]{1,0:T(8,128)(2,1)S(1)}, bf16[272,1024]{1,0:T(8,128)(2,1)S(1)}, u32[]{:S(2)}, u32[]{:S(2)}) collective-permute-start(bf16[272,1024]{1,0:T(8,128)(2,1)S(1)} %get-tuple-element.34), channel_id=1, source_target_pairs={{8,16},{12,20},{16,8},{20,12},{9,17},{13,21},{17,9},{21,13},{10,18... | collective-permute-start | bytes 1671176 | tf_op jit(solution)/shard_map/ppermute | solution.py:507
  9.4 25.1 %collective-permute-start.1 = (bf16[272,1024]{1,0:T(8,128)(2,1)S(1)}, bf16[272,1024]{1,0:T(8,128)(2,1)S(1)}, u32[]{:S(2)}, u32[]{:S(2)}) collective-permute-start(bf16[272,1024]{1,0:T(8,128)(2,1)S(1)} %get-tuple-element.32), channel_id=1, source_target_pairs={{0,4},{8,12},{16,20},{24,28},{4,0},{12,8},{20,16},{28,24},{1,5},{9... | collective-permute-start | bytes 1671176 | tf_op jit(solution)/shard_map/ppermute | solution.py:507
  11.0 23.5 %collective-permute-start.2 = (bf16[272,1024]{1,0:T(8,128)(2,1)S(1)}, bf16[272,1024]{1,0:T(8,128)(2,1)S(1)}, u32[]{:S(2)}, u32[]{:S(2)}) collective-permute-start(bf16[272,1024]{1,0:T(8,128)(2,1)S(1)} %get-tuple-element.33), channel_id=1, source_target_pairs={{4,8},{12,16},{20,24},{8,4},{16,12},{24,20},{5,9},{13,17},{21,25},... | collective-permute-start | bytes 1671176 | tf_op jit(solution)/shard_map/ppermute | solution.py:507
  22.2 25.3 %collective-permute-start.4 = (bf16[272,1024]{1,0:T(8,128)(2,1)S(1)}, bf16[272,1024]{1,0:T(8,128)(2,1)S(1)}, u32[]{:S(2)}, u32[]{:S(2)}) collective-permute-start(bf16[272,1024]{1,0:T(8,128)(2,1)S(1)} %get-tuple-element.36), channel_id=1, source_target_pairs={{0,12},{4,16},{8,20},{12,0},{16,4},{20,8},{1,13},{5,17},{9,21},{13... | collective-permute-start | bytes 1671176 | tf_op jit(solution)/shard_map/ppermute | solution.py:507
  29.6 20.2 %collective-permute-start.6 = (bf16[272,1024]{1,0:T(8,128)(2,1)S(1)}, bf16[272,1024]{1,0:T(8,128)(2,1)S(1)}, u32[]{:S(2)}, u32[]{:S(2)}) collective-permute-start(bf16[272,1024]{1,0:T(8,128)(2,1)S(1)} %get-tuple-element.40.refs_0_), channel_id=1, source_target_pairs={{0,2},{1,3},{2,0},{3,1},{4,6},{5,7},{6,4},{7,5},{8,10},{9,11},{10,... | collective-permute-start | bytes 1671176 | tf_op jit(solution)/shard_map/ppermute | solution.py:496
  31.1 29.9 %collective-permute-start.7 = (bf16[272,1024]{1,0:T(8,128)(2,1)S(1)}, bf16[272,1024]{1,0:T(8,128)(2,1)S(1)}, u32[]{:S(2)}, u32[]{:S(2)}) collective-permute-start(bf16[272,1024]{1,0:T(8,128)(2,1)S(1)} %get-tuple-element.40.refs_0_), channel_id=1, source_target_pairs={{0,1},{1,0},{2,3},{3,2},{4,5},{5,4},{6,7},{7,6},{8,9},{9,8},{10,11... | collective-permute-start | bytes 1671176 | tf_op jit(solution)/shard_map/ppermute | solution.py:497
  48.2 14.7 %copy-start.1 = (s32[8,8]{1,0:T(8,128)S(1)}, s32[8,8]{1,0:T(8,128)}, u32[]{:S(2)}) copy-start(s32[8,8]{1,0:T(8,128)} %rows_ref.7) | copy-start | bytes 772
  48.2 14.7 %copy-start.6 = (f32[1,3]{1,0:T(1,128)S(1)}, f32[1,3]{1,0:T(1,128)}, u32[]{:S(2)}) copy-start(f32[1,3]{1,0:T(1,128)} %levels.7) | copy-start | bytes 40
  48.2 12.1 %collective-permute-start.9 = (bf16[256,1024]{1,0:T(8,128)(2,1)S(1)}, bf16[256,1024]{1,0:T(8,128)(2,1)S(1)}, u32[]{:S(2)}, u32[]{:S(2)}) collective-permute-start(bf16[256,1024]{1,0:T(8,128)(2,1)S(1)} %pack_group.4.refs_4_), channel_id=1, source_target_pairs={{0,2},{1,3},{2,0},{3,1},{4,6},{5,7},{6,4},{7,5},{8,10},{9,11},{10,... | collective-permute-start | bytes 1572872 | tf_op jit(solution)/shard_map/ppermute | solution.py:496
  49.8 12.9 %collective-permute-start.8 = (bf16[272,1024]{1,0:T(8,128)(2,1)S(1)}, bf16[272,1024]{1,0:T(8,128)(2,1)S(1)}, u32[]{:S(2)}, u32[]{:S(2)}) collective-permute-start(bf16[272,1024]{1,0:T(8,128)(2,1)S(1)} %collective-permute-done.6.refs_1_), channel_id=1, source_target_pairs={{0,1},{1,0},{2,3},{3,2},{4,5},{5,4},{6,7},{7,6},{8,9},{9,8},{10,11... | collective-permute-start | bytes 1671176 | tf_op jit(solution)/shard_map/ppermute | solution.py:499
  49.8 25.4 %collective-permute-start.5 = (bf16[272,1024]{1,0:T(8,128)(2,1)S(1)}, bf16[272,1024]{1,0:T(8,128)(2,1)S(1)}, u32[]{:S(2)}, u32[]{:S(2)}) collective-permute-start(bf16[272,1024]{1,0:T(8,128)(2,1)S(1)} %get-tuple-element.38), channel_id=1, source_target_pairs={{12,24},{16,28},{24,12},{28,16},{13,25},{17,29},{25,13},{29,17},{1... | collective-permute-start | bytes 1671176 | tf_op jit(solution)/shard_map/ppermute | solution.py:507
  50.5 12.4 %collective-permute-start.10 = (bf16[256,1024]{1,0:T(8,128)(2,1)S(1)}, bf16[256,1024]{1,0:T(8,128)(2,1)S(1)}, u32[]{:S(2)}, u32[]{:S(2)}) collective-permute-start(bf16[256,1024]{1,0:T(8,128)(2,1)S(1)} %pack_group.4.refs_4_), channel_id=1, source_target_pairs={{0,1},{1,0},{2,3},{3,2},{4,5},{5,4},{6,7},{7,6},{8,9},{9,8},{10,11... | collective-permute-start | bytes 1572872 | tf_op jit(solution)/shard_map/ppermute | solution.py:497
  60.3 2.6 %collective-permute-start.11 = (bf16[256,1024]{1,0:T(8,128)(2,1)S(1)}, bf16[256,1024]{1,0:T(8,128)(2,1)S(1)}, u32[]{:S(2)}, u32[]{:S(2)}) collective-permute-start(bf16[256,1024]{1,0:T(8,128)(2,1)S(1)} %collective-permute-done.9.refs_5_), channel_id=1, source_target_pairs={{0,1},{1,0},{2,3},{3,2},{4,5},{5,4},{6,7},{7,6},{8,9},{9,8},{10,11... | collective-permute-start | bytes 1572872 | tf_op jit(solution)/shard_map/ppermute | solution.py:499
  61.1 14.4 %collective-permute-start.12 = (bf16[256,1024]{1,0:T(8,128)(2,1)S(1)}, bf16[256,1024]{1,0:T(8,128)(2,1)S(1)}, u32[]{:S(2)}, u32[]{:S(2)}) collective-permute-start(bf16[256,1024]{1,0:T(8,128)(2,1)S(1)} %get-tuple-element.44.refs_8_), channel_id=1, source_target_pairs={{0,2},{1,3},{2,0},{3,1},{4,6},{5,7},{6,4},{7,5},{8,10},{9,11},{10,... | collective-permute-start | bytes 1572872 | tf_op jit(solution)/shard_map/ppermute | solution.py:496
  62.7 15.7 %collective-permute-start.13 = (bf16[256,1024]{1,0:T(8,128)(2,1)S(1)}, bf16[256,1024]{1,0:T(8,128)(2,1)S(1)}, u32[]{:S(2)}, u32[]{:S(2)}) collective-permute-start(bf16[256,1024]{1,0:T(8,128)(2,1)S(1)} %get-tuple-element.44.refs_8_), channel_id=1, source_target_pairs={{0,1},{1,0},{2,3},{3,2},{4,5},{5,4},{6,7},{7,6},{8,9},{9,8},{10,11... | collective-permute-start | bytes 1572872 | tf_op jit(solution)/shard_map/ppermute | solution.py:497
  62.9 12.7 %copy-start.4 = (bf16[4,128]{1,0:T(4,128)(2,1)S(1)}, bf16[4,128]{1,0:T(4,128)(2,1)}, u32[]{:S(2)}) copy-start(bf16[4,128]{1,0:T(4,128)(2,1)} %refs_0_.3) | copy-start | bytes 3076
  75.5 2.9 %collective-permute-start.14 = (bf16[256,1024]{1,0:T(8,128)(2,1)S(1)}, bf16[256,1024]{1,0:T(8,128)(2,1)S(1)}, u32[]{:S(2)}, u32[]{:S(2)}) collective-permute-start(bf16[256,1024]{1,0:T(8,128)(2,1)S(1)} %collective-permute-done.12.refs_9_), channel_id=1, source_target_pairs={{0,1},{1,0},{2,3},{3,2},{4,5},{5,4},{6,7},{7,6},{8,9},{9,8},{10,11... | collective-permute-start | bytes 1572872 | tf_op jit(solution)/shard_map/ppermute | solution.py:499
  76.4 2.0 %collective-permute-start.16 = (bf16[256,1024]{1,0:T(8,128)(2,1)S(1)}, bf16[256,1024]{1,0:T(8,128)(2,1)S(1)}, u32[]{:S(2)}, u32[]{:S(2)}) collective-permute-start(bf16[256,1024]{1,0:T(8,128)(2,1)S(1)} %get-tuple-element.47.refs_12_.refs_13_), channel_id=1, source_target_pairs={{0,1},{1,0},{2,3},{3,2},{4,5},{5,4},{6,7},{7,6},{8,9},{9,8},{10,11... | collective-permute-start | bytes 1572872 | tf_op jit(solution)/shard_map/ppermute | solution.py:528
  76.9 13.9 %collective-permute-start.15 = (bf16[256,1024]{1,0:T(8,128)(2,1)S(1)}, bf16[256,1024]{1,0:T(8,128)(2,1)S(1)}, u32[]{:S(2)}, u32[]{:S(2)}) collective-permute-start(bf16[256,1024]{1,0:T(8,128)(2,1)S(1)} %get-tuple-element.47.refs_12_.refs_13_), channel_id=1, source_target_pairs={{0,2},{1,3},{2,0},{3,1},{4,6},{5,7},{6,4},{7,5},{8,10},{9,11},{10,... | collective-permute-start | bytes 1572872 | tf_op jit(solution)/shard_map/ppermute | solution.py:530
  90.8 2.0 %collective-permute-start.17 = (bf16[256,1024]{1,0:T(8,128)(2,1)S(1)}, bf16[256,1024]{1,0:T(8,128)(2,1)S(1)}, u32[]{:S(2)}, u32[]{:S(2)}) collective-permute-start(bf16[256,1024]{1,0:T(8,128)(2,1)S(1)} %collective-permute-done.15.refs_13_), channel_id=1, source_target_pairs={{0,1},{1,0},{2,3},{3,2},{4,5},{5,4},{6,7},{7,6},{8,9},{9,8},{10,11... | collective-permute-start | bytes 1572872 | tf_op jit(solution)/shard_map/ppermute | solution.py:531
  97.8 9.1 %collective-permute-start.18 = (f32[4,64,128]{2,1,0:T(8,128)S(1)}, f32[4,64,128]{2,1,0:T(8,128)S(1)}, u32[]{:S(2)}, u32[]{:S(2)}) collective-permute-start(f32[4,64,128]{2,1,0:T(8,128)S(1)} %get-tuple-element.50), channel_id=1, source_target_pairs={{0,2},{1,3},{2,0},{3,1},{4,6},{5,7},{6,4},{7,5},{8,10},{9,11},{10,... | collective-permute-start | bytes 393224 | tf_op jit(solution)/shard_map/ppermute | solution.py:537
  107.0 1.4 %collective-permute-start.19 = (f32[6,32,128]{2,1,0:T(8,128)S(1)}, f32[6,32,128]{2,1,0:T(8,128)S(1)}, u32[]{:S(2)}, u32[]{:S(2)}) collective-permute-start(f32[6,32,128]{2,1,0:T(8,128)S(1)} %get-tuple-element.51), channel_id=1, source_target_pairs={{0,1},{1,0},{2,3},{3,2},{4,5},{5,4},{6,7},{7,6},{8,9},{9,8},{10,11... | collective-permute-start | bytes 294920 | tf_op jit(solution)/shard_map/ppermute | solution.py:541
  (4 other events, 2.7 us)

commit v6 on v5

--- a/solution.py
+++ b/solution.py
@@ -330,7 +330,7 @@
                     gap = (levels[0, i] + levels[0, j]) - own_energy - their_energy
                     rows = pl.ds((p * row_count + b) * block, block)
                     value = total[rows, pl.ds(q * block, block)]
-                    amp = jnp.where(live, value / gap, 0.0).astype(jnp.bfloat16)
+                    amp = jnp.where(live, value * pl.reciprocal(gap), 0.0).astype(jnp.bfloat16)
                     amps[:, pl.ds(p * span + q * block, block)] = amp
                     if stage == 3:
                         early = amp if b == 0 else jnp.where(aux < 2, amp, jnp.zeros_like(amp))
@@ -508,16 +508,16 @@
 
     arrived = {code: send(code - 1) for code in (1, 2, 3, 4)}
     parts = over_aux(own)
-    arrived[5] = send(4, arrived[3], arrived[4])
+    arrived[5] = send(4, *(arrived[c] for c in (1, 2, 3, 4)))
     plan, target = plan_lists(
         after(where, arrived[3]), owner_map, vir_list, own_count, frags
     )
-    arrived[6] = send(5, arrived[5])
-    known = {c: arrived[c] for c in range(1, 6)}
-    here = pack_group(2, block, plan, known)[0]
+    here = pack_group(2, block, plan, {c: arrived[c] for c in range(1, 5)})[0]
     parts += over_aux(here)
-    here, early_energy = pack_group(4, block, plan, known, vir_energy)
-    here = after(here, parts[5])
+    arrived[6] = send(5, parts[5])
+    here, early_energy = pack_group(
+        4, block, plan, {c: arrived[c] for c in range(1, 6)}, vir_energy
+    )
     shared = (where, plan, occ_energy, vir_rows)
     first = contract(0, *shared, early_energy, parts[:8])
     parts += over_aux(here, first)

time: 131 us -> 119 us (0.908)
  blocking collectives: 20 us -> 14.2 us
  waiting for transfers between devices: 41 us -> 35.9 us
    ppermute x6, waiting for transfers between devices: 24.6 us -> 18.3 us  [send(): return lax.ppermute(payload, 'frag', round_pairs(distance, parity, frags))]
    all_to_all x1, blocking collectives: 20 us -> 14.2 us  [body(): incoming = lax.all_to_all(outgoing, 'frag', 0, 0, tiled=True)]
    ppermute x3, starting transfers between devices: 0.12 us -> 1.55 us  [over_aux(): return [here, far, near, lax.ppermute(onward, 'aux', near_pairs)]]
  transfers between devices with their start and end apart: 20 -> 20, of which waited for: 8 -> 8; matrix products, arithmetic and copies ran while one was open for 0% -> 0% of each run, Pallas kernels for 22% -> 24%
where the time goes in v6:
time: 119 us
  Pallas kernels  37.7 us (32%)
  waiting for transfers between devices  35.9 us (30%)
  starting transfers between devices  27 us (23%)
  blocking collectives  14.2 us (12%)
  local copies, waits for them, and re-layouts  3.98 us (3%)
    pallas_call x4, Pallas kernels, contract(): pl.pallas_call(functools.partial(contract_kernel, stage, block, width), o...  29.7 us
    ppermute x6, waiting for transfers between devices, send(): return lax.ppermute(payload, 'frag', round_pairs(distance, parity, frags))  18.3 us
    ppermute x6, starting transfers between devices, send(): return lax.ppermute(payload, 'frag', round_pairs(distance, parity, frags))  14.2 us
    all_to_all x1, blocking collectives, body(): incoming = lax.all_to_all(outgoing, 'frag', 0, 0, tiled=True)  14.2 us
    ppermute x3, waiting for transfers between devices, over_aux(): far = lax.ppermute(here, 'aux', far_pairs)  9.93 us
    ppermute x3, starting transfers between devices, over_aux(): far = lax.ppermute(here, 'aux', far_pairs)  4.75 us
    ppermute x1, starting transfers between devices, body(): met = lax.ppermute(sent, 'aux', far_pairs)  4.71 us
    ppermute x1, waiting for transfers between devices, body(): met = lax.ppermute(sent, 'aux', far_pairs)  4.01 us
  transfers between devices with their start and end apart: 20, of which 8 were waited for; matrix products, arithmetic and copies ran while one was open for 0% of the time, Pallas kernels for 24%

profile of v6, /device:TPU:0, one launch (start us, length us, event | category | flops | bytes accessed | tf_op | source)
XLA Modules:
  0.0 119.1 jit_solution(9115263277122497950)
XLA Ops:
  0.1 1.2 %copy-done = bf16[4,128,1024]{2,1,0:T(8,128)(2,1)S(1)} copy-done((bf16[4,128,1024]{2,1,0:T(8,128)(2,1)S(1)}, bf16[4,128,1024]{2,1,0:T(8,128)(2,1)}, u32[]{:S(2)}) %copy-start) | copy-done | bytes 1048600
  4.0 1.5 %pack_to_send.1 = (bf16[272,1024]{1,0:T(8,128)(2,1)S(1)}, bf16[272,1024]{1,0:T(8,128)(2,1)S(1)}, bf16[272,1024]{1,0:T(8,128)(2,1)S(1)}, bf16[272,1024]{1,0:T(8,1...) custom-call(s32[2]{0:T(128)S(1)} %pad_add_fusion.where, ...), custom_call_target="tpu_custom_call" | custom-call | tf_op jit(solution)/shard_map/pack_to_send/pallas_call | solution.py:73
  5.6 3.1 %collective-permute-start = (bf16[272,1024]{1,0:T(8,128)(2,1)S(1)}, bf16[272,1024]{1,0:T(8,128)(2,1)S(1)}, u32[]{:S(2)}, u32[]{:S(2)}) collective-permute-start(bf16[272,1024]{1,0:T(8,128)(2,1)S(1)} %get-tuple-element.27), channel_id=1, source_target_pairs={{0,8},{4,12},{16,24},{20,28},{8,0},{12,4},{24,16},{28,20},{1,9},{5... | collective-permute-start | bytes 1671176 | tf_op jit(solution)/shard_map/ppermute | solution.py:507
  8.7 1.6 %collective-permute-start.1 = (bf16[272,1024]{1,0:T(8,128)(2,1)S(1)}, bf16[272,1024]{1,0:T(8,128)(2,1)S(1)}, u32[]{:S(2)}, u32[]{:S(2)}) collective-permute-start(bf16[272,1024]{1,0:T(8,128)(2,1)S(1)} %get-tuple-element.31), channel_id=1, source_target_pairs={{0,4},{8,12},{16,20},{24,28},{4,0},{12,8},{20,16},{28,24},{1,5},{9... | collective-permute-start | bytes 1671176 | tf_op jit(solution)/shard_map/ppermute | solution.py:507
  11.6 1.6 %collective-permute-start.7 = (bf16[272,1024]{1,0:T(8,128)(2,1)S(1)}, bf16[272,1024]{1,0:T(8,128)(2,1)S(1)}, u32[]{:S(2)}, u32[]{:S(2)}) collective-permute-start(bf16[272,1024]{1,0:T(8,128)(2,1)S(1)} %get-tuple-element.39.refs_0_), channel_id=1, source_target_pairs={{0,2},{1,3},{2,0},{3,1},{4,6},{5,7},{6,4},{7,5},{8,10},{9,11},{10,... | collective-permute-start | bytes 1671176 | tf_op jit(solution)/shard_map/ppermute | solution.py:496
  13.2 8.9 %collective-permute-done.refs_2_.refs_3_ = bf16[272,1024]{1,0:T(8,128)(2,1)S(1)} collective-permute-done((bf16[272,1024]{1,0:T(8,128)(2,1)S(1)}, bf16[272,1024]{1,0:T(8,128)(2,1)S(1)}, u32[]{:S(2)}, u32[]{:S(2)}) %collective-permute-start) | collective-permute-done | bytes 557088 | tf_op jit(solution)/shard_map/ppermute | solution.py:507
  22.1 2.2 %plan_lists.1 = (s32[4,8]{1,0:T(4,128)S(1)}, s32[8,2]{1,0:T(8,128)S(1)}) custom-call(s32[2]{0:T(128)S(1)} %pad_add_fusion.where, s32[32]{0:T(128)S(1)} %copy-done.7, s32[8,8]{1,0:T(8,128)S(1)} %copy-done.2), custom_call_target="tpu_custom_call" | custom-call | tf_op jit(solution)/shard_map/plan_lists/pallas_call | solution.py:127
  24.4 9.4 %collective-permute-done.1.refs_0_.refs_1_ = bf16[272,1024]{1,0:T(8,128)(2,1)S(1)} collective-permute-done((bf16[272,1024]{1,0:T(8,128)(2,1)S(1)}, bf16[272,1024]{1,0:T(8,128)(2,1)S(1)}, u32[]{:S(2)}, u32[]{:S(2)}) %collective-permute-start.1) | collective-permute-done | bytes 557088 | tf_op jit(solution)/shard_map/ppermute | solution.py:507
  33.8 7.5 %collective-permute-start.4 = (bf16[272,1024]{1,0:T(8,128)(2,1)S(1)}, bf16[272,1024]{1,0:T(8,128)(2,1)S(1)}, u32[]{:S(2)}, u32[]{:S(2)}) collective-permute-start(bf16[272,1024]{1,0:T(8,128)(2,1)S(1)} %get-tuple-element.35), channel_id=1, source_target_pairs={{0,12},{4,16},{8,20},{12,0},{16,4},{20,8},{1,13},{5,17},{9,21},{13... | collective-permute-start | bytes 1671176 | tf_op jit(solution)/shard_map/ppermute | solution.py:507
  42.0 1.6 %collective-permute-start.5 = (bf16[256,1024]{1,0:T(8,128)(2,1)S(1)}, bf16[256,1024]{1,0:T(8,128)(2,1)S(1)}, u32[]{:S(2)}, u32[]{:S(2)}) collective-permute-start(bf16[256,1024]{1,0:T(8,128)(2,1)S(1)} %pack_group.3.refs_4_), channel_id=1, source_target_pairs={{0,2},{1,3},{2,0},{3,1},{4,6},{5,7},{6,4},{7,5},{8,10},{9,11},{10,... | collective-permute-start | bytes 1572872 | tf_op jit(solution)/shard_map/ppermute | solution.py:496
  44.0 9.9 %collective-permute-done.5.refs_5_ = bf16[256,1024]{1,0:T(8,128)(2,1)S(1)} collective-permute-done((bf16[256,1024]{1,0:T(8,128)(2,1)S(1)}, bf16[256,1024]{1,0:T(8,128)(2,1)S(1)}, u32[]{:S(2)}, u32[]{:S(2)}) %collective-permute-start.5) | collective-permute-done | bytes 524320 | tf_op jit(solution)/shard_map/ppermute | solution.py:496
  56.0 1.6 %collective-permute-start.12 = (bf16[256,1024]{1,0:T(8,128)(2,1)S(1)}, bf16[256,1024]{1,0:T(8,128)(2,1)S(1)}, u32[]{:S(2)}, u32[]{:S(2)}) collective-permute-start(bf16[256,1024]{1,0:T(8,128)(2,1)S(1)} %get-tuple-element.42.refs_8_), channel_id=1, source_target_pairs={{0,2},{1,3},{2,0},{3,1},{4,6},{5,7},{6,4},{7,5},{8,10},{9,11},{10,... | collective-permute-start | bytes 1572872 | tf_op jit(solution)/shard_map/ppermute | solution.py:496
  57.7 12.3 %contract.4.refs_16_ = f32[2,128,128]{2,1,0:T(8,128)S(1)} custom-call(s32[2]{0:T(128)S(1)} %pad_add_fusion.where, s32[4,8]{1,0:T(4,128)S(1)} %get-tuple-element.30.plan, f32[1,3]{1,0:T(1,128)S(1)} %copy-done.6, s32[8,8]{1,0:T(8,128)S(1)} %copy-done.1, f32[8,128]{1,0:T(8,128)S(1)} %get-tuple-element.38.energy, ...), custom_call_target="tpu_custom_call" | custom-call | tf_op jit(solution)/shard_map/contract/pallas_call | solution.py:420
  70.5 0.8 pack_group.5
  71.4 1.5 %collective-permute-start.15 = (bf16[256,1024]{1,0:T(8,128)(2,1)S(1)}, bf16[256,1024]{1,0:T(8,128)(2,1)S(1)}, u32[]{:S(2)}, u32[]{:S(2)}) collective-permute-start(bf16[256,1024]{1,0:T(8,128)(2,1)S(1)} %get-tuple-element.45.refs_12_.refs_13_), channel_id=1, source_target_pairs={{0,2},{1,3},{2,0},{3,1},{4,6},{5,7},{6,4},{7,5},{8,10},{9,11},{10,... | collective-permute-start | bytes 1572872 | tf_op jit(solution)/shard_map/ppermute | solution.py:530
  73.3 4.1 %contract.6.refs_18_ = f32[1536,256]{1,0:T(8,128)S(1)} custom-call(s32[2]{0:T(128)S(1)} %pad_add_fusion.where, s32[4,8]{1,0:T(4,128)S(1)} %get-tuple-element.30.plan, f32[1,3]{1,0:T(1,128)S(1)} %copy-done.6, s32[8,8]{1,0:T(8,128)S(1)} %copy-done.1, f32[8,128]{1,0:T(8,128)S(1)} %get-tuple-element.41.energy, bf16[272,1024]{1,0:T(8,128)(2,1)S(1)} %get-tuple-element.39.refs_0_, ...), custom_call_target="tpu_custom_call" | custom-call | flops 1610612736 | bytes 786432 | tf_op jit(solution)/shard_map/contract/pallas_call | solution.py:420
  77.4 8.3 %contract.5.refs_17_ = f32[2,128,128]{2,1,0:T(8,128)S(1)} custom-call(s32[2]{0:T(128)S(1)} %pad_add_fusion.where, s32[4,8]{1,0:T(4,128)S(1)} %get-tuple-element.30.plan, f32[1,3]{1,0:T(1,128)S(1)} %copy-done.6, s32[8,8]{1,0:T(8,128)S(1)} %copy-done.1, f32[8,128]{1,0:T(8,128)S(1)} %get-tuple-element.38.energy, ...), custom_call_target="tpu_custom_call" | custom-call | flops 4831838208 | bytes 2359296 | tf_op jit(solution)/shard_map/contract/pallas_call | solution.py:420
  85.9 1.8 %collective-permute-done.17.refs_15_ = bf16[256,1024]{1,0:T(8,128)(2,1)S(1)} collective-permute-done((bf16[256,1024]{1,0:T(8,128)(2,1)S(1)}, bf16[256,1024]{1,0:T(8,128)(2,1)S(1)}, u32[]{:S(2)}, u32[]{:S(2)}) %collective-permute-start.17) | collective-permute-done | bytes 524320 | tf_op jit(solution)/shard_map/ppermute | solution.py:531
  87.7 5.0 %contract.7 = (f32[4,64,128]{2,1,0:T(8,128)S(1)}, f32[4,64,128]{2,1,0:T(8,128)S(1)}) custom-call(s32[2]{0:T(128)S(1)} %pad_add_fusion.where, s32[4,8]{1,0:T(4,128)S(1)} %get-tuple-element.30.plan, f32[1,3]{1,0:T(1,128)S(1)} %copy-done.6, s32[8,8]{1,0:T(8,128)S(1)} %copy-done.1, f32[8,128]{1,0:T(8,128)S(1)} %get-tuple-element.41.energy, ...), custom_call_target="tpu_custom_call" | custom-call | tf_op jit(solution)/shard_map/contract/pallas_call | solution.py:420
  92.7 4.7 %collective-permute-start.18 = (f32[4,64,128]{2,1,0:T(8,128)S(1)}, f32[4,64,128]{2,1,0:T(8,128)S(1)}, u32[]{:S(2)}, u32[]{:S(2)}) collective-permute-start(f32[4,64,128]{2,1,0:T(8,128)S(1)} %get-tuple-element.48), channel_id=1, source_target_pairs={{0,2},{1,3},{2,0},{3,1},{4,6},{5,7},{6,4},{7,5},{8,10},{9,11},{10,... | collective-permute-start | bytes 393224 | tf_op jit(solution)/shard_map/ppermute | solution.py:537
  97.4 4.0 %collective-permute-done.18 = f32[4,64,128]{2,1,0:T(8,128)S(1)} collective-permute-done((f32[4,64,128]{2,1,0:T(8,128)S(1)}, f32[4,64,128]{2,1,0:T(8,128)S(1)}, u32[]{:S(2)}, u32[]{:S(2)}) %collective-permute-start.18) | collective-permute-done | bytes 131104 | tf_op jit(solution)/shard_map/ppermute | solution.py:537
  101.6 1.3 %collective-permute-done.19.came = f32[6,32,128]{2,1,0:T(8,128)S(1)} collective-permute-done((f32[6,32,128]{2,1,0:T(8,128)S(1)}, f32[6,32,128]{2,1,0:T(8,128)S(1)}, u32[]{:S(2)}, u32[]{:S(2)}) %collective-permute-start.19) | collective-permute-done | bytes 98336 | tf_op jit(solution)/shard_map/ppermute | solution.py:541
  103.6 14.2 %all_to_all.5.came = f32[8,2,32,128]{3,2,1,0:T(8,128)S(1)} all-to-all(f32[8,2,32,128]{3,2,1,0:T(8,128)S(1)} %spread.1), channel_id=1, replica_groups=mesh['frag'=8,'aux'=4] {'frag'}, dimensions={0} | all-to-all | bytes 524288 | tf_op jit(solution)/shard_map/all_to_all | solution.py:543
  117.7 1.3 %collect.1 = f32[4,32,128]{2,1,0:T(8,128)} custom-call(s32[8,2]{1,0:T(8,128)S(1)} %get-tuple-element.29.target, f32[8,2,32,128]{3,2,1,0:T(8,128)S(1)} %all_to_all.5.came), custom_call_target="tpu_custom_call" | custom-call | tf_op jit(solution)/shard_map/collect/pallas_call | solution.py:470
  (48 shorter events, 9.5 us)
Async XLA Ops:
  0.1 1.2 %copy-start = (bf16[4,128,1024]{2,1,0:T(8,128)(2,1)S(1)}, bf16[4,128,1024]{2,1,0:T(8,128)(2,1)}, u32[]{:S(2)}) copy-start(bf16[4,128,1024]{2,1,0:T(8,128)(2,1)} %table.1) | copy-start | bytes 3145732
  5.6 16.6 %collective-permute-start = (bf16[272,1024]{1,0:T(8,128)(2,1)S(1)}, bf16[272,1024]{1,0:T(8,128)(2,1)S(1)}, u32[]{:S(2)}, u32[]{:S(2)}) collective-permute-start(bf16[272,1024]{1,0:T(8,128)(2,1)S(1)} %get-tuple-element.27), channel_id=1, source_target_pairs={{0,8},{4,12},{16,24},{20,28},{8,0},{12,4},{24,16},{28,20},{1,9},{5... | collective-permute-start | bytes 1671176 | tf_op jit(solution)/shard_map/ppermute | solution.py:507
  8.7 25.1 %collective-permute-start.1 = (bf16[272,1024]{1,0:T(8,128)(2,1)S(1)}, bf16[272,1024]{1,0:T(8,128)(2,1)S(1)}, u32[]{:S(2)}, u32[]{:S(2)}) collective-permute-start(bf16[272,1024]{1,0:T(8,128)(2,1)S(1)} %get-tuple-element.31), channel_id=1, source_target_pairs={{0,4},{8,12},{16,20},{24,28},{4,0},{12,8},{20,16},{28,24},{1,5},{9... | collective-permute-start | bytes 1671176 | tf_op jit(solution)/shard_map/ppermute | solution.py:507
  10.2 23.5 %collective-permute-start.2 = (bf16[272,1024]{1,0:T(8,128)(2,1)S(1)}, bf16[272,1024]{1,0:T(8,128)(2,1)S(1)}, u32[]{:S(2)}, u32[]{:S(2)}) collective-permute-start(bf16[272,1024]{1,0:T(8,128)(2,1)S(1)} %get-tuple-element.32), channel_id=1, source_target_pairs={{4,8},{12,16},{20,24},{8,4},{16,12},{24,20},{5,9},{13,17},{21,25},... | collective-permute-start | bytes 1671176 | tf_op jit(solution)/shard_map/ppermute | solution.py:507
  10.9 22.9 %collective-permute-start.3 = (bf16[272,1024]{1,0:T(8,128)(2,1)S(1)}, bf16[272,1024]{1,0:T(8,128)(2,1)S(1)}, u32[]{:S(2)}, u32[]{:S(2)}) collective-permute-start(bf16[272,1024]{1,0:T(8,128)(2,1)S(1)} %get-tuple-element.33), channel_id=1, source_target_pairs={{8,16},{12,20},{16,8},{20,12},{9,17},{13,21},{17,9},{21,13},{10,18... | collective-permute-start | bytes 1671176 | tf_op jit(solution)/shard_map/ppermute | solution.py:507
  11.6 31.9 %collective-permute-start.7 = (bf16[272,1024]{1,0:T(8,128)(2,1)S(1)}, bf16[272,1024]{1,0:T(8,128)(2,1)S(1)}, u32[]{:S(2)}, u32[]{:S(2)}) collective-permute-start(bf16[272,1024]{1,0:T(8,128)(2,1)S(1)} %get-tuple-element.39.refs_0_), channel_id=1, source_target_pairs={{0,2},{1,3},{2,0},{3,1},{4,6},{5,7},{6,4},{7,5},{8,10},{9,11},{10,... | collective-permute-start | bytes 1671176 | tf_op jit(solution)/shard_map/ppermute | solution.py:496
  33.8 21.0 %collective-permute-start.4 = (bf16[272,1024]{1,0:T(8,128)(2,1)S(1)}, bf16[272,1024]{1,0:T(8,128)(2,1)S(1)}, u32[]{:S(2)}, u32[]{:S(2)}) collective-permute-start(bf16[272,1024]{1,0:T(8,128)(2,1)S(1)} %get-tuple-element.35), channel_id=1, source_target_pairs={{0,12},{4,16},{8,20},{12,0},{16,4},{20,8},{1,13},{5,17},{9,21},{13... | collective-permute-start | bytes 1671176 | tf_op jit(solution)/shard_map/ppermute | solution.py:507
  41.9 15.7 %copy-start.1 = (s32[8,8]{1,0:T(8,128)S(1)}, s32[8,8]{1,0:T(8,128)}, u32[]{:S(2)}) copy-start(s32[8,8]{1,0:T(8,128)} %rows_ref.7) | copy-start | bytes 772
  41.9 15.7 %copy-start.6 = (f32[1,3]{1,0:T(1,128)S(1)}, f32[1,3]{1,0:T(1,128)}, u32[]{:S(2)}) copy-start(f32[1,3]{1,0:T(1,128)} %levels.7) | copy-start | bytes 40
  42.0 12.0 %collective-permute-start.5 = (bf16[256,1024]{1,0:T(8,128)(2,1)S(1)}, bf16[256,1024]{1,0:T(8,128)(2,1)S(1)}, u32[]{:S(2)}, u32[]{:S(2)}) collective-permute-start(bf16[256,1024]{1,0:T(8,128)(2,1)S(1)} %pack_group.3.refs_4_), channel_id=1, source_target_pairs={{0,2},{1,3},{2,0},{3,1},{4,6},{5,7},{6,4},{7,5},{8,10},{9,11},{10,... | collective-permute-start | bytes 1572872 | tf_op jit(solution)/shard_map/ppermute | solution.py:496
  43.5 12.5 %collective-permute-start.8 = (bf16[272,1024]{1,0:T(8,128)(2,1)S(1)}, bf16[272,1024]{1,0:T(8,128)(2,1)S(1)}, u32[]{:S(2)}, u32[]{:S(2)}) collective-permute-start(bf16[272,1024]{1,0:T(8,128)(2,1)S(1)} %get-tuple-element.39.refs_0_), channel_id=1, source_target_pairs={{0,1},{1,0},{2,3},{3,2},{4,5},{5,4},{6,7},{7,6},{8,9},{9,8},{10,11... | collective-permute-start | bytes 1671176 | tf_op jit(solution)/shard_map/ppermute | solution.py:497
  43.5 14.1 %collective-permute-start.9 = (bf16[272,1024]{1,0:T(8,128)(2,1)S(1)}, bf16[272,1024]{1,0:T(8,128)(2,1)S(1)}, u32[]{:S(2)}, u32[]{:S(2)}) collective-permute-start(bf16[272,1024]{1,0:T(8,128)(2,1)S(1)} %collective-permute-done.7.refs_1_), channel_id=1, source_target_pairs={{0,1},{1,0},{2,3},{3,2},{4,5},{5,4},{6,7},{7,6},{8,9},{9,8},{10,11... | collective-permute-start | bytes 1671176 | tf_op jit(solution)/shard_map/ppermute | solution.py:499
  54.0 16.0 %collective-permute-start.6 = (bf16[272,1024]{1,0:T(8,128)(2,1)S(1)}, bf16[272,1024]{1,0:T(8,128)(2,1)S(1)}, u32[]{:S(2)}, u32[]{:S(2)}) collective-permute-start(bf16[272,1024]{1,0:T(8,128)(2,1)S(1)} %get-tuple-element.37), channel_id=1, source_target_pairs={{12,24},{16,28},{24,12},{28,16},{13,25},{17,29},{25,13},{29,17},{1... | collective-permute-start | bytes 1671176 | tf_op jit(solution)/shard_map/ppermute | solution.py:507
  54.7 2.9 %collective-permute-start.10 = (bf16[256,1024]{1,0:T(8,128)(2,1)S(1)}, bf16[256,1024]{1,0:T(8,128)(2,1)S(1)}, u32[]{:S(2)}, u32[]{:S(2)}) collective-permute-start(bf16[256,1024]{1,0:T(8,128)(2,1)S(1)} %pack_group.3.refs_4_), channel_id=1, source_target_pairs={{0,1},{1,0},{2,3},{3,2},{4,5},{5,4},{6,7},{7,6},{8,9},{9,8},{10,11... | collective-permute-start | bytes 1572872 | tf_op jit(solution)/shard_map/ppermute | solution.py:497
  54.7 2.9 %collective-permute-start.11 = (bf16[256,1024]{1,0:T(8,128)(2,1)S(1)}, bf16[256,1024]{1,0:T(8,128)(2,1)S(1)}, u32[]{:S(2)}, u32[]{:S(2)}) collective-permute-start(bf16[256,1024]{1,0:T(8,128)(2,1)S(1)} %collective-permute-done.5.refs_5_), channel_id=1, source_target_pairs={{0,1},{1,0},{2,3},{3,2},{4,5},{5,4},{6,7},{7,6},{8,9},{9,8},{10,11... | collective-permute-start | bytes 1572872 | tf_op jit(solution)/shard_map/ppermute | solution.py:499
  56.0 14.0 %collective-permute-start.12 = (bf16[256,1024]{1,0:T(8,128)(2,1)S(1)}, bf16[256,1024]{1,0:T(8,128)(2,1)S(1)}, u32[]{:S(2)}, u32[]{:S(2)}) collective-permute-start(bf16[256,1024]{1,0:T(8,128)(2,1)S(1)} %get-tuple-element.42.refs_8_), channel_id=1, source_target_pairs={{0,2},{1,3},{2,0},{3,1},{4,6},{5,7},{6,4},{7,5},{8,10},{9,11},{10,... | collective-permute-start | bytes 1572872 | tf_op jit(solution)/shard_map/ppermute | solution.py:496
  57.6 15.3 %collective-permute-start.13 = (bf16[256,1024]{1,0:T(8,128)(2,1)S(1)}, bf16[256,1024]{1,0:T(8,128)(2,1)S(1)}, u32[]{:S(2)}, u32[]{:S(2)}) collective-permute-start(bf16[256,1024]{1,0:T(8,128)(2,1)S(1)} %get-tuple-element.42.refs_8_), channel_id=1, source_target_pairs={{0,1},{1,0},{2,3},{3,2},{4,5},{5,4},{6,7},{7,6},{8,9},{9,8},{10,11... | collective-permute-start | bytes 1572872 | tf_op jit(solution)/shard_map/ppermute | solution.py:497
  57.6 12.9 %copy-start.4 = (bf16[4,128]{1,0:T(4,128)(2,1)S(1)}, bf16[4,128]{1,0:T(4,128)(2,1)}, u32[]{:S(2)}) copy-start(bf16[4,128]{1,0:T(4,128)(2,1)} %refs_0_.3) | copy-start | bytes 3076
  70.0 2.9 %collective-permute-start.14 = (bf16[256,1024]{1,0:T(8,128)(2,1)S(1)}, bf16[256,1024]{1,0:T(8,128)(2,1)S(1)}, u32[]{:S(2)}, u32[]{:S(2)}) collective-permute-start(bf16[256,1024]{1,0:T(8,128)(2,1)S(1)} %collective-permute-done.12.refs_9_), channel_id=1, source_target_pairs={{0,1},{1,0},{2,3},{3,2},{4,5},{5,4},{6,7},{7,6},{8,9},{9,8},{10,11... | collective-permute-start | bytes 1572872 | tf_op jit(solution)/shard_map/ppermute | solution.py:499
  71.3 2.0 %collective-permute-start.16 = (bf16[256,1024]{1,0:T(8,128)(2,1)S(1)}, bf16[256,1024]{1,0:T(8,128)(2,1)S(1)}, u32[]{:S(2)}, u32[]{:S(2)}) collective-permute-start(bf16[256,1024]{1,0:T(8,128)(2,1)S(1)} %get-tuple-element.45.refs_12_.refs_13_), channel_id=1, source_target_pairs={{0,1},{1,0},{2,3},{3,2},{4,5},{5,4},{6,7},{7,6},{8,9},{9,8},{10,11... | collective-permute-start | bytes 1572872 | tf_op jit(solution)/shard_map/ppermute | solution.py:528
  71.4 14.3 %collective-permute-start.15 = (bf16[256,1024]{1,0:T(8,128)(2,1)S(1)}, bf16[256,1024]{1,0:T(8,128)(2,1)S(1)}, u32[]{:S(2)}, u32[]{:S(2)}) collective-permute-start(bf16[256,1024]{1,0:T(8,128)(2,1)S(1)} %get-tuple-element.45.refs_12_.refs_13_), channel_id=1, source_target_pairs={{0,2},{1,3},{2,0},{3,1},{4,6},{5,7},{6,4},{7,5},{8,10},{9,11},{10,... | collective-permute-start | bytes 1572872 | tf_op jit(solution)/shard_map/ppermute | solution.py:530
  85.8 1.9 %collective-permute-start.17 = (bf16[256,1024]{1,0:T(8,128)(2,1)S(1)}, bf16[256,1024]{1,0:T(8,128)(2,1)S(1)}, u32[]{:S(2)}, u32[]{:S(2)}) collective-permute-start(bf16[256,1024]{1,0:T(8,128)(2,1)S(1)} %collective-permute-done.15.refs_13_), channel_id=1, source_target_pairs={{0,1},{1,0},{2,3},{3,2},{4,5},{5,4},{6,7},{7,6},{8,9},{9,8},{10,11... | collective-permute-start | bytes 1572872 | tf_op jit(solution)/shard_map/ppermute | solution.py:531
  92.7 8.7 %collective-permute-start.18 = (f32[4,64,128]{2,1,0:T(8,128)S(1)}, f32[4,64,128]{2,1,0:T(8,128)S(1)}, u32[]{:S(2)}, u32[]{:S(2)}) collective-permute-start(f32[4,64,128]{2,1,0:T(8,128)S(1)} %get-tuple-element.48), channel_id=1, source_target_pairs={{0,2},{1,3},{2,0},{3,1},{4,6},{5,7},{6,4},{7,5},{8,10},{9,11},{10,... | collective-permute-start | bytes 393224 | tf_op jit(solution)/shard_map/ppermute | solution.py:537
  101.5 1.4 %collective-permute-start.19 = (f32[6,32,128]{2,1,0:T(8,128)S(1)}, f32[6,32,128]{2,1,0:T(8,128)S(1)}, u32[]{:S(2)}, u32[]{:S(2)}) collective-permute-start(f32[6,32,128]{2,1,0:T(8,128)S(1)} %get-tuple-element.49), channel_id=1, source_target_pairs={{0,1},{1,0},{2,3},{3,2},{4,5},{5,4},{6,7},{7,6},{8,9},{9,8},{10,11... | collective-permute-start | bytes 294920 | tf_op jit(solution)/shard_map/ppermute | solution.py:541
  (4 other events, 2.7 us)

commit v7 on v6

--- a/solution.py
+++ b/solution.py
@@ -214,7 +214,7 @@
 
 
 def place_of(aux, b):
-    return jnp.where(aux < 2, 2 * aux + b, aux + 2 + 2 * b)
+    return aux + 4 * b
 
 
 def contract_kernel(stage, block, width, where, plan, levels, rows_ref, energy, *refs):
@@ -228,6 +228,8 @@
         before, partial, rest = rest[:2], rest[2], rest[3:]
         sent, stay, left, grid, occ, scaled, total, amps, tall, dens = rest[:10]
         left_sems, grid_sems, occ_sems = rest[10:]
+    elif stage == 1:
+        out, left, grid, occ, scaled, total, amps, tall, left_sems, grid_sems, occ_sems = rest
     else:
         out, left, grid, occ, scaled, total, amps, left_sems, grid_sems, occ_sems = rest
     me, aux = where[0], where[1]
@@ -335,6 +337,8 @@
                     if stage == 3:
                         early = amp if b == 0 else jnp.where(aux < 2, amp, jnp.zeros_like(amp))
                         tall[rows, pl.ds(q * block, block)] = early
+                    elif stage == 1 and b == 0:
+                        tall[pl.ds(p * block, block), pl.ds(q * block, block)] = amp
             wide = amps[:, pl.ds(0, len(PAIRS) * span)]
             sums.append(
                 lax.dot_general(
@@ -343,15 +347,14 @@
             )
         return sums
 
+    def late_sum(q):
+        late = tall[:, pl.ds(q * block, block)]
+        return lax.dot_general(
+            late, late, (((0,), (0,)), ((), ())), preferred_element_type=jnp.float32
+        )
+
     if stage == 0:
-
-        @pl.when(aux < 2)
-        def _():
-            out[0], out[1] = run(2, (0, 1))
-
-        @pl.when(aux >= 2)
-        def _():
-            out[...] = jnp.zeros_like(out)
+        out[0] = run(1, (0, 1))[0]
     elif stage == 1:
 
         @pl.when(aux < 2)
@@ -360,19 +363,21 @@
 
         @pl.when(aux >= 2)
         def _():
-            out[0] = run(1, (0, 1, 2))[0]
+            out[0] = run(1, (2,))[0]
             out[1] = jnp.zeros(out.shape[1:], out.dtype)
+
+        for q in range(2):
+            out[2 + q] = late_sum(q)
     elif stage == 2:
         run(2, (3,))
     else:
+        first, second = before
         sums = run(2, (3,))
-        for b in range(2):
-            dens[b] = sums[b] + (before[0][b] + before[1][b])
-        for q in range(2):
-            late = tall[:, pl.ds(q * block, block)]
-            dens[2 + q] = lax.dot_general(
-                late, late, (((0,), (0,)), ((), ())), preferred_element_type=jnp.float32
-            )
+        dens[0] = sums[0] + (first[0] + second[0])
+        share = sums[1] + second[1]
+        for q in range(4):
+            late = second[2 + q] if q < 2 else late_sum(q - 2)
+            dens[1 + q] = late + jnp.where(aux == q, share, 0.0)
         half = block // 2
         side = aux // 2
         stay[...] = dens[:, pl.ds(pl.multiple_of(side * half, half), half), :]
@@ -382,7 +387,7 @@
 def contract(stage, where, plan, levels, vir_rows, energy, parts, before=()):
     block, width = energy.shape[1], parts[0].shape[1]
     height = len(PAIRS) * 2 * block
-    span = (4, 6, 2, 2)[stage] * block
+    span = (4, 2, 2, 2)[stage] * block
     scratch = [
         pltpu.VMEM((2 * block, 4 * width), jnp.bfloat16),
         pltpu.VMEM((span, 4 * width), jnp.bfloat16),
@@ -398,14 +403,17 @@
     if stage == 3:
         scratch += [
             pltpu.VMEM((height, span), jnp.bfloat16),
-            pltpu.VMEM((4, block, block), jnp.float32),
+            pltpu.VMEM((5, block, block), jnp.float32),
         ]
-        out_shape = (jax.ShapeDtypeStruct((4, block // 2, block), jnp.float32),) * 2
+        out_shape = (jax.ShapeDtypeStruct((5, block // 2, block), jnp.float32),) * 2
         out_specs = (VMEM, VMEM)
     elif stage == 2:
         out_shape = jax.ShapeDtypeStruct((height, span), jnp.float32)
+    elif stage == 1:
+        scratch += [pltpu.VMEM((height // 2, span), jnp.bfloat16)]
+        out_shape = jax.ShapeDtypeStruct((4, block, block), jnp.float32)
     else:
-        out_shape = jax.ShapeDtypeStruct((2, block, block), jnp.float32)
+        out_shape = jax.ShapeDtypeStruct((1, block, block), jnp.float32)
     scratch += [
         pltpu.SemaphoreType.DMA((2, 4)),
         pltpu.SemaphoreType.DMA((3, 4)),
@@ -413,7 +421,7 @@
     ]
     cost = NO_COST
     if stage in (1, 2):
-        units = (8, 6, 2)[stage] * len(PAIRS) * block * block
+        units = (4, 4, 2)[stage] * len(PAIRS) * block * block
         cost = pl.CostEstimate(
             flops=2 * units * 4 * width, bytes_accessed=units * 4, transcendentals=0
         )
@@ -432,16 +440,16 @@
 def spread_kernel(own_count, where, plan, kept, came, out):
     aux = where[1]
     out[...] = jnp.zeros_like(out)
-    holders = (aux, aux ^ 2, aux ^ 1, aux ^ 3)
-    late = [kept[4 + q] + came[4 + q] for q in range(2)]
-    for index, holder in enumerate(holders):
-        source = kept if index < 2 else came
-        for b in range(2):
-            place = place_of(holder, b)
-            value = source[2 * (index % 2) + b]
-            if b == 1:
-                value += jnp.where(place == 6, late[0], jnp.where(place == 7, late[1], 0.0))
-            out[plan[2, place] // own_count, plan[1, place]] = value
+
+    def put(place, value):
+        out[plan[2, place] // own_count, plan[1, place]] = value
+
+    put(aux, kept[0])
+    put(aux ^ 2, kept[1])
+    put(aux ^ 1, came[0])
+    put(aux ^ 3, came[1])
+    for q in range(4):
+        put(4 + q, kept[2 + q] + came[2 + q])
 
 
 def spread(where, plan, kept, came, frags, own_count):
@@ -535,7 +543,7 @@
     quarter = block // aux_count
     core = aux % 2
     met = lax.ppermute(sent, "aux", far_pairs)
-    both = jnp.concatenate([stay[:2], met[:2], stay[2:] + met[2:]], axis=0)
+    both = jnp.concatenate([stay[:1], met[:1], stay[1:] + met[1:]], axis=0)
     sent = lax.dynamic_slice_in_dim(both, (1 - core) * quarter, quarter, 1)
     kept = lax.dynamic_slice_in_dim(both, core * quarter, quarter, 1)
     came = lax.ppermute(sent, "aux", near_pairs)

time: 119 us -> 117 us (0.983)
  waiting for transfers between devices: 35.9 us -> 41.9 us
  Pallas kernels: 37.7 us -> 32.7 us
  starting transfers between devices: 27 us -> 23.8 us
    ppermute x3, waiting for transfers between devices: 9.93 us -> 15.3 us  [over_aux(): far = lax.ppermute(here, 'aux', far_pairs)]
    pallas_call x4, Pallas kernels: 29.7 us -> 24.8 us  [contract(): pl.pallas_call(functools.partial(contract_kernel, stage, block, width), o...]
    ppermute x1, starting transfers between devices: 4.71 us -> 1.09 us  [body(): met = lax.ppermute(sent, 'aux', far_pairs)]
    ppermute x1, waiting for transfers between devices: 4.01 us -> 5.42 us  [body(): met = lax.ppermute(sent, 'aux', far_pairs)]
  transfers between devices with their start and end apart: 20 -> 20, of which waited for: 8 -> 7; matrix products, arithmetic and copies ran while one was open for 0% -> 0% of each run, Pallas kernels for 24% -> 21%
where the time goes in v7:
time: 117 us
  waiting for transfers between devices  41.9 us (36%)
  Pallas kernels  32.7 us (28%)
  starting transfers between devices  23.8 us (20%)
  blocking collectives  14.2 us (12%)
  local copies, waits for them, and re-layouts  3.99 us (3%)
    pallas_call x4, Pallas kernels, contract(): pl.pallas_call(functools.partial(contract_kernel, stage, block, width), o...  24.8 us
    ppermute x6, waiting for transfers between devices, send(): return lax.ppermute(payload, 'frag', round_pairs(distance, parity, frags))  18.3 us
    ppermute x3, waiting for transfers between devices, over_aux(): far = lax.ppermute(here, 'aux', far_pairs)  15.3 us
    ppermute x6, starting transfers between devices, send(): return lax.ppermute(payload, 'frag', round_pairs(distance, parity, frags))  14.3 us
    all_to_all x1, blocking collectives, body(): incoming = lax.all_to_all(outgoing, 'frag', 0, 0, tiled=True)  14.2 us
    ppermute x1, waiting for transfers between devices, body(): met = lax.ppermute(sent, 'aux', far_pairs)  5.42 us
    ppermute x3, starting transfers between devices, over_aux(): far = lax.ppermute(here, 'aux', far_pairs)  4.75 us
    unnamed x16, local copies, waits for them, and re-layouts  3.96 us
  transfers between devices with their start and end apart: 20, of which 7 were waited for; matrix products, arithmetic and copies ran while one was open for 0% of the time, Pallas kernels for 21%

profile of v7, /device:TPU:0, one launch (start us, length us, event | category | flops | bytes accessed | tf_op | source)
XLA Modules:
  0.0 116.9 jit_solution(9586018117998412042)
XLA Ops:
  0.1 1.2 %copy-done = bf16[4,128,1024]{2,1,0:T(8,128)(2,1)S(1)} copy-done((bf16[4,128,1024]{2,1,0:T(8,128)(2,1)S(1)}, bf16[4,128,1024]{2,1,0:T(8,128)(2,1)}, u32[]{:S(2)}) %copy-start) | copy-done | bytes 1048600
  4.0 1.5 %pack_to_send.1 = (bf16[272,1024]{1,0:T(8,128)(2,1)S(1)}, bf16[272,1024]{1,0:T(8,128)(2,1)S(1)}, bf16[272,1024]{1,0:T(8,128)(2,1)S(1)}, bf16[272,1024]{1,0:T(8,1...) custom-call(s32[2]{0:T(128)S(1)} %pad_add_fusion.where, ...), custom_call_target="tpu_custom_call" | custom-call | tf_op jit(solution)/shard_map/pack_to_send/pallas_call | solution.py:73
  5.6 3.1 %collective-permute-start = (bf16[272,1024]{1,0:T(8,128)(2,1)S(1)}, bf16[272,1024]{1,0:T(8,128)(2,1)S(1)}, u32[]{:S(2)}, u32[]{:S(2)}) collective-permute-start(bf16[272,1024]{1,0:T(8,128)(2,1)S(1)} %get-tuple-element.27), channel_id=1, source_target_pairs={{0,8},{4,12},{16,24},{20,28},{8,0},{12,4},{24,16},{28,20},{1,9},{5... | collective-permute-start | bytes 1671176 | tf_op jit(solution)/shard_map/ppermute | solution.py:515
  8.7 1.5 %collective-permute-start.1 = (bf16[272,1024]{1,0:T(8,128)(2,1)S(1)}, bf16[272,1024]{1,0:T(8,128)(2,1)S(1)}, u32[]{:S(2)}, u32[]{:S(2)}) collective-permute-start(bf16[272,1024]{1,0:T(8,128)(2,1)S(1)} %get-tuple-element.31), channel_id=1, source_target_pairs={{0,4},{8,12},{16,20},{24,28},{4,0},{12,8},{20,16},{28,24},{1,5},{9... | collective-permute-start | bytes 1671176 | tf_op jit(solution)/shard_map/ppermute | solution.py:515
  11.6 1.6 %collective-permute-start.7 = (bf16[272,1024]{1,0:T(8,128)(2,1)S(1)}, bf16[272,1024]{1,0:T(8,128)(2,1)S(1)}, u32[]{:S(2)}, u32[]{:S(2)}) collective-permute-start(bf16[272,1024]{1,0:T(8,128)(2,1)S(1)} %get-tuple-element.39.refs_0_), channel_id=1, source_target_pairs={{0,2},{1,3},{2,0},{3,1},{4,6},{5,7},{6,4},{7,5},{8,10},{9,11},{10,... | collective-permute-start | bytes 1671176 | tf_op jit(solution)/shard_map/ppermute | solution.py:504
  13.2 9.0 %collective-permute-done.refs_2_.refs_3_ = bf16[272,1024]{1,0:T(8,128)(2,1)S(1)} collective-permute-done((bf16[272,1024]{1,0:T(8,128)(2,1)S(1)}, bf16[272,1024]{1,0:T(8,128)(2,1)S(1)}, u32[]{:S(2)}, u32[]{:S(2)}) %collective-permute-start) | collective-permute-done | bytes 557088 | tf_op jit(solution)/shard_map/ppermute | solution.py:515
  22.1 2.2 %plan_lists.1 = (s32[4,8]{1,0:T(4,128)S(1)}, s32[8,2]{1,0:T(8,128)S(1)}) custom-call(s32[2]{0:T(128)S(1)} %pad_add_fusion.where, s32[32]{0:T(128)S(1)} %copy-done.7, s32[8,8]{1,0:T(8,128)S(1)} %copy-done.2), custom_call_target="tpu_custom_call" | custom-call | tf_op jit(solution)/shard_map/plan_lists/pallas_call | solution.py:127
  24.4 9.3 %collective-permute-done.1.refs_0_.refs_1_ = bf16[272,1024]{1,0:T(8,128)(2,1)S(1)} collective-permute-done((bf16[272,1024]{1,0:T(8,128)(2,1)S(1)}, bf16[272,1024]{1,0:T(8,128)(2,1)S(1)}, u32[]{:S(2)}, u32[]{:S(2)}) %collective-permute-start.1) | collective-permute-done | bytes 557088 | tf_op jit(solution)/shard_map/ppermute | solution.py:515
  33.7 7.6 %collective-permute-start.4 = (bf16[272,1024]{1,0:T(8,128)(2,1)S(1)}, bf16[272,1024]{1,0:T(8,128)(2,1)S(1)}, u32[]{:S(2)}, u32[]{:S(2)}) collective-permute-start(bf16[272,1024]{1,0:T(8,128)(2,1)S(1)} %get-tuple-element.35), channel_id=1, source_target_pairs={{0,12},{4,16},{8,20},{12,0},{16,4},{20,8},{1,13},{5,17},{9,21},{13... | collective-permute-start | bytes 1671176 | tf_op jit(solution)/shard_map/ppermute | solution.py:515
  42.0 1.6 %collective-permute-start.5 = (bf16[256,1024]{1,0:T(8,128)(2,1)S(1)}, bf16[256,1024]{1,0:T(8,128)(2,1)S(1)}, u32[]{:S(2)}, u32[]{:S(2)}) collective-permute-start(bf16[256,1024]{1,0:T(8,128)(2,1)S(1)} %pack_group.3.refs_4_), channel_id=1, source_target_pairs={{0,2},{1,3},{2,0},{3,1},{4,6},{5,7},{6,4},{7,5},{8,10},{9,11},{10,... | collective-permute-start | bytes 1572872 | tf_op jit(solution)/shard_map/ppermute | solution.py:504
  44.1 9.9 %collective-permute-done.5.refs_5_ = bf16[256,1024]{1,0:T(8,128)(2,1)S(1)} collective-permute-done((bf16[256,1024]{1,0:T(8,128)(2,1)S(1)}, bf16[256,1024]{1,0:T(8,128)(2,1)S(1)}, u32[]{:S(2)}, u32[]{:S(2)}) %collective-permute-start.5) | collective-permute-done | bytes 524320 | tf_op jit(solution)/shard_map/ppermute | solution.py:504
  56.1 1.6 %collective-permute-start.12 = (bf16[256,1024]{1,0:T(8,128)(2,1)S(1)}, bf16[256,1024]{1,0:T(8,128)(2,1)S(1)}, u32[]{:S(2)}, u32[]{:S(2)}) collective-permute-start(bf16[256,1024]{1,0:T(8,128)(2,1)S(1)} %get-tuple-element.42.refs_8_), channel_id=1, source_target_pairs={{0,2},{1,3},{2,0},{3,1},{4,6},{5,7},{6,4},{7,5},{8,10},{9,11},{10,... | collective-permute-start | bytes 1572872 | tf_op jit(solution)/shard_map/ppermute | solution.py:504
  57.7 6.9 %contract.4.refs_16_ = f32[1,128,128]{2,1,0:T(8,128)S(1)} custom-call(s32[2]{0:T(128)S(1)} %pad_add_fusion.where, s32[4,8]{1,0:T(4,128)S(1)} %get-tuple-element.30.plan, f32[1,3]{1,0:T(1,128)S(1)} %copy-done.6, s32[8,8]{1,0:T(8,128)S(1)} %copy-done.1, f32[8,128]{1,0:T(8,128)S(1)} %get-tuple-element.38.energy, ...), custom_call_target="tpu_custom_call" | custom-call | tf_op jit(solution)/shard_map/contract/pallas_call | solution.py:428
  64.7 5.4 %collective-permute-done.12.refs_9_ = bf16[256,1024]{1,0:T(8,128)(2,1)S(1)} collective-permute-done((bf16[256,1024]{1,0:T(8,128)(2,1)S(1)}, bf16[256,1024]{1,0:T(8,128)(2,1)S(1)}, u32[]{:S(2)}, u32[]{:S(2)}) %collective-permute-start.12) | collective-permute-done | bytes 524320 | tf_op jit(solution)/shard_map/ppermute | solution.py:504
  71.4 1.5 %collective-permute-start.15 = (bf16[256,1024]{1,0:T(8,128)(2,1)S(1)}, bf16[256,1024]{1,0:T(8,128)(2,1)S(1)}, u32[]{:S(2)}, u32[]{:S(2)}) collective-permute-start(bf16[256,1024]{1,0:T(8,128)(2,1)S(1)} %get-tuple-element.45.refs_12_.refs_13_), channel_id=1, source_target_pairs={{0,2},{1,3},{2,0},{3,1},{4,6},{5,7},{6,4},{7,5},{8,10},{9,11},{10,... | collective-permute-start | bytes 1572872 | tf_op jit(solution)/shard_map/ppermute | solution.py:538
  73.0 4.1 %contract.6.refs_18_ = f32[1536,256]{1,0:T(8,128)S(1)} custom-call(s32[2]{0:T(128)S(1)} %pad_add_fusion.where, s32[4,8]{1,0:T(4,128)S(1)} %get-tuple-element.30.plan, f32[1,3]{1,0:T(1,128)S(1)} %copy-done.6, s32[8,8]{1,0:T(8,128)S(1)} %copy-done.1, f32[8,128]{1,0:T(8,128)S(1)} %get-tuple-element.41.energy, bf16[272,1024]{1,0:T(8,128)(2,1)S(1)} %get-tuple-element.39.refs_0_, ...), custom_call_target="tpu_custom_call" | custom-call | flops 1610612736 | bytes 786432 | tf_op jit(solution)/shard_map/contract/pallas_call | solution.py:428
  77.1 8.7 %contract.5.refs_17_ = f32[4,128,128]{2,1,0:T(8,128)S(1)} custom-call(s32[2]{0:T(128)S(1)} %pad_add_fusion.where, s32[4,8]{1,0:T(4,128)S(1)} %get-tuple-element.30.plan, f32[1,3]{1,0:T(1,128)S(1)} %copy-done.6, s32[8,8]{1,0:T(8,128)S(1)} %copy-done.1, f32[8,128]{1,0:T(8,128)S(1)} %get-tuple-element.38.energy, ...), custom_call_target="tpu_custom_call" | custom-call | flops 3221225472 | bytes 1572864 | tf_op jit(solution)/shard_map/contract/pallas_call | solution.py:428
  86.2 1.6 %collective-permute-done.17.refs_15_ = bf16[256,1024]{1,0:T(8,128)(2,1)S(1)} collective-permute-done((bf16[256,1024]{1,0:T(8,128)(2,1)S(1)}, bf16[256,1024]{1,0:T(8,128)(2,1)S(1)}, u32[]{:S(2)}, u32[]{:S(2)}) %collective-permute-start.17) | collective-permute-done | bytes 524320 | tf_op jit(solution)/shard_map/ppermute | solution.py:539
  87.8 5.0 %contract.7 = (f32[5,64,128]{2,1,0:T(8,128)S(1)}, f32[5,64,128]{2,1,0:T(8,128)S(1)}) custom-call(s32[2]{0:T(128)S(1)} %pad_add_fusion.where, s32[4,8]{1,0:T(4,128)S(1)} %get-tuple-element.30.plan, f32[1,3]{1,0:T(1,128)S(1)} %copy-done.6, s32[8,8]{1,0:T(8,128)S(1)} %copy-done.1, f32[8,128]{1,0:T(8,128)S(1)} %get-tuple-element.41.energy, ...), custom_call_target="tpu_custom_call" | custom-call | tf_op jit(solution)/shard_map/contract/pallas_call | solution.py:428
  92.8 1.1 collective-permute-start.18
  93.9 5.4 %collective-permute-done.18 = f32[5,64,128]{2,1,0:T(8,128)S(1)} collective-permute-done((f32[5,64,128]{2,1,0:T(8,128)S(1)}, f32[5,64,128]{2,1,0:T(8,128)S(1)}, u32[]{:S(2)}, u32[]{:S(2)}) %collective-permute-start.18) | collective-permute-done | bytes 163872 | tf_op jit(solution)/shard_map/ppermute | solution.py:545
  99.5 1.3 %collective-permute-done.19.came = f32[6,32,128]{2,1,0:T(8,128)S(1)} collective-permute-done((f32[6,32,128]{2,1,0:T(8,128)S(1)}, f32[6,32,128]{2,1,0:T(8,128)S(1)}, u32[]{:S(2)}, u32[]{:S(2)}) %collective-permute-start.19) | collective-permute-done | bytes 98336 | tf_op jit(solution)/shard_map/ppermute | solution.py:549
  101.4 14.2 %all_to_all.5.came = f32[8,2,32,128]{3,2,1,0:T(8,128)S(1)} all-to-all(f32[8,2,32,128]{3,2,1,0:T(8,128)S(1)} %spread.1), channel_id=1, replica_groups=mesh['frag'=8,'aux'=4] {'frag'}, dimensions={0} | all-to-all | bytes 524288 | tf_op jit(solution)/shard_map/all_to_all | solution.py:551
  115.6 1.3 %collect.1 = f32[4,32,128]{2,1,0:T(8,128)} custom-call(s32[8,2]{1,0:T(8,128)S(1)} %get-tuple-element.29.target, f32[8,2,32,128]{3,2,1,0:T(8,128)S(1)} %all_to_all.5.came), custom_call_target="tpu_custom_call" | custom-call | tf_op jit(solution)/shard_map/collect/pallas_call | solution.py:478
  (50 shorter events, 10.0 us)
Async XLA Ops:
  0.1 1.2 %copy-start = (bf16[4,128,1024]{2,1,0:T(8,128)(2,1)S(1)}, bf16[4,128,1024]{2,1,0:T(8,128)(2,1)}, u32[]{:S(2)}) copy-start(bf16[4,128,1024]{2,1,0:T(8,128)(2,1)} %table.1) | copy-start | bytes 3145732
  5.6 16.6 %collective-permute-start = (bf16[272,1024]{1,0:T(8,128)(2,1)S(1)}, bf16[272,1024]{1,0:T(8,128)(2,1)S(1)}, u32[]{:S(2)}, u32[]{:S(2)}) collective-permute-start(bf16[272,1024]{1,0:T(8,128)(2,1)S(1)} %get-tuple-element.27), channel_id=1, source_target_pairs={{0,8},{4,12},{16,24},{20,28},{8,0},{12,4},{24,16},{28,20},{1,9},{5... | collective-permute-start | bytes 1671176 | tf_op jit(solution)/shard_map/ppermute | solution.py:515
  8.7 25.0 %collective-permute-start.1 = (bf16[272,1024]{1,0:T(8,128)(2,1)S(1)}, bf16[272,1024]{1,0:T(8,128)(2,1)S(1)}, u32[]{:S(2)}, u32[]{:S(2)}) collective-permute-start(bf16[272,1024]{1,0:T(8,128)(2,1)S(1)} %get-tuple-element.31), channel_id=1, source_target_pairs={{0,4},{8,12},{16,20},{24,28},{4,0},{12,8},{20,16},{28,24},{1,5},{9... | collective-permute-start | bytes 1671176 | tf_op jit(solution)/shard_map/ppermute | solution.py:515
  10.2 23.5 %collective-permute-start.2 = (bf16[272,1024]{1,0:T(8,128)(2,1)S(1)}, bf16[272,1024]{1,0:T(8,128)(2,1)S(1)}, u32[]{:S(2)}, u32[]{:S(2)}) collective-permute-start(bf16[272,1024]{1,0:T(8,128)(2,1)S(1)} %get-tuple-element.32), channel_id=1, source_target_pairs={{4,8},{12,16},{20,24},{8,4},{16,12},{24,20},{5,9},{13,17},{21,25},... | collective-permute-start | bytes 1671176 | tf_op jit(solution)/shard_map/ppermute | solution.py:515
  10.9 22.9 %collective-permute-start.3 = (bf16[272,1024]{1,0:T(8,128)(2,1)S(1)}, bf16[272,1024]{1,0:T(8,128)(2,1)S(1)}, u32[]{:S(2)}, u32[]{:S(2)}) collective-permute-start(bf16[272,1024]{1,0:T(8,128)(2,1)S(1)} %get-tuple-element.33), channel_id=1, source_target_pairs={{8,16},{12,20},{16,8},{20,12},{9,17},{13,21},{17,9},{21,13},{10,18... | collective-permute-start | bytes 1671176 | tf_op jit(solution)/shard_map/ppermute | solution.py:515
  11.6 32.0 %collective-permute-start.7 = (bf16[272,1024]{1,0:T(8,128)(2,1)S(1)}, bf16[272,1024]{1,0:T(8,128)(2,1)S(1)}, u32[]{:S(2)}, u32[]{:S(2)}) collective-permute-start(bf16[272,1024]{1,0:T(8,128)(2,1)S(1)} %get-tuple-element.39.refs_0_), channel_id=1, source_target_pairs={{0,2},{1,3},{2,0},{3,1},{4,6},{5,7},{6,4},{7,5},{8,10},{9,11},{10,... | collective-permute-start | bytes 1671176 | tf_op jit(solution)/shard_map/ppermute | solution.py:504
  33.7 21.1 %collective-permute-start.4 = (bf16[272,1024]{1,0:T(8,128)(2,1)S(1)}, bf16[272,1024]{1,0:T(8,128)(2,1)S(1)}, u32[]{:S(2)}, u32[]{:S(2)}) collective-permute-start(bf16[272,1024]{1,0:T(8,128)(2,1)S(1)} %get-tuple-element.35), channel_id=1, source_target_pairs={{0,12},{4,16},{8,20},{12,0},{16,4},{20,8},{1,13},{5,17},{9,21},{13... | collective-permute-start | bytes 1671176 | tf_op jit(solution)/shard_map/ppermute | solution.py:515
  42.0 15.7 %copy-start.1 = (s32[8,8]{1,0:T(8,128)S(1)}, s32[8,8]{1,0:T(8,128)}, u32[]{:S(2)}) copy-start(s32[8,8]{1,0:T(8,128)} %rows_ref.7) | copy-start | bytes 772
  42.0 15.7 %copy-start.6 = (f32[1,3]{1,0:T(1,128)S(1)}, f32[1,3]{1,0:T(1,128)}, u32[]{:S(2)}) copy-start(f32[1,3]{1,0:T(1,128)} %levels.7) | copy-start | bytes 40
  42.0 12.0 %collective-permute-start.5 = (bf16[256,1024]{1,0:T(8,128)(2,1)S(1)}, bf16[256,1024]{1,0:T(8,128)(2,1)S(1)}, u32[]{:S(2)}, u32[]{:S(2)}) collective-permute-start(bf16[256,1024]{1,0:T(8,128)(2,1)S(1)} %pack_group.3.refs_4_), channel_id=1, source_target_pairs={{0,2},{1,3},{2,0},{3,1},{4,6},{5,7},{6,4},{7,5},{8,10},{9,11},{10,... | collective-permute-start | bytes 1572872 | tf_op jit(solution)/shard_map/ppermute | solution.py:504
  43.6 12.5 %collective-permute-start.8 = (bf16[272,1024]{1,0:T(8,128)(2,1)S(1)}, bf16[272,1024]{1,0:T(8,128)(2,1)S(1)}, u32[]{:S(2)}, u32[]{:S(2)}) collective-permute-start(bf16[272,1024]{1,0:T(8,128)(2,1)S(1)} %get-tuple-element.39.refs_0_), channel_id=1, source_target_pairs={{0,1},{1,0},{2,3},{3,2},{4,5},{5,4},{6,7},{7,6},{8,9},{9,8},{10,11... | collective-permute-start | bytes 1671176 | tf_op jit(solution)/shard_map/ppermute | solution.py:505
  43.6 14.1 %collective-permute-start.9 = (bf16[272,1024]{1,0:T(8,128)(2,1)S(1)}, bf16[272,1024]{1,0:T(8,128)(2,1)S(1)}, u32[]{:S(2)}, u32[]{:S(2)}) collective-permute-start(bf16[272,1024]{1,0:T(8,128)(2,1)S(1)} %collective-permute-done.7.refs_1_), channel_id=1, source_target_pairs={{0,1},{1,0},{2,3},{3,2},{4,5},{5,4},{6,7},{7,6},{8,9},{9,8},{10,11... | collective-permute-start | bytes 1671176 | tf_op jit(solution)/shard_map/ppermute | solution.py:507
  54.0 10.6 %collective-permute-start.6 = (bf16[272,1024]{1,0:T(8,128)(2,1)S(1)}, bf16[272,1024]{1,0:T(8,128)(2,1)S(1)}, u32[]{:S(2)}, u32[]{:S(2)}) collective-permute-start(bf16[272,1024]{1,0:T(8,128)(2,1)S(1)} %get-tuple-element.37), channel_id=1, source_target_pairs={{12,24},{16,28},{24,12},{28,16},{13,25},{17,29},{25,13},{29,17},{1... | collective-permute-start | bytes 1671176 | tf_op jit(solution)/shard_map/ppermute | solution.py:515
  54.7 2.9 %collective-permute-start.10 = (bf16[256,1024]{1,0:T(8,128)(2,1)S(1)}, bf16[256,1024]{1,0:T(8,128)(2,1)S(1)}, u32[]{:S(2)}, u32[]{:S(2)}) collective-permute-start(bf16[256,1024]{1,0:T(8,128)(2,1)S(1)} %pack_group.3.refs_4_), channel_id=1, source_target_pairs={{0,1},{1,0},{2,3},{3,2},{4,5},{5,4},{6,7},{7,6},{8,9},{9,8},{10,11... | collective-permute-start | bytes 1572872 | tf_op jit(solution)/shard_map/ppermute | solution.py:505
  54.8 2.9 %collective-permute-start.11 = (bf16[256,1024]{1,0:T(8,128)(2,1)S(1)}, bf16[256,1024]{1,0:T(8,128)(2,1)S(1)}, u32[]{:S(2)}, u32[]{:S(2)}) collective-permute-start(bf16[256,1024]{1,0:T(8,128)(2,1)S(1)} %collective-permute-done.5.refs_5_), channel_id=1, source_target_pairs={{0,1},{1,0},{2,3},{3,2},{4,5},{5,4},{6,7},{7,6},{8,9},{9,8},{10,11... | collective-permute-start | bytes 1572872 | tf_op jit(solution)/shard_map/ppermute | solution.py:507
  56.1 14.0 %collective-permute-start.12 = (bf16[256,1024]{1,0:T(8,128)(2,1)S(1)}, bf16[256,1024]{1,0:T(8,128)(2,1)S(1)}, u32[]{:S(2)}, u32[]{:S(2)}) collective-permute-start(bf16[256,1024]{1,0:T(8,128)(2,1)S(1)} %get-tuple-element.42.refs_8_), channel_id=1, source_target_pairs={{0,2},{1,3},{2,0},{3,1},{4,6},{5,7},{6,4},{7,5},{8,10},{9,11},{10,... | collective-permute-start | bytes 1572872 | tf_op jit(solution)/shard_map/ppermute | solution.py:504
  57.7 15.3 %collective-permute-start.13 = (bf16[256,1024]{1,0:T(8,128)(2,1)S(1)}, bf16[256,1024]{1,0:T(8,128)(2,1)S(1)}, u32[]{:S(2)}, u32[]{:S(2)}) collective-permute-start(bf16[256,1024]{1,0:T(8,128)(2,1)S(1)} %get-tuple-element.42.refs_8_), channel_id=1, source_target_pairs={{0,1},{1,0},{2,3},{3,2},{4,5},{5,4},{6,7},{7,6},{8,9},{9,8},{10,11... | collective-permute-start | bytes 1572872 | tf_op jit(solution)/shard_map/ppermute | solution.py:505
  57.7 12.4 %copy-start.4 = (bf16[4,128]{1,0:T(4,128)(2,1)S(1)}, bf16[4,128]{1,0:T(4,128)(2,1)}, u32[]{:S(2)}) copy-start(bf16[4,128]{1,0:T(4,128)(2,1)} %refs_0_.3) | copy-start | bytes 3076
  70.1 2.9 %collective-permute-start.14 = (bf16[256,1024]{1,0:T(8,128)(2,1)S(1)}, bf16[256,1024]{1,0:T(8,128)(2,1)S(1)}, u32[]{:S(2)}, u32[]{:S(2)}) collective-permute-start(bf16[256,1024]{1,0:T(8,128)(2,1)S(1)} %collective-permute-done.12.refs_9_), channel_id=1, source_target_pairs={{0,1},{1,0},{2,3},{3,2},{4,5},{5,4},{6,7},{7,6},{8,9},{9,8},{10,11... | collective-permute-start | bytes 1572872 | tf_op jit(solution)/shard_map/ppermute | solution.py:507
  70.9 2.1 %collective-permute-start.16 = (bf16[256,1024]{1,0:T(8,128)(2,1)S(1)}, bf16[256,1024]{1,0:T(8,128)(2,1)S(1)}, u32[]{:S(2)}, u32[]{:S(2)}) collective-permute-start(bf16[256,1024]{1,0:T(8,128)(2,1)S(1)} %get-tuple-element.45.refs_12_.refs_13_), channel_id=1, source_target_pairs={{0,1},{1,0},{2,3},{3,2},{4,5},{5,4},{6,7},{7,6},{8,9},{9,8},{10,11... | collective-permute-start | bytes 1572872 | tf_op jit(solution)/shard_map/ppermute | solution.py:536
  71.4 14.3 %collective-permute-start.15 = (bf16[256,1024]{1,0:T(8,128)(2,1)S(1)}, bf16[256,1024]{1,0:T(8,128)(2,1)S(1)}, u32[]{:S(2)}, u32[]{:S(2)}) collective-permute-start(bf16[256,1024]{1,0:T(8,128)(2,1)S(1)} %get-tuple-element.45.refs_12_.refs_13_), channel_id=1, source_target_pairs={{0,2},{1,3},{2,0},{3,1},{4,6},{5,7},{6,4},{7,5},{8,10},{9,11},{10,... | collective-permute-start | bytes 1572872 | tf_op jit(solution)/shard_map/ppermute | solution.py:538
  85.8 2.0 %collective-permute-start.17 = (bf16[256,1024]{1,0:T(8,128)(2,1)S(1)}, bf16[256,1024]{1,0:T(8,128)(2,1)S(1)}, u32[]{:S(2)}, u32[]{:S(2)}) collective-permute-start(bf16[256,1024]{1,0:T(8,128)(2,1)S(1)} %collective-permute-done.15.refs_13_), channel_id=1, source_target_pairs={{0,1},{1,0},{2,3},{3,2},{4,5},{5,4},{6,7},{7,6},{8,9},{9,8},{10,11... | collective-permute-start | bytes 1572872 | tf_op jit(solution)/shard_map/ppermute | solution.py:539
  92.8 6.5 %collective-permute-start.18 = (f32[5,64,128]{2,1,0:T(8,128)S(1)}, f32[5,64,128]{2,1,0:T(8,128)S(1)}, u32[]{:S(2)}, u32[]{:S(2)}) collective-permute-start(f32[5,64,128]{2,1,0:T(8,128)S(1)} %get-tuple-element.48), channel_id=1, source_target_pairs={{0,2},{1,3},{2,0},{3,1},{4,6},{5,7},{6,4},{7,5},{8,10},{9,11},{10,... | collective-permute-start | bytes 491528 | tf_op jit(solution)/shard_map/ppermute | solution.py:545
  99.4 1.4 %collective-permute-start.19 = (f32[6,32,128]{2,1,0:T(8,128)S(1)}, f32[6,32,128]{2,1,0:T(8,128)S(1)}, u32[]{:S(2)}, u32[]{:S(2)}) collective-permute-start(f32[6,32,128]{2,1,0:T(8,128)S(1)} %get-tuple-element.49), channel_id=1, source_target_pairs={{0,1},{1,0},{2,3},{3,2},{4,5},{5,4},{6,7},{7,6},{8,9},{9,8},{10,11... | collective-permute-start | bytes 294920 | tf_op jit(solution)/shard_map/ppermute | solution.py:549
  (4 other events, 2.7 us)

commit v8 on v7

--- a/solution.py
+++ b/solution.py
@@ -23,26 +23,39 @@
     return up + [(b, a) for a, b in up]
 
 
-def pick(map_ref, list_ref, list_len, own_count, fragment, owner):
-    count = jnp.int32(0)
-    picked = [jnp.int32(0)] * CAP
-    for k in range(list_len):
-        row = map_ref[list_ref[fragment, k]]
-        hit = row // own_count == owner
-        for r in range(CAP):
-            picked[r] = jnp.where(hit & (count == r), row % own_count, picked[r])
-        count = count + hit.astype(jnp.int32)
-    return picked, count
-
-
-def send_kernel(frags, own_count, list_len, where, map_ref, list_ref, energy, occ, table, *refs):
+class Lists:
+    def __init__(self, ref, frags, own_count, list_len):
+        self.ref, self.frags, self.own_count, self.list_len = ref, frags, own_count, list_len
+        self.listed = 2 + frags * own_count
+        self.me, self.aux = ref[0], ref[1]
+
+    def row(self, fragment, k):
+        return self.ref[2 + self.ref[self.listed + fragment * self.list_len + k]]
+
+    def live(self, fragment, k):
+        return self.ref[self.listed + (self.frags + fragment) * self.list_len + k]
+
+    def pick(self, fragment, owner):
+        count = jnp.int32(0)
+        picked = [jnp.int32(0)] * CAP
+        for k in range(self.list_len):
+            row = self.row(fragment, k)
+            hit = row // self.own_count == owner
+            for r in range(CAP):
+                picked[r] = jnp.where(hit & (count == r), row % self.own_count, picked[r])
+            count = count + hit.astype(jnp.int32)
+        return picked, count
+
+
+def send_kernel(sizes, ints, tails, table, *refs):
     outs, own, sems = refs[:6], refs[6], refs[7]
-    me = where[0]
+    lists = Lists(ints, *sizes)
+    me, frags = lists.me, lists.frags
     block = table.shape[1]
     copies = []
 
     def start(out, index, fragment, inside):
-        picked, count = pick(map_ref, list_ref, list_len, own_count, fragment, me)
+        picked, count = lists.pick(fragment, me)
         for r in range(CAP):
             copy = pltpu.make_async_copy(
                 table.at[picked[r]], out.at[pl.ds(r * block, block)], sems.at[index, r]
@@ -57,36 +70,34 @@
         inside = (partner >= 0) & (partner < frags)
         start(outs[index], index, jnp.clip(partner, 0, frags - 1), inside)
     start(own, 6, me, me >= 0)
-    for out in outs + (own,):
-        out[pl.ds(CAP * block, TAIL), :] = jnp.zeros((TAIL, out.shape[1]), out.dtype)
+    own[pl.ds(CAP * block, TAIL), :] = tails[pl.ds(0, TAIL), :]
     for out in outs:
-        out[pl.ds(CAP * block, own_count), pl.ds(0, block)] = energy[...]
-    own[pl.ds(CAP * block, occ.shape[0]), :] = occ[...]
+        out[pl.ds(CAP * block, TAIL), :] = tails[pl.ds(TAIL, TAIL), :]
     for needed, copy in copies:
         pl.when(needed)(copy.wait)
 
 
-def pack_to_send(where, owner_map, vir_list, energy, occ, table, frags):
-    own_count, block_rows, cols = table.shape
-    list_len = vir_list.shape[1]
+def pack_to_send(ints, tails, table, sizes):
+    _, block_rows, cols = table.shape
     part = jax.ShapeDtypeStruct((CAP * block_rows + TAIL, cols), table.dtype)
     return pl.pallas_call(
-        functools.partial(send_kernel, frags, own_count, list_len),
+        functools.partial(send_kernel, sizes),
         out_shape=(part,) * 7,
-        in_specs=[SMEM, SMEM, SMEM, VMEM, VMEM, ANY],
+        in_specs=[SMEM, VMEM, ANY],
         out_specs=(VMEM,) * 7,
         scratch_shapes=[pltpu.SemaphoreType.DMA((7, CAP))],
         compiler_params=pltpu.CompilerParams(vmem_limit_bytes=8 * MIB),
         cost_estimate=NO_COST,
         name="pack_to_send",
-    )(where, owner_map, vir_list, energy, occ, table)
-
-
-def plan_kernel(frags, own_count, list_len, where, map_ref, list_ref, plan, target):
-    me = where[0]
+    )(ints, tails, table)
+
+
+def plan_kernel(sizes, ints, plan, target):
+    lists = Lists(ints, *sizes)
+    me, (frags, own_count, list_len) = lists.me, sizes
     rows, owners, codes, classes = [], [], [], []
     for k in range(list_len):
-        row = map_ref[list_ref[me, k]]
+        row = lists.row(me, k)
         owner = row // own_count
         low = jnp.minimum(me, owner)
         far = jnp.abs(owner - me)
@@ -111,10 +122,10 @@
         plan[0, place] = codes[k]
         plan[1, place] = rank
         plan[2, place] = rows[k]
-        plan[3, place] = jnp.int32(k)
+        plan[3, place] = lists.live(me, k)
 
     def one(fragment, carry):
-        picked, _ = pick(map_ref, list_ref, list_len, own_count, fragment, me)
+        picked, _ = lists.pick(fragment, me)
         for r in range(CAP):
             target[fragment, r] = picked[r]
         return carry
@@ -122,20 +133,20 @@
     lax.fori_loop(0, frags, one, 0)
 
 
-def plan_lists(where, owner_map, vir_list, own_count, frags):
-    list_len = vir_list.shape[1]
+def plan_lists(ints, sizes):
+    frags, _, list_len = sizes
     return pl.pallas_call(
-        functools.partial(plan_kernel, frags, own_count, list_len),
+        functools.partial(plan_kernel, sizes),
         out_shape=(
             jax.ShapeDtypeStruct((4, list_len), jnp.int32),
             jax.ShapeDtypeStruct((frags, CAP), jnp.int32),
         ),
-        in_specs=[SMEM, SMEM, SMEM],
+        in_specs=[SMEM],
         out_specs=(SMEM, SMEM),
         compiler_params=pltpu.CompilerParams(vmem_limit_bytes=4 * MIB),
         cost_estimate=NO_COST,
         name="plan_lists",
-    )(where, owner_map, vir_list)
+    )(ints)
 
 
 def pack_kernel(first, codes, block, with_energy, plan, *refs):
@@ -217,7 +228,7 @@
     return aux + 4 * b
 
 
-def contract_kernel(stage, block, width, where, plan, levels, rows_ref, energy, *refs):
+def contract_kernel(stage, block, width, where, plan, levels, energy, *refs):
     groups = min(stage + 2, 4)
     parts, rest = refs[: groups * 4], refs[groups * 4 :]
     quarters = {2: (0, 2), 3: (1, 3)}.get(stage, (0, 1, 2, 3))
@@ -232,7 +243,7 @@
         out, left, grid, occ, scaled, total, amps, tall, left_sems, grid_sems, occ_sems = rest
     else:
         out, left, grid, occ, scaled, total, amps, left_sems, grid_sems, occ_sems = rest
-    me, aux = where[0], where[1]
+    aux = where[1]
     places = (place_of(aux, 0), place_of(aux, 1))
 
     def occ_copy(quarter):
@@ -323,11 +334,11 @@
         for b in range(row_count):
             own_row = energy[pl.ds(places[b], 1), :]
             own_energy = jnp.transpose(jnp.broadcast_to(own_row, (block, block)))
-            own_live = sub < rows_ref[me, plan[3, places[b]]]
+            own_live = sub < plan[3, places[b]]
             for q in range(2 * len(group_list)):
                 place = 2 * group_list[q // 2] + q % 2
                 their_energy = energy[place : place + 1, :]
-                live = own_live & (lane < rows_ref[me, plan[3, place]])
+                live = own_live & (lane < plan[3, place])
                 for p, (i, j) in enumerate(PAIRS):
                     gap = (levels[0, i] + levels[0, j]) - own_energy - their_energy
                     rows = pl.ds((p * row_count + b) * block, block)
@@ -384,7 +395,7 @@
         sent[...] = dens[:, pl.ds(pl.multiple_of((1 - side) * half, half), half), :]
 
 
-def contract(stage, where, plan, levels, vir_rows, energy, parts, before=()):
+def contract(stage, where, plan, levels, energy, parts, before=()):
     block, width = energy.shape[1], parts[0].shape[1]
     height = len(PAIRS) * 2 * block
     span = (4, 2, 2, 2)[stage] * block
@@ -428,13 +439,13 @@
     return pl.pallas_call(
         functools.partial(contract_kernel, stage, block, width),
         out_shape=out_shape,
-        in_specs=[SMEM] * 4 + [VMEM] + [ANY] * len(parts) + [VMEM] * len(before),
+        in_specs=[SMEM] * 3 + [VMEM] + [ANY] * len(parts) + [VMEM] * len(before),
         out_specs=out_specs,
         scratch_shapes=scratch,
         compiler_params=pltpu.CompilerParams(vmem_limit_bytes=26 * MIB),
         cost_estimate=cost,
         name="contract",
-    )(where, plan, levels, vir_rows, energy, *parts, *before)
+    )(where, plan, levels, energy, *parts, *before)
 
 
 def spread_kernel(own_count, where, plan, kept, came, out):
@@ -452,7 +463,7 @@
         put(4 + q, kept[2 + q] + came[2 + q])
 
 
-def spread(where, plan, kept, came, frags, own_count):
+def spread(ints, plan, kept, came, frags, own_count):
     return pl.pallas_call(
         functools.partial(spread_kernel, own_count),
         out_shape=jax.ShapeDtypeStruct((frags, CAP) + kept.shape[1:], kept.dtype),
@@ -460,7 +471,7 @@
         out_specs=VMEM,
         compiler_params=pltpu.CompilerParams(vmem_limit_bytes=4 * MIB),
         name="spread",
-    )(where, plan, kept, came)
+    )(ints, plan, kept, came)
 
 
 def collect_kernel(target, came, out):
@@ -492,13 +503,19 @@
     aux = lax.axis_index("aux").astype(jnp.int32)
     own_count, block, width = vir_grid.shape
     list_len = vir_list.shape[1]
-    where = jnp.stack([me, aux])
+    sizes = (frags, own_count, list_len)
+    ints = jnp.concatenate(
+        [me[None], aux[None], owner_map, vir_list.reshape(-1), vir_rows.reshape(-1)]
+    )
+    occ_count = occ_grid.shape[1]
+    tails = jnp.concatenate([
+        jnp.pad(occ_grid[0], ((0, TAIL - occ_count), (0, 0))),
+        jnp.pad(vir_energy, ((0, TAIL - own_count), (0, width - block))),
+    ])
     far_pairs = [(i, i ^ 2) for i in range(aux_count)]
     near_pairs = [(i, i ^ 1) for i in range(aux_count)]
 
-    *outgoing, own = pack_to_send(
-        where, owner_map, vir_list, vir_energy, occ_grid[0], vir_grid, frags
-    )
+    *outgoing, own = pack_to_send(ints, tails, vir_grid, sizes)
 
     def over_aux(here, *others):
         far = lax.ppermute(here, "aux", far_pairs)
@@ -517,27 +534,24 @@
     arrived = {code: send(code - 1) for code in (1, 2, 3, 4)}
     parts = over_aux(own)
     arrived[5] = send(4, *(arrived[c] for c in (1, 2, 3, 4)))
-    plan, target = plan_lists(
-        after(where, arrived[3]), owner_map, vir_list, own_count, frags
-    )
+    plan, target = plan_lists(after(ints, arrived[3]), sizes)
     here = pack_group(2, block, plan, {c: arrived[c] for c in range(1, 5)})[0]
     parts += over_aux(here)
     arrived[6] = send(5, parts[5])
     here, early_energy = pack_group(
         4, block, plan, {c: arrived[c] for c in range(1, 6)}, vir_energy
     )
-    shared = (where, plan, occ_energy, vir_rows)
+    shared = (ints, plan, occ_energy)
     first = contract(0, *shared, early_energy, parts[:8])
-    parts += over_aux(here, first)
     arrived[6] = after(arrived[6], first)
-    here, energy = pack_group(6, block, plan, arrived, vir_energy)
-    here = after(here, parts[9])
+    last, energy = pack_group(6, block, plan, arrived, vir_energy)
+    near = lax.ppermute(last, "aux", near_pairs)
+    far = lax.ppermute(last, "aux", far_pairs)
+    parts += over_aux(here, near)
     second = contract(1, *shared, early_energy, parts[:12])
-    near = lax.ppermute(here, "aux", near_pairs)
-    partial = contract(2, *shared, energy, parts + [here, here, near, near])
-    far = lax.ppermute(here, "aux", far_pairs)
+    partial = contract(2, *shared, energy, parts + [last, last, near, near])
     far_near = lax.ppermute(after(far, second, partial), "aux", near_pairs)
-    parts += [here, far, near, far_near]
+    parts += [last, far, near, far_near]
     sent, stay = contract(3, *shared, energy, parts, (first, second, partial))
 
     quarter = block // aux_count
@@ -547,7 +561,7 @@
     sent = lax.dynamic_slice_in_dim(both, (1 - core) * quarter, quarter, 1)
     kept = lax.dynamic_slice_in_dim(both, core * quarter, quarter, 1)
     came = lax.ppermute(sent, "aux", near_pairs)
-    outgoing = spread(where, plan, kept, came, frags, own_count)
+    outgoing = spread(ints, plan, kept, came, frags, own_count)
     incoming = lax.all_to_all(outgoing, "frag", 0, 0, tiled=True)
     return collect(target, incoming, own_count)
 

time: 117 us -> 116 us (level)
    unnamed x16 -> x6, local copies, waits for them, and re-layouts: 3.96 us -> 1.24 us
    reshape x0 -> x2, local copies, waits for them, and re-layouts: none -> 1.53 us  [the longest x1 0.77 us: body(): vir_rows.reshape(-1)]
    ppermute x3, waiting for transfers between devices: 15.3 us -> 14 us  [over_aux(): far = lax.ppermute(here, 'aux', far_pairs)]
  transfers between devices with their start and end apart: 20 -> 20, of which waited for: 7 -> 8; matrix products, arithmetic and copies ran while one was open for 0% -> 0% of each run, Pallas kernels for 21% -> 21%
where the time goes in v8:
time: 116 us
  waiting for transfers between devices  40.9 us (35%)
  Pallas kernels  32.4 us (28%)
  starting transfers between devices  23.7 us (20%)
  blocking collectives  14.2 us (12%)
  local copies, waits for them, and re-layouts  3.53 us (3%)
    pallas_call x4, Pallas kernels, contract(): pl.pallas_call(functools.partial(contract_kernel, stage, block, width), o...  24.5 us
    ppermute x6, waiting for transfers between devices, send(): return lax.ppermute(payload, 'frag', round_pairs(distance, parity, frags))  18.4 us
    ppermute x6, starting transfers between devices, send(): return lax.ppermute(payload, 'frag', round_pairs(distance, parity, frags))  14.2 us
    all_to_all x1, blocking collectives, body(): incoming = lax.all_to_all(outgoing, 'frag', 0, 0, tiled=True)  14.2 us
    ppermute x3, waiting for transfers between devices, over_aux(): far = lax.ppermute(here, 'aux', far_pairs)  14 us
    ppermute x1, waiting for transfers between devices, body(): met = lax.ppermute(sent, 'aux', far_pairs)  5.03 us
    ppermute x3, starting transfers between devices, over_aux(): far = lax.ppermute(here, 'aux', far_pairs)  4.75 us
  transfers between devices with their start and end apart: 20, of which 8 were waited for; matrix products, arithmetic and copies ran while one was open for 0% of the time, Pallas kernels for 21%

profile of v8, /device:TPU:0, one launch (start us, length us, event | category | flops | bytes accessed | tf_op | source)
XLA Modules:
  0.0 115.7 jit_solution(7071143192792500598)
XLA Ops:
  3.0 1.2 %copy-done = bf16[4,128,1024]{2,1,0:T(8,128)(2,1)S(1)} copy-done((bf16[4,128,1024]{2,1,0:T(8,128)(2,1)S(1)}, bf16[4,128,1024]{2,1,0:T(8,128)(2,1)}, u32[]{:S(2)}) %copy-start) | copy-done | bytes 1048600
  4.2 1.5 %pack_to_send.1 = (bf16[272,1024]{1,0:T(8,128)(2,1)S(1)}, bf16[272,1024]{1,0:T(8,128)(2,1)S(1)}, bf16[272,1024]{1,0:T(8,128)(2,1)S(1)}, bf16[272,1024]{1,0:T(8,1...) custom-call(s32[162]{0:T(256)S(1)} %concatenate.9.ints.where, ...), custom_call_target="tpu_custom_call" | custom-call | tf_op jit(solution)/shard_map/pack_to_send/pallas_call | solution.py:83
  5.7 3.1 %collective-permute-start = (bf16[272,1024]{1,0:T(8,128)(2,1)S(1)}, bf16[272,1024]{1,0:T(8,128)(2,1)S(1)}, u32[]{:S(2)}, u32[]{:S(2)}) collective-permute-start(bf16[272,1024]{1,0:T(8,128)(2,1)S(1)} %get-tuple-element.26), channel_id=1, source_target_pairs={{0,8},{4,12},{16,24},{20,28},{8,0},{12,4},{24,16},{28,20},{1,9},{5... | collective-permute-start | bytes 1671176 | tf_op jit(solution)/shard_map/ppermute | solution.py:532
  8.8 1.5 %collective-permute-start.1 = (bf16[272,1024]{1,0:T(8,128)(2,1)S(1)}, bf16[272,1024]{1,0:T(8,128)(2,1)S(1)}, u32[]{:S(2)}, u32[]{:S(2)}) collective-permute-start(bf16[272,1024]{1,0:T(8,128)(2,1)S(1)} %get-tuple-element.30), channel_id=1, source_target_pairs={{0,4},{8,12},{16,20},{24,28},{4,0},{12,8},{20,16},{28,24},{1,5},{9... | collective-permute-start | bytes 1671176 | tf_op jit(solution)/shard_map/ppermute | solution.py:532
  11.7 1.6 %collective-permute-start.7 = (bf16[272,1024]{1,0:T(8,128)(2,1)S(1)}, bf16[272,1024]{1,0:T(8,128)(2,1)S(1)}, u32[]{:S(2)}, u32[]{:S(2)}) collective-permute-start(bf16[272,1024]{1,0:T(8,128)(2,1)S(1)} %get-tuple-element.38.refs_0_), channel_id=1, source_target_pairs={{0,2},{1,3},{2,0},{3,1},{4,6},{5,7},{6,4},{7,5},{8,10},{9,11},{10,... | collective-permute-start | bytes 1671176 | tf_op jit(solution)/shard_map/ppermute | solution.py:521
  13.3 9.0 %collective-permute-done.refs_2_.refs_3_ = bf16[272,1024]{1,0:T(8,128)(2,1)S(1)} collective-permute-done((bf16[272,1024]{1,0:T(8,128)(2,1)S(1)}, bf16[272,1024]{1,0:T(8,128)(2,1)S(1)}, u32[]{:S(2)}, u32[]{:S(2)}) %collective-permute-start) | collective-permute-done | bytes 557088 | tf_op jit(solution)/shard_map/ppermute | solution.py:532
  22.3 2.2 %plan_lists.1 = (s32[4,8]{1,0:T(4,128)S(1)}, s32[8,2]{1,0:T(8,128)S(1)}) custom-call(s32[162]{0:T(256)S(1)} %concatenate.9.ints.where), custom_call_target="tpu_custom_call" | custom-call | tf_op jit(solution)/shard_map/plan_lists/pallas_call | solution.py:138
  24.5 9.4 %collective-permute-done.1.refs_0_.refs_1_ = bf16[272,1024]{1,0:T(8,128)(2,1)S(1)} collective-permute-done((bf16[272,1024]{1,0:T(8,128)(2,1)S(1)}, bf16[272,1024]{1,0:T(8,128)(2,1)S(1)}, u32[]{:S(2)}, u32[]{:S(2)}) %collective-permute-start.1) | collective-permute-done | bytes 557088 | tf_op jit(solution)/shard_map/ppermute | solution.py:532
  33.9 7.6 %collective-permute-start.4 = (bf16[272,1024]{1,0:T(8,128)(2,1)S(1)}, bf16[272,1024]{1,0:T(8,128)(2,1)S(1)}, u32[]{:S(2)}, u32[]{:S(2)}) collective-permute-start(bf16[272,1024]{1,0:T(8,128)(2,1)S(1)} %get-tuple-element.34), channel_id=1, source_target_pairs={{0,12},{4,16},{8,20},{12,0},{16,4},{20,8},{1,13},{5,17},{9,21},{13... | collective-permute-start | bytes 1671176 | tf_op jit(solution)/shard_map/ppermute | solution.py:532
  42.2 1.6 %collective-permute-start.5 = (bf16[256,1024]{1,0:T(8,128)(2,1)S(1)}, bf16[256,1024]{1,0:T(8,128)(2,1)S(1)}, u32[]{:S(2)}, u32[]{:S(2)}) collective-permute-start(bf16[256,1024]{1,0:T(8,128)(2,1)S(1)} %pack_group.3.refs_4_), channel_id=1, source_target_pairs={{0,2},{1,3},{2,0},{3,1},{4,6},{5,7},{6,4},{7,5},{8,10},{9,11},{10,... | collective-permute-start | bytes 1572872 | tf_op jit(solution)/shard_map/ppermute | solution.py:521
  44.3 9.9 %collective-permute-done.5.refs_5_ = bf16[256,1024]{1,0:T(8,128)(2,1)S(1)} collective-permute-done((bf16[256,1024]{1,0:T(8,128)(2,1)S(1)}, bf16[256,1024]{1,0:T(8,128)(2,1)S(1)}, u32[]{:S(2)}, u32[]{:S(2)}) %collective-permute-start.5) | collective-permute-done | bytes 524320 | tf_op jit(solution)/shard_map/ppermute | solution.py:521
  56.2 1.6 %collective-permute-start.12 = (bf16[256,1024]{1,0:T(8,128)(2,1)S(1)}, bf16[256,1024]{1,0:T(8,128)(2,1)S(1)}, u32[]{:S(2)}, u32[]{:S(2)}) collective-permute-start(bf16[256,1024]{1,0:T(8,128)(2,1)S(1)} %get-tuple-element.41.refs_8_), channel_id=1, source_target_pairs={{0,2},{1,3},{2,0},{3,1},{4,6},{5,7},{6,4},{7,5},{8,10},{9,11},{10,... | collective-permute-start | bytes 1572872 | tf_op jit(solution)/shard_map/ppermute | solution.py:521
  57.8 6.9 %contract.4.refs_16_ = f32[1,128,128]{2,1,0:T(8,128)S(1)} custom-call(s32[162]{0:T(256)S(1)} %concatenate.9.ints.where, s32[4,8]{1,0:T(4,128)S(1)} %get-tuple-element.29.plan, f32[1,3]{1,0:T(1,128)S(1)} %copy-done.2, f32[8,128]{1,0:T(8,128)S(1)} %get-tuple-element.37.energy, bf16[272,1024]{1,0:T(8,128)(2,1)S(1)} %get-tuple-element.38.refs_0_, ...), custom_call_target="tpu_custom_call" | custom-call | tf_op jit(solution)/shard_map/contract/pallas_call | solution.py:439
  66.1 4.1 %collective-permute-done.12.refs_9_ = bf16[256,1024]{1,0:T(8,128)(2,1)S(1)} collective-permute-done((bf16[256,1024]{1,0:T(8,128)(2,1)S(1)}, bf16[256,1024]{1,0:T(8,128)(2,1)S(1)}, u32[]{:S(2)}, u32[]{:S(2)}) %collective-permute-start.12) | collective-permute-done | bytes 524320 | tf_op jit(solution)/shard_map/ppermute | solution.py:521
  70.2 1.5 %collective-permute-start.16 = (bf16[256,1024]{1,0:T(8,128)(2,1)S(1)}, bf16[256,1024]{1,0:T(8,128)(2,1)S(1)}, u32[]{:S(2)}, u32[]{:S(2)}) collective-permute-start(bf16[256,1024]{1,0:T(8,128)(2,1)S(1)} %get-tuple-element.42.refs_12_.refs_13_), channel_id=1, source_target_pairs={{0,2},{1,3},{2,0},{3,1},{4,6},{5,7},{6,4},{7,5},{8,10},{9,11},{10,... | collective-permute-start | bytes 1572872 | tf_op jit(solution)/shard_map/ppermute | solution.py:549
  72.1 4.0 %contract.6.refs_18_ = f32[1536,256]{1,0:T(8,128)S(1)} custom-call(s32[162]{0:T(256)S(1)} %concatenate.9.ints.where, s32[4,8]{1,0:T(4,128)S(1)} %get-tuple-element.29.plan, f32[1,3]{1,0:T(1,128)S(1)} %copy-done.2, f32[8,128]{1,0:T(8,128)S(1)} %get-tuple-element.40.energy, bf16[272,1024]{1,0:T(8,128)(2,1)S(1)} %get-tuple-element.38.refs_0_, ...), custom_call_target="tpu_custom_call" | custom-call | flops 1610612736 | bytes 786432 | tf_op jit(solution)/shard_map/contract/pallas_call | solution.py:439
  76.1 8.6 %contract.5.refs_17_ = f32[4,128,128]{2,1,0:T(8,128)S(1)} custom-call(s32[162]{0:T(256)S(1)} %concatenate.9.ints.where, s32[4,8]{1,0:T(4,128)S(1)} %get-tuple-element.29.plan, f32[1,3]{1,0:T(1,128)S(1)} %copy-done.2, f32[8,128]{1,0:T(8,128)S(1)} %get-tuple-element.37.energy, bf16[272,1024]{1,0:T(8,128)(2,1)S(1)} %get-tuple-element.38.refs_0_, ...), custom_call_target="tpu_custom_call" | custom-call | flops 3221225472 | bytes 1572864 | tf_op jit(solution)/shard_map/contract/pallas_call | solution.py:439
  85.0 1.8 %collective-permute-done.17.refs_15_ = bf16[256,1024]{1,0:T(8,128)(2,1)S(1)} collective-permute-done((bf16[256,1024]{1,0:T(8,128)(2,1)S(1)}, bf16[256,1024]{1,0:T(8,128)(2,1)S(1)}, u32[]{:S(2)}, u32[]{:S(2)}) %collective-permute-start.17) | collective-permute-done | bytes 524320 | tf_op jit(solution)/shard_map/ppermute | solution.py:553
  86.8 5.0 %contract.7 = (f32[5,64,128]{2,1,0:T(8,128)S(1)}, f32[5,64,128]{2,1,0:T(8,128)S(1)}) custom-call(s32[162]{0:T(256)S(1)} %concatenate.9.ints.where, s32[4,8]{1,0:T(4,128)S(1)} %get-tuple-element.29.plan, f32[1,3]{1,0:T(1,128)S(1)} %copy-done.2, f32[8,128]{1,0:T(8,128)S(1)} %get-tuple-element.40.energy, bf16[272,1024]{1,0:T(8,128)(2,1)S(1)} %get-tuple-element.38.refs_0_, ...), custom_call_target="tpu_custom_call" | custom-call | tf_op jit(solution)/shard_map/contract/pallas_call | solution.py:439
  91.8 1.3 %collective-permute-start.18 = (f32[5,64,128]{2,1,0:T(8,128)S(1)}, f32[5,64,128]{2,1,0:T(8,128)S(1)}, u32[]{:S(2)}, u32[]{:S(2)}) collective-permute-start(f32[5,64,128]{2,1,0:T(8,128)S(1)} %get-tuple-element.46), channel_id=1, source_target_pairs={{0,2},{1,3},{2,0},{3,1},{4,6},{5,7},{6,4},{7,5},{8,10},{9,11},{10,... | collective-permute-start | bytes 491528 | tf_op jit(solution)/shard_map/ppermute | solution.py:559
  93.0 5.0 %collective-permute-done.18 = f32[5,64,128]{2,1,0:T(8,128)S(1)} collective-permute-done((f32[5,64,128]{2,1,0:T(8,128)S(1)}, f32[5,64,128]{2,1,0:T(8,128)S(1)}, u32[]{:S(2)}, u32[]{:S(2)}) %collective-permute-start.18) | collective-permute-done | bytes 163872 | tf_op jit(solution)/shard_map/ppermute | solution.py:559
  98.2 1.3 %collective-permute-done.19.came = f32[6,32,128]{2,1,0:T(8,128)S(1)} collective-permute-done((f32[6,32,128]{2,1,0:T(8,128)S(1)}, f32[6,32,128]{2,1,0:T(8,128)S(1)}, u32[]{:S(2)}, u32[]{:S(2)}) %collective-permute-start.19) | collective-permute-done | bytes 98336 | tf_op jit(solution)/shard_map/ppermute | solution.py:563
  100.2 14.2 %all_to_all.5.came = f32[8,2,32,128]{3,2,1,0:T(8,128)S(1)} all-to-all(f32[8,2,32,128]{3,2,1,0:T(8,128)S(1)} %spread.1), channel_id=1, replica_groups=mesh['frag'=8,'aux'=4] {'frag'}, dimensions={0} | all-to-all | bytes 524288 | tf_op jit(solution)/shard_map/all_to_all | solution.py:565
  114.3 1.3 %collect.1 = f32[4,32,128]{2,1,0:T(8,128)} custom-call(s32[8,2]{1,0:T(8,128)S(1)} %get-tuple-element.28.target, f32[8,2,32,128]{3,2,1,0:T(8,128)S(1)} %all_to_all.5.came), custom_call_target="tpu_custom_call" | custom-call | tf_op jit(solution)/shard_map/collect/pallas_call | solution.py:489
  (43 shorter events, 10.3 us)
Async XLA Ops:
  3.0 1.2 %copy-start = (bf16[4,128,1024]{2,1,0:T(8,128)(2,1)S(1)}, bf16[4,128,1024]{2,1,0:T(8,128)(2,1)}, u32[]{:S(2)}) copy-start(bf16[4,128,1024]{2,1,0:T(8,128)(2,1)} %table.1) | copy-start | bytes 3145732
  5.7 49.7 %copy-start.1 = (bf16[4,128]{1,0:T(4,128)(2,1)S(1)}, bf16[4,128]{1,0:T(4,128)(2,1)}, u32[]{:S(2)}) copy-start(bf16[4,128]{1,0:T(4,128)(2,1)} %refs_0_.3) | copy-start | bytes 3076
  5.7 16.6 %collective-permute-start = (bf16[272,1024]{1,0:T(8,128)(2,1)S(1)}, bf16[272,1024]{1,0:T(8,128)(2,1)S(1)}, u32[]{:S(2)}, u32[]{:S(2)}) collective-permute-start(bf16[272,1024]{1,0:T(8,128)(2,1)S(1)} %get-tuple-element.26), channel_id=1, source_target_pairs={{0,8},{4,12},{16,24},{20,28},{8,0},{12,4},{24,16},{28,20},{1,9},{5... | collective-permute-start | bytes 1671176 | tf_op jit(solution)/shard_map/ppermute | solution.py:532
  8.8 25.0 %collective-permute-start.1 = (bf16[272,1024]{1,0:T(8,128)(2,1)S(1)}, bf16[272,1024]{1,0:T(8,128)(2,1)S(1)}, u32[]{:S(2)}, u32[]{:S(2)}) collective-permute-start(bf16[272,1024]{1,0:T(8,128)(2,1)S(1)} %get-tuple-element.30), channel_id=1, source_target_pairs={{0,4},{8,12},{16,20},{24,28},{4,0},{12,8},{20,16},{28,24},{1,5},{9... | collective-permute-start | bytes 1671176 | tf_op jit(solution)/shard_map/ppermute | solution.py:532
  10.3 23.5 %collective-permute-start.2 = (bf16[272,1024]{1,0:T(8,128)(2,1)S(1)}, bf16[272,1024]{1,0:T(8,128)(2,1)S(1)}, u32[]{:S(2)}, u32[]{:S(2)}) collective-permute-start(bf16[272,1024]{1,0:T(8,128)(2,1)S(1)} %get-tuple-element.31), channel_id=1, source_target_pairs={{4,8},{12,16},{20,24},{8,4},{16,12},{24,20},{5,9},{13,17},{21,25},... | collective-permute-start | bytes 1671176 | tf_op jit(solution)/shard_map/ppermute | solution.py:532
  11.0 22.9 %collective-permute-start.3 = (bf16[272,1024]{1,0:T(8,128)(2,1)S(1)}, bf16[272,1024]{1,0:T(8,128)(2,1)S(1)}, u32[]{:S(2)}, u32[]{:S(2)}) collective-permute-start(bf16[272,1024]{1,0:T(8,128)(2,1)S(1)} %get-tuple-element.32), channel_id=1, source_target_pairs={{8,16},{12,20},{16,8},{20,12},{9,17},{13,21},{17,9},{21,13},{10,18... | collective-permute-start | bytes 1671176 | tf_op jit(solution)/shard_map/ppermute | solution.py:532
  11.7 32.0 %collective-permute-start.7 = (bf16[272,1024]{1,0:T(8,128)(2,1)S(1)}, bf16[272,1024]{1,0:T(8,128)(2,1)S(1)}, u32[]{:S(2)}, u32[]{:S(2)}) collective-permute-start(bf16[272,1024]{1,0:T(8,128)(2,1)S(1)} %get-tuple-element.38.refs_0_), channel_id=1, source_target_pairs={{0,2},{1,3},{2,0},{3,1},{4,6},{5,7},{6,4},{7,5},{8,10},{9,11},{10,... | collective-permute-start | bytes 1671176 | tf_op jit(solution)/shard_map/ppermute | solution.py:521
  33.9 21.1 %collective-permute-start.4 = (bf16[272,1024]{1,0:T(8,128)(2,1)S(1)}, bf16[272,1024]{1,0:T(8,128)(2,1)S(1)}, u32[]{:S(2)}, u32[]{:S(2)}) collective-permute-start(bf16[272,1024]{1,0:T(8,128)(2,1)S(1)} %get-tuple-element.34), channel_id=1, source_target_pairs={{0,12},{4,16},{8,20},{12,0},{16,4},{20,8},{1,13},{5,17},{9,21},{13... | collective-permute-start | bytes 1671176 | tf_op jit(solution)/shard_map/ppermute | solution.py:532
  42.2 15.7 %copy-start.2 = (f32[1,3]{1,0:T(1,128)S(1)}, f32[1,3]{1,0:T(1,128)}, u32[]{:S(2)}) copy-start(f32[1,3]{1,0:T(1,128)} %levels.7) | copy-start | bytes 40
  42.2 12.0 %collective-permute-start.5 = (bf16[256,1024]{1,0:T(8,128)(2,1)S(1)}, bf16[256,1024]{1,0:T(8,128)(2,1)S(1)}, u32[]{:S(2)}, u32[]{:S(2)}) collective-permute-start(bf16[256,1024]{1,0:T(8,128)(2,1)S(1)} %pack_group.3.refs_4_), channel_id=1, source_target_pairs={{0,2},{1,3},{2,0},{3,1},{4,6},{5,7},{6,4},{7,5},{8,10},{9,11},{10,... | collective-permute-start | bytes 1572872 | tf_op jit(solution)/shard_map/ppermute | solution.py:521
  43.8 12.5 %collective-permute-start.8 = (bf16[272,1024]{1,0:T(8,128)(2,1)S(1)}, bf16[272,1024]{1,0:T(8,128)(2,1)S(1)}, u32[]{:S(2)}, u32[]{:S(2)}) collective-permute-start(bf16[272,1024]{1,0:T(8,128)(2,1)S(1)} %get-tuple-element.38.refs_0_), channel_id=1, source_target_pairs={{0,1},{1,0},{2,3},{3,2},{4,5},{5,4},{6,7},{7,6},{8,9},{9,8},{10,11... | collective-permute-start | bytes 1671176 | tf_op jit(solution)/shard_map/ppermute | solution.py:522
  43.8 14.1 %collective-permute-start.9 = (bf16[272,1024]{1,0:T(8,128)(2,1)S(1)}, bf16[272,1024]{1,0:T(8,128)(2,1)S(1)}, u32[]{:S(2)}, u32[]{:S(2)}) collective-permute-start(bf16[272,1024]{1,0:T(8,128)(2,1)S(1)} %collective-permute-done.7.refs_1_), channel_id=1, source_target_pairs={{0,1},{1,0},{2,3},{3,2},{4,5},{5,4},{6,7},{7,6},{8,9},{9,8},{10,11... | collective-permute-start | bytes 1671176 | tf_op jit(solution)/shard_map/ppermute | solution.py:524
  54.2 10.6 %collective-permute-start.6 = (bf16[272,1024]{1,0:T(8,128)(2,1)S(1)}, bf16[272,1024]{1,0:T(8,128)(2,1)S(1)}, u32[]{:S(2)}, u32[]{:S(2)}) collective-permute-start(bf16[272,1024]{1,0:T(8,128)(2,1)S(1)} %get-tuple-element.36), channel_id=1, source_target_pairs={{12,24},{16,28},{24,12},{28,16},{13,25},{17,29},{25,13},{29,17},{1... | collective-permute-start | bytes 1671176 | tf_op jit(solution)/shard_map/ppermute | solution.py:532
  54.9 3.0 %collective-permute-start.10 = (bf16[256,1024]{1,0:T(8,128)(2,1)S(1)}, bf16[256,1024]{1,0:T(8,128)(2,1)S(1)}, u32[]{:S(2)}, u32[]{:S(2)}) collective-permute-start(bf16[256,1024]{1,0:T(8,128)(2,1)S(1)} %pack_group.3.refs_4_), channel_id=1, source_target_pairs={{0,1},{1,0},{2,3},{3,2},{4,5},{5,4},{6,7},{7,6},{8,9},{9,8},{10,11... | collective-permute-start | bytes 1572872 | tf_op jit(solution)/shard_map/ppermute | solution.py:522
  55.0 2.9 %collective-permute-start.11 = (bf16[256,1024]{1,0:T(8,128)(2,1)S(1)}, bf16[256,1024]{1,0:T(8,128)(2,1)S(1)}, u32[]{:S(2)}, u32[]{:S(2)}) collective-permute-start(bf16[256,1024]{1,0:T(8,128)(2,1)S(1)} %collective-permute-done.5.refs_5_), channel_id=1, source_target_pairs={{0,1},{1,0},{2,3},{3,2},{4,5},{5,4},{6,7},{7,6},{8,9},{9,8},{10,11... | collective-permute-start | bytes 1572872 | tf_op jit(solution)/shard_map/ppermute | solution.py:524
  56.2 14.0 %collective-permute-start.12 = (bf16[256,1024]{1,0:T(8,128)(2,1)S(1)}, bf16[256,1024]{1,0:T(8,128)(2,1)S(1)}, u32[]{:S(2)}, u32[]{:S(2)}) collective-permute-start(bf16[256,1024]{1,0:T(8,128)(2,1)S(1)} %get-tuple-element.41.refs_8_), channel_id=1, source_target_pairs={{0,2},{1,3},{2,0},{3,1},{4,6},{5,7},{6,4},{7,5},{8,10},{9,11},{10,... | collective-permute-start | bytes 1572872 | tf_op jit(solution)/shard_map/ppermute | solution.py:521
  65.5 4.7 %collective-permute-start.14 = (bf16[256,1024]{1,0:T(8,128)(2,1)S(1)}, bf16[256,1024]{1,0:T(8,128)(2,1)S(1)}, u32[]{:S(2)}, u32[]{:S(2)}) collective-permute-start(bf16[256,1024]{1,0:T(8,128)(2,1)S(1)} %get-tuple-element.42.refs_12_.refs_13_), channel_id=1, source_target_pairs={{0,1},{1,0},{2,3},{3,2},{4,5},{5,4},{6,7},{7,6},{8,9},{9,8},{10,11... | collective-permute-start | bytes 1572872 | tf_op jit(solution)/shard_map/ppermute | solution.py:548
  65.6 6.1 %collective-permute-start.13 = (bf16[256,1024]{1,0:T(8,128)(2,1)S(1)}, bf16[256,1024]{1,0:T(8,128)(2,1)S(1)}, u32[]{:S(2)}, u32[]{:S(2)}) collective-permute-start(bf16[256,1024]{1,0:T(8,128)(2,1)S(1)} %get-tuple-element.41.refs_8_), channel_id=1, source_target_pairs={{0,1},{1,0},{2,3},{3,2},{4,5},{5,4},{6,7},{7,6},{8,9},{9,8},{10,11... | collective-permute-start | bytes 1572872 | tf_op jit(solution)/shard_map/ppermute | solution.py:522
  70.2 1.9 %collective-permute-start.15 = (bf16[256,1024]{1,0:T(8,128)(2,1)S(1)}, bf16[256,1024]{1,0:T(8,128)(2,1)S(1)}, u32[]{:S(2)}, u32[]{:S(2)}) collective-permute-start(bf16[256,1024]{1,0:T(8,128)(2,1)S(1)} %collective-permute-done.12.refs_9_), channel_id=1, source_target_pairs={{0,1},{1,0},{2,3},{3,2},{4,5},{5,4},{6,7},{7,6},{8,9},{9,8},{10,11... | collective-permute-start | bytes 1572872 | tf_op jit(solution)/shard_map/ppermute | solution.py:524
  70.2 14.6 %collective-permute-start.16 = (bf16[256,1024]{1,0:T(8,128)(2,1)S(1)}, bf16[256,1024]{1,0:T(8,128)(2,1)S(1)}, u32[]{:S(2)}, u32[]{:S(2)}) collective-permute-start(bf16[256,1024]{1,0:T(8,128)(2,1)S(1)} %get-tuple-element.42.refs_12_.refs_13_), channel_id=1, source_target_pairs={{0,2},{1,3},{2,0},{3,1},{4,6},{5,7},{6,4},{7,5},{8,10},{9,11},{10,... | collective-permute-start | bytes 1572872 | tf_op jit(solution)/shard_map/ppermute | solution.py:549
  84.8 2.0 %collective-permute-start.17 = (bf16[256,1024]{1,0:T(8,128)(2,1)S(1)}, bf16[256,1024]{1,0:T(8,128)(2,1)S(1)}, u32[]{:S(2)}, u32[]{:S(2)}) collective-permute-start(bf16[256,1024]{1,0:T(8,128)(2,1)S(1)} %collective-permute-done.16.refs_13_), channel_id=1, source_target_pairs={{0,1},{1,0},{2,3},{3,2},{4,5},{5,4},{6,7},{7,6},{8,9},{9,8},{10,11... | collective-permute-start | bytes 1572872 | tf_op jit(solution)/shard_map/ppermute | solution.py:553
  91.8 6.3 %collective-permute-start.18 = (f32[5,64,128]{2,1,0:T(8,128)S(1)}, f32[5,64,128]{2,1,0:T(8,128)S(1)}, u32[]{:S(2)}, u32[]{:S(2)}) collective-permute-start(f32[5,64,128]{2,1,0:T(8,128)S(1)} %get-tuple-element.46), channel_id=1, source_target_pairs={{0,2},{1,3},{2,0},{3,1},{4,6},{5,7},{6,4},{7,5},{8,10},{9,11},{10,... | collective-permute-start | bytes 491528 | tf_op jit(solution)/shard_map/ppermute | solution.py:559
  98.2 1.4 %collective-permute-start.19 = (f32[6,32,128]{2,1,0:T(8,128)S(1)}, f32[6,32,128]{2,1,0:T(8,128)S(1)}, u32[]{:S(2)}, u32[]{:S(2)}) collective-permute-start(f32[6,32,128]{2,1,0:T(8,128)S(1)} %get-tuple-element.47), channel_id=1, source_target_pairs={{0,1},{1,0},{2,3},{3,2},{4,5},{5,4},{6,7},{7,6},{8,9},{9,8},{10,11... | collective-permute-start | bytes 294920 | tf_op jit(solution)/shard_map/ppermute | solution.py:563

commit v9 on v7

--- a/solution.py
+++ b/solution.py
@@ -23,11 +23,12 @@
     return up + [(b, a) for a, b in up]
 
 
-def pick(map_ref, list_ref, list_len, own_count, fragment, owner):
+def pick(row_of, sizes, fragment, owner):
+    _, own_count, list_len = sizes
     count = jnp.int32(0)
     picked = [jnp.int32(0)] * CAP
     for k in range(list_len):
-        row = map_ref[list_ref[fragment, k]]
+        row = row_of(fragment, k)
         hit = row // own_count == owner
         for r in range(CAP):
             picked[r] = jnp.where(hit & (count == r), row % own_count, picked[r])
@@ -35,14 +36,14 @@
     return picked, count
 
 
-def send_kernel(frags, own_count, list_len, where, map_ref, list_ref, energy, occ, table, *refs):
-    outs, own, sems = refs[:6], refs[6], refs[7]
-    me = where[0]
+def send_kernel(sizes, where, map_ref, list_ref, live_ref, energy, occ, table, *refs):
+    outs, own, rows, plan, sems = refs[:6], refs[6], refs[7], refs[8], refs[9]
+    me, frags = where[0], sizes[0]
     block = table.shape[1]
     copies = []
 
     def start(out, index, fragment, inside):
-        picked, count = pick(map_ref, list_ref, list_len, own_count, fragment, me)
+        picked, count = pick(lambda f, k: map_ref[list_ref[f, k]], sizes, fragment, me)
         for r in range(CAP):
             copy = pltpu.make_async_copy(
                 table.at[picked[r]], out.at[pl.ds(r * block, block)], sems.at[index, r]
@@ -57,36 +58,47 @@
         inside = (partner >= 0) & (partner < frags)
         start(outs[index], index, jnp.clip(partner, 0, frags - 1), inside)
     start(own, 6, me, me >= 0)
+
+    def look_up(fragment, carry):
+        for k in range(sizes[2]):
+            rows[fragment, k] = map_ref[list_ref[fragment, k]]
+        return carry
+
+    lax.fori_loop(0, frags, look_up, 0)
+    make_plan(sizes, me, rows, live_ref, plan)
     for out in outs + (own,):
         out[pl.ds(CAP * block, TAIL), :] = jnp.zeros((TAIL, out.shape[1]), out.dtype)
     for out in outs:
-        out[pl.ds(CAP * block, own_count), pl.ds(0, block)] = energy[...]
+        out[pl.ds(CAP * block, energy.shape[0]), pl.ds(0, block)] = energy[...]
     own[pl.ds(CAP * block, occ.shape[0]), :] = occ[...]
     for needed, copy in copies:
         pl.when(needed)(copy.wait)
 
 
-def pack_to_send(where, owner_map, vir_list, energy, occ, table, frags):
-    own_count, block_rows, cols = table.shape
-    list_len = vir_list.shape[1]
+def pack_to_send(where, owner_map, vir_list, vir_rows, energy, occ, table, sizes):
+    _, block_rows, cols = table.shape
     part = jax.ShapeDtypeStruct((CAP * block_rows + TAIL, cols), table.dtype)
     return pl.pallas_call(
-        functools.partial(send_kernel, frags, own_count, list_len),
-        out_shape=(part,) * 7,
-        in_specs=[SMEM, SMEM, SMEM, VMEM, VMEM, ANY],
-        out_specs=(VMEM,) * 7,
+        functools.partial(send_kernel, sizes),
+        out_shape=(part,) * 7
+        + (
+            jax.ShapeDtypeStruct(vir_list.shape, jnp.int32),
+            jax.ShapeDtypeStruct((4, vir_list.shape[1]), jnp.int32),
+        ),
+        in_specs=[SMEM, SMEM, SMEM, SMEM, VMEM, VMEM, ANY],
+        out_specs=(VMEM,) * 7 + (SMEM, SMEM),
         scratch_shapes=[pltpu.SemaphoreType.DMA((7, CAP))],
-        compiler_params=pltpu.CompilerParams(vmem_limit_bytes=8 * MIB),
+        compiler_params=pltpu.CompilerParams(vmem_limit_bytes=58 * MIB),
         cost_estimate=NO_COST,
         name="pack_to_send",
-    )(where, owner_map, vir_list, energy, occ, table)
-
-
-def plan_kernel(frags, own_count, list_len, where, map_ref, list_ref, plan, target):
-    me = where[0]
+    )(where, owner_map, vir_list, vir_rows, energy, occ, table)
+
+
+def make_plan(sizes, me, rows_ref, live_ref, plan):
+    _, own_count, list_len = sizes
     rows, owners, codes, classes = [], [], [], []
     for k in range(list_len):
-        row = map_ref[list_ref[me, k]]
+        row = rows_ref[me, k]
         owner = row // own_count
         low = jnp.minimum(me, owner)
         far = jnp.abs(owner - me)
@@ -111,31 +123,7 @@
         plan[0, place] = codes[k]
         plan[1, place] = rank
         plan[2, place] = rows[k]
-        plan[3, place] = jnp.int32(k)
-
-    def one(fragment, carry):
-        picked, _ = pick(map_ref, list_ref, list_len, own_count, fragment, me)
-        for r in range(CAP):
-            target[fragment, r] = picked[r]
-        return carry
-
-    lax.fori_loop(0, frags, one, 0)
-
-
-def plan_lists(where, owner_map, vir_list, own_count, frags):
-    list_len = vir_list.shape[1]
-    return pl.pallas_call(
-        functools.partial(plan_kernel, frags, own_count, list_len),
-        out_shape=(
-            jax.ShapeDtypeStruct((4, list_len), jnp.int32),
-            jax.ShapeDtypeStruct((frags, CAP), jnp.int32),
-        ),
-        in_specs=[SMEM, SMEM, SMEM],
-        out_specs=(SMEM, SMEM),
-        compiler_params=pltpu.CompilerParams(vmem_limit_bytes=4 * MIB),
-        cost_estimate=NO_COST,
-        name="plan_lists",
-    )(where, owner_map, vir_list)
+        plan[3, place] = live_ref[me, k]
 
 
 def pack_kernel(first, codes, block, with_energy, plan, *refs):
@@ -217,7 +205,7 @@
     return aux + 4 * b
 
 
-def contract_kernel(stage, block, width, where, plan, levels, rows_ref, energy, *refs):
+def contract_kernel(stage, block, width, own_count, where, plan, levels, energy, *refs):
     groups = min(stage + 2, 4)
     parts, rest = refs[: groups * 4], refs[groups * 4 :]
     quarters = {2: (0, 2), 3: (1, 3)}.get(stage, (0, 1, 2, 3))
@@ -229,10 +217,12 @@
         sent, stay, left, grid, occ, scaled, total, amps, tall, dens = rest[:10]
         left_sems, grid_sems, occ_sems = rest[10:]
     elif stage == 1:
-        out, left, grid, occ, scaled, total, amps, tall, left_sems, grid_sems, occ_sems = rest
-    else:
-        out, left, grid, occ, scaled, total, amps, left_sems, grid_sems, occ_sems = rest
-    me, aux = where[0], where[1]
+        (out, left, grid, occ, scaled, total, amps, tall), rest = rest[:8], rest[8:]
+        left_sems, grid_sems, occ_sems = rest
+    elif stage == 0:
+        rows_ref, out, target, left, grid, occ, scaled, total, amps = rest[:9]
+        left_sems, grid_sems, occ_sems = rest[9:]
+    aux = where[1]
     places = (place_of(aux, 0), place_of(aux, 1))
 
     def occ_copy(quarter):
@@ -323,11 +313,11 @@
         for b in range(row_count):
             own_row = energy[pl.ds(places[b], 1), :]
             own_energy = jnp.transpose(jnp.broadcast_to(own_row, (block, block)))
-            own_live = sub < rows_ref[me, plan[3, places[b]]]
+            own_live = sub < plan[3, places[b]]
             for q in range(2 * len(group_list)):
                 place = 2 * group_list[q // 2] + q % 2
                 their_energy = energy[place : place + 1, :]
-                live = own_live & (lane < rows_ref[me, plan[3, place]])
+                live = own_live & (lane < plan[3, place])
                 for p, (i, j) in enumerate(PAIRS):
                     gap = (levels[0, i] + levels[0, j]) - own_energy - their_energy
                     rows = pl.ds((p * row_count + b) * block, block)
@@ -354,6 +344,16 @@
         )
 
     if stage == 0:
+        frags, list_len = rows_ref.shape
+
+        def one(fragment, carry):
+            sizes = (frags, own_count, list_len)
+            picked, _ = pick(lambda f, k: rows_ref[f, k], sizes, fragment, where[0])
+            for r in range(CAP):
+                target[fragment, r] = picked[r]
+            return carry
+
+        lax.fori_loop(0, frags, one, 0)
         out[0] = run(1, (0, 1))[0]
     elif stage == 1:
 
@@ -384,7 +384,7 @@
         sent[...] = dens[:, pl.ds(pl.multiple_of((1 - side) * half, half), half), :]
 
 
-def contract(stage, where, plan, levels, vir_rows, energy, parts, before=()):
+def contract(stage, where, plan, levels, energy, parts, before=(), rows=None, own_count=0):
     block, width = energy.shape[1], parts[0].shape[1]
     height = len(PAIRS) * 2 * block
     span = (4, 2, 2, 2)[stage] * block
@@ -413,12 +413,17 @@
         scratch += [pltpu.VMEM((height // 2, span), jnp.bfloat16)]
         out_shape = jax.ShapeDtypeStruct((4, block, block), jnp.float32)
     else:
-        out_shape = jax.ShapeDtypeStruct((1, block, block), jnp.float32)
+        out_shape = (
+            jax.ShapeDtypeStruct((1, block, block), jnp.float32),
+            jax.ShapeDtypeStruct((rows.shape[0], CAP), jnp.int32),
+        )
+        out_specs = (VMEM, SMEM)
     scratch += [
         pltpu.SemaphoreType.DMA((2, 4)),
         pltpu.SemaphoreType.DMA((3, 4)),
         pltpu.SemaphoreType.DMA((4,)),
     ]
+    tables = () if rows is None else (rows,)
     cost = NO_COST
     if stage in (1, 2):
         units = (4, 4, 2)[stage] * len(PAIRS) * block * block
@@ -426,15 +431,19 @@
             flops=2 * units * 4 * width, bytes_accessed=units * 4, transcendentals=0
         )
     return pl.pallas_call(
-        functools.partial(contract_kernel, stage, block, width),
+        functools.partial(contract_kernel, stage, block, width, own_count),
         out_shape=out_shape,
-        in_specs=[SMEM] * 4 + [VMEM] + [ANY] * len(parts) + [VMEM] * len(before),
+        in_specs=[SMEM] * 3
+        + [VMEM]
+        + [ANY] * len(parts)
+        + [VMEM] * len(before)
+        + [SMEM] * len(tables),
         out_specs=out_specs,
         scratch_shapes=scratch,
         compiler_params=pltpu.CompilerParams(vmem_limit_bytes=26 * MIB),
         cost_estimate=cost,
         name="contract",
-    )(where, plan, levels, vir_rows, energy, *parts, *before)
+    )(where, plan, levels, energy, *parts, *before, *tables)
 
 
 def spread_kernel(own_count, where, plan, kept, came, out):
@@ -492,12 +501,13 @@
     aux = lax.axis_index("aux").astype(jnp.int32)
     own_count, block, width = vir_grid.shape
     list_len = vir_list.shape[1]
+    sizes = (frags, own_count, list_len)
     where = jnp.stack([me, aux])
     far_pairs = [(i, i ^ 2) for i in range(aux_count)]
     near_pairs = [(i, i ^ 1) for i in range(aux_count)]
 
-    *outgoing, own = pack_to_send(
-        where, owner_map, vir_list, vir_energy, occ_grid[0], vir_grid, frags
+    *outgoing, own, rows, plan = pack_to_send(
+        where, owner_map, vir_list, vir_rows, vir_energy, occ_grid[0], vir_grid, sizes
     )
 
     def over_aux(here, *others):
@@ -517,27 +527,25 @@
     arrived = {code: send(code - 1) for code in (1, 2, 3, 4)}
     parts = over_aux(own)
     arrived[5] = send(4, *(arrived[c] for c in (1, 2, 3, 4)))
-    plan, target = plan_lists(
-        after(where, arrived[3]), owner_map, vir_list, own_count, frags
-    )
     here = pack_group(2, block, plan, {c: arrived[c] for c in range(1, 5)})[0]
     parts += over_aux(here)
     arrived[6] = send(5, parts[5])
     here, early_energy = pack_group(
         4, block, plan, {c: arrived[c] for c in range(1, 6)}, vir_energy
     )
-    shared = (where, plan, occ_energy, vir_rows)
-    first = contract(0, *shared, early_energy, parts[:8])
-    parts += over_aux(here, first)
+    shared = (where, plan, occ_energy)
+    first, target = contract(
+        0, *shared, early_energy, parts[:8], rows=rows, own_count=own_count
+    )
     arrived[6] = after(arrived[6], first)
-    here, energy = pack_group(6, block, plan, arrived, vir_energy)
-    here = after(here, parts[9])
+    last, energy = pack_group(6, block, plan, arrived, vir_energy)
+    near = lax.ppermute(last, "aux", near_pairs)
+    far = lax.ppermute(last, "aux", far_pairs)
+    parts += over_aux(here, near)
     second = contract(1, *shared, early_energy, parts[:12])
-    near = lax.ppermute(here, "aux", near_pairs)
-    partial = contract(2, *shared, energy, parts + [here, here, near, near])
-    far = lax.ppermute(here, "aux", far_pairs)
+    partial = contract(2, *shared, energy, parts + [last, last, near, near])
     far_near = lax.ppermute(after(far, second, partial), "aux", near_pairs)
-    parts += [here, far, near, far_near]
+    parts += [last, far, near, far_near]
     sent, stay = contract(3, *shared, energy, parts, (first, second, partial))
 
     quarter = block // aux_count

time: 117 us -> 117 us (level)
  local copies, waits for them, and re-layouts: 3.99 us -> 0.73 us
  waiting for transfers between devices: 41.9 us -> 44.3 us
  starting transfers between devices: 23.8 us -> 22.3 us
  Pallas kernels: 32.7 us -> 33.9 us
    ppermute x6, waiting for transfers between devices: 18.3 us -> 22.1 us  [send(): return lax.ppermute(payload, 'frag', round_pairs(distance, parity, frags))]
    unnamed x16, local copies, waits for them, and re-layouts: 3.96 us -> 0.7 us
    ppermute x3, waiting for transfers between devices: 15.3 us -> 13.7 us  [over_aux(): far = lax.ppermute(here, 'aux', far_pairs)]
    ppermute x6, starting transfers between devices: 14.3 us -> 12.8 us  [send(): return lax.ppermute(payload, 'frag', round_pairs(distance, parity, frags))]
    pallas_call x6 -> x5, Pallas kernels: 28.5 us -> 29.7 us  [the longest x4 25.1 us: contract(): pl.pallas_call(functools.partial(contract_kernel, stage, block, width, ow...]
  transfers between devices with their start and end apart: 20 -> 20, of which waited for: 7 -> 8; matrix products, arithmetic and copies ran while one was open for 0% -> 0% of each run, Pallas kernels for 21% -> 19%
where the time goes in v9:
time: 117 us
  waiting for transfers between devices  44.3 us (38%)
  Pallas kernels  33.9 us (29%)
  starting transfers between devices  22.3 us (19%)
  blocking collectives  14.5 us (12%)
    pallas_call x4, Pallas kernels, contract(): pl.pallas_call(functools.partial(contract_kernel, stage, block, width, ow...  25.1 us
    ppermute x6, waiting for transfers between devices, send(): return lax.ppermute(payload, 'frag', round_pairs(distance, parity, frags))  22.1 us
    all_to_all x1, blocking collectives, body(): incoming = lax.all_to_all(outgoing, 'frag', 0, 0, tiled=True)  14.5 us
    ppermute x3, waiting for transfers between devices, over_aux(): far = lax.ppermute(here, 'aux', far_pairs)  13.7 us
    ppermute x6, starting transfers between devices, send(): return lax.ppermute(payload, 'frag', round_pairs(distance, parity, frags))  12.8 us
    ppermute x1, waiting for transfers between devices, body(): met = lax.ppermute(sent, 'aux', far_pairs)  5.02 us
    ppermute x3, starting transfers between devices, over_aux(): far = lax.ppermute(here, 'aux', far_pairs)  4.79 us
    pallas_call x1, Pallas kernels, pack_to_send(): pl.pallas_call(functools.partial(send_kernel, sizes), out_shape=(part,) *...  4.63 us
  transfers between devices with their start and end apart: 20, of which 8 were waited for; matrix products, arithmetic and copies ran while one was open for 0% of the time, Pallas kernels for 19%

profile of v9, /device:TPU:0, one launch (start us, length us, event | category | flops | bytes accessed | tf_op | source)
XLA Modules:
  0.0 116.7 jit_solution(4459238697972893481)
XLA Ops:
  0.6 4.6 %pack_to_send.1 = (bf16[272,1024]{1,0:T(8,128)(2,1)}, bf16[272,1024]{1,0:T(8,128)(2,1)}, bf16[272,1024]{1,0:T(8,128)(2,1)}, bf16[272,1024]{1,0:T(8,128)(2,1)}, b...) custom-call(s32[2]{0:T(128)} %pad_add_fusion.where, ...), custom_call_target="tpu_custom_call" | custom-call | tf_op jit(solution)/shard_map/pack_to_send/pallas_call | solution.py:81
  5.3 3.0 %collective-permute-start = (bf16[272,1024]{1,0:T(8,128)(2,1)}, bf16[272,1024]{1,0:T(8,128)(2,1)S(1)}, u32[]{:S(2)}, u32[]{:S(2)}) collective-permute-start(bf16[272,1024]{1,0:T(8,128)(2,1)} %get-tuple-element.28), channel_id=1, source_target_pairs={{0,4},{8,12},{16,20},{24,28},{4,0},{12,8},{20,16},{28,24},{1,5},{9... | collective-permute-start | bytes 1671176 | tf_op jit(solution)/shard_map/ppermute | solution.py:525
  9.0 3.2 %collective-permute-start.2 = (bf16[272,1024]{1,0:T(8,128)(2,1)}, bf16[272,1024]{1,0:T(8,128)(2,1)S(1)}, u32[]{:S(2)}, u32[]{:S(2)}) collective-permute-start(bf16[272,1024]{1,0:T(8,128)(2,1)} %get-tuple-element.30), channel_id=1, source_target_pairs={{0,8},{4,12},{16,24},{20,28},{8,0},{12,4},{24,16},{28,20},{1,9},{5... | collective-permute-start | bytes 1671176 | tf_op jit(solution)/shard_map/ppermute | solution.py:525
  12.9 1.6 %collective-permute-start.5 = (bf16[272,1024]{1,0:T(8,128)(2,1)}, bf16[272,1024]{1,0:T(8,128)(2,1)S(1)}, u32[]{:S(2)}, u32[]{:S(2)}) collective-permute-start(bf16[272,1024]{1,0:T(8,128)(2,1)} %get-tuple-element.35.refs_0_), channel_id=1, source_target_pairs={{0,2},{1,3},{2,0},{3,1},{4,6},{5,7},{6,4},{7,5},{8,10},{9,11},{10,... | collective-permute-start | bytes 1671176 | tf_op jit(solution)/shard_map/ppermute | solution.py:514
  14.5 17.9 %collective-permute-done.refs_1_.refs_0_ = bf16[272,1024]{1,0:T(8,128)(2,1)S(1)} collective-permute-done((bf16[272,1024]{1,0:T(8,128)(2,1)}, bf16[272,1024]{1,0:T(8,128)(2,1)S(1)}, u32[]{:S(2)}, u32[]{:S(2)}) %collective-permute-start) | collective-permute-done | bytes 557088 | tf_op jit(solution)/shard_map/ppermute | solution.py:525
  32.4 4.2 %collective-permute-done.2.refs_3_.refs_2_ = bf16[272,1024]{1,0:T(8,128)(2,1)S(1)} collective-permute-done((bf16[272,1024]{1,0:T(8,128)(2,1)}, bf16[272,1024]{1,0:T(8,128)(2,1)S(1)}, u32[]{:S(2)}, u32[]{:S(2)}) %collective-permute-start.2) | collective-permute-done | bytes 557088 | tf_op jit(solution)/shard_map/ppermute | solution.py:525
  36.7 4.5 %collective-permute-start.4 = (bf16[272,1024]{1,0:T(8,128)(2,1)}, bf16[272,1024]{1,0:T(8,128)(2,1)S(1)}, u32[]{:S(2)}, u32[]{:S(2)}) collective-permute-start(bf16[272,1024]{1,0:T(8,128)(2,1)} %get-tuple-element.33), channel_id=1, source_target_pairs={{0,12},{4,16},{8,20},{12,0},{16,4},{20,8},{1,13},{5,17},{9,21},{13... | collective-permute-start | bytes 1671176 | tf_op jit(solution)/shard_map/ppermute | solution.py:525
  42.6 1.6 %collective-permute-start.8 = (bf16[256,1024]{1,0:T(8,128)(2,1)S(1)}, bf16[256,1024]{1,0:T(8,128)(2,1)S(1)}, u32[]{:S(2)}, u32[]{:S(2)}) collective-permute-start(bf16[256,1024]{1,0:T(8,128)(2,1)S(1)} %pack_group.4.refs_4_), channel_id=1, source_target_pairs={{0,2},{1,3},{2,0},{3,1},{4,6},{5,7},{6,4},{7,5},{8,10},{9,11},{10,... | collective-permute-start | bytes 1572872 | tf_op jit(solution)/shard_map/ppermute | solution.py:514
  44.7 10.2 %collective-permute-done.8.refs_5_ = bf16[256,1024]{1,0:T(8,128)(2,1)S(1)} collective-permute-done((bf16[256,1024]{1,0:T(8,128)(2,1)S(1)}, bf16[256,1024]{1,0:T(8,128)(2,1)S(1)}, u32[]{:S(2)}, u32[]{:S(2)}) %collective-permute-start.8) | collective-permute-done | bytes 524320 | tf_op jit(solution)/shard_map/ppermute | solution.py:514
  56.2 0.8 pack_group.3
  56.9 1.6 %collective-permute-start.12 = (bf16[256,1024]{1,0:T(8,128)(2,1)S(1)}, bf16[256,1024]{1,0:T(8,128)(2,1)S(1)}, u32[]{:S(2)}, u32[]{:S(2)}) collective-permute-start(bf16[256,1024]{1,0:T(8,128)(2,1)S(1)} %get-tuple-element.43.refs_8_), channel_id=1, source_target_pairs={{0,2},{1,3},{2,0},{3,1},{4,6},{5,7},{6,4},{7,5},{8,10},{9,11},{10,... | collective-permute-start | bytes 1572872 | tf_op jit(solution)/shard_map/ppermute | solution.py:514
  58.6 7.5 %contract.4 = (f32[1,128,128]{2,1,0:T(8,128)S(1)}, s32[8,2]{1,0:T(8,128)S(1)}) custom-call(s32[2]{0:T(128)S(1)} %copy-done.3, s32[4,8]{1,0:T(4,128)S(1)} %copy-done.1, f32[1,3]{1,0:T(1,128)S(1)} %copy-done.5, f32[8,128]{1,0:T(8,128)S(1)} %get-tuple-element.34.energy, bf16[272,1024]{1,0:T(8,128)(2,1)S(1)} %copy-done, ...), custom_call_target="tpu_custom_call" | custom-call | tf_op jit(solution)/shard_map/contract/pallas_call | solution.py:433
  66.1 0.8 pack_group.5
  67.5 3.5 %collective-permute-done.12.refs_9_ = bf16[256,1024]{1,0:T(8,128)(2,1)S(1)} collective-permute-done((bf16[256,1024]{1,0:T(8,128)(2,1)S(1)}, bf16[256,1024]{1,0:T(8,128)(2,1)S(1)}, u32[]{:S(2)}, u32[]{:S(2)}) %collective-permute-start.12) | collective-permute-done | bytes 524320 | tf_op jit(solution)/shard_map/ppermute | solution.py:514
  70.9 1.5 %collective-permute-start.16 = (bf16[256,1024]{1,0:T(8,128)(2,1)S(1)}, bf16[256,1024]{1,0:T(8,128)(2,1)S(1)}, u32[]{:S(2)}, u32[]{:S(2)}) collective-permute-start(bf16[256,1024]{1,0:T(8,128)(2,1)S(1)} %get-tuple-element.44.refs_12_.refs_13_), channel_id=1, source_target_pairs={{0,2},{1,3},{2,0},{3,1},{4,6},{5,7},{6,4},{7,5},{8,10},{9,11},{10,... | collective-permute-start | bytes 1572872 | tf_op jit(solution)/shard_map/ppermute | solution.py:543
  72.8 4.0 %contract.6.refs_18_ = f32[1536,256]{1,0:T(8,128)S(1)} custom-call(s32[2]{0:T(128)S(1)} %copy-done.3, s32[4,8]{1,0:T(4,128)S(1)} %copy-done.1, f32[1,3]{1,0:T(1,128)S(1)} %copy-done.5, f32[8,128]{1,0:T(8,128)S(1)} %get-tuple-element.42.energy, bf16[272,1024]{1,0:T(8,128)(2,1)S(1)} %copy-done, bf16[272,1024]{1,0:T(8,128)(2,1)S(1)} %collective-permute-done.5.refs_1_, ...), custom_call_target="tpu_custom_call" | custom-call | flops 1610612736 | bytes 786432 | tf_op jit(solution)/shard_map/contract/pallas_call | solution.py:433
  76.8 8.6 %contract.5.refs_17_ = f32[4,128,128]{2,1,0:T(8,128)S(1)} custom-call(s32[2]{0:T(128)S(1)} %copy-done.3, s32[4,8]{1,0:T(4,128)S(1)} %copy-done.1, f32[1,3]{1,0:T(1,128)S(1)} %copy-done.5, f32[8,128]{1,0:T(8,128)S(1)} %get-tuple-element.34.energy, bf16[272,1024]{1,0:T(8,128)(2,1)S(1)} %copy-done, bf16[272,1024]{1,0:T(8,128)(2,1)S(1)} %collective-permute-done.5.refs_1_, ...), custom_call_target="tpu_custom_call" | custom-call | flops 3221225472 | bytes 1572864 | tf_op jit(solution)/shard_map/contract/pallas_call | solution.py:433
  85.7 1.8 %collective-permute-done.17.refs_15_ = bf16[256,1024]{1,0:T(8,128)(2,1)S(1)} collective-permute-done((bf16[256,1024]{1,0:T(8,128)(2,1)S(1)}, bf16[256,1024]{1,0:T(8,128)(2,1)S(1)}, u32[]{:S(2)}, u32[]{:S(2)}) %collective-permute-start.17) | collective-permute-done | bytes 524320 | tf_op jit(solution)/shard_map/ppermute | solution.py:547
  87.5 4.9 %contract.7 = (f32[5,64,128]{2,1,0:T(8,128)S(1)}, f32[5,64,128]{2,1,0:T(8,128)S(1)}) custom-call(s32[2]{0:T(128)S(1)} %copy-done.3, s32[4,8]{1,0:T(4,128)S(1)} %copy-done.1, f32[1,3]{1,0:T(1,128)S(1)} %copy-done.5, f32[8,128]{1,0:T(8,128)S(1)} %get-tuple-element.42.energy, bf16[272,1024]{1,0:T(8,128)(2,1)S(1)} %copy-done, ...), custom_call_target="tpu_custom_call" | custom-call | tf_op jit(solution)/shard_map/contract/pallas_call | solution.py:433
  92.4 1.3 %collective-permute-start.18 = (f32[5,64,128]{2,1,0:T(8,128)S(1)}, f32[5,64,128]{2,1,0:T(8,128)S(1)}, u32[]{:S(2)}, u32[]{:S(2)}) collective-permute-start(f32[5,64,128]{2,1,0:T(8,128)S(1)} %get-tuple-element.48), channel_id=1, source_target_pairs={{0,2},{1,3},{2,0},{3,1},{4,6},{5,7},{6,4},{7,5},{8,10},{9,11},{10,... | collective-permute-start | bytes 491528 | tf_op jit(solution)/shard_map/ppermute | solution.py:553
  93.7 5.0 %collective-permute-done.18 = f32[5,64,128]{2,1,0:T(8,128)S(1)} collective-permute-done((f32[5,64,128]{2,1,0:T(8,128)S(1)}, f32[5,64,128]{2,1,0:T(8,128)S(1)}, u32[]{:S(2)}, u32[]{:S(2)}) %collective-permute-start.18) | collective-permute-done | bytes 163872 | tf_op jit(solution)/shard_map/ppermute | solution.py:553
  98.9 1.3 %collective-permute-done.19.came = f32[6,32,128]{2,1,0:T(8,128)S(1)} collective-permute-done((f32[6,32,128]{2,1,0:T(8,128)S(1)}, f32[6,32,128]{2,1,0:T(8,128)S(1)}, u32[]{:S(2)}, u32[]{:S(2)}) %collective-permute-start.19) | collective-permute-done | bytes 98336 | tf_op jit(solution)/shard_map/ppermute | solution.py:557
  100.8 14.5 %all_to_all.5.came = f32[8,2,32,128]{3,2,1,0:T(8,128)S(1)} all-to-all(f32[8,2,32,128]{3,2,1,0:T(8,128)S(1)} %spread.1), channel_id=1, replica_groups=mesh['frag'=8,'aux'=4] {'frag'}, dimensions={0} | all-to-all | bytes 524288 | tf_op jit(solution)/shard_map/all_to_all | solution.py:559
  115.3 1.3 %collect.1 = f32[4,32,128]{2,1,0:T(8,128)} custom-call(s32[8,2]{1,0:T(8,128)S(1)} %get-tuple-element.37.target, f32[8,2,32,128]{3,2,1,0:T(8,128)S(1)} %all_to_all.5.came), custom_call_target="tpu_custom_call" | custom-call | tf_op jit(solution)/shard_map/collect/pallas_call | solution.py:487
  (49 shorter events, 7.1 us)
Async XLA Ops:
  0.6 55.5 %copy-start.4 = (bf16[4,128]{1,0:T(4,128)(2,1)S(1)}, bf16[4,128]{1,0:T(4,128)(2,1)}, u32[]{:S(2)}) copy-start(bf16[4,128]{1,0:T(4,128)(2,1)} %refs_0_.3) | copy-start | bytes 3076
  5.3 38.9 %copy-start = (bf16[272,1024]{1,0:T(8,128)(2,1)S(1)}, bf16[272,1024]{1,0:T(8,128)(2,1)}, u32[]{:S(2)}) copy-start(bf16[272,1024]{1,0:T(8,128)(2,1)} %get-tuple-element.35.refs_0_) | copy-start | bytes 1671172
  5.3 27.2 %collective-permute-start = (bf16[272,1024]{1,0:T(8,128)(2,1)}, bf16[272,1024]{1,0:T(8,128)(2,1)S(1)}, u32[]{:S(2)}, u32[]{:S(2)}) collective-permute-start(bf16[272,1024]{1,0:T(8,128)(2,1)} %get-tuple-element.28), channel_id=1, source_target_pairs={{0,4},{8,12},{16,20},{24,28},{4,0},{12,8},{20,16},{28,24},{1,5},{9... | collective-permute-start | bytes 1671176 | tf_op jit(solution)/shard_map/ppermute | solution.py:525
  8.3 24.1 %collective-permute-start.1 = (bf16[272,1024]{1,0:T(8,128)(2,1)}, bf16[272,1024]{1,0:T(8,128)(2,1)S(1)}, u32[]{:S(2)}, u32[]{:S(2)}) collective-permute-start(bf16[272,1024]{1,0:T(8,128)(2,1)} %get-tuple-element.29), channel_id=1, source_target_pairs={{4,8},{12,16},{20,24},{8,4},{16,12},{24,20},{5,9},{13,17},{21,25},... | collective-permute-start | bytes 1671176 | tf_op jit(solution)/shard_map/ppermute | solution.py:525
  9.0 27.7 %collective-permute-start.2 = (bf16[272,1024]{1,0:T(8,128)(2,1)}, bf16[272,1024]{1,0:T(8,128)(2,1)S(1)}, u32[]{:S(2)}, u32[]{:S(2)}) collective-permute-start(bf16[272,1024]{1,0:T(8,128)(2,1)} %get-tuple-element.30), channel_id=1, source_target_pairs={{0,8},{4,12},{16,24},{20,28},{8,0},{12,4},{24,16},{28,20},{1,9},{5... | collective-permute-start | bytes 1671176 | tf_op jit(solution)/shard_map/ppermute | solution.py:525
  12.2 24.4 %collective-permute-start.3 = (bf16[272,1024]{1,0:T(8,128)(2,1)}, bf16[272,1024]{1,0:T(8,128)(2,1)S(1)}, u32[]{:S(2)}, u32[]{:S(2)}) collective-permute-start(bf16[272,1024]{1,0:T(8,128)(2,1)} %get-tuple-element.31), channel_id=1, source_target_pairs={{8,16},{12,20},{16,8},{20,12},{9,17},{13,21},{17,9},{21,13},{10,18... | collective-permute-start | bytes 1671176 | tf_op jit(solution)/shard_map/ppermute | solution.py:525
  12.9 31.3 %collective-permute-start.5 = (bf16[272,1024]{1,0:T(8,128)(2,1)}, bf16[272,1024]{1,0:T(8,128)(2,1)S(1)}, u32[]{:S(2)}, u32[]{:S(2)}) collective-permute-start(bf16[272,1024]{1,0:T(8,128)(2,1)} %get-tuple-element.35.refs_0_), channel_id=1, source_target_pairs={{0,2},{1,3},{2,0},{3,1},{4,6},{5,7},{6,4},{7,5},{8,10},{9,11},{10,... | collective-permute-start | bytes 1671176 | tf_op jit(solution)/shard_map/ppermute | solution.py:514
  36.7 19.0 %collective-permute-start.4 = (bf16[272,1024]{1,0:T(8,128)(2,1)}, bf16[272,1024]{1,0:T(8,128)(2,1)S(1)}, u32[]{:S(2)}, u32[]{:S(2)}) collective-permute-start(bf16[272,1024]{1,0:T(8,128)(2,1)} %get-tuple-element.33), channel_id=1, source_target_pairs={{0,12},{4,16},{8,20},{12,0},{16,4},{20,8},{1,13},{5,17},{9,21},{13... | collective-permute-start | bytes 1671176 | tf_op jit(solution)/shard_map/ppermute | solution.py:525
  42.5 16.0 %copy-start.3 = (s32[2]{0:T(128)S(1)}, s32[2]{0:T(128)}, u32[]{:S(2)}) copy-start(s32[2]{0:T(128)} %pad_add_fusion.where) | copy-start | bytes 28
  42.6 16.0 %copy-start.5 = (f32[1,3]{1,0:T(1,128)S(1)}, f32[1,3]{1,0:T(1,128)}, u32[]{:S(2)}) copy-start(f32[1,3]{1,0:T(1,128)} %levels.7) | copy-start | bytes 40
  42.6 12.3 %collective-permute-start.8 = (bf16[256,1024]{1,0:T(8,128)(2,1)S(1)}, bf16[256,1024]{1,0:T(8,128)(2,1)S(1)}, u32[]{:S(2)}, u32[]{:S(2)}) collective-permute-start(bf16[256,1024]{1,0:T(8,128)(2,1)S(1)} %pack_group.4.refs_4_), channel_id=1, source_target_pairs={{0,2},{1,3},{2,0},{3,1},{4,6},{5,7},{6,4},{7,5},{8,10},{9,11},{10,... | collective-permute-start | bytes 1572872 | tf_op jit(solution)/shard_map/ppermute | solution.py:514
  44.2 12.8 %collective-permute-start.6 = (bf16[272,1024]{1,0:T(8,128)(2,1)S(1)}, bf16[272,1024]{1,0:T(8,128)(2,1)S(1)}, u32[]{:S(2)}, u32[]{:S(2)}) collective-permute-start(bf16[272,1024]{1,0:T(8,128)(2,1)S(1)} %copy-done), channel_id=1, source_target_pairs={{0,1},{1,0},{2,3},{3,2},{4,5},{5,4},{6,7},{7,6},{8,9},{9,8},{10,11... | collective-permute-start | bytes 1671176 | tf_op jit(solution)/shard_map/ppermute | solution.py:515
  44.2 14.4 %collective-permute-start.7 = (bf16[272,1024]{1,0:T(8,128)(2,1)S(1)}, bf16[272,1024]{1,0:T(8,128)(2,1)S(1)}, u32[]{:S(2)}, u32[]{:S(2)}) collective-permute-start(bf16[272,1024]{1,0:T(8,128)(2,1)S(1)} %collective-permute-done.5.refs_1_), channel_id=1, source_target_pairs={{0,1},{1,0},{2,3},{3,2},{4,5},{5,4},{6,7},{7,6},{8,9},{9,8},{10,11... | collective-permute-start | bytes 1671176 | tf_op jit(solution)/shard_map/ppermute | solution.py:517
  54.9 11.2 %collective-permute-start.11 = (bf16[272,1024]{1,0:T(8,128)(2,1)S(1)}, bf16[272,1024]{1,0:T(8,128)(2,1)S(1)}, u32[]{:S(2)}, u32[]{:S(2)}) collective-permute-start(bf16[272,1024]{1,0:T(8,128)(2,1)S(1)} %copy-done.7), channel_id=1, source_target_pairs={{12,24},{16,28},{24,12},{28,16},{13,25},{17,29},{25,13},{29,17},{1... | collective-permute-start | bytes 1671176 | tf_op jit(solution)/shard_map/ppermute | solution.py:525
  55.6 3.0 %collective-permute-start.9 = (bf16[256,1024]{1,0:T(8,128)(2,1)S(1)}, bf16[256,1024]{1,0:T(8,128)(2,1)S(1)}, u32[]{:S(2)}, u32[]{:S(2)}) collective-permute-start(bf16[256,1024]{1,0:T(8,128)(2,1)S(1)} %pack_group.4.refs_4_), channel_id=1, source_target_pairs={{0,1},{1,0},{2,3},{3,2},{4,5},{5,4},{6,7},{7,6},{8,9},{9,8},{10,11... | collective-permute-start | bytes 1572872 | tf_op jit(solution)/shard_map/ppermute | solution.py:515
  55.7 2.9 %collective-permute-start.10 = (bf16[256,1024]{1,0:T(8,128)(2,1)S(1)}, bf16[256,1024]{1,0:T(8,128)(2,1)S(1)}, u32[]{:S(2)}, u32[]{:S(2)}) collective-permute-start(bf16[256,1024]{1,0:T(8,128)(2,1)S(1)} %collective-permute-done.8.refs_5_), channel_id=1, source_target_pairs={{0,1},{1,0},{2,3},{3,2},{4,5},{5,4},{6,7},{7,6},{8,9},{9,8},{10,11... | collective-permute-start | bytes 1572872 | tf_op jit(solution)/shard_map/ppermute | solution.py:517
  56.9 14.0 %collective-permute-start.12 = (bf16[256,1024]{1,0:T(8,128)(2,1)S(1)}, bf16[256,1024]{1,0:T(8,128)(2,1)S(1)}, u32[]{:S(2)}, u32[]{:S(2)}) collective-permute-start(bf16[256,1024]{1,0:T(8,128)(2,1)S(1)} %get-tuple-element.43.refs_8_), channel_id=1, source_target_pairs={{0,2},{1,3},{2,0},{3,1},{4,6},{5,7},{6,4},{7,5},{8,10},{9,11},{10,... | collective-permute-start | bytes 1572872 | tf_op jit(solution)/shard_map/ppermute | solution.py:514
  66.9 4.0 %collective-permute-start.14 = (bf16[256,1024]{1,0:T(8,128)(2,1)S(1)}, bf16[256,1024]{1,0:T(8,128)(2,1)S(1)}, u32[]{:S(2)}, u32[]{:S(2)}) collective-permute-start(bf16[256,1024]{1,0:T(8,128)(2,1)S(1)} %get-tuple-element.44.refs_12_.refs_13_), channel_id=1, source_target_pairs={{0,1},{1,0},{2,3},{3,2},{4,5},{5,4},{6,7},{7,6},{8,9},{9,8},{10,11... | collective-permute-start | bytes 1572872 | tf_op jit(solution)/shard_map/ppermute | solution.py:542
  67.0 5.5 %collective-permute-start.13 = (bf16[256,1024]{1,0:T(8,128)(2,1)S(1)}, bf16[256,1024]{1,0:T(8,128)(2,1)S(1)}, u32[]{:S(2)}, u32[]{:S(2)}) collective-permute-start(bf16[256,1024]{1,0:T(8,128)(2,1)S(1)} %get-tuple-element.43.refs_8_), channel_id=1, source_target_pairs={{0,1},{1,0},{2,3},{3,2},{4,5},{5,4},{6,7},{7,6},{8,9},{9,8},{10,11... | collective-permute-start | bytes 1572872 | tf_op jit(solution)/shard_map/ppermute | solution.py:515
  70.9 1.9 %collective-permute-start.15 = (bf16[256,1024]{1,0:T(8,128)(2,1)S(1)}, bf16[256,1024]{1,0:T(8,128)(2,1)S(1)}, u32[]{:S(2)}, u32[]{:S(2)}) collective-permute-start(bf16[256,1024]{1,0:T(8,128)(2,1)S(1)} %collective-permute-done.12.refs_9_), channel_id=1, source_target_pairs={{0,1},{1,0},{2,3},{3,2},{4,5},{5,4},{6,7},{7,6},{8,9},{9,8},{10,11... | collective-permute-start | bytes 1572872 | tf_op jit(solution)/shard_map/ppermute | solution.py:517
  70.9 14.6 %collective-permute-start.16 = (bf16[256,1024]{1,0:T(8,128)(2,1)S(1)}, bf16[256,1024]{1,0:T(8,128)(2,1)S(1)}, u32[]{:S(2)}, u32[]{:S(2)}) collective-permute-start(bf16[256,1024]{1,0:T(8,128)(2,1)S(1)} %get-tuple-element.44.refs_12_.refs_13_), channel_id=1, source_target_pairs={{0,2},{1,3},{2,0},{3,1},{4,6},{5,7},{6,4},{7,5},{8,10},{9,11},{10,... | collective-permute-start | bytes 1572872 | tf_op jit(solution)/shard_map/ppermute | solution.py:543
  85.5 2.0 %collective-permute-start.17 = (bf16[256,1024]{1,0:T(8,128)(2,1)S(1)}, bf16[256,1024]{1,0:T(8,128)(2,1)S(1)}, u32[]{:S(2)}, u32[]{:S(2)}) collective-permute-start(bf16[256,1024]{1,0:T(8,128)(2,1)S(1)} %collective-permute-done.16.refs_13_), channel_id=1, source_target_pairs={{0,1},{1,0},{2,3},{3,2},{4,5},{5,4},{6,7},{7,6},{8,9},{9,8},{10,11... | collective-permute-start | bytes 1572872 | tf_op jit(solution)/shard_map/ppermute | solution.py:547
  92.4 6.3 %collective-permute-start.18 = (f32[5,64,128]{2,1,0:T(8,128)S(1)}, f32[5,64,128]{2,1,0:T(8,128)S(1)}, u32[]{:S(2)}, u32[]{:S(2)}) collective-permute-start(f32[5,64,128]{2,1,0:T(8,128)S(1)} %get-tuple-element.48), channel_id=1, source_target_pairs={{0,2},{1,3},{2,0},{3,1},{4,6},{5,7},{6,4},{7,5},{8,10},{9,11},{10,... | collective-permute-start | bytes 491528 | tf_op jit(solution)/shard_map/ppermute | solution.py:553
  98.8 1.4 %collective-permute-start.19 = (f32[6,32,128]{2,1,0:T(8,128)S(1)}, f32[6,32,128]{2,1,0:T(8,128)S(1)}, u32[]{:S(2)}, u32[]{:S(2)}) collective-permute-start(f32[6,32,128]{2,1,0:T(8,128)S(1)} %get-tuple-element.49), channel_id=1, source_target_pairs={{0,1},{1,0},{2,3},{3,2},{4,5},{5,4},{6,7},{7,6},{8,9},{9,8},{10,11... | collective-permute-start | bytes 294920 | tf_op jit(solution)/shard_map/ppermute | solution.py:557
  (4 other events, 44.4 us)

commit v10 on v8

--- a/solution.py
+++ b/solution.py
@@ -392,7 +392,8 @@
         half = block // 2
         side = aux // 2
         stay[...] = dens[:, pl.ds(pl.multiple_of(side * half, half), half), :]
-        sent[...] = dens[:, pl.ds(pl.multiple_of((1 - side) * half, half), half), :]
+        away = dens[:, pl.ds(pl.multiple_of((1 - side) * half, half), half), :]
+        sent[...] = away.astype(jnp.bfloat16)
 
 
 def contract(stage, where, plan, levels, energy, parts, before=()):
@@ -416,7 +417,10 @@
             pltpu.VMEM((height, span), jnp.bfloat16),
             pltpu.VMEM((5, block, block), jnp.float32),
         ]
-        out_shape = (jax.ShapeDtypeStruct((5, block // 2, block), jnp.float32),) * 2
+        out_shape = tuple(
+            jax.ShapeDtypeStruct((5, block // 2, block), dtype)
+            for dtype in (jnp.bfloat16, jnp.float32)
+        )
         out_specs = (VMEM, VMEM)
     elif stage == 2:
         out_shape = jax.ShapeDtypeStruct((height, span), jnp.float32)
@@ -453,7 +457,7 @@
     out[...] = jnp.zeros_like(out)
 
     def put(place, value):
-        out[plan[2, place] // own_count, plan[1, place]] = value
+        out[plan[2, place] // own_count, plan[1, place]] = value.astype(out.dtype)
 
     put(aux, kept[0])
     put(aux ^ 2, kept[1])
@@ -466,7 +470,7 @@
 def spread(ints, plan, kept, came, frags, own_count):
     return pl.pallas_call(
         functools.partial(spread_kernel, own_count),
-        out_shape=jax.ShapeDtypeStruct((frags, CAP) + kept.shape[1:], kept.dtype),
+        out_shape=jax.ShapeDtypeStruct((frags, CAP) + kept.shape[1:], jnp.bfloat16),
         in_specs=[SMEM, SMEM, VMEM, VMEM],
         out_specs=VMEM,
         compiler_params=pltpu.CompilerParams(vmem_limit_bytes=4 * MIB),
@@ -479,7 +483,7 @@
 
     def one(fragment, carry):
         for r in range(CAP):
-            out[target[fragment, r]] += came[fragment, r]
+            out[target[fragment, r]] += came[fragment, r].astype(jnp.float32)
         return carry
 
     lax.fori_loop(0, came.shape[0], one, 0)
@@ -488,7 +492,7 @@
 def collect(target, came, own_count):
     return pl.pallas_call(
         collect_kernel,
-        out_shape=jax.ShapeDtypeStruct((own_count,) + came.shape[2:], came.dtype),
+        out_shape=jax.ShapeDtypeStruct((own_count,) + came.shape[2:], jnp.float32),
         in_specs=[SMEM, VMEM],
         out_specs=VMEM,
         compiler_params=pltpu.CompilerParams(vmem_limit_bytes=4 * MIB),
@@ -556,7 +560,7 @@
 
     quarter = block // aux_count
     core = aux % 2
-    met = lax.ppermute(sent, "aux", far_pairs)
+    met = lax.ppermute(sent, "aux", far_pairs).astype(jnp.float32)
     both = jnp.concatenate([stay[:1], met[:1], stay[1:] + met[1:]], axis=0)
     sent = lax.dynamic_slice_in_dim(both, (1 - core) * quarter, quarter, 1)
     kept = lax.dynamic_slice_in_dim(both, core * quarter, quarter, 1)

time: 116 us -> 112 us (0.966)
  blocking collectives: 14.2 us -> 12.3 us
  waiting for transfers between devices: 40.9 us -> 39.1 us
    all_to_all x1, blocking collectives: 14.2 us -> 12.3 us  [body(): incoming = lax.all_to_all(outgoing, 'frag', 0, 0, tiled=True)]
    ppermute x1, waiting for transfers between devices: 5.03 us -> 3.29 us  [body(): met = lax.ppermute(sent, 'aux', far_pairs).astype(jnp.float32)]
where the time goes in v10:
time: 112 us
  waiting for transfers between devices  39.1 us (35%)
  Pallas kernels  32.3 us (29%)
  starting transfers between devices  23.7 us (21%)
  blocking collectives  12.3 us (11%)
  local copies, waits for them, and re-layouts  3.53 us (3%)
    pallas_call x4, Pallas kernels, contract(): pl.pallas_call(functools.partial(contract_kernel, stage, block, width), o...  24.5 us
    ppermute x6, waiting for transfers between devices, send(): return lax.ppermute(payload, 'frag', round_pairs(distance, parity, frags))  18.4 us
    ppermute x6, starting transfers between devices, send(): return lax.ppermute(payload, 'frag', round_pairs(distance, parity, frags))  14.3 us
    ppermute x3, waiting for transfers between devices, over_aux(): far = lax.ppermute(here, 'aux', far_pairs)  14 us
    all_to_all x1, blocking collectives, body(): incoming = lax.all_to_all(outgoing, 'frag', 0, 0, tiled=True)  12.3 us
    ppermute x3, starting transfers between devices, over_aux(): far = lax.ppermute(here, 'aux', far_pairs)  4.75 us
    ppermute x1, waiting for transfers between devices, body(): met = lax.ppermute(sent, 'aux', far_pairs).astype(jnp.float32)  3.29 us
  transfers between devices with their start and end apart: 20, of which 8 were waited for; matrix products, arithmetic and copies ran while one was open for 0% of the time, Pallas kernels for 21%

profile of v10, /device:TPU:0, one launch (start us, length us, event | category | flops | bytes accessed | tf_op | source)
XLA Modules:
  0.0 112.0 jit_solution(17587489036494622712)
XLA Ops:
  3.0 1.2 %copy-done = bf16[4,128,1024]{2,1,0:T(8,128)(2,1)S(1)} copy-done((bf16[4,128,1024]{2,1,0:T(8,128)(2,1)S(1)}, bf16[4,128,1024]{2,1,0:T(8,128)(2,1)}, u32[]{:S(2)}) %copy-start) | copy-done | bytes 1048600
  4.2 1.4 %pack_to_send.1 = (bf16[272,1024]{1,0:T(8,128)(2,1)S(1)}, bf16[272,1024]{1,0:T(8,128)(2,1)S(1)}, bf16[272,1024]{1,0:T(8,128)(2,1)S(1)}, bf16[272,1024]{1,0:T(8,1...) custom-call(s32[162]{0:T(256)S(1)} %concatenate.9.ints.where, ...), custom_call_target="tpu_custom_call" | custom-call | tf_op jit(solution)/shard_map/pack_to_send/pallas_call | solution.py:83
  5.7 3.2 %collective-permute-start = (bf16[272,1024]{1,0:T(8,128)(2,1)S(1)}, bf16[272,1024]{1,0:T(8,128)(2,1)S(1)}, u32[]{:S(2)}, u32[]{:S(2)}) collective-permute-start(bf16[272,1024]{1,0:T(8,128)(2,1)S(1)} %get-tuple-element.26), channel_id=1, source_target_pairs={{0,8},{4,12},{16,24},{20,28},{8,0},{12,4},{24,16},{28,20},{1,9},{5... | collective-permute-start | bytes 1671176 | tf_op jit(solution)/shard_map/ppermute | solution.py:536
  8.9 1.5 %collective-permute-start.1 = (bf16[272,1024]{1,0:T(8,128)(2,1)S(1)}, bf16[272,1024]{1,0:T(8,128)(2,1)S(1)}, u32[]{:S(2)}, u32[]{:S(2)}) collective-permute-start(bf16[272,1024]{1,0:T(8,128)(2,1)S(1)} %get-tuple-element.30), channel_id=1, source_target_pairs={{0,4},{8,12},{16,20},{24,28},{4,0},{12,8},{20,16},{28,24},{1,5},{9... | collective-permute-start | bytes 1671176 | tf_op jit(solution)/shard_map/ppermute | solution.py:536
  11.8 1.6 %collective-permute-start.7 = (bf16[272,1024]{1,0:T(8,128)(2,1)S(1)}, bf16[272,1024]{1,0:T(8,128)(2,1)S(1)}, u32[]{:S(2)}, u32[]{:S(2)}) collective-permute-start(bf16[272,1024]{1,0:T(8,128)(2,1)S(1)} %get-tuple-element.38.refs_0_), channel_id=1, source_target_pairs={{0,2},{1,3},{2,0},{3,1},{4,6},{5,7},{6,4},{7,5},{8,10},{9,11},{10,... | collective-permute-start | bytes 1671176 | tf_op jit(solution)/shard_map/ppermute | solution.py:525
  13.4 9.0 %collective-permute-done.refs_2_.refs_3_ = bf16[272,1024]{1,0:T(8,128)(2,1)S(1)} collective-permute-done((bf16[272,1024]{1,0:T(8,128)(2,1)S(1)}, bf16[272,1024]{1,0:T(8,128)(2,1)S(1)}, u32[]{:S(2)}, u32[]{:S(2)}) %collective-permute-start) | collective-permute-done | bytes 557088 | tf_op jit(solution)/shard_map/ppermute | solution.py:536
  22.3 2.2 %plan_lists.1 = (s32[4,8]{1,0:T(4,128)S(1)}, s32[8,2]{1,0:T(8,128)S(1)}) custom-call(s32[162]{0:T(256)S(1)} %concatenate.9.ints.where), custom_call_target="tpu_custom_call" | custom-call | tf_op jit(solution)/shard_map/plan_lists/pallas_call | solution.py:138
  24.5 9.4 %collective-permute-done.1.refs_0_.refs_1_ = bf16[272,1024]{1,0:T(8,128)(2,1)S(1)} collective-permute-done((bf16[272,1024]{1,0:T(8,128)(2,1)S(1)}, bf16[272,1024]{1,0:T(8,128)(2,1)S(1)}, u32[]{:S(2)}, u32[]{:S(2)}) %collective-permute-start.1) | collective-permute-done | bytes 557088 | tf_op jit(solution)/shard_map/ppermute | solution.py:536
  33.9 7.5 %collective-permute-start.4 = (bf16[272,1024]{1,0:T(8,128)(2,1)S(1)}, bf16[272,1024]{1,0:T(8,128)(2,1)S(1)}, u32[]{:S(2)}, u32[]{:S(2)}) collective-permute-start(bf16[272,1024]{1,0:T(8,128)(2,1)S(1)} %get-tuple-element.34), channel_id=1, source_target_pairs={{0,12},{4,16},{8,20},{12,0},{16,4},{20,8},{1,13},{5,17},{9,21},{13... | collective-permute-start | bytes 1671176 | tf_op jit(solution)/shard_map/ppermute | solution.py:536
  42.1 1.6 %collective-permute-start.5 = (bf16[256,1024]{1,0:T(8,128)(2,1)S(1)}, bf16[256,1024]{1,0:T(8,128)(2,1)S(1)}, u32[]{:S(2)}, u32[]{:S(2)}) collective-permute-start(bf16[256,1024]{1,0:T(8,128)(2,1)S(1)} %pack_group.3.refs_4_), channel_id=1, source_target_pairs={{0,2},{1,3},{2,0},{3,1},{4,6},{5,7},{6,4},{7,5},{8,10},{9,11},{10,... | collective-permute-start | bytes 1572872 | tf_op jit(solution)/shard_map/ppermute | solution.py:525
  44.2 9.9 %collective-permute-done.5.refs_5_ = bf16[256,1024]{1,0:T(8,128)(2,1)S(1)} collective-permute-done((bf16[256,1024]{1,0:T(8,128)(2,1)S(1)}, bf16[256,1024]{1,0:T(8,128)(2,1)S(1)}, u32[]{:S(2)}, u32[]{:S(2)}) %collective-permute-start.5) | collective-permute-done | bytes 524320 | tf_op jit(solution)/shard_map/ppermute | solution.py:525
  56.2 1.6 %collective-permute-start.12 = (bf16[256,1024]{1,0:T(8,128)(2,1)S(1)}, bf16[256,1024]{1,0:T(8,128)(2,1)S(1)}, u32[]{:S(2)}, u32[]{:S(2)}) collective-permute-start(bf16[256,1024]{1,0:T(8,128)(2,1)S(1)} %get-tuple-element.41.refs_8_), channel_id=1, source_target_pairs={{0,2},{1,3},{2,0},{3,1},{4,6},{5,7},{6,4},{7,5},{8,10},{9,11},{10,... | collective-permute-start | bytes 1572872 | tf_op jit(solution)/shard_map/ppermute | solution.py:525
  57.8 6.9 %contract.4.refs_16_ = f32[1,128,128]{2,1,0:T(8,128)S(1)} custom-call(s32[162]{0:T(256)S(1)} %concatenate.9.ints.where, s32[4,8]{1,0:T(4,128)S(1)} %get-tuple-element.29.plan, f32[1,3]{1,0:T(1,128)S(1)} %copy-done.2, f32[8,128]{1,0:T(8,128)S(1)} %get-tuple-element.37.energy, bf16[272,1024]{1,0:T(8,128)(2,1)S(1)} %get-tuple-element.38.refs_0_, ...), custom_call_target="tpu_custom_call" | custom-call | tf_op jit(solution)/shard_map/contract/pallas_call | solution.py:443
  66.1 4.1 %collective-permute-done.12.refs_9_ = bf16[256,1024]{1,0:T(8,128)(2,1)S(1)} collective-permute-done((bf16[256,1024]{1,0:T(8,128)(2,1)S(1)}, bf16[256,1024]{1,0:T(8,128)(2,1)S(1)}, u32[]{:S(2)}, u32[]{:S(2)}) %collective-permute-start.12) | collective-permute-done | bytes 524320 | tf_op jit(solution)/shard_map/ppermute | solution.py:525
  70.2 1.5 %collective-permute-start.16 = (bf16[256,1024]{1,0:T(8,128)(2,1)S(1)}, bf16[256,1024]{1,0:T(8,128)(2,1)S(1)}, u32[]{:S(2)}, u32[]{:S(2)}) collective-permute-start(bf16[256,1024]{1,0:T(8,128)(2,1)S(1)} %get-tuple-element.42.refs_12_.refs_13_), channel_id=1, source_target_pairs={{0,2},{1,3},{2,0},{3,1},{4,6},{5,7},{6,4},{7,5},{8,10},{9,11},{10,... | collective-permute-start | bytes 1572872 | tf_op jit(solution)/shard_map/ppermute | solution.py:553
  72.1 4.0 %contract.6.refs_18_ = f32[1536,256]{1,0:T(8,128)S(1)} custom-call(s32[162]{0:T(256)S(1)} %concatenate.9.ints.where, s32[4,8]{1,0:T(4,128)S(1)} %get-tuple-element.29.plan, f32[1,3]{1,0:T(1,128)S(1)} %copy-done.2, f32[8,128]{1,0:T(8,128)S(1)} %get-tuple-element.40.energy, bf16[272,1024]{1,0:T(8,128)(2,1)S(1)} %get-tuple-element.38.refs_0_, ...), custom_call_target="tpu_custom_call" | custom-call | flops 1610612736 | bytes 786432 | tf_op jit(solution)/shard_map/contract/pallas_call | solution.py:443
  76.1 8.6 %contract.5.refs_17_ = f32[4,128,128]{2,1,0:T(8,128)S(1)} custom-call(s32[162]{0:T(256)S(1)} %concatenate.9.ints.where, s32[4,8]{1,0:T(4,128)S(1)} %get-tuple-element.29.plan, f32[1,3]{1,0:T(1,128)S(1)} %copy-done.2, f32[8,128]{1,0:T(8,128)S(1)} %get-tuple-element.37.energy, bf16[272,1024]{1,0:T(8,128)(2,1)S(1)} %get-tuple-element.38.refs_0_, ...), custom_call_target="tpu_custom_call" | custom-call | flops 3221225472 | bytes 1572864 | tf_op jit(solution)/shard_map/contract/pallas_call | solution.py:443
  85.0 1.8 %collective-permute-done.17.refs_15_ = bf16[256,1024]{1,0:T(8,128)(2,1)S(1)} collective-permute-done((bf16[256,1024]{1,0:T(8,128)(2,1)S(1)}, bf16[256,1024]{1,0:T(8,128)(2,1)S(1)}, u32[]{:S(2)}, u32[]{:S(2)}) %collective-permute-start.17) | collective-permute-done | bytes 524320 | tf_op jit(solution)/shard_map/ppermute | solution.py:557
  86.7 5.0 %contract.7 = (bf16[5,64,128]{2,1,0:T(8,128)(2,1)S(1)}, f32[5,64,128]{2,1,0:T(8,128)S(1)}) custom-call(s32[162]{0:T(256)S(1)} %concatenate.9.ints.where, s32[4,8]{1,0:T(4,128)S(1)} %get-tuple-element.29.plan, f32[1,3]{1,0:T(1,128)S(1)} %copy-done.2, f32[8,128]{1,0:T(8,128)S(1)} %get-tuple-element.40.energy, bf16[272,1024]{1,0:T(8,128)(2,1)S(1)} %get-tuple-element.38.refs_0_, ...), custom_call_target="tpu_custom_call" | custom-call | tf_op jit(solution)/shard_map/contract/pallas_call | solution.py:443
  91.7 1.3 %collective-permute-start.18 = (bf16[5,64,128]{2,1,0:T(8,128)(2,1)S(1)}, bf16[5,64,128]{2,1,0:T(8,128)(2,1)S(1)}, u32[]{:S(2)}, u32[]{:S(2)}) collective-permute-start(bf16[5,64,128]{2,1,0:T(8,128)(2,1)S(1)} %get-tuple-element.46), channel_id=1, source_target_pairs={{0,2},{1,3},{2,0},{3,1},{4,6},{5,7},{6,4},{7,5},{8,10},{9,11},{10,... | collective-permute-start | bytes 245768 | tf_op jit(solution)/shard_map/ppermute | solution.py:563
  93.0 3.3 %collective-permute-done.18 = bf16[5,64,128]{2,1,0:T(8,128)(2,1)S(1)} collective-permute-done((bf16[5,64,128]{2,1,0:T(8,128)(2,1)S(1)}, bf16[5,64,128]{2,1,0:T(8,128)(2,1)S(1)}, u32[]{:S(2)}, u32[]{:S(2)}) %collective-permute-start.18) | collective-permute-done | bytes 81952 | tf_op jit(solution)/shard_map/ppermute | solution.py:563
  96.5 1.3 %collective-permute-done.19.came = f32[6,32,128]{2,1,0:T(8,128)S(1)} collective-permute-done((f32[6,32,128]{2,1,0:T(8,128)S(1)}, f32[6,32,128]{2,1,0:T(8,128)S(1)}, u32[]{:S(2)}, u32[]{:S(2)}) %collective-permute-start.19) | collective-permute-done | bytes 98336 | tf_op jit(solution)/shard_map/ppermute | solution.py:567
  98.4 12.3 %all_to_all.5.came = bf16[8,2,32,128]{3,2,1,0:T(8,128)(2,1)S(1)} all-to-all(bf16[8,2,32,128]{3,2,1,0:T(8,128)(2,1)S(1)} %spread.1), channel_id=1, replica_groups=mesh['frag'=8,'aux'=4] {'frag'}, dimensions={0} | all-to-all | bytes 262144 | tf_op jit(solution)/shard_map/all_to_all | solution.py:569
  110.7 1.3 %collect.1 = f32[4,32,128]{2,1,0:T(8,128)} custom-call(s32[8,2]{1,0:T(8,128)S(1)} %get-tuple-element.28.target, bf16[8,2,32,128]{3,2,1,0:T(8,128)(2,1)S(1)} %all_to_all.5.came), custom_call_target="tpu_custom_call" | custom-call | tf_op jit(solution)/shard_map/collect/pallas_call | solution.py:493
  (44 shorter events, 10.4 us)
Async XLA Ops:
  3.0 1.2 %copy-start = (bf16[4,128,1024]{2,1,0:T(8,128)(2,1)S(1)}, bf16[4,128,1024]{2,1,0:T(8,128)(2,1)}, u32[]{:S(2)}) copy-start(bf16[4,128,1024]{2,1,0:T(8,128)(2,1)} %table.1) | copy-start | bytes 3145732
  5.7 49.7 %copy-start.1 = (bf16[4,128]{1,0:T(4,128)(2,1)S(1)}, bf16[4,128]{1,0:T(4,128)(2,1)}, u32[]{:S(2)}) copy-start(bf16[4,128]{1,0:T(4,128)(2,1)} %refs_0_.3) | copy-start | bytes 3076
  5.7 16.6 %collective-permute-start = (bf16[272,1024]{1,0:T(8,128)(2,1)S(1)}, bf16[272,1024]{1,0:T(8,128)(2,1)S(1)}, u32[]{:S(2)}, u32[]{:S(2)}) collective-permute-start(bf16[272,1024]{1,0:T(8,128)(2,1)S(1)} %get-tuple-element.26), channel_id=1, source_target_pairs={{0,8},{4,12},{16,24},{20,28},{8,0},{12,4},{24,16},{28,20},{1,9},{5... | collective-permute-start | bytes 1671176 | tf_op jit(solution)/shard_map/ppermute | solution.py:536
  8.9 25.1 %collective-permute-start.1 = (bf16[272,1024]{1,0:T(8,128)(2,1)S(1)}, bf16[272,1024]{1,0:T(8,128)(2,1)S(1)}, u32[]{:S(2)}, u32[]{:S(2)}) collective-permute-start(bf16[272,1024]{1,0:T(8,128)(2,1)S(1)} %get-tuple-element.30), channel_id=1, source_target_pairs={{0,4},{8,12},{16,20},{24,28},{4,0},{12,8},{20,16},{28,24},{1,5},{9... | collective-permute-start | bytes 1671176 | tf_op jit(solution)/shard_map/ppermute | solution.py:536
  10.4 23.5 %collective-permute-start.2 = (bf16[272,1024]{1,0:T(8,128)(2,1)S(1)}, bf16[272,1024]{1,0:T(8,128)(2,1)S(1)}, u32[]{:S(2)}, u32[]{:S(2)}) collective-permute-start(bf16[272,1024]{1,0:T(8,128)(2,1)S(1)} %get-tuple-element.31), channel_id=1, source_target_pairs={{4,8},{12,16},{20,24},{8,4},{16,12},{24,20},{5,9},{13,17},{21,25},... | collective-permute-start | bytes 1671176 | tf_op jit(solution)/shard_map/ppermute | solution.py:536
  11.1 22.9 %collective-permute-start.3 = (bf16[272,1024]{1,0:T(8,128)(2,1)S(1)}, bf16[272,1024]{1,0:T(8,128)(2,1)S(1)}, u32[]{:S(2)}, u32[]{:S(2)}) collective-permute-start(bf16[272,1024]{1,0:T(8,128)(2,1)S(1)} %get-tuple-element.32), channel_id=1, source_target_pairs={{8,16},{12,20},{16,8},{20,12},{9,17},{13,21},{17,9},{21,13},{10,18... | collective-permute-start | bytes 1671176 | tf_op jit(solution)/shard_map/ppermute | solution.py:536
  11.8 31.9 %collective-permute-start.7 = (bf16[272,1024]{1,0:T(8,128)(2,1)S(1)}, bf16[272,1024]{1,0:T(8,128)(2,1)S(1)}, u32[]{:S(2)}, u32[]{:S(2)}) collective-permute-start(bf16[272,1024]{1,0:T(8,128)(2,1)S(1)} %get-tuple-element.38.refs_0_), channel_id=1, source_target_pairs={{0,2},{1,3},{2,0},{3,1},{4,6},{5,7},{6,4},{7,5},{8,10},{9,11},{10,... | collective-permute-start | bytes 1671176 | tf_op jit(solution)/shard_map/ppermute | solution.py:525
  33.9 21.0 %collective-permute-start.4 = (bf16[272,1024]{1,0:T(8,128)(2,1)S(1)}, bf16[272,1024]{1,0:T(8,128)(2,1)S(1)}, u32[]{:S(2)}, u32[]{:S(2)}) collective-permute-start(bf16[272,1024]{1,0:T(8,128)(2,1)S(1)} %get-tuple-element.34), channel_id=1, source_target_pairs={{0,12},{4,16},{8,20},{12,0},{16,4},{20,8},{1,13},{5,17},{9,21},{13... | collective-permute-start | bytes 1671176 | tf_op jit(solution)/shard_map/ppermute | solution.py:536
  42.1 15.7 %copy-start.2 = (f32[1,3]{1,0:T(1,128)S(1)}, f32[1,3]{1,0:T(1,128)}, u32[]{:S(2)}) copy-start(f32[1,3]{1,0:T(1,128)} %levels.7) | copy-start | bytes 40
  42.1 12.0 %collective-permute-start.5 = (bf16[256,1024]{1,0:T(8,128)(2,1)S(1)}, bf16[256,1024]{1,0:T(8,128)(2,1)S(1)}, u32[]{:S(2)}, u32[]{:S(2)}) collective-permute-start(bf16[256,1024]{1,0:T(8,128)(2,1)S(1)} %pack_group.3.refs_4_), channel_id=1, source_target_pairs={{0,2},{1,3},{2,0},{3,1},{4,6},{5,7},{6,4},{7,5},{8,10},{9,11},{10,... | collective-permute-start | bytes 1572872 | tf_op jit(solution)/shard_map/ppermute | solution.py:525
  43.7 12.5 %collective-permute-start.8 = (bf16[272,1024]{1,0:T(8,128)(2,1)S(1)}, bf16[272,1024]{1,0:T(8,128)(2,1)S(1)}, u32[]{:S(2)}, u32[]{:S(2)}) collective-permute-start(bf16[272,1024]{1,0:T(8,128)(2,1)S(1)} %get-tuple-element.38.refs_0_), channel_id=1, source_target_pairs={{0,1},{1,0},{2,3},{3,2},{4,5},{5,4},{6,7},{7,6},{8,9},{9,8},{10,11... | collective-permute-start | bytes 1671176 | tf_op jit(solution)/shard_map/ppermute | solution.py:526
  43.7 14.1 %collective-permute-start.9 = (bf16[272,1024]{1,0:T(8,128)(2,1)S(1)}, bf16[272,1024]{1,0:T(8,128)(2,1)S(1)}, u32[]{:S(2)}, u32[]{:S(2)}) collective-permute-start(bf16[272,1024]{1,0:T(8,128)(2,1)S(1)} %collective-permute-done.7.refs_1_), channel_id=1, source_target_pairs={{0,1},{1,0},{2,3},{3,2},{4,5},{5,4},{6,7},{7,6},{8,9},{9,8},{10,11... | collective-permute-start | bytes 1671176 | tf_op jit(solution)/shard_map/ppermute | solution.py:528
  54.1 10.5 %collective-permute-start.6 = (bf16[272,1024]{1,0:T(8,128)(2,1)S(1)}, bf16[272,1024]{1,0:T(8,128)(2,1)S(1)}, u32[]{:S(2)}, u32[]{:S(2)}) collective-permute-start(bf16[272,1024]{1,0:T(8,128)(2,1)S(1)} %get-tuple-element.36), channel_id=1, source_target_pairs={{12,24},{16,28},{24,12},{28,16},{13,25},{17,29},{25,13},{29,17},{1... | collective-permute-start | bytes 1671176 | tf_op jit(solution)/shard_map/ppermute | solution.py:536
  54.8 3.0 %collective-permute-start.10 = (bf16[256,1024]{1,0:T(8,128)(2,1)S(1)}, bf16[256,1024]{1,0:T(8,128)(2,1)S(1)}, u32[]{:S(2)}, u32[]{:S(2)}) collective-permute-start(bf16[256,1024]{1,0:T(8,128)(2,1)S(1)} %pack_group.3.refs_4_), channel_id=1, source_target_pairs={{0,1},{1,0},{2,3},{3,2},{4,5},{5,4},{6,7},{7,6},{8,9},{9,8},{10,11... | collective-permute-start | bytes 1572872 | tf_op jit(solution)/shard_map/ppermute | solution.py:526
  54.9 2.9 %collective-permute-start.11 = (bf16[256,1024]{1,0:T(8,128)(2,1)S(1)}, bf16[256,1024]{1,0:T(8,128)(2,1)S(1)}, u32[]{:S(2)}, u32[]{:S(2)}) collective-permute-start(bf16[256,1024]{1,0:T(8,128)(2,1)S(1)} %collective-permute-done.5.refs_5_), channel_id=1, source_target_pairs={{0,1},{1,0},{2,3},{3,2},{4,5},{5,4},{6,7},{7,6},{8,9},{9,8},{10,11... | collective-permute-start | bytes 1572872 | tf_op jit(solution)/shard_map/ppermute | solution.py:528
  56.2 14.0 %collective-permute-start.12 = (bf16[256,1024]{1,0:T(8,128)(2,1)S(1)}, bf16[256,1024]{1,0:T(8,128)(2,1)S(1)}, u32[]{:S(2)}, u32[]{:S(2)}) collective-permute-start(bf16[256,1024]{1,0:T(8,128)(2,1)S(1)} %get-tuple-element.41.refs_8_), channel_id=1, source_target_pairs={{0,2},{1,3},{2,0},{3,1},{4,6},{5,7},{6,4},{7,5},{8,10},{9,11},{10,... | collective-permute-start | bytes 1572872 | tf_op jit(solution)/shard_map/ppermute | solution.py:525
  65.5 4.7 %collective-permute-start.14 = (bf16[256,1024]{1,0:T(8,128)(2,1)S(1)}, bf16[256,1024]{1,0:T(8,128)(2,1)S(1)}, u32[]{:S(2)}, u32[]{:S(2)}) collective-permute-start(bf16[256,1024]{1,0:T(8,128)(2,1)S(1)} %get-tuple-element.42.refs_12_.refs_13_), channel_id=1, source_target_pairs={{0,1},{1,0},{2,3},{3,2},{4,5},{5,4},{6,7},{7,6},{8,9},{9,8},{10,11... | collective-permute-start | bytes 1572872 | tf_op jit(solution)/shard_map/ppermute | solution.py:552
  65.6 6.1 %collective-permute-start.13 = (bf16[256,1024]{1,0:T(8,128)(2,1)S(1)}, bf16[256,1024]{1,0:T(8,128)(2,1)S(1)}, u32[]{:S(2)}, u32[]{:S(2)}) collective-permute-start(bf16[256,1024]{1,0:T(8,128)(2,1)S(1)} %get-tuple-element.41.refs_8_), channel_id=1, source_target_pairs={{0,1},{1,0},{2,3},{3,2},{4,5},{5,4},{6,7},{7,6},{8,9},{9,8},{10,11... | collective-permute-start | bytes 1572872 | tf_op jit(solution)/shard_map/ppermute | solution.py:526
  70.2 1.9 %collective-permute-start.15 = (bf16[256,1024]{1,0:T(8,128)(2,1)S(1)}, bf16[256,1024]{1,0:T(8,128)(2,1)S(1)}, u32[]{:S(2)}, u32[]{:S(2)}) collective-permute-start(bf16[256,1024]{1,0:T(8,128)(2,1)S(1)} %collective-permute-done.12.refs_9_), channel_id=1, source_target_pairs={{0,1},{1,0},{2,3},{3,2},{4,5},{5,4},{6,7},{7,6},{8,9},{9,8},{10,11... | collective-permute-start | bytes 1572872 | tf_op jit(solution)/shard_map/ppermute | solution.py:528
  70.2 14.6 %collective-permute-start.16 = (bf16[256,1024]{1,0:T(8,128)(2,1)S(1)}, bf16[256,1024]{1,0:T(8,128)(2,1)S(1)}, u32[]{:S(2)}, u32[]{:S(2)}) collective-permute-start(bf16[256,1024]{1,0:T(8,128)(2,1)S(1)} %get-tuple-element.42.refs_12_.refs_13_), channel_id=1, source_target_pairs={{0,2},{1,3},{2,0},{3,1},{4,6},{5,7},{6,4},{7,5},{8,10},{9,11},{10,... | collective-permute-start | bytes 1572872 | tf_op jit(solution)/shard_map/ppermute | solution.py:553
  84.8 2.0 %collective-permute-start.17 = (bf16[256,1024]{1,0:T(8,128)(2,1)S(1)}, bf16[256,1024]{1,0:T(8,128)(2,1)S(1)}, u32[]{:S(2)}, u32[]{:S(2)}) collective-permute-start(bf16[256,1024]{1,0:T(8,128)(2,1)S(1)} %collective-permute-done.16.refs_13_), channel_id=1, source_target_pairs={{0,1},{1,0},{2,3},{3,2},{4,5},{5,4},{6,7},{7,6},{8,9},{9,8},{10,11... | collective-permute-start | bytes 1572872 | tf_op jit(solution)/shard_map/ppermute | solution.py:557
  91.7 4.6 %collective-permute-start.18 = (bf16[5,64,128]{2,1,0:T(8,128)(2,1)S(1)}, bf16[5,64,128]{2,1,0:T(8,128)(2,1)S(1)}, u32[]{:S(2)}, u32[]{:S(2)}) collective-permute-start(bf16[5,64,128]{2,1,0:T(8,128)(2,1)S(1)} %get-tuple-element.46), channel_id=1, source_target_pairs={{0,2},{1,3},{2,0},{3,1},{4,6},{5,7},{6,4},{7,5},{8,10},{9,11},{10,... | collective-permute-start | bytes 245768 | tf_op jit(solution)/shard_map/ppermute | solution.py:563
  96.4 1.4 %collective-permute-start.19 = (f32[6,32,128]{2,1,0:T(8,128)S(1)}, f32[6,32,128]{2,1,0:T(8,128)S(1)}, u32[]{:S(2)}, u32[]{:S(2)}) collective-permute-start(f32[6,32,128]{2,1,0:T(8,128)S(1)} %get-tuple-element.47), channel_id=1, source_target_pairs={{0,1},{1,0},{2,3},{3,2},{4,5},{5,4},{6,7},{7,6},{8,9},{9,8},{10,11... | collective-permute-start | bytes 294920 | tf_op jit(solution)/shard_map/ppermute | solution.py:567

commit v11 on v10

--- a/solution.py
+++ b/solution.py
@@ -24,16 +24,13 @@
 
 
 class Lists:
-    def __init__(self, ref, frags, own_count, list_len):
-        self.ref, self.frags, self.own_count, self.list_len = ref, frags, own_count, list_len
-        self.listed = 2 + frags * own_count
-        self.me, self.aux = ref[0], ref[1]
+    def __init__(self, ints, listed, frags, own_count, list_len):
+        self.ints, self.listed = ints, listed
+        self.frags, self.own_count, self.list_len = frags, own_count, list_len
+        self.me = ints[0]
 
     def row(self, fragment, k):
-        return self.ref[2 + self.ref[self.listed + fragment * self.list_len + k]]
-
-    def live(self, fragment, k):
-        return self.ref[self.listed + (self.frags + fragment) * self.list_len + k]
+        return self.ints[2 + self.listed[fragment, k]]
 
     def pick(self, fragment, owner):
         count = jnp.int32(0)
@@ -47,9 +44,9 @@
         return picked, count
 
 
-def send_kernel(sizes, ints, tails, table, *refs):
+def send_kernel(sizes, ints, listed, tails, table, *refs):
     outs, own, sems = refs[:6], refs[6], refs[7]
-    lists = Lists(ints, *sizes)
+    lists = Lists(ints, listed, *sizes)
     me, frags = lists.me, lists.frags
     block = table.shape[1]
     copies = []
@@ -77,23 +74,23 @@
         pl.when(needed)(copy.wait)
 
 
-def pack_to_send(ints, tails, table, sizes):
+def pack_to_send(ints, vir_list, tails, table, sizes):
     _, block_rows, cols = table.shape
     part = jax.ShapeDtypeStruct((CAP * block_rows + TAIL, cols), table.dtype)
     return pl.pallas_call(
         functools.partial(send_kernel, sizes),
         out_shape=(part,) * 7,
-        in_specs=[SMEM, VMEM, ANY],
+        in_specs=[SMEM, SMEM, VMEM, ANY],
         out_specs=(VMEM,) * 7,
         scratch_shapes=[pltpu.SemaphoreType.DMA((7, CAP))],
         compiler_params=pltpu.CompilerParams(vmem_limit_bytes=8 * MIB),
         cost_estimate=NO_COST,
         name="pack_to_send",
-    )(ints, tails, table)
-
-
-def plan_kernel(sizes, ints, plan, target):
-    lists = Lists(ints, *sizes)
+    )(ints, vir_list, tails, table)
+
+
+def plan_kernel(sizes, ints, listed, plan, target):
+    lists = Lists(ints, listed, *sizes)
     me, (frags, own_count, list_len) = lists.me, sizes
     rows, owners, codes, classes = [], [], [], []
     for k in range(list_len):
@@ -122,7 +119,7 @@
         plan[0, place] = codes[k]
         plan[1, place] = rank
         plan[2, place] = rows[k]
-        plan[3, place] = lists.live(me, k)
+        plan[3, place] = jnp.int32(k)
 
     def one(fragment, carry):
         picked, _ = lists.pick(fragment, me)
@@ -133,7 +130,7 @@
     lax.fori_loop(0, frags, one, 0)
 
 
-def plan_lists(ints, sizes):
+def plan_lists(ints, vir_list, sizes):
     frags, _, list_len = sizes
     return pl.pallas_call(
         functools.partial(plan_kernel, sizes),
@@ -141,12 +138,12 @@
             jax.ShapeDtypeStruct((4, list_len), jnp.int32),
             jax.ShapeDtypeStruct((frags, CAP), jnp.int32),
         ),
-        in_specs=[SMEM],
+        in_specs=[SMEM, SMEM],
         out_specs=(SMEM, SMEM),
         compiler_params=pltpu.CompilerParams(vmem_limit_bytes=4 * MIB),
         cost_estimate=NO_COST,
         name="plan_lists",
-    )(ints)
+    )(ints, vir_list)
 
 
 def pack_kernel(first, codes, block, with_energy, plan, *refs):
@@ -228,7 +225,7 @@
     return aux + 4 * b
 
 
-def contract_kernel(stage, block, width, where, plan, levels, energy, *refs):
+def contract_kernel(stage, block, width, where, plan, levels, rows_ref, energy, *refs):
     groups = min(stage + 2, 4)
     parts, rest = refs[: groups * 4], refs[groups * 4 :]
     quarters = {2: (0, 2), 3: (1, 3)}.get(stage, (0, 1, 2, 3))
@@ -334,11 +331,11 @@
         for b in range(row_count):
             own_row = energy[pl.ds(places[b], 1), :]
             own_energy = jnp.transpose(jnp.broadcast_to(own_row, (block, block)))
-            own_live = sub < plan[3, places[b]]
+            own_live = sub < rows_ref[where[0], plan[3, places[b]]]
             for q in range(2 * len(group_list)):
                 place = 2 * group_list[q // 2] + q % 2
                 their_energy = energy[place : place + 1, :]
-                live = own_live & (lane < plan[3, place])
+                live = own_live & (lane < rows_ref[where[0], plan[3, place]])
                 for p, (i, j) in enumerate(PAIRS):
                     gap = (levels[0, i] + levels[0, j]) - own_energy - their_energy
                     rows = pl.ds((p * row_count + b) * block, block)
@@ -396,7 +393,7 @@
         sent[...] = away.astype(jnp.bfloat16)
 
 
-def contract(stage, where, plan, levels, energy, parts, before=()):
+def contract(stage, where, plan, levels, vir_rows, energy, parts, before=()):
     block, width = energy.shape[1], parts[0].shape[1]
     height = len(PAIRS) * 2 * block
     span = (4, 2, 2, 2)[stage] * block
@@ -443,13 +440,13 @@
     return pl.pallas_call(
         functools.partial(contract_kernel, stage, block, width),
         out_shape=out_shape,
-        in_specs=[SMEM] * 3 + [VMEM] + [ANY] * len(parts) + [VMEM] * len(before),
+        in_specs=[SMEM] * 4 + [VMEM] + [ANY] * len(parts) + [VMEM] * len(before),
         out_specs=out_specs,
         scratch_shapes=scratch,
         compiler_params=pltpu.CompilerParams(vmem_limit_bytes=26 * MIB),
         cost_estimate=cost,
         name="contract",
-    )(where, plan, levels, energy, *parts, *before)
+    )(where, plan, levels, vir_rows, energy, *parts, *before)
 
 
 def spread_kernel(own_count, where, plan, kept, came, out):
@@ -508,9 +505,7 @@
     own_count, block, width = vir_grid.shape
     list_len = vir_list.shape[1]
     sizes = (frags, own_count, list_len)
-    ints = jnp.concatenate(
-        [me[None], aux[None], owner_map, vir_list.reshape(-1), vir_rows.reshape(-1)]
-    )
+    ints = jnp.concatenate([me[None], aux[None], owner_map])
     occ_count = occ_grid.shape[1]
     tails = jnp.concatenate([
         jnp.pad(occ_grid[0], ((0, TAIL - occ_count), (0, 0))),
@@ -519,7 +514,7 @@
     far_pairs = [(i, i ^ 2) for i in range(aux_count)]
     near_pairs = [(i, i ^ 1) for i in range(aux_count)]
 
-    *outgoing, own = pack_to_send(ints, tails, vir_grid, sizes)
+    *outgoing, own = pack_to_send(ints, vir_list, tails, vir_grid, sizes)
 
     def over_aux(here, *others):
         far = lax.ppermute(here, "aux", far_pairs)
@@ -538,14 +533,14 @@
     arrived = {code: send(code - 1) for code in (1, 2, 3, 4)}
     parts = over_aux(own)
     arrived[5] = send(4, *(arrived[c] for c in (1, 2, 3, 4)))
-    plan, target = plan_lists(after(ints, arrived[3]), sizes)
+    plan, target = plan_lists(after(ints, arrived[3]), vir_list, sizes)
     here = pack_group(2, block, plan, {c: arrived[c] for c in range(1, 5)})[0]
     parts += over_aux(here)
     arrived[6] = send(5, parts[5])
     here, early_energy = pack_group(
         4, block, plan, {c: arrived[c] for c in range(1, 6)}, vir_energy
     )
-    shared = (ints, plan, occ_energy)
+    shared = (ints, plan, occ_energy, vir_rows)
     first = contract(0, *shared, early_energy, parts[:8])
     arrived[6] = after(arrived[6], first)
     last, energy = pack_group(6, block, plan, arrived, vir_energy)

time: 112 us -> 112 us (level)
  local copies, waits for them, and re-layouts: 3.53 us -> 1.96 us
    reshape x2 -> x0, local copies, waits for them, and re-layouts: 1.53 us -> none  [the longest x1 0.77 us: body(): vir_rows.reshape(-1)]
  transfers between devices with their start and end apart: 20 -> 20, of which waited for: 8 -> 8; matrix products, arithmetic and copies ran while one was open for 0% -> 0% of each run, Pallas kernels for 21% -> 22%
where the time goes in v11:
time: 112 us; the launch traced here: 111 us
  waiting for transfers between devices  39.2 us (35%)
  Pallas kernels  32.7 us (29%)
  starting transfers between devices  23.5 us (21%)
  blocking collectives  12.3 us (11%)
  local copies, waits for them, and re-layouts  1.96 us (2%)
  other arithmetic  1.5 us (1%)
    pallas_call x4, Pallas kernels, contract(): pl.pallas_call(functools.partial(contract_kernel, stage, block, width), o...  24.8 us
    ppermute x6, waiting for transfers between devices, send(): return lax.ppermute(payload, 'frag', round_pairs(distance, parity, frags))  18.3 us
    ppermute x6, starting transfers between devices, send(): return lax.ppermute(payload, 'frag', round_pairs(distance, parity, frags))  14.2 us
    ppermute x3, waiting for transfers between devices, over_aux(): far = lax.ppermute(here, 'aux', far_pairs)  13.9 us
    all_to_all x1, blocking collectives, body(): incoming = lax.all_to_all(outgoing, 'frag', 0, 0, tiled=True)  12.3 us
    ppermute x3, starting transfers between devices, over_aux(): far = lax.ppermute(here, 'aux', far_pairs)  4.75 us
    ppermute x1, waiting for transfers between devices, body(): met = lax.ppermute(sent, 'aux', far_pairs).astype(jnp.float32)  3.41 us
  transfers between devices with their start and end apart: 20, of which 8 were waited for; matrix products, arithmetic and copies ran while one was open for 0% of the time, Pallas kernels for 22%

profile of v11, /device:TPU:0, one launch (start us, length us, event | category | flops | bytes accessed | tf_op | source)
XLA Modules:
  0.0 111.4 jit_solution(15051898969109599817)
XLA Ops:
  1.5 1.2 %copy-done = bf16[4,128,1024]{2,1,0:T(8,128)(2,1)S(1)} copy-done((bf16[4,128,1024]{2,1,0:T(8,128)(2,1)S(1)}, bf16[4,128,1024]{2,1,0:T(8,128)(2,1)}, u32[]{:S(2)}) %copy-start) | copy-done | bytes 1048600
  3.4 1.5 %pack_to_send.1 = (bf16[272,1024]{1,0:T(8,128)(2,1)S(1)}, bf16[272,1024]{1,0:T(8,128)(2,1)S(1)}, bf16[272,1024]{1,0:T(8,128)(2,1)S(1)}, bf16[272,1024]{1,0:T(8,1...) custom-call(s32[34]{0:T(128)S(1)} %pad_add_fusion.ints.where, ...), custom_call_target="tpu_custom_call" | custom-call | tf_op jit(solution)/shard_map/pack_to_send/pallas_call | solution.py:80
  4.9 3.1 %collective-permute-start = (bf16[272,1024]{1,0:T(8,128)(2,1)S(1)}, bf16[272,1024]{1,0:T(8,128)(2,1)S(1)}, u32[]{:S(2)}, u32[]{:S(2)}) collective-permute-start(bf16[272,1024]{1,0:T(8,128)(2,1)S(1)} %get-tuple-element.26), channel_id=1, source_target_pairs={{0,8},{4,12},{16,24},{20,28},{8,0},{12,4},{24,16},{28,20},{1,9},{5... | collective-permute-start | bytes 1671176 | tf_op jit(solution)/shard_map/ppermute | solution.py:531
  8.0 1.5 %collective-permute-start.1 = (bf16[272,1024]{1,0:T(8,128)(2,1)S(1)}, bf16[272,1024]{1,0:T(8,128)(2,1)S(1)}, u32[]{:S(2)}, u32[]{:S(2)}) collective-permute-start(bf16[272,1024]{1,0:T(8,128)(2,1)S(1)} %get-tuple-element.30), channel_id=1, source_target_pairs={{0,4},{8,12},{16,20},{24,28},{4,0},{12,8},{20,16},{28,24},{1,5},{9... | collective-permute-start | bytes 1671176 | tf_op jit(solution)/shard_map/ppermute | solution.py:531
  11.0 1.6 %collective-permute-start.7 = (bf16[272,1024]{1,0:T(8,128)(2,1)S(1)}, bf16[272,1024]{1,0:T(8,128)(2,1)S(1)}, u32[]{:S(2)}, u32[]{:S(2)}) collective-permute-start(bf16[272,1024]{1,0:T(8,128)(2,1)S(1)} %get-tuple-element.38.refs_0_), channel_id=1, source_target_pairs={{0,2},{1,3},{2,0},{3,1},{4,6},{5,7},{6,4},{7,5},{8,10},{9,11},{10,... | collective-permute-start | bytes 1671176 | tf_op jit(solution)/shard_map/ppermute | solution.py:520
  12.6 8.9 %collective-permute-done.refs_2_.refs_3_ = bf16[272,1024]{1,0:T(8,128)(2,1)S(1)} collective-permute-done((bf16[272,1024]{1,0:T(8,128)(2,1)S(1)}, bf16[272,1024]{1,0:T(8,128)(2,1)S(1)}, u32[]{:S(2)}, u32[]{:S(2)}) %collective-permute-start) | collective-permute-done | bytes 557088 | tf_op jit(solution)/shard_map/ppermute | solution.py:531
  21.5 2.2 %plan_lists.1 = (s32[4,8]{1,0:T(4,128)S(1)}, s32[8,2]{1,0:T(8,128)S(1)}) custom-call(s32[34]{0:T(128)S(1)} %pad_add_fusion.ints.where, s32[8,8]{1,0:T(8,128)S(1)} %copy-done.2), custom_call_target="tpu_custom_call" | custom-call | tf_op jit(solution)/shard_map/plan_lists/pallas_call | solution.py:135
  23.7 9.4 %collective-permute-done.1.refs_0_.refs_1_ = bf16[272,1024]{1,0:T(8,128)(2,1)S(1)} collective-permute-done((bf16[272,1024]{1,0:T(8,128)(2,1)S(1)}, bf16[272,1024]{1,0:T(8,128)(2,1)S(1)}, u32[]{:S(2)}, u32[]{:S(2)}) %collective-permute-start.1) | collective-permute-done | bytes 557088 | tf_op jit(solution)/shard_map/ppermute | solution.py:531
  33.1 7.5 %collective-permute-start.4 = (bf16[272,1024]{1,0:T(8,128)(2,1)S(1)}, bf16[272,1024]{1,0:T(8,128)(2,1)S(1)}, u32[]{:S(2)}, u32[]{:S(2)}) collective-permute-start(bf16[272,1024]{1,0:T(8,128)(2,1)S(1)} %get-tuple-element.34), channel_id=1, source_target_pairs={{0,12},{4,16},{8,20},{12,0},{16,4},{20,8},{1,13},{5,17},{9,21},{13... | collective-permute-start | bytes 1671176 | tf_op jit(solution)/shard_map/ppermute | solution.py:531
  41.3 1.6 %collective-permute-start.5 = (bf16[256,1024]{1,0:T(8,128)(2,1)S(1)}, bf16[256,1024]{1,0:T(8,128)(2,1)S(1)}, u32[]{:S(2)}, u32[]{:S(2)}) collective-permute-start(bf16[256,1024]{1,0:T(8,128)(2,1)S(1)} %pack_group.3.refs_4_), channel_id=1, source_target_pairs={{0,2},{1,3},{2,0},{3,1},{4,6},{5,7},{6,4},{7,5},{8,10},{9,11},{10,... | collective-permute-start | bytes 1572872 | tf_op jit(solution)/shard_map/ppermute | solution.py:520
  43.4 9.9 %collective-permute-done.5.refs_5_ = bf16[256,1024]{1,0:T(8,128)(2,1)S(1)} collective-permute-done((bf16[256,1024]{1,0:T(8,128)(2,1)S(1)}, bf16[256,1024]{1,0:T(8,128)(2,1)S(1)}, u32[]{:S(2)}, u32[]{:S(2)}) %collective-permute-start.5) | collective-permute-done | bytes 524320 | tf_op jit(solution)/shard_map/ppermute | solution.py:520
  55.4 1.6 %collective-permute-start.12 = (bf16[256,1024]{1,0:T(8,128)(2,1)S(1)}, bf16[256,1024]{1,0:T(8,128)(2,1)S(1)}, u32[]{:S(2)}, u32[]{:S(2)}) collective-permute-start(bf16[256,1024]{1,0:T(8,128)(2,1)S(1)} %get-tuple-element.41.refs_8_), channel_id=1, source_target_pairs={{0,2},{1,3},{2,0},{3,1},{4,6},{5,7},{6,4},{7,5},{8,10},{9,11},{10,... | collective-permute-start | bytes 1572872 | tf_op jit(solution)/shard_map/ppermute | solution.py:520
  57.0 6.9 %contract.4.refs_16_ = f32[1,128,128]{2,1,0:T(8,128)S(1)} custom-call(s32[34]{0:T(128)S(1)} %pad_add_fusion.ints.where, s32[4,8]{1,0:T(4,128)S(1)} %get-tuple-element.29.plan, f32[1,3]{1,0:T(1,128)S(1)} %copy-done.4, s32[8,8]{1,0:T(8,128)S(1)} %copy-done.1, f32[8,128]{1,0:T(8,128)S(1)} %get-tuple-element.37.energy, ...), custom_call_target="tpu_custom_call" | custom-call | tf_op jit(solution)/shard_map/contract/pallas_call | solution.py:440
  65.4 4.0 %collective-permute-done.12.refs_9_ = bf16[256,1024]{1,0:T(8,128)(2,1)S(1)} collective-permute-done((bf16[256,1024]{1,0:T(8,128)(2,1)S(1)}, bf16[256,1024]{1,0:T(8,128)(2,1)S(1)}, u32[]{:S(2)}, u32[]{:S(2)}) %collective-permute-start.12) | collective-permute-done | bytes 524320 | tf_op jit(solution)/shard_map/ppermute | solution.py:520
  69.4 1.5 %collective-permute-start.16 = (bf16[256,1024]{1,0:T(8,128)(2,1)S(1)}, bf16[256,1024]{1,0:T(8,128)(2,1)S(1)}, u32[]{:S(2)}, u32[]{:S(2)}) collective-permute-start(bf16[256,1024]{1,0:T(8,128)(2,1)S(1)} %get-tuple-element.42.refs_12_.refs_13_), channel_id=1, source_target_pairs={{0,2},{1,3},{2,0},{3,1},{4,6},{5,7},{6,4},{7,5},{8,10},{9,11},{10,... | collective-permute-start | bytes 1572872 | tf_op jit(solution)/shard_map/ppermute | solution.py:548
  71.3 4.1 %contract.6.refs_18_ = f32[1536,256]{1,0:T(8,128)S(1)} custom-call(s32[34]{0:T(128)S(1)} %pad_add_fusion.ints.where, s32[4,8]{1,0:T(4,128)S(1)} %get-tuple-element.29.plan, f32[1,3]{1,0:T(1,128)S(1)} %copy-done.4, s32[8,8]{1,0:T(8,128)S(1)} %copy-done.1, f32[8,128]{1,0:T(8,128)S(1)} %get-tuple-element.40.energy, ...), custom_call_target="tpu_custom_call" | custom-call | flops 1610612736 | bytes 786432 | tf_op jit(solution)/shard_map/contract/pallas_call | solution.py:440
  75.4 8.7 %contract.5.refs_17_ = f32[4,128,128]{2,1,0:T(8,128)S(1)} custom-call(s32[34]{0:T(128)S(1)} %pad_add_fusion.ints.where, s32[4,8]{1,0:T(4,128)S(1)} %get-tuple-element.29.plan, f32[1,3]{1,0:T(1,128)S(1)} %copy-done.4, s32[8,8]{1,0:T(8,128)S(1)} %copy-done.1, f32[8,128]{1,0:T(8,128)S(1)} %get-tuple-element.37.energy, ...), custom_call_target="tpu_custom_call" | custom-call | flops 3221225472 | bytes 1572864 | tf_op jit(solution)/shard_map/contract/pallas_call | solution.py:440
  84.3 1.8 %collective-permute-done.17.refs_15_ = bf16[256,1024]{1,0:T(8,128)(2,1)S(1)} collective-permute-done((bf16[256,1024]{1,0:T(8,128)(2,1)S(1)}, bf16[256,1024]{1,0:T(8,128)(2,1)S(1)}, u32[]{:S(2)}, u32[]{:S(2)}) %collective-permute-start.17) | collective-permute-done | bytes 524320 | tf_op jit(solution)/shard_map/ppermute | solution.py:552
  86.1 5.1 %contract.7 = (bf16[5,64,128]{2,1,0:T(8,128)(2,1)S(1)}, f32[5,64,128]{2,1,0:T(8,128)S(1)}) custom-call(s32[34]{0:T(128)S(1)} %pad_add_fusion.ints.where, s32[4,8]{1,0:T(4,128)S(1)} %get-tuple-element.29.plan, f32[1,3]{1,0:T(1,128)S(1)} %copy-done.4, s32[8,8]{1,0:T(8,128)S(1)} %copy-done.1, f32[8,128]{1,0:T(8,128)S(1)} %get-tuple-element.40.energy, ...), custom_call_target="tpu_custom_call" | custom-call | tf_op jit(solution)/shard_map/contract/pallas_call | solution.py:440
  91.1 1.1 %collective-permute-start.18 = (bf16[5,64,128]{2,1,0:T(8,128)(2,1)S(1)}, bf16[5,64,128]{2,1,0:T(8,128)(2,1)S(1)}, u32[]{:S(2)}, u32[]{:S(2)}) collective-permute-start(bf16[5,64,128]{2,1,0:T(8,128)(2,1)S(1)} %get-tuple-element.46), channel_id=1, source_target_pairs={{0,2},{1,3},{2,0},{3,1},{4,6},{5,7},{6,4},{7,5},{8,10},{9,11},{10,... | collective-permute-start | bytes 245768 | tf_op jit(solution)/shard_map/ppermute | solution.py:558
  92.3 3.4 %collective-permute-done.18 = bf16[5,64,128]{2,1,0:T(8,128)(2,1)S(1)} collective-permute-done((bf16[5,64,128]{2,1,0:T(8,128)(2,1)S(1)}, bf16[5,64,128]{2,1,0:T(8,128)(2,1)S(1)}, u32[]{:S(2)}, u32[]{:S(2)}) %collective-permute-start.18) | collective-permute-done | bytes 81952 | tf_op jit(solution)/shard_map/ppermute | solution.py:558
  95.9 1.3 %collective-permute-done.19.came = f32[6,32,128]{2,1,0:T(8,128)S(1)} collective-permute-done((f32[6,32,128]{2,1,0:T(8,128)S(1)}, f32[6,32,128]{2,1,0:T(8,128)S(1)}, u32[]{:S(2)}, u32[]{:S(2)}) %collective-permute-start.19) | collective-permute-done | bytes 98336 | tf_op jit(solution)/shard_map/ppermute | solution.py:562
  97.8 12.3 %all_to_all.5.came = bf16[8,2,32,128]{3,2,1,0:T(8,128)(2,1)S(1)} all-to-all(bf16[8,2,32,128]{3,2,1,0:T(8,128)(2,1)S(1)} %spread.1), channel_id=1, replica_groups=mesh['frag'=8,'aux'=4] {'frag'}, dimensions={0} | all-to-all | bytes 262144 | tf_op jit(solution)/shard_map/all_to_all | solution.py:564
  110.1 1.3 %collect.1 = f32[4,32,128]{2,1,0:T(8,128)} custom-call(s32[8,2]{1,0:T(8,128)S(1)} %get-tuple-element.28.target, bf16[8,2,32,128]{3,2,1,0:T(8,128)(2,1)S(1)} %all_to_all.5.came), custom_call_target="tpu_custom_call" | custom-call | tf_op jit(solution)/shard_map/collect/pallas_call | solution.py:490
  (46 shorter events, 9.5 us)
Async XLA Ops:
  1.5 1.2 %copy-start = (bf16[4,128,1024]{2,1,0:T(8,128)(2,1)S(1)}, bf16[4,128,1024]{2,1,0:T(8,128)(2,1)}, u32[]{:S(2)}) copy-start(bf16[4,128,1024]{2,1,0:T(8,128)(2,1)} %table.1) | copy-start | bytes 3145732
  4.9 49.7 %copy-start.3 = (bf16[4,128]{1,0:T(4,128)(2,1)S(1)}, bf16[4,128]{1,0:T(4,128)(2,1)}, u32[]{:S(2)}) copy-start(bf16[4,128]{1,0:T(4,128)(2,1)} %refs_0_.3) | copy-start | bytes 3076
  4.9 16.6 %collective-permute-start = (bf16[272,1024]{1,0:T(8,128)(2,1)S(1)}, bf16[272,1024]{1,0:T(8,128)(2,1)S(1)}, u32[]{:S(2)}, u32[]{:S(2)}) collective-permute-start(bf16[272,1024]{1,0:T(8,128)(2,1)S(1)} %get-tuple-element.26), channel_id=1, source_target_pairs={{0,8},{4,12},{16,24},{20,28},{8,0},{12,4},{24,16},{28,20},{1,9},{5... | collective-permute-start | bytes 1671176 | tf_op jit(solution)/shard_map/ppermute | solution.py:531
  8.0 25.1 %collective-permute-start.1 = (bf16[272,1024]{1,0:T(8,128)(2,1)S(1)}, bf16[272,1024]{1,0:T(8,128)(2,1)S(1)}, u32[]{:S(2)}, u32[]{:S(2)}) collective-permute-start(bf16[272,1024]{1,0:T(8,128)(2,1)S(1)} %get-tuple-element.30), channel_id=1, source_target_pairs={{0,4},{8,12},{16,20},{24,28},{4,0},{12,8},{20,16},{28,24},{1,5},{9... | collective-permute-start | bytes 1671176 | tf_op jit(solution)/shard_map/ppermute | solution.py:531
  9.6 23.5 %collective-permute-start.2 = (bf16[272,1024]{1,0:T(8,128)(2,1)S(1)}, bf16[272,1024]{1,0:T(8,128)(2,1)S(1)}, u32[]{:S(2)}, u32[]{:S(2)}) collective-permute-start(bf16[272,1024]{1,0:T(8,128)(2,1)S(1)} %get-tuple-element.31), channel_id=1, source_target_pairs={{4,8},{12,16},{20,24},{8,4},{16,12},{24,20},{5,9},{13,17},{21,25},... | collective-permute-start | bytes 1671176 | tf_op jit(solution)/shard_map/ppermute | solution.py:531
  10.3 22.9 %collective-permute-start.3 = (bf16[272,1024]{1,0:T(8,128)(2,1)S(1)}, bf16[272,1024]{1,0:T(8,128)(2,1)S(1)}, u32[]{:S(2)}, u32[]{:S(2)}) collective-permute-start(bf16[272,1024]{1,0:T(8,128)(2,1)S(1)} %get-tuple-element.32), channel_id=1, source_target_pairs={{8,16},{12,20},{16,8},{20,12},{9,17},{13,21},{17,9},{21,13},{10,18... | collective-permute-start | bytes 1671176 | tf_op jit(solution)/shard_map/ppermute | solution.py:531
  11.0 32.0 %collective-permute-start.7 = (bf16[272,1024]{1,0:T(8,128)(2,1)S(1)}, bf16[272,1024]{1,0:T(8,128)(2,1)S(1)}, u32[]{:S(2)}, u32[]{:S(2)}) collective-permute-start(bf16[272,1024]{1,0:T(8,128)(2,1)S(1)} %get-tuple-element.38.refs_0_), channel_id=1, source_target_pairs={{0,2},{1,3},{2,0},{3,1},{4,6},{5,7},{6,4},{7,5},{8,10},{9,11},{10,... | collective-permute-start | bytes 1671176 | tf_op jit(solution)/shard_map/ppermute | solution.py:520
  33.1 21.0 %collective-permute-start.4 = (bf16[272,1024]{1,0:T(8,128)(2,1)S(1)}, bf16[272,1024]{1,0:T(8,128)(2,1)S(1)}, u32[]{:S(2)}, u32[]{:S(2)}) collective-permute-start(bf16[272,1024]{1,0:T(8,128)(2,1)S(1)} %get-tuple-element.34), channel_id=1, source_target_pairs={{0,12},{4,16},{8,20},{12,0},{16,4},{20,8},{1,13},{5,17},{9,21},{13... | collective-permute-start | bytes 1671176 | tf_op jit(solution)/shard_map/ppermute | solution.py:531
  41.3 15.7 %copy-start.1 = (s32[8,8]{1,0:T(8,128)S(1)}, s32[8,8]{1,0:T(8,128)}, u32[]{:S(2)}) copy-start(s32[8,8]{1,0:T(8,128)} %rows_ref.7) | copy-start | bytes 772
  41.3 15.7 %copy-start.4 = (f32[1,3]{1,0:T(1,128)S(1)}, f32[1,3]{1,0:T(1,128)}, u32[]{:S(2)}) copy-start(f32[1,3]{1,0:T(1,128)} %levels.7) | copy-start | bytes 40
  41.3 12.0 %collective-permute-start.5 = (bf16[256,1024]{1,0:T(8,128)(2,1)S(1)}, bf16[256,1024]{1,0:T(8,128)(2,1)S(1)}, u32[]{:S(2)}, u32[]{:S(2)}) collective-permute-start(bf16[256,1024]{1,0:T(8,128)(2,1)S(1)} %pack_group.3.refs_4_), channel_id=1, source_target_pairs={{0,2},{1,3},{2,0},{3,1},{4,6},{5,7},{6,4},{7,5},{8,10},{9,11},{10,... | collective-permute-start | bytes 1572872 | tf_op jit(solution)/shard_map/ppermute | solution.py:520
  42.9 12.5 %collective-permute-start.8 = (bf16[272,1024]{1,0:T(8,128)(2,1)S(1)}, bf16[272,1024]{1,0:T(8,128)(2,1)S(1)}, u32[]{:S(2)}, u32[]{:S(2)}) collective-permute-start(bf16[272,1024]{1,0:T(8,128)(2,1)S(1)} %get-tuple-element.38.refs_0_), channel_id=1, source_target_pairs={{0,1},{1,0},{2,3},{3,2},{4,5},{5,4},{6,7},{7,6},{8,9},{9,8},{10,11... | collective-permute-start | bytes 1671176 | tf_op jit(solution)/shard_map/ppermute | solution.py:521
  42.9 14.1 %collective-permute-start.9 = (bf16[272,1024]{1,0:T(8,128)(2,1)S(1)}, bf16[272,1024]{1,0:T(8,128)(2,1)S(1)}, u32[]{:S(2)}, u32[]{:S(2)}) collective-permute-start(bf16[272,1024]{1,0:T(8,128)(2,1)S(1)} %collective-permute-done.7.refs_1_), channel_id=1, source_target_pairs={{0,1},{1,0},{2,3},{3,2},{4,5},{5,4},{6,7},{7,6},{8,9},{9,8},{10,11... | collective-permute-start | bytes 1671176 | tf_op jit(solution)/shard_map/ppermute | solution.py:523
  53.4 10.6 %collective-permute-start.6 = (bf16[272,1024]{1,0:T(8,128)(2,1)S(1)}, bf16[272,1024]{1,0:T(8,128)(2,1)S(1)}, u32[]{:S(2)}, u32[]{:S(2)}) collective-permute-start(bf16[272,1024]{1,0:T(8,128)(2,1)S(1)} %get-tuple-element.36), channel_id=1, source_target_pairs={{12,24},{16,28},{24,12},{28,16},{13,25},{17,29},{25,13},{29,17},{1... | collective-permute-start | bytes 1671176 | tf_op jit(solution)/shard_map/ppermute | solution.py:531
  54.0 3.0 %collective-permute-start.10 = (bf16[256,1024]{1,0:T(8,128)(2,1)S(1)}, bf16[256,1024]{1,0:T(8,128)(2,1)S(1)}, u32[]{:S(2)}, u32[]{:S(2)}) collective-permute-start(bf16[256,1024]{1,0:T(8,128)(2,1)S(1)} %pack_group.3.refs_4_), channel_id=1, source_target_pairs={{0,1},{1,0},{2,3},{3,2},{4,5},{5,4},{6,7},{7,6},{8,9},{9,8},{10,11... | collective-permute-start | bytes 1572872 | tf_op jit(solution)/shard_map/ppermute | solution.py:521
  54.1 2.9 %collective-permute-start.11 = (bf16[256,1024]{1,0:T(8,128)(2,1)S(1)}, bf16[256,1024]{1,0:T(8,128)(2,1)S(1)}, u32[]{:S(2)}, u32[]{:S(2)}) collective-permute-start(bf16[256,1024]{1,0:T(8,128)(2,1)S(1)} %collective-permute-done.5.refs_5_), channel_id=1, source_target_pairs={{0,1},{1,0},{2,3},{3,2},{4,5},{5,4},{6,7},{7,6},{8,9},{9,8},{10,11... | collective-permute-start | bytes 1572872 | tf_op jit(solution)/shard_map/ppermute | solution.py:523
  55.4 14.0 %collective-permute-start.12 = (bf16[256,1024]{1,0:T(8,128)(2,1)S(1)}, bf16[256,1024]{1,0:T(8,128)(2,1)S(1)}, u32[]{:S(2)}, u32[]{:S(2)}) collective-permute-start(bf16[256,1024]{1,0:T(8,128)(2,1)S(1)} %get-tuple-element.41.refs_8_), channel_id=1, source_target_pairs={{0,2},{1,3},{2,0},{3,1},{4,6},{5,7},{6,4},{7,5},{8,10},{9,11},{10,... | collective-permute-start | bytes 1572872 | tf_op jit(solution)/shard_map/ppermute | solution.py:520
  64.8 4.6 %collective-permute-start.14 = (bf16[256,1024]{1,0:T(8,128)(2,1)S(1)}, bf16[256,1024]{1,0:T(8,128)(2,1)S(1)}, u32[]{:S(2)}, u32[]{:S(2)}) collective-permute-start(bf16[256,1024]{1,0:T(8,128)(2,1)S(1)} %get-tuple-element.42.refs_12_.refs_13_), channel_id=1, source_target_pairs={{0,1},{1,0},{2,3},{3,2},{4,5},{5,4},{6,7},{7,6},{8,9},{9,8},{10,11... | collective-permute-start | bytes 1572872 | tf_op jit(solution)/shard_map/ppermute | solution.py:547
  64.9 6.0 %collective-permute-start.13 = (bf16[256,1024]{1,0:T(8,128)(2,1)S(1)}, bf16[256,1024]{1,0:T(8,128)(2,1)S(1)}, u32[]{:S(2)}, u32[]{:S(2)}) collective-permute-start(bf16[256,1024]{1,0:T(8,128)(2,1)S(1)} %get-tuple-element.41.refs_8_), channel_id=1, source_target_pairs={{0,1},{1,0},{2,3},{3,2},{4,5},{5,4},{6,7},{7,6},{8,9},{9,8},{10,11... | collective-permute-start | bytes 1572872 | tf_op jit(solution)/shard_map/ppermute | solution.py:521
  69.4 1.9 %collective-permute-start.15 = (bf16[256,1024]{1,0:T(8,128)(2,1)S(1)}, bf16[256,1024]{1,0:T(8,128)(2,1)S(1)}, u32[]{:S(2)}, u32[]{:S(2)}) collective-permute-start(bf16[256,1024]{1,0:T(8,128)(2,1)S(1)} %collective-permute-done.12.refs_9_), channel_id=1, source_target_pairs={{0,1},{1,0},{2,3},{3,2},{4,5},{5,4},{6,7},{7,6},{8,9},{9,8},{10,11... | collective-permute-start | bytes 1572872 | tf_op jit(solution)/shard_map/ppermute | solution.py:523
  69.4 14.7 %collective-permute-start.16 = (bf16[256,1024]{1,0:T(8,128)(2,1)S(1)}, bf16[256,1024]{1,0:T(8,128)(2,1)S(1)}, u32[]{:S(2)}, u32[]{:S(2)}) collective-permute-start(bf16[256,1024]{1,0:T(8,128)(2,1)S(1)} %get-tuple-element.42.refs_12_.refs_13_), channel_id=1, source_target_pairs={{0,2},{1,3},{2,0},{3,1},{4,6},{5,7},{6,4},{7,5},{8,10},{9,11},{10,... | collective-permute-start | bytes 1572872 | tf_op jit(solution)/shard_map/ppermute | solution.py:548
  84.1 2.0 %collective-permute-start.17 = (bf16[256,1024]{1,0:T(8,128)(2,1)S(1)}, bf16[256,1024]{1,0:T(8,128)(2,1)S(1)}, u32[]{:S(2)}, u32[]{:S(2)}) collective-permute-start(bf16[256,1024]{1,0:T(8,128)(2,1)S(1)} %collective-permute-done.16.refs_13_), channel_id=1, source_target_pairs={{0,1},{1,0},{2,3},{3,2},{4,5},{5,4},{6,7},{7,6},{8,9},{9,8},{10,11... | collective-permute-start | bytes 1572872 | tf_op jit(solution)/shard_map/ppermute | solution.py:552
  91.1 4.5 %collective-permute-start.18 = (bf16[5,64,128]{2,1,0:T(8,128)(2,1)S(1)}, bf16[5,64,128]{2,1,0:T(8,128)(2,1)S(1)}, u32[]{:S(2)}, u32[]{:S(2)}) collective-permute-start(bf16[5,64,128]{2,1,0:T(8,128)(2,1)S(1)} %get-tuple-element.46), channel_id=1, source_target_pairs={{0,2},{1,3},{2,0},{3,1},{4,6},{5,7},{6,4},{7,5},{8,10},{9,11},{10,... | collective-permute-start | bytes 245768 | tf_op jit(solution)/shard_map/ppermute | solution.py:558
  95.8 1.4 %collective-permute-start.19 = (f32[6,32,128]{2,1,0:T(8,128)S(1)}, f32[6,32,128]{2,1,0:T(8,128)S(1)}, u32[]{:S(2)}, u32[]{:S(2)}) collective-permute-start(f32[6,32,128]{2,1,0:T(8,128)S(1)} %get-tuple-element.47), channel_id=1, source_target_pairs={{0,1},{1,0},{2,3},{3,2},{4,5},{5,4},{6,7},{7,6},{8,9},{9,8},{10,11... | collective-permute-start | bytes 294920 | tf_op jit(solution)/shard_map/ppermute | solution.py:562
  (1 other events, 0.7 us)

commit v12 on v11

--- a/solution.py
+++ b/solution.py
@@ -83,7 +83,7 @@
         in_specs=[SMEM, SMEM, VMEM, ANY],
         out_specs=(VMEM,) * 7,
         scratch_shapes=[pltpu.SemaphoreType.DMA((7, CAP))],
-        compiler_params=pltpu.CompilerParams(vmem_limit_bytes=8 * MIB),
+        compiler_params=pltpu.CompilerParams(vmem_limit_bytes=50 * MIB),
         cost_estimate=NO_COST,
         name="pack_to_send",
     )(ints, vir_list, tails, table)

time: 112 us -> 112 us (level)
  local copies, waits for them, and re-layouts: 1.96 us -> 0.74 us
    unnamed x10 -> x8, local copies, waits for them, and re-layouts: 1.93 us -> 0.71 us
where the time goes in v12:
time: 112 us; the launch traced here: 111 us
  waiting for transfers between devices  39.2 us (35%)
  Pallas kernels  33.6 us (30%)
  starting transfers between devices  23.5 us (21%)
  blocking collectives  12.3 us (11%)
  other arithmetic  1.5 us (1%)
    pallas_call x4, Pallas kernels, contract(): pl.pallas_call(functools.partial(contract_kernel, stage, block, width), o...  24.8 us
    ppermute x6, waiting for transfers between devices, send(): return lax.ppermute(payload, 'frag', round_pairs(distance, parity, frags))  18.3 us
    ppermute x6, starting transfers between devices, send(): return lax.ppermute(payload, 'frag', round_pairs(distance, parity, frags))  14.2 us
    ppermute x3, waiting for transfers between devices, over_aux(): far = lax.ppermute(here, 'aux', far_pairs)  14 us
    all_to_all x1, blocking collectives, body(): incoming = lax.all_to_all(outgoing, 'frag', 0, 0, tiled=True)  12.3 us
    ppermute x3, starting transfers between devices, over_aux(): far = lax.ppermute(here, 'aux', far_pairs)  4.75 us
    ppermute x1, waiting for transfers between devices, body(): met = lax.ppermute(sent, 'aux', far_pairs).astype(jnp.float32)  3.4 us
    pallas_call x1, Pallas kernels, pack_to_send(): pl.pallas_call(functools.partial(send_kernel, sizes), out_shape=(part,) *...  2.4 us
  transfers between devices with their start and end apart: 20, of which 8 were waited for; matrix products, arithmetic and copies ran while one was open for 0% of the time, Pallas kernels for 22%

profile of v12, /device:TPU:0, one launch (start us, length us, event | category | flops | bytes accessed | tf_op | source)
XLA Modules:
  0.0 111.1 jit_solution(12709524411473799397)
XLA Ops:
  2.1 2.4 %pack_to_send.1 = (bf16[272,1024]{1,0:T(8,128)(2,1)S(1)}, bf16[272,1024]{1,0:T(8,128)(2,1)S(1)}, bf16[272,1024]{1,0:T(8,128)(2,1)S(1)}, bf16[272,1024]{1,0:T(8,1...) custom-call(s32[34]{0:T(128)S(1)} %pad_add_fusion.ints.where, ...), custom_call_target="tpu_custom_call" | custom-call | tf_op jit(solution)/shard_map/pack_to_send/pallas_call | solution.py:80
  4.6 3.1 %collective-permute-start = (bf16[272,1024]{1,0:T(8,128)(2,1)S(1)}, bf16[272,1024]{1,0:T(8,128)(2,1)S(1)}, u32[]{:S(2)}, u32[]{:S(2)}) collective-permute-start(bf16[272,1024]{1,0:T(8,128)(2,1)S(1)} %get-tuple-element.26), channel_id=1, source_target_pairs={{0,8},{4,12},{16,24},{20,28},{8,0},{12,4},{24,16},{28,20},{1,9},{5... | collective-permute-start | bytes 1671176 | tf_op jit(solution)/shard_map/ppermute | solution.py:531
  7.7 1.7 %collective-permute-start.1 = (bf16[272,1024]{1,0:T(8,128)(2,1)S(1)}, bf16[272,1024]{1,0:T(8,128)(2,1)S(1)}, u32[]{:S(2)}, u32[]{:S(2)}) collective-permute-start(bf16[272,1024]{1,0:T(8,128)(2,1)S(1)} %get-tuple-element.30), channel_id=1, source_target_pairs={{0,4},{8,12},{16,20},{24,28},{4,0},{12,8},{20,16},{28,24},{1,5},{9... | collective-permute-start | bytes 1671176 | tf_op jit(solution)/shard_map/ppermute | solution.py:531
  10.7 1.6 %collective-permute-start.7 = (bf16[272,1024]{1,0:T(8,128)(2,1)S(1)}, bf16[272,1024]{1,0:T(8,128)(2,1)S(1)}, u32[]{:S(2)}, u32[]{:S(2)}) collective-permute-start(bf16[272,1024]{1,0:T(8,128)(2,1)S(1)} %get-tuple-element.38.refs_0_), channel_id=1, source_target_pairs={{0,2},{1,3},{2,0},{3,1},{4,6},{5,7},{6,4},{7,5},{8,10},{9,11},{10,... | collective-permute-start | bytes 1671176 | tf_op jit(solution)/shard_map/ppermute | solution.py:520
  12.3 8.8 %collective-permute-done.refs_2_.refs_3_ = bf16[272,1024]{1,0:T(8,128)(2,1)S(1)} collective-permute-done((bf16[272,1024]{1,0:T(8,128)(2,1)S(1)}, bf16[272,1024]{1,0:T(8,128)(2,1)S(1)}, u32[]{:S(2)}, u32[]{:S(2)}) %collective-permute-start) | collective-permute-done | bytes 557088 | tf_op jit(solution)/shard_map/ppermute | solution.py:531
  21.1 2.2 %plan_lists.1 = (s32[4,8]{1,0:T(4,128)S(1)}, s32[8,2]{1,0:T(8,128)S(1)}) custom-call(s32[34]{0:T(128)S(1)} %pad_add_fusion.ints.where, s32[8,8]{1,0:T(8,128)S(1)} %copy-done.1), custom_call_target="tpu_custom_call" | custom-call | tf_op jit(solution)/shard_map/plan_lists/pallas_call | solution.py:135
  23.4 9.5 %collective-permute-done.1.refs_0_.refs_1_ = bf16[272,1024]{1,0:T(8,128)(2,1)S(1)} collective-permute-done((bf16[272,1024]{1,0:T(8,128)(2,1)S(1)}, bf16[272,1024]{1,0:T(8,128)(2,1)S(1)}, u32[]{:S(2)}, u32[]{:S(2)}) %collective-permute-start.1) | collective-permute-done | bytes 557088 | tf_op jit(solution)/shard_map/ppermute | solution.py:531
  32.9 7.4 %collective-permute-start.4 = (bf16[272,1024]{1,0:T(8,128)(2,1)S(1)}, bf16[272,1024]{1,0:T(8,128)(2,1)S(1)}, u32[]{:S(2)}, u32[]{:S(2)}) collective-permute-start(bf16[272,1024]{1,0:T(8,128)(2,1)S(1)} %get-tuple-element.34), channel_id=1, source_target_pairs={{0,12},{4,16},{8,20},{12,0},{16,4},{20,8},{1,13},{5,17},{9,21},{13... | collective-permute-start | bytes 1671176 | tf_op jit(solution)/shard_map/ppermute | solution.py:531
  41.0 1.6 %collective-permute-start.5 = (bf16[256,1024]{1,0:T(8,128)(2,1)S(1)}, bf16[256,1024]{1,0:T(8,128)(2,1)S(1)}, u32[]{:S(2)}, u32[]{:S(2)}) collective-permute-start(bf16[256,1024]{1,0:T(8,128)(2,1)S(1)} %pack_group.3.refs_4_), channel_id=1, source_target_pairs={{0,2},{1,3},{2,0},{3,1},{4,6},{5,7},{6,4},{7,5},{8,10},{9,11},{10,... | collective-permute-start | bytes 1572872 | tf_op jit(solution)/shard_map/ppermute | solution.py:520
  43.1 9.9 %collective-permute-done.5.refs_5_ = bf16[256,1024]{1,0:T(8,128)(2,1)S(1)} collective-permute-done((bf16[256,1024]{1,0:T(8,128)(2,1)S(1)}, bf16[256,1024]{1,0:T(8,128)(2,1)S(1)}, u32[]{:S(2)}, u32[]{:S(2)}) %collective-permute-start.5) | collective-permute-done | bytes 524320 | tf_op jit(solution)/shard_map/ppermute | solution.py:520
  55.1 1.6 %collective-permute-start.12 = (bf16[256,1024]{1,0:T(8,128)(2,1)S(1)}, bf16[256,1024]{1,0:T(8,128)(2,1)S(1)}, u32[]{:S(2)}, u32[]{:S(2)}) collective-permute-start(bf16[256,1024]{1,0:T(8,128)(2,1)S(1)} %get-tuple-element.41.refs_8_), channel_id=1, source_target_pairs={{0,2},{1,3},{2,0},{3,1},{4,6},{5,7},{6,4},{7,5},{8,10},{9,11},{10,... | collective-permute-start | bytes 1572872 | tf_op jit(solution)/shard_map/ppermute | solution.py:520
  56.7 6.9 %contract.4.refs_16_ = f32[1,128,128]{2,1,0:T(8,128)S(1)} custom-call(s32[34]{0:T(128)S(1)} %pad_add_fusion.ints.where, s32[4,8]{1,0:T(4,128)S(1)} %get-tuple-element.29.plan, f32[1,3]{1,0:T(1,128)S(1)} %copy-done.3, s32[8,8]{1,0:T(8,128)S(1)} %copy-done, f32[8,128]{1,0:T(8,128)S(1)} %get-tuple-element.37.energy, ...), custom_call_target="tpu_custom_call" | custom-call | tf_op jit(solution)/shard_map/contract/pallas_call | solution.py:440
  63.6 0.8 pack_group.5
  65.0 4.0 %collective-permute-done.12.refs_9_ = bf16[256,1024]{1,0:T(8,128)(2,1)S(1)} collective-permute-done((bf16[256,1024]{1,0:T(8,128)(2,1)S(1)}, bf16[256,1024]{1,0:T(8,128)(2,1)S(1)}, u32[]{:S(2)}, u32[]{:S(2)}) %collective-permute-start.12) | collective-permute-done | bytes 524320 | tf_op jit(solution)/shard_map/ppermute | solution.py:520
  69.1 1.5 %collective-permute-start.16 = (bf16[256,1024]{1,0:T(8,128)(2,1)S(1)}, bf16[256,1024]{1,0:T(8,128)(2,1)S(1)}, u32[]{:S(2)}, u32[]{:S(2)}) collective-permute-start(bf16[256,1024]{1,0:T(8,128)(2,1)S(1)} %get-tuple-element.42.refs_12_.refs_13_), channel_id=1, source_target_pairs={{0,2},{1,3},{2,0},{3,1},{4,6},{5,7},{6,4},{7,5},{8,10},{9,11},{10,... | collective-permute-start | bytes 1572872 | tf_op jit(solution)/shard_map/ppermute | solution.py:548
  71.0 4.1 %contract.6.refs_18_ = f32[1536,256]{1,0:T(8,128)S(1)} custom-call(s32[34]{0:T(128)S(1)} %pad_add_fusion.ints.where, s32[4,8]{1,0:T(4,128)S(1)} %get-tuple-element.29.plan, f32[1,3]{1,0:T(1,128)S(1)} %copy-done.3, s32[8,8]{1,0:T(8,128)S(1)} %copy-done, f32[8,128]{1,0:T(8,128)S(1)} %get-tuple-element.40.energy, ...), custom_call_target="tpu_custom_call" | custom-call | flops 1610612736 | bytes 786432 | tf_op jit(solution)/shard_map/contract/pallas_call | solution.py:440
  75.0 8.7 %contract.5.refs_17_ = f32[4,128,128]{2,1,0:T(8,128)S(1)} custom-call(s32[34]{0:T(128)S(1)} %pad_add_fusion.ints.where, s32[4,8]{1,0:T(4,128)S(1)} %get-tuple-element.29.plan, f32[1,3]{1,0:T(1,128)S(1)} %copy-done.3, s32[8,8]{1,0:T(8,128)S(1)} %copy-done, f32[8,128]{1,0:T(8,128)S(1)} %get-tuple-element.37.energy, ...), custom_call_target="tpu_custom_call" | custom-call | flops 3221225472 | bytes 1572864 | tf_op jit(solution)/shard_map/contract/pallas_call | solution.py:440
  84.0 1.8 %collective-permute-done.17.refs_15_ = bf16[256,1024]{1,0:T(8,128)(2,1)S(1)} collective-permute-done((bf16[256,1024]{1,0:T(8,128)(2,1)S(1)}, bf16[256,1024]{1,0:T(8,128)(2,1)S(1)}, u32[]{:S(2)}, u32[]{:S(2)}) %collective-permute-start.17) | collective-permute-done | bytes 524320 | tf_op jit(solution)/shard_map/ppermute | solution.py:552
  85.7 5.1 %contract.7 = (bf16[5,64,128]{2,1,0:T(8,128)(2,1)S(1)}, f32[5,64,128]{2,1,0:T(8,128)S(1)}) custom-call(s32[34]{0:T(128)S(1)} %pad_add_fusion.ints.where, s32[4,8]{1,0:T(4,128)S(1)} %get-tuple-element.29.plan, f32[1,3]{1,0:T(1,128)S(1)} %copy-done.3, s32[8,8]{1,0:T(8,128)S(1)} %copy-done, f32[8,128]{1,0:T(8,128)S(1)} %get-tuple-element.40.energy, ...), custom_call_target="tpu_custom_call" | custom-call | tf_op jit(solution)/shard_map/contract/pallas_call | solution.py:440
  90.8 1.1 %collective-permute-start.18 = (bf16[5,64,128]{2,1,0:T(8,128)(2,1)S(1)}, bf16[5,64,128]{2,1,0:T(8,128)(2,1)S(1)}, u32[]{:S(2)}, u32[]{:S(2)}) collective-permute-start(bf16[5,64,128]{2,1,0:T(8,128)(2,1)S(1)} %get-tuple-element.46), channel_id=1, source_target_pairs={{0,2},{1,3},{2,0},{3,1},{4,6},{5,7},{6,4},{7,5},{8,10},{9,11},{10,... | collective-permute-start | bytes 245768 | tf_op jit(solution)/shard_map/ppermute | solution.py:558
  91.9 3.4 %collective-permute-done.18 = bf16[5,64,128]{2,1,0:T(8,128)(2,1)S(1)} collective-permute-done((bf16[5,64,128]{2,1,0:T(8,128)(2,1)S(1)}, bf16[5,64,128]{2,1,0:T(8,128)(2,1)S(1)}, u32[]{:S(2)}, u32[]{:S(2)}) %collective-permute-start.18) | collective-permute-done | bytes 81952 | tf_op jit(solution)/shard_map/ppermute | solution.py:558
  95.5 1.3 %collective-permute-done.19.came = f32[6,32,128]{2,1,0:T(8,128)S(1)} collective-permute-done((f32[6,32,128]{2,1,0:T(8,128)S(1)}, f32[6,32,128]{2,1,0:T(8,128)S(1)}, u32[]{:S(2)}, u32[]{:S(2)}) %collective-permute-start.19) | collective-permute-done | bytes 98336 | tf_op jit(solution)/shard_map/ppermute | solution.py:562
  97.5 12.3 %all_to_all.5.came = bf16[8,2,32,128]{3,2,1,0:T(8,128)(2,1)S(1)} all-to-all(bf16[8,2,32,128]{3,2,1,0:T(8,128)(2,1)S(1)} %spread.1), channel_id=1, replica_groups=mesh['frag'=8,'aux'=4] {'frag'}, dimensions={0} | all-to-all | bytes 262144 | tf_op jit(solution)/shard_map/all_to_all | solution.py:564
  109.7 1.3 %collect.1 = f32[4,32,128]{2,1,0:T(8,128)} custom-call(s32[8,2]{1,0:T(8,128)S(1)} %get-tuple-element.28.target, bf16[8,2,32,128]{3,2,1,0:T(8,128)(2,1)S(1)} %all_to_all.5.came), custom_call_target="tpu_custom_call" | custom-call | tf_op jit(solution)/shard_map/collect/pallas_call | solution.py:490
  (44 shorter events, 8.7 us)
Async XLA Ops:
  1.5 0.7 copy-start.1
  4.6 49.7 %copy-start.2 = (bf16[4,128]{1,0:T(4,128)(2,1)S(1)}, bf16[4,128]{1,0:T(4,128)(2,1)}, u32[]{:S(2)}) copy-start(bf16[4,128]{1,0:T(4,128)(2,1)} %refs_0_.3) | copy-start | bytes 3076
  4.6 16.6 %collective-permute-start = (bf16[272,1024]{1,0:T(8,128)(2,1)S(1)}, bf16[272,1024]{1,0:T(8,128)(2,1)S(1)}, u32[]{:S(2)}, u32[]{:S(2)}) collective-permute-start(bf16[272,1024]{1,0:T(8,128)(2,1)S(1)} %get-tuple-element.26), channel_id=1, source_target_pairs={{0,8},{4,12},{16,24},{20,28},{8,0},{12,4},{24,16},{28,20},{1,9},{5... | collective-permute-start | bytes 1671176 | tf_op jit(solution)/shard_map/ppermute | solution.py:531
  7.7 25.2 %collective-permute-start.1 = (bf16[272,1024]{1,0:T(8,128)(2,1)S(1)}, bf16[272,1024]{1,0:T(8,128)(2,1)S(1)}, u32[]{:S(2)}, u32[]{:S(2)}) collective-permute-start(bf16[272,1024]{1,0:T(8,128)(2,1)S(1)} %get-tuple-element.30), channel_id=1, source_target_pairs={{0,4},{8,12},{16,20},{24,28},{4,0},{12,8},{20,16},{28,24},{1,5},{9... | collective-permute-start | bytes 1671176 | tf_op jit(solution)/shard_map/ppermute | solution.py:531
  9.3 23.5 %collective-permute-start.2 = (bf16[272,1024]{1,0:T(8,128)(2,1)S(1)}, bf16[272,1024]{1,0:T(8,128)(2,1)S(1)}, u32[]{:S(2)}, u32[]{:S(2)}) collective-permute-start(bf16[272,1024]{1,0:T(8,128)(2,1)S(1)} %get-tuple-element.31), channel_id=1, source_target_pairs={{4,8},{12,16},{20,24},{8,4},{16,12},{24,20},{5,9},{13,17},{21,25},... | collective-permute-start | bytes 1671176 | tf_op jit(solution)/shard_map/ppermute | solution.py:531
  10.0 22.9 %collective-permute-start.3 = (bf16[272,1024]{1,0:T(8,128)(2,1)S(1)}, bf16[272,1024]{1,0:T(8,128)(2,1)S(1)}, u32[]{:S(2)}, u32[]{:S(2)}) collective-permute-start(bf16[272,1024]{1,0:T(8,128)(2,1)S(1)} %get-tuple-element.32), channel_id=1, source_target_pairs={{8,16},{12,20},{16,8},{20,12},{9,17},{13,21},{17,9},{21,13},{10,18... | collective-permute-start | bytes 1671176 | tf_op jit(solution)/shard_map/ppermute | solution.py:531
  10.7 31.9 %collective-permute-start.7 = (bf16[272,1024]{1,0:T(8,128)(2,1)S(1)}, bf16[272,1024]{1,0:T(8,128)(2,1)S(1)}, u32[]{:S(2)}, u32[]{:S(2)}) collective-permute-start(bf16[272,1024]{1,0:T(8,128)(2,1)S(1)} %get-tuple-element.38.refs_0_), channel_id=1, source_target_pairs={{0,2},{1,3},{2,0},{3,1},{4,6},{5,7},{6,4},{7,5},{8,10},{9,11},{10,... | collective-permute-start | bytes 1671176 | tf_op jit(solution)/shard_map/ppermute | solution.py:520
  32.9 20.9 %collective-permute-start.4 = (bf16[272,1024]{1,0:T(8,128)(2,1)S(1)}, bf16[272,1024]{1,0:T(8,128)(2,1)S(1)}, u32[]{:S(2)}, u32[]{:S(2)}) collective-permute-start(bf16[272,1024]{1,0:T(8,128)(2,1)S(1)} %get-tuple-element.34), channel_id=1, source_target_pairs={{0,12},{4,16},{8,20},{12,0},{16,4},{20,8},{1,13},{5,17},{9,21},{13... | collective-permute-start | bytes 1671176 | tf_op jit(solution)/shard_map/ppermute | solution.py:531
  41.0 15.7 %copy-start = (s32[8,8]{1,0:T(8,128)S(1)}, s32[8,8]{1,0:T(8,128)}, u32[]{:S(2)}) copy-start(s32[8,8]{1,0:T(8,128)} %rows_ref.7) | copy-start | bytes 772
  41.0 15.7 %copy-start.3 = (f32[1,3]{1,0:T(1,128)S(1)}, f32[1,3]{1,0:T(1,128)}, u32[]{:S(2)}) copy-start(f32[1,3]{1,0:T(1,128)} %levels.7) | copy-start | bytes 40
  41.0 12.0 %collective-permute-start.5 = (bf16[256,1024]{1,0:T(8,128)(2,1)S(1)}, bf16[256,1024]{1,0:T(8,128)(2,1)S(1)}, u32[]{:S(2)}, u32[]{:S(2)}) collective-permute-start(bf16[256,1024]{1,0:T(8,128)(2,1)S(1)} %pack_group.3.refs_4_), channel_id=1, source_target_pairs={{0,2},{1,3},{2,0},{3,1},{4,6},{5,7},{6,4},{7,5},{8,10},{9,11},{10,... | collective-permute-start | bytes 1572872 | tf_op jit(solution)/shard_map/ppermute | solution.py:520
  42.6 12.5 %collective-permute-start.8 = (bf16[272,1024]{1,0:T(8,128)(2,1)S(1)}, bf16[272,1024]{1,0:T(8,128)(2,1)S(1)}, u32[]{:S(2)}, u32[]{:S(2)}) collective-permute-start(bf16[272,1024]{1,0:T(8,128)(2,1)S(1)} %get-tuple-element.38.refs_0_), channel_id=1, source_target_pairs={{0,1},{1,0},{2,3},{3,2},{4,5},{5,4},{6,7},{7,6},{8,9},{9,8},{10,11... | collective-permute-start | bytes 1671176 | tf_op jit(solution)/shard_map/ppermute | solution.py:521
  42.6 14.1 %collective-permute-start.9 = (bf16[272,1024]{1,0:T(8,128)(2,1)S(1)}, bf16[272,1024]{1,0:T(8,128)(2,1)S(1)}, u32[]{:S(2)}, u32[]{:S(2)}) collective-permute-start(bf16[272,1024]{1,0:T(8,128)(2,1)S(1)} %collective-permute-done.7.refs_1_), channel_id=1, source_target_pairs={{0,1},{1,0},{2,3},{3,2},{4,5},{5,4},{6,7},{7,6},{8,9},{9,8},{10,11... | collective-permute-start | bytes 1671176 | tf_op jit(solution)/shard_map/ppermute | solution.py:523
  53.0 10.6 %collective-permute-start.6 = (bf16[272,1024]{1,0:T(8,128)(2,1)S(1)}, bf16[272,1024]{1,0:T(8,128)(2,1)S(1)}, u32[]{:S(2)}, u32[]{:S(2)}) collective-permute-start(bf16[272,1024]{1,0:T(8,128)(2,1)S(1)} %get-tuple-element.36), channel_id=1, source_target_pairs={{12,24},{16,28},{24,12},{28,16},{13,25},{17,29},{25,13},{29,17},{1... | collective-permute-start | bytes 1671176 | tf_op jit(solution)/shard_map/ppermute | solution.py:531
  53.7 3.0 %collective-permute-start.10 = (bf16[256,1024]{1,0:T(8,128)(2,1)S(1)}, bf16[256,1024]{1,0:T(8,128)(2,1)S(1)}, u32[]{:S(2)}, u32[]{:S(2)}) collective-permute-start(bf16[256,1024]{1,0:T(8,128)(2,1)S(1)} %pack_group.3.refs_4_), channel_id=1, source_target_pairs={{0,1},{1,0},{2,3},{3,2},{4,5},{5,4},{6,7},{7,6},{8,9},{9,8},{10,11... | collective-permute-start | bytes 1572872 | tf_op jit(solution)/shard_map/ppermute | solution.py:521
  53.8 2.9 %collective-permute-start.11 = (bf16[256,1024]{1,0:T(8,128)(2,1)S(1)}, bf16[256,1024]{1,0:T(8,128)(2,1)S(1)}, u32[]{:S(2)}, u32[]{:S(2)}) collective-permute-start(bf16[256,1024]{1,0:T(8,128)(2,1)S(1)} %collective-permute-done.5.refs_5_), channel_id=1, source_target_pairs={{0,1},{1,0},{2,3},{3,2},{4,5},{5,4},{6,7},{7,6},{8,9},{9,8},{10,11... | collective-permute-start | bytes 1572872 | tf_op jit(solution)/shard_map/ppermute | solution.py:523
  55.1 14.0 %collective-permute-start.12 = (bf16[256,1024]{1,0:T(8,128)(2,1)S(1)}, bf16[256,1024]{1,0:T(8,128)(2,1)S(1)}, u32[]{:S(2)}, u32[]{:S(2)}) collective-permute-start(bf16[256,1024]{1,0:T(8,128)(2,1)S(1)} %get-tuple-element.41.refs_8_), channel_id=1, source_target_pairs={{0,2},{1,3},{2,0},{3,1},{4,6},{5,7},{6,4},{7,5},{8,10},{9,11},{10,... | collective-permute-start | bytes 1572872 | tf_op jit(solution)/shard_map/ppermute | solution.py:520
  64.4 4.6 %collective-permute-start.14 = (bf16[256,1024]{1,0:T(8,128)(2,1)S(1)}, bf16[256,1024]{1,0:T(8,128)(2,1)S(1)}, u32[]{:S(2)}, u32[]{:S(2)}) collective-permute-start(bf16[256,1024]{1,0:T(8,128)(2,1)S(1)} %get-tuple-element.42.refs_12_.refs_13_), channel_id=1, source_target_pairs={{0,1},{1,0},{2,3},{3,2},{4,5},{5,4},{6,7},{7,6},{8,9},{9,8},{10,11... | collective-permute-start | bytes 1572872 | tf_op jit(solution)/shard_map/ppermute | solution.py:547
  64.5 6.1 %collective-permute-start.13 = (bf16[256,1024]{1,0:T(8,128)(2,1)S(1)}, bf16[256,1024]{1,0:T(8,128)(2,1)S(1)}, u32[]{:S(2)}, u32[]{:S(2)}) collective-permute-start(bf16[256,1024]{1,0:T(8,128)(2,1)S(1)} %get-tuple-element.41.refs_8_), channel_id=1, source_target_pairs={{0,1},{1,0},{2,3},{3,2},{4,5},{5,4},{6,7},{7,6},{8,9},{9,8},{10,11... | collective-permute-start | bytes 1572872 | tf_op jit(solution)/shard_map/ppermute | solution.py:521
  69.1 1.9 %collective-permute-start.15 = (bf16[256,1024]{1,0:T(8,128)(2,1)S(1)}, bf16[256,1024]{1,0:T(8,128)(2,1)S(1)}, u32[]{:S(2)}, u32[]{:S(2)}) collective-permute-start(bf16[256,1024]{1,0:T(8,128)(2,1)S(1)} %collective-permute-done.12.refs_9_), channel_id=1, source_target_pairs={{0,1},{1,0},{2,3},{3,2},{4,5},{5,4},{6,7},{7,6},{8,9},{9,8},{10,11... | collective-permute-start | bytes 1572872 | tf_op jit(solution)/shard_map/ppermute | solution.py:523
  69.1 14.7 %collective-permute-start.16 = (bf16[256,1024]{1,0:T(8,128)(2,1)S(1)}, bf16[256,1024]{1,0:T(8,128)(2,1)S(1)}, u32[]{:S(2)}, u32[]{:S(2)}) collective-permute-start(bf16[256,1024]{1,0:T(8,128)(2,1)S(1)} %get-tuple-element.42.refs_12_.refs_13_), channel_id=1, source_target_pairs={{0,2},{1,3},{2,0},{3,1},{4,6},{5,7},{6,4},{7,5},{8,10},{9,11},{10,... | collective-permute-start | bytes 1572872 | tf_op jit(solution)/shard_map/ppermute | solution.py:548
  83.8 2.0 %collective-permute-start.17 = (bf16[256,1024]{1,0:T(8,128)(2,1)S(1)}, bf16[256,1024]{1,0:T(8,128)(2,1)S(1)}, u32[]{:S(2)}, u32[]{:S(2)}) collective-permute-start(bf16[256,1024]{1,0:T(8,128)(2,1)S(1)} %collective-permute-done.16.refs_13_), channel_id=1, source_target_pairs={{0,1},{1,0},{2,3},{3,2},{4,5},{5,4},{6,7},{7,6},{8,9},{9,8},{10,11... | collective-permute-start | bytes 1572872 | tf_op jit(solution)/shard_map/ppermute | solution.py:552
  90.8 4.5 %collective-permute-start.18 = (bf16[5,64,128]{2,1,0:T(8,128)(2,1)S(1)}, bf16[5,64,128]{2,1,0:T(8,128)(2,1)S(1)}, u32[]{:S(2)}, u32[]{:S(2)}) collective-permute-start(bf16[5,64,128]{2,1,0:T(8,128)(2,1)S(1)} %get-tuple-element.46), channel_id=1, source_target_pairs={{0,2},{1,3},{2,0},{3,1},{4,6},{5,7},{6,4},{7,5},{8,10},{9,11},{10,... | collective-permute-start | bytes 245768 | tf_op jit(solution)/shard_map/ppermute | solution.py:558
  95.5 1.4 %collective-permute-start.19 = (f32[6,32,128]{2,1,0:T(8,128)S(1)}, f32[6,32,128]{2,1,0:T(8,128)S(1)}, u32[]{:S(2)}, u32[]{:S(2)}) collective-permute-start(f32[6,32,128]{2,1,0:T(8,128)S(1)} %get-tuple-element.47), channel_id=1, source_target_pairs={{0,1},{1,0},{2,3},{3,2},{4,5},{5,4},{6,7},{7,6},{8,9},{9,8},{10,11... | collective-permute-start | bytes 294920 | tf_op jit(solution)/shard_map/ppermute | solution.py:562

commit v13 on v12

--- a/solution.py
+++ b/solution.py
@@ -483,7 +483,7 @@
             out[target[fragment, r]] += came[fragment, r].astype(jnp.float32)
         return carry
 
-    lax.fori_loop(0, came.shape[0], one, 0)
+    lax.fori_loop(0, came.shape[0], one, 0, unroll=8)
 
 
 def collect(target, came, own_count):

time: 112 us -> 111 us (level)
  no operation moved by 1% of the time
where the time goes in v13:
time: 111 us
  waiting for transfers between devices  39.2 us (35%)
  Pallas kernels  33.6 us (30%)
  starting transfers between devices  23.6 us (21%)
  blocking collectives  12.3 us (11%)
  other arithmetic  1.5 us (1%)
    pallas_call x4, Pallas kernels, contract(): pl.pallas_call(functools.partial(contract_kernel, stage, block, width), o...  24.7 us
    ppermute x6, waiting for transfers between devices, send(): return lax.ppermute(payload, 'frag', round_pairs(distance, parity, frags))  18.3 us
    ppermute x6, starting transfers between devices, send(): return lax.ppermute(payload, 'frag', round_pairs(distance, parity, frags))  14.2 us
    ppermute x3, waiting for transfers between devices, over_aux(): far = lax.ppermute(here, 'aux', far_pairs)  14 us
    all_to_all x1, blocking collectives, body(): incoming = lax.all_to_all(outgoing, 'frag', 0, 0, tiled=True)  12.3 us
    ppermute x3, starting transfers between devices, over_aux(): far = lax.ppermute(here, 'aux', far_pairs)  4.75 us
    ppermute x1, waiting for transfers between devices, body(): met = lax.ppermute(sent, 'aux', far_pairs).astype(jnp.float32)  3.41 us
    pallas_call x1, Pallas kernels, pack_to_send(): pl.pallas_call(functools.partial(send_kernel, sizes), out_shape=(part,) *...  2.42 us
  transfers between devices with their start and end apart: 20, of which 8 were waited for; matrix products, arithmetic and copies ran while one was open for 0% of the time, Pallas kernels for 22%

profile of v13, /device:TPU:0, one launch (start us, length us, event | category | flops | bytes accessed | tf_op | source)
XLA Modules:
  0.0 111.1 jit_solution(7721229457040217129)
XLA Ops:
  2.1 2.4 %pack_to_send.1 = (bf16[272,1024]{1,0:T(8,128)(2,1)S(1)}, bf16[272,1024]{1,0:T(8,128)(2,1)S(1)}, bf16[272,1024]{1,0:T(8,128)(2,1)S(1)}, bf16[272,1024]{1,0:T(8,1...) custom-call(s32[34]{0:T(128)S(1)} %pad_add_fusion.ints.where, ...), custom_call_target="tpu_custom_call" | custom-call | tf_op jit(solution)/shard_map/pack_to_send/pallas_call | solution.py:80
  4.6 3.2 %collective-permute-start = (bf16[272,1024]{1,0:T(8,128)(2,1)S(1)}, bf16[272,1024]{1,0:T(8,128)(2,1)S(1)}, u32[]{:S(2)}, u32[]{:S(2)}) collective-permute-start(bf16[272,1024]{1,0:T(8,128)(2,1)S(1)} %get-tuple-element.26), channel_id=1, source_target_pairs={{0,8},{4,12},{16,24},{20,28},{8,0},{12,4},{24,16},{28,20},{1,9},{5... | collective-permute-start | bytes 1671176 | tf_op jit(solution)/shard_map/ppermute | solution.py:531
  7.8 1.7 %collective-permute-start.1 = (bf16[272,1024]{1,0:T(8,128)(2,1)S(1)}, bf16[272,1024]{1,0:T(8,128)(2,1)S(1)}, u32[]{:S(2)}, u32[]{:S(2)}) collective-permute-start(bf16[272,1024]{1,0:T(8,128)(2,1)S(1)} %get-tuple-element.30), channel_id=1, source_target_pairs={{0,4},{8,12},{16,20},{24,28},{4,0},{12,8},{20,16},{28,24},{1,5},{9... | collective-permute-start | bytes 1671176 | tf_op jit(solution)/shard_map/ppermute | solution.py:531
  10.9 1.6 %collective-permute-start.7 = (bf16[272,1024]{1,0:T(8,128)(2,1)S(1)}, bf16[272,1024]{1,0:T(8,128)(2,1)S(1)}, u32[]{:S(2)}, u32[]{:S(2)}) collective-permute-start(bf16[272,1024]{1,0:T(8,128)(2,1)S(1)} %get-tuple-element.38.refs_0_), channel_id=1, source_target_pairs={{0,2},{1,3},{2,0},{3,1},{4,6},{5,7},{6,4},{7,5},{8,10},{9,11},{10,... | collective-permute-start | bytes 1671176 | tf_op jit(solution)/shard_map/ppermute | solution.py:520
  12.5 8.8 %collective-permute-done.refs_2_.refs_3_ = bf16[272,1024]{1,0:T(8,128)(2,1)S(1)} collective-permute-done((bf16[272,1024]{1,0:T(8,128)(2,1)S(1)}, bf16[272,1024]{1,0:T(8,128)(2,1)S(1)}, u32[]{:S(2)}, u32[]{:S(2)}) %collective-permute-start) | collective-permute-done | bytes 557088 | tf_op jit(solution)/shard_map/ppermute | solution.py:531
  21.3 2.2 %plan_lists.1 = (s32[4,8]{1,0:T(4,128)S(1)}, s32[8,2]{1,0:T(8,128)S(1)}) custom-call(s32[34]{0:T(128)S(1)} %pad_add_fusion.ints.where, s32[8,8]{1,0:T(8,128)S(1)} %copy-done.1), custom_call_target="tpu_custom_call" | custom-call | tf_op jit(solution)/shard_map/plan_lists/pallas_call | solution.py:135
  23.5 9.5 %collective-permute-done.1.refs_0_.refs_1_ = bf16[272,1024]{1,0:T(8,128)(2,1)S(1)} collective-permute-done((bf16[272,1024]{1,0:T(8,128)(2,1)S(1)}, bf16[272,1024]{1,0:T(8,128)(2,1)S(1)}, u32[]{:S(2)}, u32[]{:S(2)}) %collective-permute-start.1) | collective-permute-done | bytes 557088 | tf_op jit(solution)/shard_map/ppermute | solution.py:531
  33.0 7.3 %collective-permute-start.4 = (bf16[272,1024]{1,0:T(8,128)(2,1)S(1)}, bf16[272,1024]{1,0:T(8,128)(2,1)S(1)}, u32[]{:S(2)}, u32[]{:S(2)}) collective-permute-start(bf16[272,1024]{1,0:T(8,128)(2,1)S(1)} %get-tuple-element.34), channel_id=1, source_target_pairs={{0,12},{4,16},{8,20},{12,0},{16,4},{20,8},{1,13},{5,17},{9,21},{13... | collective-permute-start | bytes 1671176 | tf_op jit(solution)/shard_map/ppermute | solution.py:531
  41.0 1.6 %collective-permute-start.5 = (bf16[256,1024]{1,0:T(8,128)(2,1)S(1)}, bf16[256,1024]{1,0:T(8,128)(2,1)S(1)}, u32[]{:S(2)}, u32[]{:S(2)}) collective-permute-start(bf16[256,1024]{1,0:T(8,128)(2,1)S(1)} %pack_group.3.refs_4_), channel_id=1, source_target_pairs={{0,2},{1,3},{2,0},{3,1},{4,6},{5,7},{6,4},{7,5},{8,10},{9,11},{10,... | collective-permute-start | bytes 1572872 | tf_op jit(solution)/shard_map/ppermute | solution.py:520
  43.1 9.9 %collective-permute-done.5.refs_5_ = bf16[256,1024]{1,0:T(8,128)(2,1)S(1)} collective-permute-done((bf16[256,1024]{1,0:T(8,128)(2,1)S(1)}, bf16[256,1024]{1,0:T(8,128)(2,1)S(1)}, u32[]{:S(2)}, u32[]{:S(2)}) %collective-permute-start.5) | collective-permute-done | bytes 524320 | tf_op jit(solution)/shard_map/ppermute | solution.py:520
  55.1 1.6 %collective-permute-start.12 = (bf16[256,1024]{1,0:T(8,128)(2,1)S(1)}, bf16[256,1024]{1,0:T(8,128)(2,1)S(1)}, u32[]{:S(2)}, u32[]{:S(2)}) collective-permute-start(bf16[256,1024]{1,0:T(8,128)(2,1)S(1)} %get-tuple-element.41.refs_8_), channel_id=1, source_target_pairs={{0,2},{1,3},{2,0},{3,1},{4,6},{5,7},{6,4},{7,5},{8,10},{9,11},{10,... | collective-permute-start | bytes 1572872 | tf_op jit(solution)/shard_map/ppermute | solution.py:520
  56.7 6.9 %contract.4.refs_16_ = f32[1,128,128]{2,1,0:T(8,128)S(1)} custom-call(s32[34]{0:T(128)S(1)} %pad_add_fusion.ints.where, s32[4,8]{1,0:T(4,128)S(1)} %get-tuple-element.29.plan, f32[1,3]{1,0:T(1,128)S(1)} %copy-done.3, s32[8,8]{1,0:T(8,128)S(1)} %copy-done, f32[8,128]{1,0:T(8,128)S(1)} %get-tuple-element.37.energy, ...), custom_call_target="tpu_custom_call" | custom-call | tf_op jit(solution)/shard_map/contract/pallas_call | solution.py:440
  63.6 0.8 pack_group.5
  65.0 4.0 %collective-permute-done.12.refs_9_ = bf16[256,1024]{1,0:T(8,128)(2,1)S(1)} collective-permute-done((bf16[256,1024]{1,0:T(8,128)(2,1)S(1)}, bf16[256,1024]{1,0:T(8,128)(2,1)S(1)}, u32[]{:S(2)}, u32[]{:S(2)}) %collective-permute-start.12) | collective-permute-done | bytes 524320 | tf_op jit(solution)/shard_map/ppermute | solution.py:520
  69.1 1.5 %collective-permute-start.16 = (bf16[256,1024]{1,0:T(8,128)(2,1)S(1)}, bf16[256,1024]{1,0:T(8,128)(2,1)S(1)}, u32[]{:S(2)}, u32[]{:S(2)}) collective-permute-start(bf16[256,1024]{1,0:T(8,128)(2,1)S(1)} %get-tuple-element.42.refs_12_.refs_13_), channel_id=1, source_target_pairs={{0,2},{1,3},{2,0},{3,1},{4,6},{5,7},{6,4},{7,5},{8,10},{9,11},{10,... | collective-permute-start | bytes 1572872 | tf_op jit(solution)/shard_map/ppermute | solution.py:548
  71.0 4.1 %contract.6.refs_18_ = f32[1536,256]{1,0:T(8,128)S(1)} custom-call(s32[34]{0:T(128)S(1)} %pad_add_fusion.ints.where, s32[4,8]{1,0:T(4,128)S(1)} %get-tuple-element.29.plan, f32[1,3]{1,0:T(1,128)S(1)} %copy-done.3, s32[8,8]{1,0:T(8,128)S(1)} %copy-done, f32[8,128]{1,0:T(8,128)S(1)} %get-tuple-element.40.energy, ...), custom_call_target="tpu_custom_call" | custom-call | flops 1610612736 | bytes 786432 | tf_op jit(solution)/shard_map/contract/pallas_call | solution.py:440
  75.0 8.7 %contract.5.refs_17_ = f32[4,128,128]{2,1,0:T(8,128)S(1)} custom-call(s32[34]{0:T(128)S(1)} %pad_add_fusion.ints.where, s32[4,8]{1,0:T(4,128)S(1)} %get-tuple-element.29.plan, f32[1,3]{1,0:T(1,128)S(1)} %copy-done.3, s32[8,8]{1,0:T(8,128)S(1)} %copy-done, f32[8,128]{1,0:T(8,128)S(1)} %get-tuple-element.37.energy, ...), custom_call_target="tpu_custom_call" | custom-call | flops 3221225472 | bytes 1572864 | tf_op jit(solution)/shard_map/contract/pallas_call | solution.py:440
  84.0 1.8 %collective-permute-done.17.refs_15_ = bf16[256,1024]{1,0:T(8,128)(2,1)S(1)} collective-permute-done((bf16[256,1024]{1,0:T(8,128)(2,1)S(1)}, bf16[256,1024]{1,0:T(8,128)(2,1)S(1)}, u32[]{:S(2)}, u32[]{:S(2)}) %collective-permute-start.17) | collective-permute-done | bytes 524320 | tf_op jit(solution)/shard_map/ppermute | solution.py:552
  85.8 5.0 %contract.7 = (bf16[5,64,128]{2,1,0:T(8,128)(2,1)S(1)}, f32[5,64,128]{2,1,0:T(8,128)S(1)}) custom-call(s32[34]{0:T(128)S(1)} %pad_add_fusion.ints.where, s32[4,8]{1,0:T(4,128)S(1)} %get-tuple-element.29.plan, f32[1,3]{1,0:T(1,128)S(1)} %copy-done.3, s32[8,8]{1,0:T(8,128)S(1)} %copy-done, f32[8,128]{1,0:T(8,128)S(1)} %get-tuple-element.40.energy, ...), custom_call_target="tpu_custom_call" | custom-call | tf_op jit(solution)/shard_map/contract/pallas_call | solution.py:440
  90.8 1.2 %collective-permute-start.18 = (bf16[5,64,128]{2,1,0:T(8,128)(2,1)S(1)}, bf16[5,64,128]{2,1,0:T(8,128)(2,1)S(1)}, u32[]{:S(2)}, u32[]{:S(2)}) collective-permute-start(bf16[5,64,128]{2,1,0:T(8,128)(2,1)S(1)} %get-tuple-element.46), channel_id=1, source_target_pairs={{0,2},{1,3},{2,0},{3,1},{4,6},{5,7},{6,4},{7,5},{8,10},{9,11},{10,... | collective-permute-start | bytes 245768 | tf_op jit(solution)/shard_map/ppermute | solution.py:558
  91.9 3.4 %collective-permute-done.18 = bf16[5,64,128]{2,1,0:T(8,128)(2,1)S(1)} collective-permute-done((bf16[5,64,128]{2,1,0:T(8,128)(2,1)S(1)}, bf16[5,64,128]{2,1,0:T(8,128)(2,1)S(1)}, u32[]{:S(2)}, u32[]{:S(2)}) %collective-permute-start.18) | collective-permute-done | bytes 81952 | tf_op jit(solution)/shard_map/ppermute | solution.py:558
  95.5 1.3 %collective-permute-done.19.came = f32[6,32,128]{2,1,0:T(8,128)S(1)} collective-permute-done((f32[6,32,128]{2,1,0:T(8,128)S(1)}, f32[6,32,128]{2,1,0:T(8,128)S(1)}, u32[]{:S(2)}, u32[]{:S(2)}) %collective-permute-start.19) | collective-permute-done | bytes 98336 | tf_op jit(solution)/shard_map/ppermute | solution.py:562
  97.5 12.3 %all_to_all.5.came = bf16[8,2,32,128]{3,2,1,0:T(8,128)(2,1)S(1)} all-to-all(bf16[8,2,32,128]{3,2,1,0:T(8,128)(2,1)S(1)} %spread.1), channel_id=1, replica_groups=mesh['frag'=8,'aux'=4] {'frag'}, dimensions={0} | all-to-all | bytes 262144 | tf_op jit(solution)/shard_map/all_to_all | solution.py:564
  109.8 1.3 %collect.1 = f32[4,32,128]{2,1,0:T(8,128)} custom-call(s32[8,2]{1,0:T(8,128)S(1)} %get-tuple-element.28.target, bf16[8,2,32,128]{3,2,1,0:T(8,128)(2,1)S(1)} %all_to_all.5.came), custom_call_target="tpu_custom_call" | custom-call | tf_op jit(solution)/shard_map/collect/pallas_call | solution.py:490
  (44 shorter events, 8.7 us)
Async XLA Ops:
  1.5 0.7 copy-start.1
  4.6 49.7 %copy-start.2 = (bf16[4,128]{1,0:T(4,128)(2,1)S(1)}, bf16[4,128]{1,0:T(4,128)(2,1)}, u32[]{:S(2)}) copy-start(bf16[4,128]{1,0:T(4,128)(2,1)} %refs_0_.3) | copy-start | bytes 3076
  4.6 16.7 %collective-permute-start = (bf16[272,1024]{1,0:T(8,128)(2,1)S(1)}, bf16[272,1024]{1,0:T(8,128)(2,1)S(1)}, u32[]{:S(2)}, u32[]{:S(2)}) collective-permute-start(bf16[272,1024]{1,0:T(8,128)(2,1)S(1)} %get-tuple-element.26), channel_id=1, source_target_pairs={{0,8},{4,12},{16,24},{20,28},{8,0},{12,4},{24,16},{28,20},{1,9},{5... | collective-permute-start | bytes 1671176 | tf_op jit(solution)/shard_map/ppermute | solution.py:531
  7.8 25.2 %collective-permute-start.1 = (bf16[272,1024]{1,0:T(8,128)(2,1)S(1)}, bf16[272,1024]{1,0:T(8,128)(2,1)S(1)}, u32[]{:S(2)}, u32[]{:S(2)}) collective-permute-start(bf16[272,1024]{1,0:T(8,128)(2,1)S(1)} %get-tuple-element.30), channel_id=1, source_target_pairs={{0,4},{8,12},{16,20},{24,28},{4,0},{12,8},{20,16},{28,24},{1,5},{9... | collective-permute-start | bytes 1671176 | tf_op jit(solution)/shard_map/ppermute | solution.py:531
  9.5 23.5 %collective-permute-start.2 = (bf16[272,1024]{1,0:T(8,128)(2,1)S(1)}, bf16[272,1024]{1,0:T(8,128)(2,1)S(1)}, u32[]{:S(2)}, u32[]{:S(2)}) collective-permute-start(bf16[272,1024]{1,0:T(8,128)(2,1)S(1)} %get-tuple-element.31), channel_id=1, source_target_pairs={{4,8},{12,16},{20,24},{8,4},{16,12},{24,20},{5,9},{13,17},{21,25},... | collective-permute-start | bytes 1671176 | tf_op jit(solution)/shard_map/ppermute | solution.py:531
  10.2 22.9 %collective-permute-start.3 = (bf16[272,1024]{1,0:T(8,128)(2,1)S(1)}, bf16[272,1024]{1,0:T(8,128)(2,1)S(1)}, u32[]{:S(2)}, u32[]{:S(2)}) collective-permute-start(bf16[272,1024]{1,0:T(8,128)(2,1)S(1)} %get-tuple-element.32), channel_id=1, source_target_pairs={{8,16},{12,20},{16,8},{20,12},{9,17},{13,21},{17,9},{21,13},{10,18... | collective-permute-start | bytes 1671176 | tf_op jit(solution)/shard_map/ppermute | solution.py:531
  10.9 31.7 %collective-permute-start.7 = (bf16[272,1024]{1,0:T(8,128)(2,1)S(1)}, bf16[272,1024]{1,0:T(8,128)(2,1)S(1)}, u32[]{:S(2)}, u32[]{:S(2)}) collective-permute-start(bf16[272,1024]{1,0:T(8,128)(2,1)S(1)} %get-tuple-element.38.refs_0_), channel_id=1, source_target_pairs={{0,2},{1,3},{2,0},{3,1},{4,6},{5,7},{6,4},{7,5},{8,10},{9,11},{10,... | collective-permute-start | bytes 1671176 | tf_op jit(solution)/shard_map/ppermute | solution.py:520
  33.0 20.8 %collective-permute-start.4 = (bf16[272,1024]{1,0:T(8,128)(2,1)S(1)}, bf16[272,1024]{1,0:T(8,128)(2,1)S(1)}, u32[]{:S(2)}, u32[]{:S(2)}) collective-permute-start(bf16[272,1024]{1,0:T(8,128)(2,1)S(1)} %get-tuple-element.34), channel_id=1, source_target_pairs={{0,12},{4,16},{8,20},{12,0},{16,4},{20,8},{1,13},{5,17},{9,21},{13... | collective-permute-start | bytes 1671176 | tf_op jit(solution)/shard_map/ppermute | solution.py:531
  41.0 15.7 %copy-start = (s32[8,8]{1,0:T(8,128)S(1)}, s32[8,8]{1,0:T(8,128)}, u32[]{:S(2)}) copy-start(s32[8,8]{1,0:T(8,128)} %rows_ref.7) | copy-start | bytes 772
  41.0 15.7 %copy-start.3 = (f32[1,3]{1,0:T(1,128)S(1)}, f32[1,3]{1,0:T(1,128)}, u32[]{:S(2)}) copy-start(f32[1,3]{1,0:T(1,128)} %levels.7) | copy-start | bytes 40
  41.0 12.0 %collective-permute-start.5 = (bf16[256,1024]{1,0:T(8,128)(2,1)S(1)}, bf16[256,1024]{1,0:T(8,128)(2,1)S(1)}, u32[]{:S(2)}, u32[]{:S(2)}) collective-permute-start(bf16[256,1024]{1,0:T(8,128)(2,1)S(1)} %pack_group.3.refs_4_), channel_id=1, source_target_pairs={{0,2},{1,3},{2,0},{3,1},{4,6},{5,7},{6,4},{7,5},{8,10},{9,11},{10,... | collective-permute-start | bytes 1572872 | tf_op jit(solution)/shard_map/ppermute | solution.py:520
  42.6 12.5 %collective-permute-start.8 = (bf16[272,1024]{1,0:T(8,128)(2,1)S(1)}, bf16[272,1024]{1,0:T(8,128)(2,1)S(1)}, u32[]{:S(2)}, u32[]{:S(2)}) collective-permute-start(bf16[272,1024]{1,0:T(8,128)(2,1)S(1)} %get-tuple-element.38.refs_0_), channel_id=1, source_target_pairs={{0,1},{1,0},{2,3},{3,2},{4,5},{5,4},{6,7},{7,6},{8,9},{9,8},{10,11... | collective-permute-start | bytes 1671176 | tf_op jit(solution)/shard_map/ppermute | solution.py:521
  42.6 14.1 %collective-permute-start.9 = (bf16[272,1024]{1,0:T(8,128)(2,1)S(1)}, bf16[272,1024]{1,0:T(8,128)(2,1)S(1)}, u32[]{:S(2)}, u32[]{:S(2)}) collective-permute-start(bf16[272,1024]{1,0:T(8,128)(2,1)S(1)} %collective-permute-done.7.refs_1_), channel_id=1, source_target_pairs={{0,1},{1,0},{2,3},{3,2},{4,5},{5,4},{6,7},{7,6},{8,9},{9,8},{10,11... | collective-permute-start | bytes 1671176 | tf_op jit(solution)/shard_map/ppermute | solution.py:523
  53.0 10.6 %collective-permute-start.6 = (bf16[272,1024]{1,0:T(8,128)(2,1)S(1)}, bf16[272,1024]{1,0:T(8,128)(2,1)S(1)}, u32[]{:S(2)}, u32[]{:S(2)}) collective-permute-start(bf16[272,1024]{1,0:T(8,128)(2,1)S(1)} %get-tuple-element.36), channel_id=1, source_target_pairs={{12,24},{16,28},{24,12},{28,16},{13,25},{17,29},{25,13},{29,17},{1... | collective-permute-start | bytes 1671176 | tf_op jit(solution)/shard_map/ppermute | solution.py:531
  53.7 3.0 %collective-permute-start.10 = (bf16[256,1024]{1,0:T(8,128)(2,1)S(1)}, bf16[256,1024]{1,0:T(8,128)(2,1)S(1)}, u32[]{:S(2)}, u32[]{:S(2)}) collective-permute-start(bf16[256,1024]{1,0:T(8,128)(2,1)S(1)} %pack_group.3.refs_4_), channel_id=1, source_target_pairs={{0,1},{1,0},{2,3},{3,2},{4,5},{5,4},{6,7},{7,6},{8,9},{9,8},{10,11... | collective-permute-start | bytes 1572872 | tf_op jit(solution)/shard_map/ppermute | solution.py:521
  53.8 2.9 %collective-permute-start.11 = (bf16[256,1024]{1,0:T(8,128)(2,1)S(1)}, bf16[256,1024]{1,0:T(8,128)(2,1)S(1)}, u32[]{:S(2)}, u32[]{:S(2)}) collective-permute-start(bf16[256,1024]{1,0:T(8,128)(2,1)S(1)} %collective-permute-done.5.refs_5_), channel_id=1, source_target_pairs={{0,1},{1,0},{2,3},{3,2},{4,5},{5,4},{6,7},{7,6},{8,9},{9,8},{10,11... | collective-permute-start | bytes 1572872 | tf_op jit(solution)/shard_map/ppermute | solution.py:523
  55.1 14.0 %collective-permute-start.12 = (bf16[256,1024]{1,0:T(8,128)(2,1)S(1)}, bf16[256,1024]{1,0:T(8,128)(2,1)S(1)}, u32[]{:S(2)}, u32[]{:S(2)}) collective-permute-start(bf16[256,1024]{1,0:T(8,128)(2,1)S(1)} %get-tuple-element.41.refs_8_), channel_id=1, source_target_pairs={{0,2},{1,3},{2,0},{3,1},{4,6},{5,7},{6,4},{7,5},{8,10},{9,11},{10,... | collective-permute-start | bytes 1572872 | tf_op jit(solution)/shard_map/ppermute | solution.py:520
  64.4 4.6 %collective-permute-start.14 = (bf16[256,1024]{1,0:T(8,128)(2,1)S(1)}, bf16[256,1024]{1,0:T(8,128)(2,1)S(1)}, u32[]{:S(2)}, u32[]{:S(2)}) collective-permute-start(bf16[256,1024]{1,0:T(8,128)(2,1)S(1)} %get-tuple-element.42.refs_12_.refs_13_), channel_id=1, source_target_pairs={{0,1},{1,0},{2,3},{3,2},{4,5},{5,4},{6,7},{7,6},{8,9},{9,8},{10,11... | collective-permute-start | bytes 1572872 | tf_op jit(solution)/shard_map/ppermute | solution.py:547
  64.5 6.1 %collective-permute-start.13 = (bf16[256,1024]{1,0:T(8,128)(2,1)S(1)}, bf16[256,1024]{1,0:T(8,128)(2,1)S(1)}, u32[]{:S(2)}, u32[]{:S(2)}) collective-permute-start(bf16[256,1024]{1,0:T(8,128)(2,1)S(1)} %get-tuple-element.41.refs_8_), channel_id=1, source_target_pairs={{0,1},{1,0},{2,3},{3,2},{4,5},{5,4},{6,7},{7,6},{8,9},{9,8},{10,11... | collective-permute-start | bytes 1572872 | tf_op jit(solution)/shard_map/ppermute | solution.py:521
  69.1 1.9 %collective-permute-start.15 = (bf16[256,1024]{1,0:T(8,128)(2,1)S(1)}, bf16[256,1024]{1,0:T(8,128)(2,1)S(1)}, u32[]{:S(2)}, u32[]{:S(2)}) collective-permute-start(bf16[256,1024]{1,0:T(8,128)(2,1)S(1)} %collective-permute-done.12.refs_9_), channel_id=1, source_target_pairs={{0,1},{1,0},{2,3},{3,2},{4,5},{5,4},{6,7},{7,6},{8,9},{9,8},{10,11... | collective-permute-start | bytes 1572872 | tf_op jit(solution)/shard_map/ppermute | solution.py:523
  69.1 14.7 %collective-permute-start.16 = (bf16[256,1024]{1,0:T(8,128)(2,1)S(1)}, bf16[256,1024]{1,0:T(8,128)(2,1)S(1)}, u32[]{:S(2)}, u32[]{:S(2)}) collective-permute-start(bf16[256,1024]{1,0:T(8,128)(2,1)S(1)} %get-tuple-element.42.refs_12_.refs_13_), channel_id=1, source_target_pairs={{0,2},{1,3},{2,0},{3,1},{4,6},{5,7},{6,4},{7,5},{8,10},{9,11},{10,... | collective-permute-start | bytes 1572872 | tf_op jit(solution)/shard_map/ppermute | solution.py:548
  83.8 2.0 %collective-permute-start.17 = (bf16[256,1024]{1,0:T(8,128)(2,1)S(1)}, bf16[256,1024]{1,0:T(8,128)(2,1)S(1)}, u32[]{:S(2)}, u32[]{:S(2)}) collective-permute-start(bf16[256,1024]{1,0:T(8,128)(2,1)S(1)} %collective-permute-done.16.refs_13_), channel_id=1, source_target_pairs={{0,1},{1,0},{2,3},{3,2},{4,5},{5,4},{6,7},{7,6},{8,9},{9,8},{10,11... | collective-permute-start | bytes 1572872 | tf_op jit(solution)/shard_map/ppermute | solution.py:552
  90.8 4.6 %collective-permute-start.18 = (bf16[5,64,128]{2,1,0:T(8,128)(2,1)S(1)}, bf16[5,64,128]{2,1,0:T(8,128)(2,1)S(1)}, u32[]{:S(2)}, u32[]{:S(2)}) collective-permute-start(bf16[5,64,128]{2,1,0:T(8,128)(2,1)S(1)} %get-tuple-element.46), channel_id=1, source_target_pairs={{0,2},{1,3},{2,0},{3,1},{4,6},{5,7},{6,4},{7,5},{8,10},{9,11},{10,... | collective-permute-start | bytes 245768 | tf_op jit(solution)/shard_map/ppermute | solution.py:558
  95.5 1.4 %collective-permute-start.19 = (f32[6,32,128]{2,1,0:T(8,128)S(1)}, f32[6,32,128]{2,1,0:T(8,128)S(1)}, u32[]{:S(2)}, u32[]{:S(2)}) collective-permute-start(f32[6,32,128]{2,1,0:T(8,128)S(1)} %get-tuple-element.47), channel_id=1, source_target_pairs={{0,1},{1,0},{2,3},{3,2},{4,5},{5,4},{6,7},{7,6},{8,9},{9,8},{10,11... | collective-permute-start | bytes 294920 | tf_op jit(solution)/shard_map/ppermute | solution.py:562

commit v14 on v13

--- a/solution.py
+++ b/solution.py
@@ -532,9 +532,9 @@
 
     arrived = {code: send(code - 1) for code in (1, 2, 3, 4)}
     parts = over_aux(own)
-    arrived[5] = send(4, *(arrived[c] for c in (1, 2, 3, 4)))
     plan, target = plan_lists(after(ints, arrived[3]), vir_list, sizes)
     here = pack_group(2, block, plan, {c: arrived[c] for c in range(1, 5)})[0]
+    arrived[5] = send(4, here)
     parts += over_aux(here)
     arrived[6] = send(5, parts[5])
     here, early_energy = pack_group(

time: 111 us -> 111 us (level)
  no operation moved by 1% of the time
where the time goes in v14:
time: 111 us
  waiting for transfers between devices  39.2 us (35%)
  Pallas kernels  33.6 us (30%)
  starting transfers between devices  23.6 us (21%)
  blocking collectives  12.3 us (11%)
  other arithmetic  1.5 us (1%)
    pallas_call x4, Pallas kernels, contract(): pl.pallas_call(functools.partial(contract_kernel, stage, block, width), o...  24.7 us
    ppermute x6, waiting for transfers between devices, send(): return lax.ppermute(payload, 'frag', round_pairs(distance, parity, frags))  18.3 us
    ppermute x6, starting transfers between devices, send(): return lax.ppermute(payload, 'frag', round_pairs(distance, parity, frags))  14.2 us
    ppermute x3, waiting for transfers between devices, over_aux(): far = lax.ppermute(here, 'aux', far_pairs)  14 us
    all_to_all x1, blocking collectives, body(): incoming = lax.all_to_all(outgoing, 'frag', 0, 0, tiled=True)  12.3 us
    ppermute x3, starting transfers between devices, over_aux(): far = lax.ppermute(here, 'aux', far_pairs)  4.75 us
    ppermute x1, waiting for transfers between devices, body(): met = lax.ppermute(sent, 'aux', far_pairs).astype(jnp.float32)  3.43 us
    pallas_call x1, Pallas kernels, pack_to_send(): pl.pallas_call(functools.partial(send_kernel, sizes), out_shape=(part,) *...  2.42 us
  transfers between devices with their start and end apart: 20, of which 8 were waited for; matrix products, arithmetic and copies ran while one was open for 0% of the time, Pallas kernels for 22%

profile of v14, /device:TPU:0, one launch (start us, length us, event | category | flops | bytes accessed | tf_op | source)
XLA Modules:
  0.0 111.1 jit_solution(1672478637745326869)
XLA Ops:
  2.1 2.4 %pack_to_send.1 = (bf16[272,1024]{1,0:T(8,128)(2,1)S(1)}, bf16[272,1024]{1,0:T(8,128)(2,1)S(1)}, bf16[272,1024]{1,0:T(8,128)(2,1)S(1)}, bf16[272,1024]{1,0:T(8,1...) custom-call(s32[34]{0:T(128)S(1)} %pad_add_fusion.ints.where, ...), custom_call_target="tpu_custom_call" | custom-call | tf_op jit(solution)/shard_map/pack_to_send/pallas_call | solution.py:80
  4.6 3.5 %collective-permute-start = (bf16[272,1024]{1,0:T(8,128)(2,1)S(1)}, bf16[272,1024]{1,0:T(8,128)(2,1)S(1)}, u32[]{:S(2)}, u32[]{:S(2)}) collective-permute-start(bf16[272,1024]{1,0:T(8,128)(2,1)S(1)} %get-tuple-element.26), channel_id=1, source_target_pairs={{0,8},{4,12},{16,24},{20,28},{8,0},{12,4},{24,16},{28,20},{1,9},{5... | collective-permute-start | bytes 1671176 | tf_op jit(solution)/shard_map/ppermute | solution.py:531
  8.1 1.1 %collective-permute-start.1 = (bf16[272,1024]{1,0:T(8,128)(2,1)S(1)}, bf16[272,1024]{1,0:T(8,128)(2,1)S(1)}, u32[]{:S(2)}, u32[]{:S(2)}) collective-permute-start(bf16[272,1024]{1,0:T(8,128)(2,1)S(1)} %get-tuple-element.30), channel_id=1, source_target_pairs={{0,4},{8,12},{16,20},{24,28},{4,0},{12,8},{20,16},{28,24},{1,5},{9... | collective-permute-start | bytes 1671176 | tf_op jit(solution)/shard_map/ppermute | solution.py:531
  10.6 1.6 %collective-permute-start.7 = (bf16[272,1024]{1,0:T(8,128)(2,1)S(1)}, bf16[272,1024]{1,0:T(8,128)(2,1)S(1)}, u32[]{:S(2)}, u32[]{:S(2)}) collective-permute-start(bf16[272,1024]{1,0:T(8,128)(2,1)S(1)} %get-tuple-element.38.refs_0_), channel_id=1, source_target_pairs={{0,2},{1,3},{2,0},{3,1},{4,6},{5,7},{6,4},{7,5},{8,10},{9,11},{10,... | collective-permute-start | bytes 1671176 | tf_op jit(solution)/shard_map/ppermute | solution.py:520
  12.2 9.4 %collective-permute-done.refs_2_.refs_3_ = bf16[272,1024]{1,0:T(8,128)(2,1)S(1)} collective-permute-done((bf16[272,1024]{1,0:T(8,128)(2,1)S(1)}, bf16[272,1024]{1,0:T(8,128)(2,1)S(1)}, u32[]{:S(2)}, u32[]{:S(2)}) %collective-permute-start) | collective-permute-done | bytes 557088 | tf_op jit(solution)/shard_map/ppermute | solution.py:531
  21.6 2.2 %plan_lists.1 = (s32[4,8]{1,0:T(4,128)S(1)}, s32[8,2]{1,0:T(8,128)S(1)}) custom-call(s32[34]{0:T(128)S(1)} %pad_add_fusion.ints.where, s32[8,8]{1,0:T(8,128)S(1)} %copy-done.1), custom_call_target="tpu_custom_call" | custom-call | tf_op jit(solution)/shard_map/plan_lists/pallas_call | solution.py:135
  23.8 9.0 %collective-permute-done.1.refs_0_.refs_1_ = bf16[272,1024]{1,0:T(8,128)(2,1)S(1)} collective-permute-done((bf16[272,1024]{1,0:T(8,128)(2,1)S(1)}, bf16[272,1024]{1,0:T(8,128)(2,1)S(1)}, u32[]{:S(2)}, u32[]{:S(2)}) %collective-permute-start.1) | collective-permute-done | bytes 557088 | tf_op jit(solution)/shard_map/ppermute | solution.py:531
  33.5 7.5 %collective-permute-start.4 = (bf16[272,1024]{1,0:T(8,128)(2,1)S(1)}, bf16[272,1024]{1,0:T(8,128)(2,1)S(1)}, u32[]{:S(2)}, u32[]{:S(2)}) collective-permute-start(bf16[272,1024]{1,0:T(8,128)(2,1)S(1)} %get-tuple-element.34), channel_id=1, source_target_pairs={{0,12},{4,16},{8,20},{12,0},{16,4},{20,8},{1,13},{5,17},{9,21},{13... | collective-permute-start | bytes 1671176 | tf_op jit(solution)/shard_map/ppermute | solution.py:531
  41.0 1.6 %collective-permute-start.5 = (bf16[256,1024]{1,0:T(8,128)(2,1)S(1)}, bf16[256,1024]{1,0:T(8,128)(2,1)S(1)}, u32[]{:S(2)}, u32[]{:S(2)}) collective-permute-start(bf16[256,1024]{1,0:T(8,128)(2,1)S(1)} %pack_group.3.refs_4_), channel_id=1, source_target_pairs={{0,2},{1,3},{2,0},{3,1},{4,6},{5,7},{6,4},{7,5},{8,10},{9,11},{10,... | collective-permute-start | bytes 1572872 | tf_op jit(solution)/shard_map/ppermute | solution.py:520
  43.1 9.9 %collective-permute-done.5.refs_5_ = bf16[256,1024]{1,0:T(8,128)(2,1)S(1)} collective-permute-done((bf16[256,1024]{1,0:T(8,128)(2,1)S(1)}, bf16[256,1024]{1,0:T(8,128)(2,1)S(1)}, u32[]{:S(2)}, u32[]{:S(2)}) %collective-permute-start.5) | collective-permute-done | bytes 524320 | tf_op jit(solution)/shard_map/ppermute | solution.py:520
  55.1 1.6 %collective-permute-start.12 = (bf16[256,1024]{1,0:T(8,128)(2,1)S(1)}, bf16[256,1024]{1,0:T(8,128)(2,1)S(1)}, u32[]{:S(2)}, u32[]{:S(2)}) collective-permute-start(bf16[256,1024]{1,0:T(8,128)(2,1)S(1)} %get-tuple-element.41.refs_8_), channel_id=1, source_target_pairs={{0,2},{1,3},{2,0},{3,1},{4,6},{5,7},{6,4},{7,5},{8,10},{9,11},{10,... | collective-permute-start | bytes 1572872 | tf_op jit(solution)/shard_map/ppermute | solution.py:520
  56.7 6.9 %contract.4.refs_16_ = f32[1,128,128]{2,1,0:T(8,128)S(1)} custom-call(s32[34]{0:T(128)S(1)} %pad_add_fusion.ints.where, s32[4,8]{1,0:T(4,128)S(1)} %get-tuple-element.29.plan, f32[1,3]{1,0:T(1,128)S(1)} %copy-done.3, s32[8,8]{1,0:T(8,128)S(1)} %copy-done, f32[8,128]{1,0:T(8,128)S(1)} %get-tuple-element.37.energy, ...), custom_call_target="tpu_custom_call" | custom-call | tf_op jit(solution)/shard_map/contract/pallas_call | solution.py:440
  63.6 0.8 pack_group.5
  65.0 4.0 %collective-permute-done.12.refs_9_ = bf16[256,1024]{1,0:T(8,128)(2,1)S(1)} collective-permute-done((bf16[256,1024]{1,0:T(8,128)(2,1)S(1)}, bf16[256,1024]{1,0:T(8,128)(2,1)S(1)}, u32[]{:S(2)}, u32[]{:S(2)}) %collective-permute-start.12) | collective-permute-done | bytes 524320 | tf_op jit(solution)/shard_map/ppermute | solution.py:520
  69.1 1.5 %collective-permute-start.16 = (bf16[256,1024]{1,0:T(8,128)(2,1)S(1)}, bf16[256,1024]{1,0:T(8,128)(2,1)S(1)}, u32[]{:S(2)}, u32[]{:S(2)}) collective-permute-start(bf16[256,1024]{1,0:T(8,128)(2,1)S(1)} %get-tuple-element.42.refs_12_.refs_13_), channel_id=1, source_target_pairs={{0,2},{1,3},{2,0},{3,1},{4,6},{5,7},{6,4},{7,5},{8,10},{9,11},{10,... | collective-permute-start | bytes 1572872 | tf_op jit(solution)/shard_map/ppermute | solution.py:548
  71.0 4.1 %contract.6.refs_18_ = f32[1536,256]{1,0:T(8,128)S(1)} custom-call(s32[34]{0:T(128)S(1)} %pad_add_fusion.ints.where, s32[4,8]{1,0:T(4,128)S(1)} %get-tuple-element.29.plan, f32[1,3]{1,0:T(1,128)S(1)} %copy-done.3, s32[8,8]{1,0:T(8,128)S(1)} %copy-done, f32[8,128]{1,0:T(8,128)S(1)} %get-tuple-element.40.energy, ...), custom_call_target="tpu_custom_call" | custom-call | flops 1610612736 | bytes 786432 | tf_op jit(solution)/shard_map/contract/pallas_call | solution.py:440
  75.0 8.7 %contract.5.refs_17_ = f32[4,128,128]{2,1,0:T(8,128)S(1)} custom-call(s32[34]{0:T(128)S(1)} %pad_add_fusion.ints.where, s32[4,8]{1,0:T(4,128)S(1)} %get-tuple-element.29.plan, f32[1,3]{1,0:T(1,128)S(1)} %copy-done.3, s32[8,8]{1,0:T(8,128)S(1)} %copy-done, f32[8,128]{1,0:T(8,128)S(1)} %get-tuple-element.37.energy, ...), custom_call_target="tpu_custom_call" | custom-call | flops 3221225472 | bytes 1572864 | tf_op jit(solution)/shard_map/contract/pallas_call | solution.py:440
  84.0 1.8 %collective-permute-done.17.refs_15_ = bf16[256,1024]{1,0:T(8,128)(2,1)S(1)} collective-permute-done((bf16[256,1024]{1,0:T(8,128)(2,1)S(1)}, bf16[256,1024]{1,0:T(8,128)(2,1)S(1)}, u32[]{:S(2)}, u32[]{:S(2)}) %collective-permute-start.17) | collective-permute-done | bytes 524320 | tf_op jit(solution)/shard_map/ppermute | solution.py:552
  85.7 5.1 %contract.7 = (bf16[5,64,128]{2,1,0:T(8,128)(2,1)S(1)}, f32[5,64,128]{2,1,0:T(8,128)S(1)}) custom-call(s32[34]{0:T(128)S(1)} %pad_add_fusion.ints.where, s32[4,8]{1,0:T(4,128)S(1)} %get-tuple-element.29.plan, f32[1,3]{1,0:T(1,128)S(1)} %copy-done.3, s32[8,8]{1,0:T(8,128)S(1)} %copy-done, f32[8,128]{1,0:T(8,128)S(1)} %get-tuple-element.40.energy, ...), custom_call_target="tpu_custom_call" | custom-call | tf_op jit(solution)/shard_map/contract/pallas_call | solution.py:440
  90.8 1.1 %collective-permute-start.18 = (bf16[5,64,128]{2,1,0:T(8,128)(2,1)S(1)}, bf16[5,64,128]{2,1,0:T(8,128)(2,1)S(1)}, u32[]{:S(2)}, u32[]{:S(2)}) collective-permute-start(bf16[5,64,128]{2,1,0:T(8,128)(2,1)S(1)} %get-tuple-element.46), channel_id=1, source_target_pairs={{0,2},{1,3},{2,0},{3,1},{4,6},{5,7},{6,4},{7,5},{8,10},{9,11},{10,... | collective-permute-start | bytes 245768 | tf_op jit(solution)/shard_map/ppermute | solution.py:558
  91.9 3.4 %collective-permute-done.18 = bf16[5,64,128]{2,1,0:T(8,128)(2,1)S(1)} collective-permute-done((bf16[5,64,128]{2,1,0:T(8,128)(2,1)S(1)}, bf16[5,64,128]{2,1,0:T(8,128)(2,1)S(1)}, u32[]{:S(2)}, u32[]{:S(2)}) %collective-permute-start.18) | collective-permute-done | bytes 81952 | tf_op jit(solution)/shard_map/ppermute | solution.py:558
  95.6 1.3 %collective-permute-done.19.came = f32[6,32,128]{2,1,0:T(8,128)S(1)} collective-permute-done((f32[6,32,128]{2,1,0:T(8,128)S(1)}, f32[6,32,128]{2,1,0:T(8,128)S(1)}, u32[]{:S(2)}, u32[]{:S(2)}) %collective-permute-start.19) | collective-permute-done | bytes 98336 | tf_op jit(solution)/shard_map/ppermute | solution.py:562
  97.5 12.3 %all_to_all.5.came = bf16[8,2,32,128]{3,2,1,0:T(8,128)(2,1)S(1)} all-to-all(bf16[8,2,32,128]{3,2,1,0:T(8,128)(2,1)S(1)} %spread.1), channel_id=1, replica_groups=mesh['frag'=8,'aux'=4] {'frag'}, dimensions={0} | all-to-all | bytes 262144 | tf_op jit(solution)/shard_map/all_to_all | solution.py:564
  109.7 1.3 %collect.1 = f32[4,32,128]{2,1,0:T(8,128)} custom-call(s32[8,2]{1,0:T(8,128)S(1)} %get-tuple-element.28.target, bf16[8,2,32,128]{3,2,1,0:T(8,128)(2,1)S(1)} %all_to_all.5.came), custom_call_target="tpu_custom_call" | custom-call | tf_op jit(solution)/shard_map/collect/pallas_call | solution.py:490
  (44 shorter events, 8.7 us)
Async XLA Ops:
  1.5 0.7 copy-start.1
  4.6 49.7 %copy-start.2 = (bf16[4,128]{1,0:T(4,128)(2,1)S(1)}, bf16[4,128]{1,0:T(4,128)(2,1)}, u32[]{:S(2)}) copy-start(bf16[4,128]{1,0:T(4,128)(2,1)} %refs_0_.3) | copy-start | bytes 3076
  4.6 17.0 %collective-permute-start = (bf16[272,1024]{1,0:T(8,128)(2,1)S(1)}, bf16[272,1024]{1,0:T(8,128)(2,1)S(1)}, u32[]{:S(2)}, u32[]{:S(2)}) collective-permute-start(bf16[272,1024]{1,0:T(8,128)(2,1)S(1)} %get-tuple-element.26), channel_id=1, source_target_pairs={{0,8},{4,12},{16,24},{20,28},{8,0},{12,4},{24,16},{28,20},{1,9},{5... | collective-permute-start | bytes 1671176 | tf_op jit(solution)/shard_map/ppermute | solution.py:531
  8.1 24.7 %collective-permute-start.1 = (bf16[272,1024]{1,0:T(8,128)(2,1)S(1)}, bf16[272,1024]{1,0:T(8,128)(2,1)S(1)}, u32[]{:S(2)}, u32[]{:S(2)}) collective-permute-start(bf16[272,1024]{1,0:T(8,128)(2,1)S(1)} %get-tuple-element.30), channel_id=1, source_target_pairs={{0,4},{8,12},{16,20},{24,28},{4,0},{12,8},{20,16},{28,24},{1,5},{9... | collective-permute-start | bytes 1671176 | tf_op jit(solution)/shard_map/ppermute | solution.py:531
  9.2 23.5 %collective-permute-start.2 = (bf16[272,1024]{1,0:T(8,128)(2,1)S(1)}, bf16[272,1024]{1,0:T(8,128)(2,1)S(1)}, u32[]{:S(2)}, u32[]{:S(2)}) collective-permute-start(bf16[272,1024]{1,0:T(8,128)(2,1)S(1)} %get-tuple-element.31), channel_id=1, source_target_pairs={{4,8},{12,16},{20,24},{8,4},{16,12},{24,20},{5,9},{13,17},{21,25},... | collective-permute-start | bytes 1671176 | tf_op jit(solution)/shard_map/ppermute | solution.py:531
  9.9 22.9 %collective-permute-start.3 = (bf16[272,1024]{1,0:T(8,128)(2,1)S(1)}, bf16[272,1024]{1,0:T(8,128)(2,1)S(1)}, u32[]{:S(2)}, u32[]{:S(2)}) collective-permute-start(bf16[272,1024]{1,0:T(8,128)(2,1)S(1)} %get-tuple-element.32), channel_id=1, source_target_pairs={{8,16},{12,20},{16,8},{20,12},{9,17},{13,21},{17,9},{21,13},{10,18... | collective-permute-start | bytes 1671176 | tf_op jit(solution)/shard_map/ppermute | solution.py:531
  10.6 32.0 %collective-permute-start.7 = (bf16[272,1024]{1,0:T(8,128)(2,1)S(1)}, bf16[272,1024]{1,0:T(8,128)(2,1)S(1)}, u32[]{:S(2)}, u32[]{:S(2)}) collective-permute-start(bf16[272,1024]{1,0:T(8,128)(2,1)S(1)} %get-tuple-element.38.refs_0_), channel_id=1, source_target_pairs={{0,2},{1,3},{2,0},{3,1},{4,6},{5,7},{6,4},{7,5},{8,10},{9,11},{10,... | collective-permute-start | bytes 1671176 | tf_op jit(solution)/shard_map/ppermute | solution.py:520
  33.5 23.2 %copy-start = (s32[8,8]{1,0:T(8,128)S(1)}, s32[8,8]{1,0:T(8,128)}, u32[]{:S(2)}) copy-start(s32[8,8]{1,0:T(8,128)} %rows_ref.7) | copy-start | bytes 772
  33.5 23.2 %copy-start.3 = (f32[1,3]{1,0:T(1,128)S(1)}, f32[1,3]{1,0:T(1,128)}, u32[]{:S(2)}) copy-start(f32[1,3]{1,0:T(1,128)} %levels.7) | copy-start | bytes 40
  33.5 20.3 %collective-permute-start.4 = (bf16[272,1024]{1,0:T(8,128)(2,1)S(1)}, bf16[272,1024]{1,0:T(8,128)(2,1)S(1)}, u32[]{:S(2)}, u32[]{:S(2)}) collective-permute-start(bf16[272,1024]{1,0:T(8,128)(2,1)S(1)} %get-tuple-element.34), channel_id=1, source_target_pairs={{0,12},{4,16},{8,20},{12,0},{16,4},{20,8},{1,13},{5,17},{9,21},{13... | collective-permute-start | bytes 1671176 | tf_op jit(solution)/shard_map/ppermute | solution.py:531
  41.0 12.0 %collective-permute-start.5 = (bf16[256,1024]{1,0:T(8,128)(2,1)S(1)}, bf16[256,1024]{1,0:T(8,128)(2,1)S(1)}, u32[]{:S(2)}, u32[]{:S(2)}) collective-permute-start(bf16[256,1024]{1,0:T(8,128)(2,1)S(1)} %pack_group.3.refs_4_), channel_id=1, source_target_pairs={{0,2},{1,3},{2,0},{3,1},{4,6},{5,7},{6,4},{7,5},{8,10},{9,11},{10,... | collective-permute-start | bytes 1572872 | tf_op jit(solution)/shard_map/ppermute | solution.py:520
  42.6 12.5 %collective-permute-start.8 = (bf16[272,1024]{1,0:T(8,128)(2,1)S(1)}, bf16[272,1024]{1,0:T(8,128)(2,1)S(1)}, u32[]{:S(2)}, u32[]{:S(2)}) collective-permute-start(bf16[272,1024]{1,0:T(8,128)(2,1)S(1)} %get-tuple-element.38.refs_0_), channel_id=1, source_target_pairs={{0,1},{1,0},{2,3},{3,2},{4,5},{5,4},{6,7},{7,6},{8,9},{9,8},{10,11... | collective-permute-start | bytes 1671176 | tf_op jit(solution)/shard_map/ppermute | solution.py:521
  42.6 14.1 %collective-permute-start.9 = (bf16[272,1024]{1,0:T(8,128)(2,1)S(1)}, bf16[272,1024]{1,0:T(8,128)(2,1)S(1)}, u32[]{:S(2)}, u32[]{:S(2)}) collective-permute-start(bf16[272,1024]{1,0:T(8,128)(2,1)S(1)} %collective-permute-done.7.refs_1_), channel_id=1, source_target_pairs={{0,1},{1,0},{2,3},{3,2},{4,5},{5,4},{6,7},{7,6},{8,9},{9,8},{10,11... | collective-permute-start | bytes 1671176 | tf_op jit(solution)/shard_map/ppermute | solution.py:523
  53.0 10.6 %collective-permute-start.6 = (bf16[272,1024]{1,0:T(8,128)(2,1)S(1)}, bf16[272,1024]{1,0:T(8,128)(2,1)S(1)}, u32[]{:S(2)}, u32[]{:S(2)}) collective-permute-start(bf16[272,1024]{1,0:T(8,128)(2,1)S(1)} %get-tuple-element.36), channel_id=1, source_target_pairs={{12,24},{16,28},{24,12},{28,16},{13,25},{17,29},{25,13},{29,17},{1... | collective-permute-start | bytes 1671176 | tf_op jit(solution)/shard_map/ppermute | solution.py:531
  53.7 3.0 %collective-permute-start.10 = (bf16[256,1024]{1,0:T(8,128)(2,1)S(1)}, bf16[256,1024]{1,0:T(8,128)(2,1)S(1)}, u32[]{:S(2)}, u32[]{:S(2)}) collective-permute-start(bf16[256,1024]{1,0:T(8,128)(2,1)S(1)} %pack_group.3.refs_4_), channel_id=1, source_target_pairs={{0,1},{1,0},{2,3},{3,2},{4,5},{5,4},{6,7},{7,6},{8,9},{9,8},{10,11... | collective-permute-start | bytes 1572872 | tf_op jit(solution)/shard_map/ppermute | solution.py:521
  53.8 2.9 %collective-permute-start.11 = (bf16[256,1024]{1,0:T(8,128)(2,1)S(1)}, bf16[256,1024]{1,0:T(8,128)(2,1)S(1)}, u32[]{:S(2)}, u32[]{:S(2)}) collective-permute-start(bf16[256,1024]{1,0:T(8,128)(2,1)S(1)} %collective-permute-done.5.refs_5_), channel_id=1, source_target_pairs={{0,1},{1,0},{2,3},{3,2},{4,5},{5,4},{6,7},{7,6},{8,9},{9,8},{10,11... | collective-permute-start | bytes 1572872 | tf_op jit(solution)/shard_map/ppermute | solution.py:523
  55.1 14.0 %collective-permute-start.12 = (bf16[256,1024]{1,0:T(8,128)(2,1)S(1)}, bf16[256,1024]{1,0:T(8,128)(2,1)S(1)}, u32[]{:S(2)}, u32[]{:S(2)}) collective-permute-start(bf16[256,1024]{1,0:T(8,128)(2,1)S(1)} %get-tuple-element.41.refs_8_), channel_id=1, source_target_pairs={{0,2},{1,3},{2,0},{3,1},{4,6},{5,7},{6,4},{7,5},{8,10},{9,11},{10,... | collective-permute-start | bytes 1572872 | tf_op jit(solution)/shard_map/ppermute | solution.py:520
  64.4 4.6 %collective-permute-start.14 = (bf16[256,1024]{1,0:T(8,128)(2,1)S(1)}, bf16[256,1024]{1,0:T(8,128)(2,1)S(1)}, u32[]{:S(2)}, u32[]{:S(2)}) collective-permute-start(bf16[256,1024]{1,0:T(8,128)(2,1)S(1)} %get-tuple-element.42.refs_12_.refs_13_), channel_id=1, source_target_pairs={{0,1},{1,0},{2,3},{3,2},{4,5},{5,4},{6,7},{7,6},{8,9},{9,8},{10,11... | collective-permute-start | bytes 1572872 | tf_op jit(solution)/shard_map/ppermute | solution.py:547
  64.5 6.1 %collective-permute-start.13 = (bf16[256,1024]{1,0:T(8,128)(2,1)S(1)}, bf16[256,1024]{1,0:T(8,128)(2,1)S(1)}, u32[]{:S(2)}, u32[]{:S(2)}) collective-permute-start(bf16[256,1024]{1,0:T(8,128)(2,1)S(1)} %get-tuple-element.41.refs_8_), channel_id=1, source_target_pairs={{0,1},{1,0},{2,3},{3,2},{4,5},{5,4},{6,7},{7,6},{8,9},{9,8},{10,11... | collective-permute-start | bytes 1572872 | tf_op jit(solution)/shard_map/ppermute | solution.py:521
  69.1 1.9 %collective-permute-start.15 = (bf16[256,1024]{1,0:T(8,128)(2,1)S(1)}, bf16[256,1024]{1,0:T(8,128)(2,1)S(1)}, u32[]{:S(2)}, u32[]{:S(2)}) collective-permute-start(bf16[256,1024]{1,0:T(8,128)(2,1)S(1)} %collective-permute-done.12.refs_9_), channel_id=1, source_target_pairs={{0,1},{1,0},{2,3},{3,2},{4,5},{5,4},{6,7},{7,6},{8,9},{9,8},{10,11... | collective-permute-start | bytes 1572872 | tf_op jit(solution)/shard_map/ppermute | solution.py:523
  69.1 14.7 %collective-permute-start.16 = (bf16[256,1024]{1,0:T(8,128)(2,1)S(1)}, bf16[256,1024]{1,0:T(8,128)(2,1)S(1)}, u32[]{:S(2)}, u32[]{:S(2)}) collective-permute-start(bf16[256,1024]{1,0:T(8,128)(2,1)S(1)} %get-tuple-element.42.refs_12_.refs_13_), channel_id=1, source_target_pairs={{0,2},{1,3},{2,0},{3,1},{4,6},{5,7},{6,4},{7,5},{8,10},{9,11},{10,... | collective-permute-start | bytes 1572872 | tf_op jit(solution)/shard_map/ppermute | solution.py:548
  83.8 2.0 %collective-permute-start.17 = (bf16[256,1024]{1,0:T(8,128)(2,1)S(1)}, bf16[256,1024]{1,0:T(8,128)(2,1)S(1)}, u32[]{:S(2)}, u32[]{:S(2)}) collective-permute-start(bf16[256,1024]{1,0:T(8,128)(2,1)S(1)} %collective-permute-done.16.refs_13_), channel_id=1, source_target_pairs={{0,1},{1,0},{2,3},{3,2},{4,5},{5,4},{6,7},{7,6},{8,9},{9,8},{10,11... | collective-permute-start | bytes 1572872 | tf_op jit(solution)/shard_map/ppermute | solution.py:552
  90.8 4.6 %collective-permute-start.18 = (bf16[5,64,128]{2,1,0:T(8,128)(2,1)S(1)}, bf16[5,64,128]{2,1,0:T(8,128)(2,1)S(1)}, u32[]{:S(2)}, u32[]{:S(2)}) collective-permute-start(bf16[5,64,128]{2,1,0:T(8,128)(2,1)S(1)} %get-tuple-element.46), channel_id=1, source_target_pairs={{0,2},{1,3},{2,0},{3,1},{4,6},{5,7},{6,4},{7,5},{8,10},{9,11},{10,... | collective-permute-start | bytes 245768 | tf_op jit(solution)/shard_map/ppermute | solution.py:558
  95.5 1.4 %collective-permute-start.19 = (f32[6,32,128]{2,1,0:T(8,128)S(1)}, f32[6,32,128]{2,1,0:T(8,128)S(1)}, u32[]{:S(2)}, u32[]{:S(2)}) collective-permute-start(f32[6,32,128]{2,1,0:T(8,128)S(1)} %get-tuple-element.47), channel_id=1, source_target_pairs={{0,1},{1,0},{2,3},{3,2},{4,5},{5,4},{6,7},{7,6},{8,9},{9,8},{10,11... | collective-permute-start | bytes 294920 | tf_op jit(solution)/shard_map/ppermute | solution.py:562
